TPU v7x, 512 devices: a whole 4x8x8 slice. The times are simulated.
512 devices in a mesh: gx: 8 (over x, core), gy: 8 (over z), gz: 8 (over y).
Axes of the slice: x: 4, y: 8, z: 8, core: 2. Of those that a mesh axis runs over, the one named last changes fastest.
Arguments:
- right_side: float32 [3, 64, 128, 1024], P(None, 'gx', 'gy', 'gz'), may hold values from -8 to 10
- iterate: float32 [3, 64, 128, 1024], P(None, 'gx', 'gy', 'gz'), may hold values from -4 to 4
- state: float32 [3, 64, 128, 1024], P(None, 'gx', 'gy', 'gz'), may hold values from -6 to 6
- classes: int32 [64, 128, 1024], P('gx', 'gy', 'gz'), may hold values from 0 to 15
- load_mask: int32 [64, 128, 1024], P('gx', 'gy', 'gz'), may hold values 0 or 1
- fixed_mask: int32 [64, 128, 1024], P('gx', 'gy', 'gz'), may hold values 0 or 1
Outputs:
- solution: float32 [3, 64, 128, 1024], P(None, 'gx', 'gy', 'gz')
- residual: float32 [3, 64, 128, 1024], P(None, 'gx', 'gy', 'gz')
- filtered: float32 [64, 128, 1024], P('gx', 'gy', 'gz')
All inputs are finite; a program needn't handle non-finite values. No bound on the sum of `load_mask` or of `fixed_mask` on one device may be relied on, other than what follows from the above.
Results may differ from a plain program's by a relative error of at most 0.0003.
Values sent between devices are 32-bit elements; how exact they have to be, the bound alone decides.
No kernel may reach another device: no remote copies, remote signals or barrier semaphores. Data moves between devices by JAX's collectives and lax.ppermute only.
A program may use at most 128 MiB of HBM per device.

v0:
```python
import math

import jax
import jax.numpy as jnp
from jax import lax
from jax.sharding import PartitionSpec as P

LEVELS = 4
COARSE_SWEEPS = 4
CLASSES = 16
RADIUS = 3


rho_floor = 0.25
penalty = 4.0
sweep_first = 0.55
sweep_second = 1.05
coarse_weight = 0.6
couple = ((2.0, 1.0, 1.0), (1.0, 2.0, 1.0), (1.0, 1.0, 2.0))


def padded_2(x, sides, width):
    for axis, dim in sides:
        devices, length = (lax.axis_size(axis), x.shape[dim])
        up = [(i, (i + 1) % devices) for i in range(devices - 1)]
        down = [(j, i) for i, j in up]
        last = lax.slice_in_dim(x, length - width, length, axis=dim)
        first = lax.slice_in_dim(x, 0, width, axis=dim)
        before = lax.ppermute(last, axis, up)
        after = lax.ppermute(first, axis, down)
        x = jnp.concatenate([before, x, after], axis=dim)
    return x


def neighbour(padded, direction, step, width):
    lead = padded.ndim - 3
    starts = [0] * padded.ndim
    limits = list(padded.shape)
    for spatial in range(3):
        starts[lead + spatial] = width
        limits[lead + spatial] = padded.shape[lead + spatial] - width
    starts[lead + direction] = starts[lead + direction] + step
    limits[lead + direction] = limits[lead + direction] + step
    return lax.slice(padded, starts, limits)


def level_ops(energy, padded, pen, scale):
    faces = []
    for direction in range(3):
        pair = []
        for step in (-1, 1):
            near = neighbour(padded, direction, step, 1)
            harmonic = 2.0 * energy * near / (energy + near)
            pair.append(jnp.where(near > 0.0, harmonic, energy))
        faces.append(pair)
    rows = []
    for component in range(3):
        total = jnp.zeros_like(energy)
        for direction in range(3):
            total = total + couple[component][direction] * (
                faces[direction][0] + faces[direction][1]
            )
        rows.append(scale * total + pen)
    return (faces, jnp.stack(rows), pen, scale)


def apply_padded(padded, field, ops):
    faces, diagonal, pen, scale = ops
    rows = []
    for component in range(3):
        total = jnp.zeros_like(pen)
        for direction in range(3):
            part = jnp.zeros_like(pen)
            for side, step in enumerate((-1, 1)):
                near = neighbour(padded[component], direction, step, 1)
                part = part + faces[direction][side] * (field[component] - near)
            total = total + couple[component][direction] * part
        rows.append(scale * total + pen * field[component])
    return jnp.stack(rows)


def restrict(field):
    shape = field.shape
    lead = tuple(shape[:-3])
    count = len(lead)
    grouped = field.reshape(lead + (shape[-3] // 2, 2, shape[-2] // 2, 2, shape[-1] // 2, 2))
    return grouped.sum(axis=(count + 1, count + 3, count + 5))


def prolong(field):
    shape = field.shape
    lead = tuple(shape[:-3])
    grouped = field[..., :, None, :, None, :, None]
    grouped = jnp.broadcast_to(grouped, lead + (shape[-3], 2, shape[-2], 2, shape[-1], 2))
    return grouped.reshape(lead + (shape[-3] * 2, shape[-2] * 2, shape[-1] * 2))


def spread_ops(energy, pen, scale):
    padded = padded_2(energy, (("gx", 0), ("gy", 1), ("gz", 2)), 1)
    return level_ops(energy, padded, pen, scale)


def level_padding(field):
    return padded_2(field, (("gx", 1), ("gy", 2), ("gz", 3)), 1)


def coarsest_padding(field):
    return padded_2(field, (("gx", 1), ("gy", 2), ("gz", 3)), 1)


def smooth(field, rhs, ops, weight):
    return field + weight * (rhs - apply_padded(level_padding(field), field, ops)) / ops[1]


def vcycle(levels, level, rhs):
    ops = levels[level]
    diagonal = ops[1]
    if level == LEVELS - 1:
        field = coarse_weight * rhs / diagonal
        for sweep in range(COARSE_SWEEPS - 1):
            field = (
                field
                + coarse_weight
                * (rhs - apply_padded(coarsest_padding(field), field, ops))
                / diagonal
            )
        return field
    field = sweep_first * rhs / diagonal
    field = smooth(field, rhs, ops, sweep_second)
    remainder = rhs - apply_padded(level_padding(field), field, ops)
    coarse = vcycle(levels, level + 1, restrict(remainder))
    field = field + prolong(coarse)
    field = smooth(field, rhs, ops, sweep_second)
    field = smooth(field, rhs, ops, sweep_first)
    return field


def sensitivity(state_pad, iter_pad):
    state_mid = neighbour(state_pad, 0, 0, 1)
    iter_mid = neighbour(iter_pad, 0, 0, 1)
    energy = jnp.zeros_like(state_mid[0])
    for component in range(3):
        for direction in range(3):
            for step in (-1, 1):
                diff_state = state_mid[component] - neighbour(
                    state_pad[component], direction, step, 1
                )
                diff_iter = iter_mid[component] - neighbour(iter_pad[component], direction, step, 1)
                energy = energy + 0.5 * couple[component][direction] * diff_state * diff_iter
    return energy


def filter_offsets():
    listing = []
    for a in range(-RADIUS, RADIUS + 1):
        for b in range(-RADIUS, RADIUS + 1):
            for c in range(-RADIUS, RADIUS + 1):
                weight = RADIUS - math.sqrt(a * a + b * b + c * c)
                if weight > 0.0:
                    listing.append((a, b, c, weight))
    return listing


def density_filter(term_pad, rho_pad, rho_own):
    shape = rho_own.shape
    weighted = jnp.zeros_like(rho_own)
    coverage = jnp.zeros_like(rho_own)
    for a, b, c, weight in filter_offsets():
        anchor = (RADIUS + a, RADIUS + b, RADIUS + c)
        ending = (anchor[0] + shape[0], anchor[1] + shape[1], anchor[2] + shape[2])
        weighted = weighted + weight * lax.slice(term_pad, anchor, ending)
        inside = jnp.where(lax.slice(rho_pad, anchor, ending) > 0.0, 1.0, 0.0).astype(rho_own.dtype)
        coverage = coverage + weight * inside
    return weighted / (rho_own * coverage)


def body(right_side, iterate, state, classes, load_mask, fixed_mask):
    rho = rho_floor + (1.0 - rho_floor) * classes.astype(jnp.float32) / (CLASSES - 1)
    energy = rho * rho * rho
    pen = penalty * fixed_mask.astype(jnp.float32)
    start_stack = jnp.concatenate([iterate, energy[None], state], 0)
    start_pad = padded_2(start_stack, (("gx", 1), ("gy", 2), ("gz", 3)), 1)
    levels = [level_ops(energy, start_pad[3], pen, 1.0)]
    for level in range(1, LEVELS):
        energy = restrict(energy) / 8.0
        pen = restrict(pen)
        if level == LEVELS - 1:
            levels.append(spread_ops(energy, pen, float(2**level)))
        else:
            levels.append(spread_ops(energy, pen, float(2**level)))
    load = right_side * load_mask.astype(jnp.float32)[None]
    start = load - apply_padded(start_pad[0:3], iterate, levels[0])
    precond = vcycle(levels, 0, start)
    direction_pad = padded_2(precond, (("gx", 1), ("gy", 2), ("gz", 3)), 1)
    image = apply_padded(direction_pad, precond, levels[0])
    upper = lax.psum(jnp.sum(start * precond), ("gx", "gy", "gz"))
    lower = lax.psum(jnp.sum(precond * image), ("gx", "gy", "gz"))
    alpha = upper / lower
    solution = iterate + alpha * precond
    residual = start - alpha * image
    iter_pad = padded_2(solution, (("gx", 1), ("gy", 2), ("gz", 3)), 1)
    stored = sensitivity(start_pad[4:7], iter_pad)
    term = rho * (-3.0 * rho * rho * stored)
    loop = padded_2(jnp.stack([term, rho]), (("gx", 1), ("gy", 2), ("gz", 3)), RADIUS)
    filtered = density_filter(loop[0], loop[1], rho)
    return (solution, residual, filtered)


def solution(mesh):
    placed = (
        P(None, "gx", "gy", "gz"),
        P(None, "gx", "gy", "gz"),
        P(None, "gx", "gy", "gz"),
        P("gx", "gy", "gz"),
        P("gx", "gy", "gz"),
        P("gx", "gy", "gz"),
    )
    return jax.shard_map(
        body,
        mesh=mesh,
        in_specs=placed,
        out_specs=(P(None, "gx", "gy", "gz"), P(None, "gx", "gy", "gz"), P("gx", "gy", "gz")),
        check_vma=False,
    )
```

profile of v0, /device:TPU:33, one launch (start us, length us, event | category | flops | bytes accessed | tf_op | source)
XLA Modules:
  0.0 752.7 jit_solution(5166418979421137988)
XLA Ops:
  7.9 5.6 reshape.1140
  18.2 4.6 collective-permute-start.2
  48.3 3.6 collective-permute-start.6
  53.9 3.6 collective-permute-start.18
  58.9 4.7 collective-permute-start.8
  64.9 4.6 collective-permute-start.20
  75.2 6.9 collective-permute-done.11
  82.1 4.6 collective-permute-done.10
  95.5 5.6 reshape.1141
  103.7 4.6 collective-permute-start.23
  109.6 5.7 collective-permute-start.14
  118.4 3.5 collective-permute-start.16
  122.0 5.9 collective-permute-done.17
  132.8 13.9 %reshape.1139 = f32[3,4,2,8,2,64,2]{6,5,4,3,2,1,0:T(8,128)} reshape(f32[3,8,16,128]{3,2,1,0:T(8,128)S(1)} %maximum_subtract_fusion.3) | data formatting | bytes 393216 | tf_op jit(solution)/shard_map/reshape | solution.py:86
  146.7 5.5 reduce_sum.113
  152.3 3.4 collective-permute-start.25
  160.6 3.6 collective-permute-start.36
  165.6 5.9 collective-permute-start.26
  172.9 5.0 collective-permute-start.38
  198.0 4.0 collective-permute-start.41
  203.3 5.2 collective-permute-start.32
  212.1 3.4 collective-permute-start.34
  240.8 5.5 collective-permute-start.44
  247.7 5.5 collective-permute-start.56
  261.7 3.8 collective-permute-start.49
  265.5 4.0 collective-permute-start.48
  272.0 4.1 collective-permute-start.59
  279.1 5.5 collective-permute-start.50
  297.1 3.9 collective-permute-start.60
  303.0 5.7 collective-permute-start.62
  319.9 5.9 collective-permute-start.66
  327.8 5.5 collective-permute-start.68
  344.1 6.2 collective-permute-start.72
  352.3 5.5 collective-permute-start.74
  360.6 3.6 collective-permute-start.76
  369.1 6.2 collective-permute-start.78
  377.3 5.7 collective-permute-start.80
  394.3 6.2 collective-permute-start.84
  402.6 5.7 collective-permute-start.86
  421.6 6.2 collective-permute-start.90
  430.0 5.7 collective-permute-start.92
  448.1 6.2 collective-permute-start.96
  456.5 5.7 collective-permute-start.98
  465.1 3.4 collective-permute-start.100
  472.7 5.2 broadcast_in_dim.221
  478.0 9.8 %reshape.1144 = f32[3,8,16,128]{3,2,1,0:T(8,128)S(1)} reshape(f32[3,4,2,8,2,64,2]{6,5,4,3,2,1,0:T(8,128)} %broadcast_in_dim.221) | data formatting | bytes 393216 | tf_op jit(solution)/shard_map/reshape | solution.py:95
  489.8 6.2 collective-permute-start.102
  498.3 5.7 collective-permute-start.104
  510.4 4.6 collective-permute-done.107
  521.0 5.4 collective-permute-start.108
  528.6 5.7 collective-permute-start.110
  540.7 5.4 collective-permute-done.113
  552.1 4.6 collective-permute-start.114
  558.9 5.7 collective-permute-start.116
  571.1 6.2 collective-permute-done.119
  581.9 103.4 %all-reduce = (f32[]{:T(128)}, f32[]{:T(128)}) all-reduce(f32[]{:T(128)} %get-tuple-element.4, f32[]{:T(128)} %get-tuple-element.3), channel_id=1, replica_groups=mesh['gx'=8,'gy'=8,'gz'=8] {'gx','gy','gz'}, use_global_device_ids=true, to_apply=%region_15.16 | all-reduce | flops 2 | bytes 16 | tf_op jit(solution)/shard_map/psum | solution.py:196
  690.0 3.6 collective-permute-start.120
  695.8 4.0 collective-permute-start.122
  706.3 6.9 collective-permute-done.125
  713.2 3.8 collective-permute-done.124
  721.1 3.4 collective-permute-start.126
  727.0 4.3 collective-permute-start.128
  738.0 6.6 collective-permute-done.131
  748.3 3.9 fusion.14
  (510 shorter events, 313.1 us)
Async XLA Ops:
  2.3 14.5 %collective-permute-start.1 = (f32[7,1,16,128]{3,2,1,0:T(8,128)S(1)}, f32[7,1,16,128]{3,2,1,0:T(8,128)S(1)}, u32[]{:S(2)}, u32[]{:S(2)}) collective-permute-start(f32[7,1,16,128]{3,2,1,0:T(8,128)S(1)} %get-tuple-element.72), channel_id=1, source_target_pairs={{64,0},{128,64},{192,128},{256,192},{320,256},{384,320},{448,384},... | collective-permute-start | bytes 172040 | tf_op jit(solution)/shard_map/ppermute | solution.py:30
  4.9 11.9 %collective-permute-start = (f32[7,1,16,128]{3,2,1,0:T(8,128)S(1)}, f32[7,1,16,128]{3,2,1,0:T(8,128)S(1)}, u32[]{:S(2)}, u32[]{:S(2)}) collective-permute-start(f32[7,1,16,128]{3,2,1,0:T(8,128)S(1)} %get-tuple-element.71), channel_id=1, source_target_pairs={{0,64},{64,128},{128,192},{192,256},{256,320},{320,384},{384,448},... | collective-permute-start | bytes 172040 | tf_op jit(solution)/shard_map/ppermute | solution.py:29
  27.0 12.1 %collective-permute-start.5 = (f32[7,10,18,1]{2,3,1,0:T(1,128)S(1)}, f32[7,10,18,1]{2,3,1,0:T(1,128)S(1)}, u32[]{:S(2)}, u32[]{:S(2)}) collective-permute-start(f32[7,10,18,1]{2,3,1,0:T(1,128)S(1)} %copy.27), channel_id=1, source_target_pairs={{1,0},{2,1},{3,2},{4,3},{5,4},{6,5},{7,6},{9,8},{10,9},{11,10},{12... | collective-permute-start | bytes 15128 | tf_op jit(solution)/shard_map/ppermute | solution.py:30
  29.6 10.1 %collective-permute-start.4 = (f32[7,10,18,1]{2,3,1,0:T(1,128)S(1)}, f32[7,10,18,1]{2,3,1,0:T(1,128)S(1)}, u32[]{:S(2)}, u32[]{:S(2)}) collective-permute-start(f32[7,10,18,1]{2,3,1,0:T(1,128)S(1)} %copy.26), channel_id=1, source_target_pairs={{0,1},{1,2},{2,3},{3,4},{4,5},{5,6},{6,7},{8,9},{9,10},{10,11},{11... | collective-permute-start | bytes 15128 | tf_op jit(solution)/shard_map/ppermute | solution.py:29
  33.4 205.3 %collective-permute-start.55 = (f32[1,2,16]{2,1,0:T(2,128)}, f32[1,2,16]{2,1,0:T(2,128)}, u32[]{:S(2)}, u32[]{:S(2)}) collective-permute-start(f32[1,2,16]{2,1,0:T(2,128)} %multiply_bitcast_fusion), channel_id=1, source_target_pairs={{64,0},{128,64},{192,128},{256,192},{320,256},{384,320},{448,384},... | collective-permute-start | bytes 392 | tf_op jit(solution)/shard_map/ppermute | solution.py:30
  36.1 202.6 %collective-permute-start.54 = (f32[1,2,16]{2,1,0:T(2,128)}, f32[1,2,16]{2,1,0:T(2,128)}, u32[]{:S(2)}, u32[]{:S(2)}) collective-permute-start(f32[1,2,16]{2,1,0:T(2,128)} %multiply_bitcast_fusion), channel_id=1, source_target_pairs={{0,64},{64,128},{128,192},{192,256},{256,320},{320,384},{384,448},... | collective-permute-start | bytes 392 | tf_op jit(solution)/shard_map/ppermute | solution.py:29
  46.3 7.5 collective-permute-start.7
  48.3 9.3 %collective-permute-start.6 = (f32[3,1,16,128]{3,2,1,0:T(8,128)S(1)}, f32[3,1,16,128]{3,2,1,0:T(8,128)S(1)}, u32[]{:S(2)}, u32[]{:S(2)}) collective-permute-start(f32[3,1,16,128]{3,2,1,0:T(8,128)S(1)} %get-tuple-element.111), channel_id=1, source_target_pairs={{0,64},{64,128},{128,192},{192,256},{256,320},{320,384},{384,448},... | collective-permute-start | bytes 73736 | tf_op jit(solution)/shard_map/ppermute | solution.py:29
  53.9 9.7 %collective-permute-start.18 = (f32[1,8,64]{2,1,0:T(8,128)S(1)}, f32[1,8,64]{2,1,0:T(8,128)S(1)}, u32[]{:S(2)}, u32[]{:S(2)}) collective-permute-start(f32[1,8,64]{2,1,0:T(8,128)S(1)} %get-tuple-element.209), channel_id=1, source_target_pairs={{0,64},{64,128},{128,192},{192,256},{256,320},{320,384},{384,448},... | collective-permute-start | bytes 6152 | tf_op jit(solution)/shard_map/ppermute | solution.py:29
  57.5 7.4 collective-permute-start.9
  58.9 10.7 %collective-permute-start.8 = (f32[3,10,1,128]{3,2,1,0:T(1,128)S(1)}, f32[3,10,1,128]{3,2,1,0:T(1,128)S(1)}, u32[]{:S(2)}, u32[]{:S(2)}) collective-permute-start(f32[3,10,1,128]{3,2,1,0:T(1,128)S(1)} %get-tuple-element.97), channel_id=1, source_target_pairs={{0,8},{8,16},{16,24},{24,32},{32,40},{40,48},{48,56},{1,9},{9,17},... | collective-permute-start | bytes 46088 | tf_op jit(solution)/shard_map/ppermute | solution.py:29
  63.6 9.5 %collective-permute-start.21 = (f32[6,1,64]{2,1,0:T(1,128)S(1)}, f32[6,1,64]{2,1,0:T(1,128)S(1)}, u32[]{:S(2)}, u32[]{:S(2)}) collective-permute-start(f32[6,1,64]{2,1,0:T(1,128)S(1)} %get-tuple-element.191), channel_id=1, source_target_pairs={{8,0},{16,8},{24,16},{32,24},{40,32},{48,40},{56,48},{9,1},{17,9},... | collective-permute-start | bytes 4616 | tf_op jit(solution)/shard_map/ppermute | solution.py:30
  64.9 10.2 %collective-permute-start.20 = (f32[6,1,64]{2,1,0:T(1,128)S(1)}, f32[6,1,64]{2,1,0:T(1,128)S(1)}, u32[]{:S(2)}, u32[]{:S(2)}) collective-permute-start(f32[6,1,64]{2,1,0:T(1,128)S(1)} %get-tuple-element.190), channel_id=1, source_target_pairs={{0,8},{8,16},{16,24},{24,32},{32,40},{40,48},{48,56},{1,9},{9,17},... | collective-permute-start | bytes 4616 | tf_op jit(solution)/shard_map/ppermute | solution.py:29
  69.8 12.3 %collective-permute-start.11 = (f32[3,10,18,1]{3,2,1,0:T(8,128)S(1)}, f32[3,10,18,1]{3,2,1,0:T(8,128)S(1)}, u32[]{:S(2)}, u32[]{:S(2)}) collective-permute-start(f32[3,10,18,1]{3,2,1,0:T(8,128)S(1)} %get-tuple-element.84), channel_id=1, source_target_pairs={{1,0},{2,1},{3,2},{4,3},{5,4},{6,5},{7,6},{9,8},{10,9},{11,10},{12... | collective-permute-start | bytes 6488 | tf_op jit(solution)/shard_map/ppermute | solution.py:30
  73.1 13.6 %collective-permute-start.10 = (f32[3,10,18,1]{3,2,1,0:T(8,128)S(1)}, f32[3,10,18,1]{3,2,1,0:T(8,128)S(1)}, u32[]{:S(2)}, u32[]{:S(2)}) collective-permute-start(f32[3,10,18,1]{3,2,1,0:T(8,128)S(1)} %get-tuple-element.83), channel_id=1, source_target_pairs={{0,1},{1,2},{2,3},{3,4},{4,5},{5,6},{6,7},{8,9},{9,10},{10,11},{11... | collective-permute-start | bytes 6488 | tf_op jit(solution)/shard_map/ppermute | solution.py:29
  87.9 15.7 %collective-permute-start.13 = (f32[3,1,16,128]{3,2,1,0:T(8,128)S(1)}, f32[3,1,16,128]{3,2,1,0:T(8,128)S(1)}, u32[]{:S(2)}, u32[]{:S(2)}) collective-permute-start(f32[3,1,16,128]{3,2,1,0:T(8,128)S(1)} %get-tuple-element.110), channel_id=1, source_target_pairs={{64,0},{128,64},{192,128},{256,192},{320,256},{384,320},{448,384},... | collective-permute-start | bytes 73736 | tf_op jit(solution)/shard_map/ppermute | solution.py:30
  90.3 18.0 %collective-permute-start.12 = (f32[3,1,16,128]{3,2,1,0:T(8,128)S(1)}, f32[3,1,16,128]{3,2,1,0:T(8,128)S(1)}, u32[]{:S(2)}, u32[]{:S(2)}) collective-permute-start(f32[3,1,16,128]{3,2,1,0:T(8,128)S(1)} %get-tuple-element.109), channel_id=1, source_target_pairs={{0,64},{64,128},{128,192},{192,256},{256,320},{320,384},{384,448},... | collective-permute-start | bytes 73736 | tf_op jit(solution)/shard_map/ppermute | solution.py:29
  93.6 16.0 %collective-permute-start.22 = (f32[6,10,1]{2,1,0:T(8,128)S(1)}, f32[6,10,1]{2,1,0:T(8,128)S(1)}, u32[]{:S(2)}, u32[]{:S(2)}) collective-permute-start(f32[6,10,1]{2,1,0:T(8,128)S(1)} %get-tuple-element.179), channel_id=1, source_target_pairs={{0,1},{1,2},{2,3},{3,4},{4,5},{5,6},{6,7},{8,9},{9,10},{10,11},{11... | collective-permute-start | bytes 728 | tf_op jit(solution)/shard_map/ppermute | solution.py:29
  103.7 11.7 %collective-permute-start.23 = (f32[6,10,1]{2,1,0:T(8,128)S(1)}, f32[6,10,1]{2,1,0:T(8,128)S(1)}, u32[]{:S(2)}, u32[]{:S(2)}) collective-permute-start(f32[6,10,1]{2,1,0:T(8,128)S(1)} %get-tuple-element.178), channel_id=1, source_target_pairs={{1,0},{2,1},{3,2},{4,3},{5,4},{6,5},{7,6},{9,8},{10,9},{11,10},{12... | collective-permute-start | bytes 728 | tf_op jit(solution)/shard_map/ppermute | solution.py:30
  108.3 7.2 collective-permute-start.15
  116.5 11.4 %collective-permute-start.17 = (f32[3,10,18,1]{3,2,1,0:T(8,128)S(1)}, f32[3,10,18,1]{3,2,1,0:T(8,128)S(1)}, u32[]{:S(2)}, u32[]{:S(2)}) collective-permute-start(f32[3,10,18,1]{3,2,1,0:T(8,128)S(1)} %get-tuple-element.82), channel_id=1, source_target_pairs={{1,0},{2,1},{3,2},{4,3},{5,4},{6,5},{7,6},{9,8},{10,9},{11,10},{12... | collective-permute-start | bytes 6488 | tf_op jit(solution)/shard_map/ppermute | solution.py:30
  118.4 12.6 %collective-permute-start.16 = (f32[3,10,18,1]{3,2,1,0:T(8,128)S(1)}, f32[3,10,18,1]{3,2,1,0:T(8,128)S(1)}, u32[]{:S(2)}, u32[]{:S(2)}) collective-permute-start(f32[3,10,18,1]{3,2,1,0:T(8,128)S(1)} %get-tuple-element.81), channel_id=1, source_target_pairs={{0,1},{1,2},{2,3},{3,4},{4,5},{5,6},{6,7},{8,9},{9,10},{10,11},{11... | collective-permute-start | bytes 6488 | tf_op jit(solution)/shard_map/ppermute | solution.py:29
  152.3 8.3 %collective-permute-start.25 = (f32[3,1,8,64]{3,2,1,0:T(8,128)S(1)}, f32[3,1,8,64]{3,2,1,0:T(8,128)S(1)}, u32[]{:S(2)}, u32[]{:S(2)}) collective-permute-start(f32[3,1,8,64]{3,2,1,0:T(8,128)S(1)} %get-tuple-element.177), channel_id=1, source_target_pairs={{64,0},{128,64},{192,128},{256,192},{320,256},{384,320},{448,384},... | collective-permute-start | bytes 18440 | tf_op jit(solution)/shard_map/ppermute | solution.py:30
  155.7 8.6 %collective-permute-start.24 = (f32[3,1,8,64]{3,2,1,0:T(8,128)S(1)}, f32[3,1,8,64]{3,2,1,0:T(8,128)S(1)}, u32[]{:S(2)}, u32[]{:S(2)}) collective-permute-start(f32[3,1,8,64]{3,2,1,0:T(8,128)S(1)} %get-tuple-element.176), channel_id=1, source_target_pairs={{0,64},{64,128},{128,192},{192,256},{256,320},{320,384},{384,448},... | collective-permute-start | bytes 18440 | tf_op jit(solution)/shard_map/ppermute | solution.py:29
  160.6 11.0 %collective-permute-start.36 = (f32[1,4,32]{2,1,0:T(4,128)S(1)}, f32[1,4,32]{2,1,0:T(4,128)S(1)}, u32[]{:S(2)}, u32[]{:S(2)}) collective-permute-start(f32[1,4,32]{2,1,0:T(4,128)S(1)} %get-tuple-element.233), channel_id=1, source_target_pairs={{0,64},{64,128},{128,192},{192,256},{256,320},{320,384},{384,448},... | collective-permute-start | bytes 1544 | tf_op jit(solution)/shard_map/ppermute | solution.py:29
  164.3 8.6 %collective-permute-start.27 = (f32[3,6,1,64]{3,2,1,0:T(1,128)S(1)}, f32[3,6,1,64]{3,2,1,0:T(1,128)S(1)}, u32[]{:S(2)}, u32[]{:S(2)}) collective-permute-start(f32[3,6,1,64]{3,2,1,0:T(1,128)S(1)} %get-tuple-element.144), channel_id=1, source_target_pairs={{8,0},{16,8},{24,16},{32,24},{40,32},{48,40},{56,48},{9,1},{17,9},... | collective-permute-start | bytes 13832 | tf_op jit(solution)/shard_map/ppermute | solution.py:30
  165.6 12.3 %collective-permute-start.26 = (f32[3,6,1,64]{3,2,1,0:T(1,128)S(1)}, f32[3,6,1,64]{3,2,1,0:T(1,128)S(1)}, u32[]{:S(2)}, u32[]{:S(2)}) collective-permute-start(f32[3,6,1,64]{3,2,1,0:T(1,128)S(1)} %get-tuple-element.143), channel_id=1, source_target_pairs={{0,8},{8,16},{16,24},{24,32},{32,40},{40,48},{48,56},{1,9},{9,17},... | collective-permute-start | bytes 13832 | tf_op jit(solution)/shard_map/ppermute | solution.py:29
  171.6 8.4 %collective-permute-start.39 = (f32[4,1,32]{2,1,0:T(1,128)S(1)}, f32[4,1,32]{2,1,0:T(1,128)S(1)}, u32[]{:S(2)}, u32[]{:S(2)}) collective-permute-start(f32[4,1,32]{2,1,0:T(1,128)S(1)} %get-tuple-element.226), channel_id=1, source_target_pairs={{8,0},{16,8},{24,16},{32,24},{40,32},{48,40},{56,48},{9,1},{17,9},... | collective-permute-start | bytes 1544 | tf_op jit(solution)/shard_map/ppermute | solution.py:30
  172.9 10.5 %collective-permute-start.38 = (f32[4,1,32]{2,1,0:T(1,128)S(1)}, f32[4,1,32]{2,1,0:T(1,128)S(1)}, u32[]{:S(2)}, u32[]{:S(2)}) collective-permute-start(f32[4,1,32]{2,1,0:T(1,128)S(1)} %get-tuple-element.225), channel_id=1, source_target_pairs={{0,8},{8,16},{16,24},{24,32},{32,40},{40,48},{48,56},{1,9},{9,17},... | collective-permute-start | bytes 1544 | tf_op jit(solution)/shard_map/ppermute | solution.py:29
  178.1 7.6 %collective-permute-start.29 = (f32[3,6,10,1]{3,2,1,0:T(8,128)S(1)}, f32[3,6,10,1]{3,2,1,0:T(8,128)S(1)}, u32[]{:S(2)}, u32[]{:S(2)}) collective-permute-start(f32[3,6,10,1]{3,2,1,0:T(8,128)S(1)} %get-tuple-element.132), channel_id=1, source_target_pairs={{1,0},{2,1},{3,2},{4,3},{5,4},{6,5},{7,6},{9,8},{10,9},{11,10},{12... | collective-permute-start | bytes 2168 | tf_op jit(solution)/shard_map/ppermute | solution.py:30
  180.0 8.6 %collective-permute-start.28 = (f32[3,6,10,1]{3,2,1,0:T(8,128)S(1)}, f32[3,6,10,1]{3,2,1,0:T(8,128)S(1)}, u32[]{:S(2)}, u32[]{:S(2)}) collective-permute-start(f32[3,6,10,1]{3,2,1,0:T(8,128)S(1)} %get-tuple-element.131), channel_id=1, source_target_pairs={{0,1},{1,2},{2,3},{3,4},{4,5},{5,6},{6,7},{8,9},{9,10},{10,11},{11... | collective-permute-start | bytes 2168 | tf_op jit(solution)/shard_map/ppermute | solution.py:29
  189.2 8.8 %collective-permute-start.31 = (f32[3,1,8,64]{3,2,1,0:T(8,128)S(1)}, f32[3,1,8,64]{3,2,1,0:T(8,128)S(1)}, u32[]{:S(2)}, u32[]{:S(2)}) collective-permute-start(f32[3,1,8,64]{3,2,1,0:T(8,128)S(1)} %get-tuple-element.175), channel_id=1, source_target_pairs={{64,0},{128,64},{192,128},{256,192},{320,256},{384,320},{448,384},... | collective-permute-start | bytes 18440 | tf_op jit(solution)/shard_map/ppermute | solution.py:30
  191.5 10.5 %collective-permute-start.30 = (f32[3,1,8,64]{3,2,1,0:T(8,128)S(1)}, f32[3,1,8,64]{3,2,1,0:T(8,128)S(1)}, u32[]{:S(2)}, u32[]{:S(2)}) collective-permute-start(f32[3,1,8,64]{3,2,1,0:T(8,128)S(1)} %get-tuple-element.174), channel_id=1, source_target_pairs={{0,64},{64,128},{128,192},{192,256},{256,320},{320,384},{384,448},... | collective-permute-start | bytes 18440 | tf_op jit(solution)/shard_map/ppermute | solution.py:29
  194.8 8.5 %collective-permute-start.40 = (f32[4,6,1]{2,1,0:T(8,128)S(1)}, f32[4,6,1]{2,1,0:T(8,128)S(1)}, u32[]{:S(2)}, u32[]{:S(2)}) collective-permute-start(f32[4,6,1]{2,1,0:T(8,128)S(1)} %get-tuple-element.208), channel_id=1, source_target_pairs={{0,1},{1,2},{2,3},{3,4},{4,5},{5,6},{6,7},{8,9},{9,10},{10,11},{11... | collective-permute-start | bytes 296 | tf_op jit(solution)/shard_map/ppermute | solution.py:29
  198.0 10.6 %collective-permute-start.41 = (f32[4,6,1]{2,1,0:T(8,128)S(1)}, f32[4,6,1]{2,1,0:T(8,128)S(1)}, u32[]{:S(2)}, u32[]{:S(2)}) collective-permute-start(f32[4,6,1]{2,1,0:T(8,128)S(1)} %get-tuple-element.207), channel_id=1, source_target_pairs={{1,0},{2,1},{3,2},{4,3},{5,4},{6,5},{7,6},{9,8},{10,9},{11,10},{12... | collective-permute-start | bytes 296 | tf_op jit(solution)/shard_map/ppermute | solution.py:30
  210.1 7.5 %collective-permute-start.35 = (f32[3,6,10,1]{3,2,1,0:T(8,128)}, f32[3,6,10,1]{3,2,1,0:T(8,128)}, u32[]{:S(2)}, u32[]{:S(2)}) collective-permute-start(f32[3,6,10,1]{3,2,1,0:T(8,128)} %get-tuple-element.127), channel_id=1, source_target_pairs={{1,0},{2,1},{3,2},{4,3},{5,4},{6,5},{7,6},{9,8},{10,9},{11,10},{12... | collective-permute-start | bytes 2168 | tf_op jit(solution)/shard_map/ppermute | solution.py:30
  212.1 8.3 %collective-permute-start.34 = (f32[3,6,10,1]{3,2,1,0:T(8,128)}, f32[3,6,10,1]{3,2,1,0:T(8,128)}, u32[]{:S(2)}, u32[]{:S(2)}) collective-permute-start(f32[3,6,10,1]{3,2,1,0:T(8,128)} %get-tuple-element.126), channel_id=1, source_target_pairs={{0,1},{1,2},{2,3},{3,4},{4,5},{5,6},{6,7},{8,9},{9,10},{10,11},{11... | collective-permute-start | bytes 2168 | tf_op jit(solution)/shard_map/ppermute | solution.py:29
  239.5 13.6 %collective-permute-start.45 = (f32[3,4,1,32]{3,2,1,0:T(1,128)S(1)}, f32[3,4,1,32]{3,2,1,0:T(1,128)S(1)}, u32[]{:S(2)}, u32[]{:S(2)}) collective-permute-start(f32[3,4,1,32]{3,2,1,0:T(1,128)S(1)} %get-tuple-element.189), channel_id=1, source_target_pairs={{8,0},{16,8},{24,16},{32,24},{40,32},{48,40},{56,48},{9,1},{17,9},... | collective-permute-start | bytes 4616 | tf_op jit(solution)/shard_map/ppermute | solution.py:30
  240.8 12.3 %collective-permute-start.44 = (f32[3,4,1,32]{3,2,1,0:T(1,128)S(1)}, f32[3,4,1,32]{3,2,1,0:T(1,128)S(1)}, u32[]{:S(2)}, u32[]{:S(2)}) collective-permute-start(f32[3,4,1,32]{3,2,1,0:T(1,128)S(1)} %get-tuple-element.188), channel_id=1, source_target_pairs={{0,8},{8,16},{16,24},{24,32},{32,40},{40,48},{48,56},{1,9},{9,17},... | collective-permute-start | bytes 4616 | tf_op jit(solution)/shard_map/ppermute | solution.py:29
  246.4 12.2 %collective-permute-start.57 = (f32[3,1,16]{2,1,0:T(1,128)S(1)}, f32[3,1,16]{2,1,0:T(1,128)S(1)}, u32[]{:S(2)}, u32[]{:S(2)}) collective-permute-start(f32[3,1,16]{2,1,0:T(1,128)S(1)} %get-tuple-element.236), channel_id=1, source_target_pairs={{8,0},{16,8},{24,16},{32,24},{40,32},{48,40},{56,48},{9,1},{17,9},... | collective-permute-start | bytes 584 | tf_op jit(solution)/shard_map/ppermute | solution.py:30
  247.7 10.9 %collective-permute-start.56 = (f32[3,1,16]{2,1,0:T(1,128)S(1)}, f32[3,1,16]{2,1,0:T(1,128)S(1)}, u32[]{:S(2)}, u32[]{:S(2)}) collective-permute-start(f32[3,1,16]{2,1,0:T(1,128)S(1)} %get-tuple-element.235), channel_id=1, source_target_pairs={{0,8},{8,16},{16,24},{24,32},{32,40},{40,48},{48,56},{1,9},{9,17},... | collective-permute-start | bytes 584 | tf_op jit(solution)/shard_map/ppermute | solution.py:29
  261.7 16.1 %collective-permute-start.49 = (f32[3,1,4,32]{3,2,1,0:T(4,128)S(1)}, f32[3,1,4,32]{3,2,1,0:T(4,128)S(1)}, u32[]{:S(2)}, u32[]{:S(2)}) collective-permute-start(f32[3,1,4,32]{3,2,1,0:T(4,128)S(1)} %get-tuple-element.216), channel_id=1, source_target_pairs={{64,0},{128,64},{192,128},{256,192},{320,256},{384,320},{448,384},... | collective-permute-start | bytes 4616 | tf_op jit(solution)/shard_map/ppermute | solution.py:30
  265.5 12.3 %collective-permute-start.48 = (f32[3,1,4,32]{3,2,1,0:T(4,128)S(1)}, f32[3,1,4,32]{3,2,1,0:T(4,128)S(1)}, u32[]{:S(2)}, u32[]{:S(2)}) collective-permute-start(f32[3,1,4,32]{3,2,1,0:T(4,128)S(1)} %get-tuple-element.215), channel_id=1, source_target_pairs={{0,64},{64,128},{128,192},{192,256},{256,320},{320,384},{384,448},... | collective-permute-start | bytes 4616 | tf_op jit(solution)/shard_map/ppermute | solution.py:29
  269.5 15.1 %collective-permute-start.58 = (f32[3,4,1]{2,1,0:T(4,128)S(1)}, f32[3,4,1]{2,1,0:T(4,128)S(1)}, u32[]{:S(2)}, u32[]{:S(2)}) collective-permute-start(f32[3,4,1]{2,1,0:T(4,128)S(1)} %get-tuple-element.230), channel_id=1, source_target_pairs={{0,1},{1,2},{2,3},{3,4},{4,5},{5,6},{6,7},{8,9},{9,10},{10,11},{11... | collective-permute-start | bytes 152 | tf_op jit(solution)/shard_map/ppermute | solution.py:29
  272.0 12.7 %collective-permute-start.59 = (f32[3,4,1]{2,1,0:T(4,128)S(1)}, f32[3,4,1]{2,1,0:T(4,128)S(1)}, u32[]{:S(2)}, u32[]{:S(2)}) collective-permute-start(f32[3,4,1]{2,1,0:T(4,128)S(1)} %get-tuple-element.229), channel_id=1, source_target_pairs={{1,0},{2,1},{3,2},{4,3},{5,4},{6,5},{7,6},{9,8},{10,9},{11,10},{12... | collective-permute-start | bytes 152 | tf_op jit(solution)/shard_map/ppermute | solution.py:30
  277.8 7.8 %collective-permute-start.51 = (f32[3,4,1,32]{3,2,1,0:T(1,128)S(1)}, f32[3,4,1,32]{3,2,1,0:T(1,128)S(1)}, u32[]{:S(2)}, u32[]{:S(2)}) collective-permute-start(f32[3,4,1,32]{3,2,1,0:T(1,128)S(1)} %get-tuple-element.187), channel_id=1, source_target_pairs={{8,0},{16,8},{24,16},{32,24},{40,32},{48,40},{56,48},{9,1},{17,9},... | collective-permute-start | bytes 4616 | tf_op jit(solution)/shard_map/ppermute | solution.py:30
  317.6 8.1 %collective-permute-start.67 = (f32[3,1,2,16]{3,2,1,0:T(2,128)S(1)}, f32[3,1,2,16]{3,2,1,0:T(2,128)S(1)}, u32[]{:S(2)}, u32[]{:S(2)}) collective-permute-start(f32[3,1,2,16]{3,2,1,0:T(2,128)S(1)} %fusion.790), channel_id=1, source_target_pairs={{64,0},{128,64},{192,128},{256,192},{320,256},{384,320},{448,384},... | collective-permute-start | bytes 1160 | tf_op jit(solution)/shard_map/ppermute | solution.py:30
  342.2 8.1 %collective-permute-start.73 = (f32[3,1,2,16]{3,2,1,0:T(2,128)S(1)}, f32[3,1,2,16]{3,2,1,0:T(2,128)S(1)}, u32[]{:S(2)}, u32[]{:S(2)}) collective-permute-start(f32[3,1,2,16]{3,2,1,0:T(2,128)S(1)} %fusion.789), channel_id=1, source_target_pairs={{64,0},{128,64},{192,128},{256,192},{320,256},{384,320},{448,384},... | collective-permute-start | bytes 1160 | tf_op jit(solution)/shard_map/ppermute | solution.py:30
  367.1 8.1 %collective-permute-start.79 = (f32[3,1,4,32]{3,2,1,0:T(4,128)S(1)}, f32[3,1,4,32]{3,2,1,0:T(4,128)S(1)}, u32[]{:S(2)}, u32[]{:S(2)}) collective-permute-start(f32[3,1,4,32]{3,2,1,0:T(4,128)S(1)} %get-tuple-element.214), channel_id=1, source_target_pairs={{64,0},{128,64},{192,128},{256,192},{320,256},{384,320},{448,384},... | collective-permute-start | bytes 4616 | tf_op jit(solution)/shard_map/ppermute | solution.py:30
  392.4 8.1 %collective-permute-start.85 = (f32[3,1,4,32]{3,2,1,0:T(4,128)S(1)}, f32[3,1,4,32]{3,2,1,0:T(4,128)S(1)}, u32[]{:S(2)}, u32[]{:S(2)}) collective-permute-start(f32[3,1,4,32]{3,2,1,0:T(4,128)S(1)} %get-tuple-element.212), channel_id=1, source_target_pairs={{64,0},{128,64},{192,128},{256,192},{320,256},{384,320},{448,384},... | collective-permute-start | bytes 4616 | tf_op jit(solution)/shard_map/ppermute | solution.py:30
  419.7 8.1 %collective-permute-start.91 = (f32[3,1,8,64]{3,2,1,0:T(8,128)S(1)}, f32[3,1,8,64]{3,2,1,0:T(8,128)S(1)}, u32[]{:S(2)}, u32[]{:S(2)}) collective-permute-start(f32[3,1,8,64]{3,2,1,0:T(8,128)S(1)} %get-tuple-element.153), channel_id=1, source_target_pairs={{64,0},{128,64},{192,128},{256,192},{320,256},{384,320},{448,384},... | collective-permute-start | bytes 18440 | tf_op jit(solution)/shard_map/ppermute | solution.py:30
  446.2 8.1 %collective-permute-start.97 = (f32[3,1,8,64]{3,2,1,0:T(8,128)S(1)}, f32[3,1,8,64]{3,2,1,0:T(8,128)S(1)}, u32[]{:S(2)}, u32[]{:S(2)}) collective-permute-start(f32[3,1,8,64]{3,2,1,0:T(8,128)S(1)} %get-tuple-element.151), channel_id=1, source_target_pairs={{64,0},{128,64},{192,128},{256,192},{320,256},{384,320},{448,384},... | collective-permute-start | bytes 18440 | tf_op jit(solution)/shard_map/ppermute | solution.py:30
  487.9 8.1 %collective-permute-start.103 = (f32[3,1,16,128]{3,2,1,0:T(8,128)S(1)}, f32[3,1,16,128]{3,2,1,0:T(8,128)S(1)}, u32[]{:S(2)}, u32[]{:S(2)}) collective-permute-start(f32[3,1,16,128]{3,2,1,0:T(8,128)S(1)} %get-tuple-element.108), channel_id=1, source_target_pairs={{64,0},{128,64},{192,128},{256,192},{320,256},{384,320},{448,384},... | collective-permute-start | bytes 73736 | tf_op jit(solution)/shard_map/ppermute | solution.py:30
  505.1 9.9 %collective-permute-start.107 = (f32[3,10,18,1]{3,2,1,0:T(8,128)S(1)}, f32[3,10,18,1]{3,2,1,0:T(8,128)S(1)}, u32[]{:S(2)}, u32[]{:S(2)}) collective-permute-start(f32[3,10,18,1]{3,2,1,0:T(8,128)S(1)} %get-tuple-element.80), channel_id=1, source_target_pairs={{1,0},{2,1},{3,2},{4,3},{5,4},{6,5},{7,6},{9,8},{10,9},{11,10},{12... | collective-permute-start | bytes 6488 | tf_op jit(solution)/shard_map/ppermute | solution.py:30
  507.0 10.9 %collective-permute-start.106 = (f32[3,10,18,1]{3,2,1,0:T(8,128)S(1)}, f32[3,10,18,1]{3,2,1,0:T(8,128)S(1)}, u32[]{:S(2)}, u32[]{:S(2)}) collective-permute-start(f32[3,10,18,1]{3,2,1,0:T(8,128)S(1)} %get-tuple-element.79), channel_id=1, source_target_pairs={{0,1},{1,2},{2,3},{3,4},{4,5},{5,6},{6,7},{8,9},{9,10},{10,11},{11... | collective-permute-start | bytes 6488 | tf_op jit(solution)/shard_map/ppermute | solution.py:29
  519.0 7.3 collective-permute-start.109
  535.4 10.7 %collective-permute-start.113 = (f32[3,10,18,1]{3,2,1,0:T(8,128)S(1)}, f32[3,10,18,1]{3,2,1,0:T(8,128)S(1)}, u32[]{:S(2)}, u32[]{:S(2)}) collective-permute-start(f32[3,10,18,1]{3,2,1,0:T(8,128)S(1)} %get-tuple-element.78), channel_id=1, source_target_pairs={{1,0},{2,1},{3,2},{4,3},{5,4},{6,5},{7,6},{9,8},{10,9},{11,10},{12... | collective-permute-start | bytes 6488 | tf_op jit(solution)/shard_map/ppermute | solution.py:30
  537.4 11.7 %collective-permute-start.112 = (f32[3,10,18,1]{3,2,1,0:T(8,128)S(1)}, f32[3,10,18,1]{3,2,1,0:T(8,128)S(1)}, u32[]{:S(2)}, u32[]{:S(2)}) collective-permute-start(f32[3,10,18,1]{3,2,1,0:T(8,128)S(1)} %get-tuple-element.77), channel_id=1, source_target_pairs={{0,1},{1,2},{2,3},{3,4},{4,5},{5,6},{6,7},{8,9},{9,10},{10,11},{11... | collective-permute-start | bytes 6488 | tf_op jit(solution)/shard_map/ppermute | solution.py:29
  565.8 11.5 %collective-permute-start.119 = (f32[3,10,18,1]{3,2,1,0:T(8,128)S(1)}, f32[3,10,18,1]{3,2,1,0:T(8,128)S(1)}, u32[]{:S(2)}, u32[]{:S(2)}) collective-permute-start(f32[3,10,18,1]{3,2,1,0:T(8,128)S(1)} %get-tuple-element.76), channel_id=1, source_target_pairs={{1,0},{2,1},{3,2},{4,3},{5,4},{6,5},{7,6},{9,8},{10,9},{11,10},{12... | collective-permute-start | bytes 6488 | tf_op jit(solution)/shard_map/ppermute | solution.py:30
  567.7 12.5 %collective-permute-start.118 = (f32[3,10,18,1]{3,2,1,0:T(8,128)S(1)}, f32[3,10,18,1]{3,2,1,0:T(8,128)S(1)}, u32[]{:S(2)}, u32[]{:S(2)}) collective-permute-start(f32[3,10,18,1]{3,2,1,0:T(8,128)S(1)} %get-tuple-element.75), channel_id=1, source_target_pairs={{0,1},{1,2},{2,3},{3,4},{4,5},{5,6},{6,7},{8,9},{9,10},{10,11},{11... | collective-permute-start | bytes 6488 | tf_op jit(solution)/shard_map/ppermute | solution.py:29
  700.9 12.3 %collective-permute-start.125 = (f32[3,10,18,1]{3,2,1,0:T(8,128)S(1)}, f32[3,10,18,1]{3,2,1,0:T(8,128)S(1)}, u32[]{:S(2)}, u32[]{:S(2)}) collective-permute-start(f32[3,10,18,1]{3,2,1,0:T(8,128)S(1)} %get-tuple-element.74), channel_id=1, source_target_pairs={{1,0},{2,1},{3,2},{4,3},{5,4},{6,5},{7,6},{9,8},{10,9},{11,10},{12... | collective-permute-start | bytes 6488 | tf_op jit(solution)/shard_map/ppermute | solution.py:30
  703.8 13.1 %collective-permute-start.124 = (f32[3,10,18,1]{3,2,1,0:T(8,128)S(1)}, f32[3,10,18,1]{3,2,1,0:T(8,128)S(1)}, u32[]{:S(2)}, u32[]{:S(2)}) collective-permute-start(f32[3,10,18,1]{3,2,1,0:T(8,128)S(1)} %get-tuple-element.73), channel_id=1, source_target_pairs={{0,1},{1,2},{2,3},{3,4},{4,5},{5,6},{6,7},{8,9},{9,10},{10,11},{11... | collective-permute-start | bytes 6488 | tf_op jit(solution)/shard_map/ppermute | solution.py:29
  732.7 11.9 %collective-permute-start.131 = (f32[2,14,22,3]{3,2,1,0:T(8,128)S(1)}, f32[2,14,22,3]{3,2,1,0:T(8,128)S(1)}, u32[]{:S(2)}, u32[]{:S(2)}) collective-permute-start(f32[2,14,22,3]{3,2,1,0:T(8,128)S(1)} %get-tuple-element.86), channel_id=1, source_target_pairs={{1,0},{2,1},{3,2},{4,3},{5,4},{6,5},{7,6},{9,8},{10,9},{11,10},{12... | collective-permute-start | bytes 22184 | tf_op jit(solution)/shard_map/ppermute | solution.py:30
  734.6 13.1 %collective-permute-start.130 = (f32[2,14,22,3]{3,2,1,0:T(8,128)S(1)}, f32[2,14,22,3]{3,2,1,0:T(8,128)S(1)}, u32[]{:S(2)}, u32[]{:S(2)}) collective-permute-start(f32[2,14,22,3]{3,2,1,0:T(8,128)S(1)} %get-tuple-element.85), channel_id=1, source_target_pairs={{0,1},{1,2},{2,3},{3,4},{4,5},{5,6},{6,7},{8,9},{9,10},{10,11},{11... | collective-permute-start | bytes 22184 | tf_op jit(solution)/shard_map/ppermute | solution.py:29
  (98 other events, 768.3 us)
where the time goes:
time: 765 us; the launch traced here: 753 us
  starting transfers between devices  414 us (54%)
  waiting for transfers between devices  120 us (16%)
  blocking collectives  103 us (13%)
  local copies, waits for them, and re-layouts  62.8 us (8%)
  other arithmetic  46.4 us (6%)
    ppermute x66, starting transfers between devices, padded_2(): before = lax.ppermute(last, axis, up)  283 us
    ppermute x66, starting transfers between devices, padded_2(): after = lax.ppermute(first, axis, down)  132 us
    psum x1, blocking collectives, body(): upper = lax.psum(jnp.sum(start * precond), ('gx', 'gy', 'gz'))  103 us
    ppermute x66, waiting for transfers between devices, padded_2(): before = lax.ppermute(last, axis, up)  73.5 us
    ppermute x66, waiting for transfers between devices, padded_2(): after = lax.ppermute(first, axis, down)  46.8 us
    reshape x4, local copies, waits for them, and re-layouts, restrict(): field.reshape(lead + (shape[-3] // 2, 2, shape[-2] // 2, 2, shape[-1] //...  25.6 us
  transfers between devices with their start and end apart: 132, of which 56 were waited for; matrix products, arithmetic and copies ran while one was open for 9% of the time, Pallas kernels for 0%

commit v1 on v0

v1 whole, which is shorter than its diff:
```python
import functools
import math

import jax
import jax.numpy as jnp
from jax import lax
from jax.experimental import pallas as pl
from jax.experimental.pallas import tpu as pltpu
from jax.sharding import PartitionSpec as P

F32 = jnp.float32
FLOOR = 0.25
CLASSES = 16
PENALTY = 4.0
FIRST = 0.55
SECOND = 1.05
COARSE = 0.6
RADIUS = 3

BX, BY, BZ = 8, 16, 128
HALO = 7
SLABS = BX + 2 * HALO
ROWS = 2 * BY
LANES = 2 * BZ

PACKED = 8
ITERATE = ((0, 0, 7), (1, 7, 7), (2, 14, 7))
RHO = (3, 21, 7)
LOAD = ((4, 28, 6), (5, 34, 6), (6, 40, 6))
PEN = (7, 46, 6)
STATE = ((9, 52, 3), (10, 55, 3), (11, 58, 3))
HALF = BZ // 2

VMEM_LIMIT = 56 * 1024 * 1024


def iota(shape, dim):
    return lax.broadcasted_iota(jnp.int32, shape, dim)


def roll(x, shift, axis):
    return pltpu.roll(x, shift % x.shape[axis], axis)


def loop(lower, upper, step):
    def run(i, carry):
        step(i)
        return carry

    lax.fori_loop(lower, upper, run, 0)


def times(x, m):
    return jnp.dot(x, m, precision=lax.Precision.HIGHEST, preferred_element_type=F32)


def matrix(shape, rule):
    return jnp.where(rule(iota(shape, 0), iota(shape, 1)), 1.0, 0.0).astype(F32)


def face(a, b):
    total = a + b
    both = (a > 0.0) & (b > 0.0)
    return jnp.where(both, 2.0 * a * b / jnp.where(both, total, 1.0), total)


def launch(kernel, outs, scratch, *operands):
    specs = [pl.BlockSpec(memory_space=pltpu.SMEM)] + [pl.BlockSpec(memory_space=pltpu.VMEM)] * (len(operands) - 1)
    return pl.pallas_call(
        kernel,
        out_shape=[jax.ShapeDtypeStruct(shape, F32) for shape in outs],
        in_specs=specs,
        out_specs=[pl.BlockSpec(memory_space=pltpu.VMEM)] * len(outs),
        scratch_shapes=[pltpu.VMEM(shape, F32) for shape in scratch],
        compiler_params=pltpu.CompilerParams(vmem_limit_bytes=VMEM_LIMIT),
    )(*operands)


def shift_along(x, axis, step):
    devices = lax.axis_size(axis)
    return lax.ppermute(x, axis, [(i, (i + step) % devices) for i in range(devices)])


def prepare(pos, right, iterate, state, classes, load_mask, fixed_mask, main, to_upper, to_lower):
    lane = iota((BY, BZ), 1)

    def slab(x):
        rho = FLOOR + (1.0 - FLOOR) * classes[x].astype(F32) / (CLASSES - 1)
        mask = load_mask[x].astype(F32)
        values = {
            RHO: rho,
            PEN: PENALTY * fixed_mask[x].astype(F32),
        }
        for c in range(3):
            values[ITERATE[c]] = iterate[c, x]
            values[LOAD[c]] = right[c, x] * mask
            values[STATE[c]] = state[c, x]
        last = jnp.zeros((BY, BZ), F32)
        first = jnp.zeros((BY, BZ), F32)
        for (tile, offset, width), value in values.items():
            if tile < PACKED:
                main[tile, x] = value
            last = jnp.where((lane >= offset) & (lane < offset + width), roll(value, offset + width, 1), last)
            low = HALF + offset
            first = jnp.where((lane >= low) & (lane < low + width), roll(value, low, 1), first)
        to_upper[x] = last
        to_lower[x] = first

    loop(0, BX, slab)


def pack_rows(pos, main, state, from_lower, from_upper, packed, to_upper, to_lower):
    below = jnp.where(pos[2] > 0, 1.0, 0.0)
    above = jnp.where(pos[2] < pos[5] - 1, 1.0, 0.0)
    lane = iota((BY, BZ), 1)
    half = BY // 2

    def slab(x):
        joined = jnp.where(lane < HALF, from_lower[x] * below, from_upper[x] * above)
        packed[x] = joined
        for tile in range(12):
            value = joined if tile == PACKED else (main[tile, x] if tile < PACKED else state[tile - 9, x])
            to_upper[tile, x] = value[half:]
            to_lower[tile, x] = value[:half]

    loop(0, BX, slab)


def pack_slabs(pos, main, packed, state, from_lower, from_upper, own, to_upper, to_lower):
    below = jnp.where(pos[1] > 0, 1.0, 0.0)
    above = jnp.where(pos[1] < pos[4] - 1, 1.0, 0.0)

    def slab(x):
        for tile in range(12):
            value = packed[x] if tile == PACKED else (main[tile, x] if tile < PACKED else state[tile - 9, x])
            own[tile, x] = jnp.concatenate([value, from_upper[tile, x] * above, from_lower[tile, x] * below], 0)

    loop(0, BX, slab)
    for tile in range(9):
        for j in range(HALO):
            to_upper[tile * HALO + j] = own[tile, j + 1]
            to_lower[tile * HALO + j] = own[tile, j]
    for c in range(3):
        for j in range(3):
            to_upper[9 * HALO + 3 * c + j] = own[9 + c, BX - 3 + j]
            to_lower[9 * HALO + 3 * c + j] = own[9 + c, j]


def neighbours(field, c, s, kx, ky, kyp, kz, kzp):
    v = field[c, s]
    x = kx[s] * field[c, s - 1] + kx[s + 1] * field[c, s + 1]
    y = ky[s] * roll(v, 1, 0) + kyp[s] * roll(v, -1, 0)
    z = kz[s] * roll(v, 1, 1) + kzp[s] * roll(v, -1, 1)
    return x + y + z + (x, y, z)[c]


def coefficients(stiff, pen, s, scale, kx, ky, kyp, kz, kzp, inverse, diagonal):
    e = stiff[s]
    upper = scale * face(e, stiff[s + 1])
    kx[s + 1] = upper
    y = scale * face(e, roll(e, 1, 0))
    ky[s] = y
    yp = roll(y, -1, 0)
    kyp[s] = yp
    z = scale * face(e, roll(e, 1, 1))
    kz[s] = z
    zp = roll(z, -1, 1)
    kzp[s] = zp
    pairs = (kx[s] + upper, y + yp, z + zp)
    total = pairs[0] + pairs[1] + pairs[2] + pen[s]
    for c in range(3):
        value = total + pairs[c]
        diagonal[c, s] = value
        inverse[c, s] = jnp.where(e > 0.0, 1.0 / jnp.where(e > 0.0, value, 1.0), 0.0)


def descend(pos, own, lower, upper, coarse, v1, start, kx, ky, kyp, kz, kzp, inverse, shifted, weights, forward,
            stiff, load, pen, u, diagonal, v0, half_rows, rows):
    below = jnp.where(pos[0] > 0, 1.0, 0.0)
    above = jnp.where(pos[0] < pos[3] - 1, 1.0, 0.0)
    lane = iota((ROWS, BZ), 1)

    def spread(raw, packed, field, store):
        tile, offset, width = field
        store[0][store[1] + (slice(None), slice(0, BZ))] = raw(tile)
        tail = jnp.where(lane >= BZ - width, roll(packed, BZ - width - offset, 1), 0.0)
        tail = jnp.where(lane < width, roll(packed, -(HALF + offset), 1), tail)
        store[0][store[1] + (slice(None), slice(BZ, LANES))] = tail

    def expand(raw, s):
        packed = raw(PACKED)
        spread(raw, packed, RHO, (stiff, (s,)))
        spread(raw, packed, PEN, (pen, (s,)))
        for c in range(3):
            spread(raw, packed, ITERATE[c], (u, (c, s)))
            spread(raw, packed, LOAD[c], (load, (c, s)))

    def expand_state(raw, packed, s):
        for c in range(3):
            spread(raw, packed, STATE[c], (forward, (c, s)))

    loop(0, HALO, lambda s: expand(lambda t: lower[t * HALO + s] * below, s))
    loop(0, BX, lambda s: expand(lambda t: own[t, s], s + HALO))
    loop(0, HALO, lambda s: expand(lambda t: upper[t * HALO + s] * above, s + HALO + BX))
    shape = (ROWS, BZ)
    loop(0, 3, lambda s: expand_state(lambda t: lower[9 * HALO + 3 * (t - 9) + s] * below, lower[PACKED * HALO + s + HALO - 3] * below, s))
    loop(0, BX, lambda s: expand_state(lambda t: own[t, s], own[PACKED, s], s + 3))
    loop(0, 3, lambda s: expand_state(lambda t: upper[9 * HALO + 3 * (t - 9) + s] * above, upper[PACKED * HALO + s] * above, s + 3 + BX))

    def keep(s):
        weights[s] = stiff[s + HALO - 3]
        for c in range(3):
            shifted[c, s] = u[c, s + HALO - 3]

    loop(0, BX + 6, keep)

    def cube(s):
        rho = stiff[s]
        stiff[s] = rho * rho * rho

    loop(0, SLABS, cube)
    kx[1] = face(stiff[0], stiff[1])
    loop(1, SLABS - 1, lambda s: coefficients(stiff, pen, s, 1.0, kx, ky, kyp, kz, kzp, inverse, diagonal))
    faces = (kx, ky, kyp, kz, kzp)

    def begin(s):
        for c in range(3):
            f = load[c, s] - (diagonal[c, s] * u[c, s] - neighbours(u, c, s, *faces))
            start[c, s] = f
            v0[c, s] = FIRST * f * inverse[c, s]

    loop(1, SLABS - 1, begin)

    def sweep(s):
        for c in range(3):
            v1[c, s] = (1.0 - SECOND) * v0[c, s] + SECOND * inverse[c, s] * (start[c, s] + neighbours(v0, c, s, *faces))

    loop(2, SLABS - 2, sweep)

    def remainder(c, s):
        r = start[c, s] - diagonal[c, s] * v1[c, s] + neighbours(v1, c, s, *faces)
        return r[:BY, :BZ]

    def gather_rows(at, value):
        half_rows[...] = value
        n = BY // 2
        rows[pl.ds(pl.multiple_of(at * n, n), n), :] = half_rows[pl.ds(0, n, stride=2), :] + half_rows[pl.ds(1, n, stride=2), :]

    def pair(i):
        for c in range(3):
            gather_rows(c * 8 + i, remainder(c, 3 + 2 * i) + remainder(c, 4 + 2 * i))

    loop(0, 8, pair)

    def pair_up(i):
        s = 1 + 2 * i
        gather_rows(24 + i, (stiff[s] + stiff[s + 1])[:BY, :BZ] * 0.125)
        gather_rows(34 + i, (pen[s] + pen[s + 1])[:BY, :BZ])

    loop(0, 10, pair_up)
    halve = matrix((BZ, BZ), lambda l, k: (l >> 1) == (k & (HALF - 1)))
    coarse[...] = times(rows[...], halve).reshape(44, 8, BZ)


def level_one(pos, own, lower, upper, chunk, v1, f, kx, ky, kyp, kz, kzp, inverse,
              stiff, pen, diagonal, v0, half_rows, rows, wide):
    below = jnp.where(pos[0] > 0, 1.0, 0.0)
    above = jnp.where(pos[0] < pos[3] - 1, 1.0, 0.0)
    slabs, ys = 18, 24
    for field, at in ((stiff, 0), (pen, 1)):
        for j in range(7):
            field[j] = lower[18 + 7 * at + j] * below
            field[11 + j] = upper[18 + 7 * at + j] * above
        for j in range(4):
            field[7 + j] = own[24 + 10 * at + 3 + j]
    for c in range(3):
        f[c, 0] = jnp.zeros((ys, BZ), F32)
        f[c, 17] = jnp.zeros((ys, BZ), F32)
        for j in range(6):
            f[c, 1 + j] = lower[6 * c + j] * below
            f[c, 11 + j] = upper[6 * c + j] * above
        for j in range(4):
            f[c, 7 + j] = own[8 * c + 2 + j]
    kx[1] = 2.0 * face(stiff[0], stiff[1])
    loop(1, slabs - 1, lambda s: coefficients(stiff, pen, s, 2.0, kx, ky, kyp, kz, kzp, inverse, diagonal))
    faces = (kx, ky, kyp, kz, kzp)

    def begin(s):
        for c in range(3):
            v0[c, s] = FIRST * f[c, s] * inverse[c, s]

    loop(1, slabs - 1, begin)

    def sweep(s):
        for c in range(3):
            v1[c, s] = (1.0 - SECOND) * v0[c, s] + SECOND * inverse[c, s] * (f[c, s] + neighbours(v0, c, s, *faces))

    loop(2, slabs - 2, sweep)

    def gather_rows(at, value):
        half_rows[...] = value
        rows[pl.ds(at * 4, 4), :] = half_rows[pl.ds(0, 4, stride=2), :] + half_rows[pl.ds(1, 4, stride=2), :]

    for i in range(2):
        s = 7 + 2 * i
        for c in range(3):
            total = 0.0
            for at in (s, s + 1):
                total = total + (f[c, at] - diagonal[c, at] * v1[c, at] + neighbours(v1, c, at, *faces))[:8]
            gather_rows(2 * c + i, total)
        gather_rows(6 + i, (stiff[s] + stiff[s + 1])[:8] * 0.125)
        gather_rows(8 + i, (pen[s] + pen[s + 1])[:8])

    def rule(j, k):
        z = jnp.where(j < 96, j, j - BZ)
        return (z >> 1) == (k & 63) - 16

    wide[...] = times(rows[...], matrix((BZ, BZ), rule))
    lane = iota((4, BZ), 1)
    chunk[...] = jnp.zeros((24, BZ), F32)
    for field in range(5):
        chunk[4 * field:4 * field + 4] = jnp.where(lane < 64, wide[8 * field:8 * field + 4], wide[8 * field + 4:8 * field + 8])


def coarse_levels(pos, gathered, out, nx, ny, work):
    (e2, p2, f2, kxm, kxp, kym, kyp, kzm, kzp, iv, dg, va, vb, tall, rows3, e3, p3, f3, jx, jym, jyp, jz, jzp, iv3, wa, wb, rows2) = work
    ys = 4 * ny
    pairs = nx
    lane = iota((ys, BZ), 1)
    row = iota((ys, BZ), 0)
    even = lane < 64
    zero = jnp.zeros((ys, BZ), F32)
    for field in (e2, p2):
        field[0] = zero
        field[pairs + 1] = zero
    for c in range(3):
        for field in (va, vb):
            field[c, 0] = zero
            field[c, pairs + 1] = zero

    def collect(g):
        for field in range(5):
            for yy in range(ny):
                value = gathered[g * ny + yy, pl.ds(4 * field, 4), :]
                if field < 3:
                    f2[field, g + 1, pl.ds(4 * yy, 4), :] = value
                else:
                    (e2, p2)[field - 3][g + 1, pl.ds(4 * yy, 4), :] = value

    loop(0, pairs, collect)

    def x_neighbours(below, mid, above):
        swapped = roll(mid, 64, 1)
        return jnp.where(even, roll(below, 64, 1), swapped), jnp.where(even, swapped, roll(above, 64, 1))

    def coefs(s):
        e = e2[s]
        xm, xp = x_neighbours(e2[s - 1], e, e2[s + 1])
        ym = jnp.where(row == 0, 0.0, roll(e, 1, 0))
        yp = jnp.where(row == ys - 1, 0.0, roll(e, -1, 0))
        a, b = 4.0 * face(e, xm), 4.0 * face(e, xp)
        c0, d = 4.0 * face(e, ym), 4.0 * face(e, yp)
        z = 4.0 * face(e, roll(e, 1, 1))
        zp = roll(z, -1, 1)
        kxm[s] = a
        kxp[s] = b
        kym[s] = jnp.where(row == 0, 0.0, c0)
        kyp[s] = jnp.where(row == ys - 1, 0.0, d)
        kzm[s] = z
        kzp[s] = zp
        sums = (a + b, c0 + d, z + zp)
        total = sums[0] + sums[1] + sums[2] + p2[s]
        for c in range(3):
            value = total + sums[c]
            dg[c, s] = value
            iv[c, s] = jnp.where(e > 0.0, 1.0 / jnp.where(e > 0.0, value, 1.0), 0.0)
            va[c, s] = FIRST * f2[c, s] * iv[c, s]

    loop(1, pairs + 1, coefs)

    def around(v, c, s):
        mid = v[c, s]
        below, above = x_neighbours(v[c, s - 1], mid, v[c, s + 1])
        x = kxm[s] * below + kxp[s] * above
        y = kym[s] * roll(mid, 1, 0) + kyp[s] * roll(mid, -1, 0)
        z = kzm[s] * roll(mid, 1, 1) + kzp[s] * roll(mid, -1, 1)
        return x + y + z + (x, y, z)[c]

    def sweep(source, target, weight):
        def step(s):
            for c in range(3):
                target[c, s] = (1.0 - weight) * source[c, s] + weight * iv[c, s] * (f2[c, s] + around(source, c, s))

        loop(1, pairs + 1, step)

    sweep(va, vb, SECOND)
    n3 = ys // 2

    def gather_rows(at, value):
        tall[...] = value
        rows3[pl.ds(pl.multiple_of(at * n3, 8), n3), :] = tall[pl.ds(0, n3, stride=2), :] + tall[pl.ds(1, n3, stride=2), :]

    def reduce(s):
        for c in range(3):
            gather_rows(c * pairs + s - 1, f2[c, s] - dg[c, s] * vb[c, s] + around(vb, c, s))
        gather_rows(3 * pairs + s - 1, e2[s] * 0.125)
        gather_rows(4 * pairs + s - 1, p2[s])

    loop(1, pairs + 1, reduce)
    down = matrix((BZ, BZ), lambda l, k: ((l & 63) >> 1) == (k & 31))
    rows3[...] = times(rows3[...], down)
    row3 = iota((n3, BZ), 0)
    zero3 = jnp.zeros((n3, BZ), F32)

    def third(at):
        return rows3[pl.ds(pl.multiple_of(at * n3, 8), n3), :]

    e3[0] = zero3
    e3[pairs + 1] = zero3
    for c in range(3):
        for field in (wa, wb):
            field[c, 0] = zero3
            field[c, pairs + 1] = zero3

    def place(s):
        e3[s] = third(3 * pairs + s - 1)

    loop(1, pairs + 1, place)

    def coefs3(s):
        e = e3[s]
        a, b = 8.0 * face(e, e3[s - 1]), 8.0 * face(e, e3[s + 1])
        c0 = 8.0 * face(e, jnp.where(row3 == 0, 0.0, roll(e, 1, 0)))
        d = 8.0 * face(e, jnp.where(row3 == n3 - 1, 0.0, roll(e, -1, 0)))
        z = 8.0 * face(e, roll(e, 1, 1))
        zp = roll(z, -1, 1)
        jx[s] = a
        jx[s + 1] = b
        jym[s] = jnp.where(row3 == 0, 0.0, c0)
        jyp[s] = jnp.where(row3 == n3 - 1, 0.0, d)
        jz[s] = z
        jzp[s] = zp
        sums = (a + b, c0 + d, z + zp)
        total = sums[0] + sums[1] + sums[2] + third(4 * pairs + s - 1)
        for c in range(3):
            value = total + sums[c]
            iv3[c, s] = jnp.where(e > 0.0, 1.0 / jnp.where(e > 0.0, value, 1.0), 0.0)
            wa[c, s] = COARSE * third(c * pairs + s - 1) * iv3[c, s]

    loop(1, pairs + 1, coefs3)
    source, target = wa, wb
    for sweep_at in range(3):
        def step(s, source=source, target=target):
            for c in range(3):
                near = neighbours(source, c, s, jx, jym, jyp, jz, jzp)
                target[c, s] = (1.0 - COARSE) * source[c, s] + COARSE * iv3[c, s] * (third(c * pairs + s - 1) + near)

        loop(1, pairs + 1, step)
        source, target = target, source
    up = matrix((BZ, BZ), lambda k, l: k == ((l & 63) >> 1))
    for c in range(3):
        rows2[...] = times(source[c, 1:pairs + 1].reshape(pairs * n3, BZ), up)

        def add(s, c=c):
            value = rows2[pl.ds(pl.multiple_of((s - 1) * n3, 8), n3), :]
            tall[pl.ds(0, n3, stride=2), :] = value
            tall[pl.ds(1, n3, stride=2), :] = value
            vb[c, s] = vb[c, s] + jnp.where(iv[c, s] > 0.0, tall[...], 0.0)

        loop(1, pairs + 1, add)
    sweep(vb, va, SECOND)

    for c in range(3):
        for at in (0, 1, pairs + 2, pairs + 3):
            out[c, at] = zero

    def last(s):
        for c in range(3):
            out[c, s + 1] = (1.0 - FIRST) * va[c, s] + FIRST * iv[c, s] * (f2[c, s] + around(va, c, s))

    loop(1, pairs + 1, last)


def ascend(pos, gathered, v1, f1, kx1, ky1, kyp1, kz1, kzp1, inverse1, v, start, kx, ky, kyp, kz, kzp, inverse,
           precond, image, sums, e2out, window, rows24, va1, vb1, rows32, spread, va, vb, *work, nx, ny):
    coarse_levels(pos, gathered, e2out, nx, ny, work)
    gx, gy = pos[0], pos[1]
    ys = 4 * ny
    turn = lax.rem(ys - 4 * gy, ys)

    def rule(k, j):
        z = jnp.where((j & 127) < 96, j & 127, (j & 127) - BZ)
        return k == 64 * (j >> 7) + (z >> 1) + 16

    grow = matrix((BZ, LANES), rule)
    for c in range(3):
        for j in range(5):
            window[pl.ds((5 * c + j) * ys, ys), :] = times(pltpu.roll(e2out[c, gx + j], turn, 0), grow)
    for c in range(3):
        for s in range(2, 16):
            x2 = (s - 7) // 2
            j, part = (x2 + 4) // 2, (x2 + 4) % 2
            base = (5 * c + j) * ys
            cols = slice(128 * part, 128 * part + 128)
            if s % 2 == 1 or s == 2:
                low = window[base:base + 8, cols]
                high = window[base + ys - 4:base + ys, cols]
                for at in (0, 1):
                    rows24[pl.ds(at, 8, stride=2), :] = low
                    rows24[pl.ds(16 + at, 4, stride=2), :] = high
            va1[c, s] = v1[c, s] + jnp.where(inverse1[c, s] > 0.0, rows24[...], 0.0)
    faces1 = (kx1, ky1, kyp1, kz1, kzp1)

    def sweep1(source, target, weight, lower, upper):
        def step(s):
            for c in range(3):
                target[c, s] = (1.0 - weight) * source[c, s] + weight * inverse1[c, s] * (
                    f1[c, s] + neighbours(source, c, s, *faces1))

        loop(lower, upper, step)

    sweep1(va1, vb1, SECOND, 3, 15)
    sweep1(vb1, va1, FIRST, 4, 14)
    grow0 = matrix((BZ, LANES), lambda j, l: j == (l >> 1))
    for c in range(3):
        spread[...] = times(va1[c, 4:14].reshape(240, BZ), grow0)

        def widen(i, c=c):
            base = pl.multiple_of(24 * i, 8)
            for half in (0, 1):
                cols = slice(BZ * half, BZ * half + BZ)
                value = spread[pl.ds(base, 24), cols]
                for at in (0, 1):
                    rows32[pl.ds(at, 12, stride=2), :] = value[:12]
                    rows32[pl.ds(24 + at, 4, stride=2), :] = value[20:]
                for at in (0, 1):
                    s = 1 + 2 * i + at
                    va[c, s, :, cols] = v[c, s, :, cols] + rows32[...]

        loop(0, 10, widen)
    faces = (kx, ky, kyp, kz, kzp)

    def sweep_one(s):
        for c in range(3):
            vb[c, s] = (1.0 - SECOND) * va[c, s] + SECOND * inverse[c, s] * (start[c, s] + neighbours(va, c, s, *faces))

    loop(3, SLABS - 3, sweep_one)

    def sweep_two(s):
        for c in range(3):
            precond[c, s - 4] = (1.0 - FIRST) * vb[c, s] + FIRST * inverse[c, s] * (start[c, s] + neighbours(vb, c, s, *faces))

    loop(4, SLABS - 4, sweep_two)

    def inner(x, carry):
        one, two = carry
        s = x + HALO
        for c in range(3):
            p = precond[c, x + 3]
            near = kx[s] * precond[c, x + 2] + kx[s + 1] * precond[c, x + 4]
            y = ky[s] * roll(p, 1, 0) + kyp[s] * roll(p, -1, 0)
            z = kz[s] * roll(p, 1, 1) + kzp[s] * roll(p, -1, 1)
            total = (near + y + z + (near, y, z)[c])[:BY, :BZ]
            mid = p[:BY, :BZ]
            value = mid / inverse[c, s][:BY, :BZ] - total
            image[c, x] = value
            one = one + start[c, s][:BY, :BZ] * mid
            two = two + mid * value
        return one, two

    zero = jnp.zeros((BY, BZ), F32)
    one, two = lax.fori_loop(0, BX, inner, (zero, zero))
    lane = iota((8, BZ), 1)
    sums[...] = jnp.where(lane == 0, jnp.sum(one), jnp.where(lane == 1, jnp.sum(two), 0.0))


def distance_weight(square):
    return max(RADIUS - math.sqrt(square), 0.0)


def finish(pos, totals, precond, image, start, iterate, weights, state, solution, residual, filtered, whole, term, inside):
    total = jnp.sum(totals[...], axis=0, keepdims=True)
    lane = iota((1, BZ), 1)
    one = jnp.sum(jnp.where(lane == 0, total, 0.0), axis=1, keepdims=True)
    two = jnp.sum(jnp.where(lane == 1, total, 0.0), axis=1, keepdims=True)
    alpha = one / two

    def update(s):
        for c in range(3):
            whole[c, s] = iterate[c, s] + alpha * precond[c, s]

    loop(0, BX + 6, update)

    def emit(x):
        for c in range(3):
            solution[c, x] = whole[c, x + 3][:BY, :BZ]
            residual[c, x] = start[c, x + HALO][:BY, :BZ] - alpha * image[c, x]

    loop(0, BX, emit)

    def energy(i):
        s = i + 1
        total = jnp.zeros((ROWS, LANES), F32)
        for c in range(3):
            a, b = state[c, s], whole[c, s]
            along = [
                (a - state[c, s - 1]) * (b - whole[c, s - 1]) + (a - state[c, s + 1]) * (b - whole[c, s + 1])
            ]
            for axis in (0, 1):
                along.append(
                    (a - roll(a, 1, axis)) * (b - roll(b, 1, axis)) + (a - roll(a, -1, axis)) * (b - roll(b, -1, axis))
                )
            total = total + (along[0] + along[1] + along[2] + along[c])
        rho = weights[s]
        term[i] = rho * (-3.0 * rho * rho * (0.5 * total))
        inside[i] = jnp.where(rho > 0.0, 1.0, 0.0)

    loop(0, BX + 4, energy)

    def column(field, x):
        classes = {}
        for a in range(-2, 3):
            t = field[x + 2 + a]
            for b, value in ((0, t), (1, roll(t, 1, 0) + roll(t, -1, 0)), (2, roll(t, 2, 0) + roll(t, -2, 0))):
                q = a * a + b * b
                classes[q] = value if q not in classes else classes[q] + value
        parts = []
        for z in (0, 1, 2):
            part = None
            for q, value in classes.items():
                w = distance_weight(q + z * z)
                if w > 0.0:
                    part = w * value if part is None else part + w * value
            parts.append(part)
        result = parts[0] + roll(parts[1], 1, 1) + roll(parts[1], -1, 1) + roll(parts[2], 2, 1) + roll(parts[2], -2, 1)
        return result[:BY, :BZ]

    def smooth(x):
        rho = weights[x + 3][:BY, :BZ]
        filtered[x] = column(term, x) / (rho * column(inside, x))

    loop(0, BX, smooth)


def body(right_side, iterate, state, classes, load_mask, fixed_mask):
    nx, ny, nz = (lax.axis_size(axis) for axis in ("gx", "gy", "gz"))
    pos = jnp.stack([lax.axis_index("gx"), lax.axis_index("gy"), lax.axis_index("gz")]).astype(jnp.int32)
    pos = jnp.concatenate([pos, jnp.array([nx, ny, nz], jnp.int32)])
    inner = (BX, BY, BZ)
    main, last, first = launch(prepare, [(8,) + inner, inner, inner], [], pos, right_side, iterate, state, classes, load_mask, fixed_mask)
    from_lower, from_upper = shift_along(last, "gz", 1), shift_along(first, "gz", -1)
    edge = (12, BX, BY // 2, BZ)
    packed, to_upper, to_lower = launch(pack_rows, [inner, edge, edge], [], pos, main, state, from_lower, from_upper)
    from_lower, from_upper = shift_along(to_upper, "gy", 1), shift_along(to_lower, "gy", -1)
    sides = (9 * HALO + 9, ROWS, BZ)
    own, to_upper, to_lower = launch(
        pack_slabs, [(12, BX, ROWS, BZ), sides, sides], [], pos, main, packed, state, from_lower, from_upper)
    from_lower, from_upper = shift_along(to_upper, "gx", 1), shift_along(to_lower, "gx", -1)

    wide = (ROWS, LANES)
    one, three = (SLABS,) + wide, (3, SLABS) + wide
    near = (3, BX + 6) + wide
    coarse, v1, start, kx, ky, kyp, kz, kzp, inverse, shifted, weights, forward = launch(
        descend,
        [(44, 8, BZ), three, three, one, one, one, one, one, three, near, (BX + 6,) + wide, near],
        [one, three, one, three, three, three, (BY, BZ), (44 * 8, BZ)],
        pos, own, from_lower, from_upper)

    at_z = pos[2]
    at_y = pos[1]
    lower, upper = shift_along(coarse, "gz", 1), shift_along(coarse, "gz", -1)
    lane = iota(coarse.shape, 2)
    coarse = jnp.where(
        lane < 64, coarse, jnp.where(lane < 96, jnp.where(at_z < nz - 1, upper, 0.0), jnp.where(at_z > 0, lower, 0.0)))
    lower, upper = shift_along(coarse, "gy", 1), shift_along(coarse, "gy", -1)
    coarse = jnp.concatenate([coarse, jnp.where(at_y < ny - 1, upper, 0.0), jnp.where(at_y > 0, lower, 0.0)], 1)
    to_lower = jnp.concatenate([coarse[2:8], coarse[10:16], coarse[18:24], coarse[27:34], coarse[37:44]], 0)
    to_upper = jnp.concatenate([coarse[0:6], coarse[8:14], coarse[16:22], coarse[24:31], coarse[34:41]], 0)
    lower, upper = shift_along(to_upper, "gx", 1), shift_along(to_lower, "gx", -1)

    wide1 = (24, BZ)
    one1, three1 = (18,) + wide1, (3, 18) + wide1
    chunk, v1_1, f1, kx1, ky1, kyp1, kz1, kzp1, inverse1 = launch(
        level_one,
        [(24, BZ), three1, three1, one1, one1, one1, one1, one1, three1],
        [one1, one1, three1, three1, (8, BZ), (40, BZ), (40, BZ)],
        pos, coarse, lower, upper)
    gathered = lax.all_to_all(jnp.broadcast_to(chunk[None], (nx * ny, 24, BZ)), ("gx", "gy"), 0, 0, tiled=True)

    wide2, wide3 = (4 * ny, BZ), (2 * ny, BZ)
    one2, three2 = (nx + 2,) + wide2, (3, nx + 2) + wide2
    one3, three3 = (nx + 2,) + wide3, (3, nx + 2) + wide3
    work = [one2, one2, three2] + [one2] * 6 + [three2] * 4 + [wide2, (5 * nx * 2 * ny, BZ)]
    work += [one3, one3, three3] + [one3] * 5 + [three3] * 3 + [(nx * 2 * ny, BZ)]
    precond, image, sums = launch(
        functools.partial(ascend, nx=nx, ny=ny),
        [near, (3,) + inner, (8, BZ)],
        [(3, nx + 4) + wide2, (15 * 4 * ny, LANES), wide1, three1, three1, (ROWS, BZ), (240, LANES), three, three] + work,
        pos, gathered, v1_1, f1, kx1, ky1, kyp1, kz1, kzp1, inverse1, v1, start, kx, ky, kyp, kz, kzp, inverse)

    total = lax.all_to_all(jnp.broadcast_to(sums[:1], (nx * ny, BZ)), ("gx", "gy"), 0, 0, tiled=True)
    total = jnp.sum(total, axis=0, keepdims=True)
    total = lax.all_to_all(jnp.broadcast_to(total, (nz, BZ)), "gz", 0, 0, tiled=True)
    return tuple(launch(
        finish,
        [(3,) + inner, (3,) + inner, inner],
        [near, (BX + 4,) + wide, (BX + 4,) + wide],
        pos, total, precond, image, start, shifted, weights, forward))


def solution(mesh):
    field, cells = P(None, "gx", "gy", "gz"), P("gx", "gy", "gz")
    return jax.shard_map(
        body,
        mesh=mesh,
        in_specs=(field, field, field, cells, cells, cells),
        out_specs=(field, field, cells),
        check_vma=False,
    )
```

time: 765 us -> 220 us (0.29)
  the two profiles are of different devices: /device:TPU:33 before, /device:TPU:1 now
where the time goes in v1:
time: 220 us; the launch traced here: 219 us
  Pallas kernels  73.2 us (33%)
  blocking collectives  58.9 us (27%)
  starting transfers between devices  42.2 us (19%)
  waiting for transfers between devices  37.2 us (17%)
  local copies, waits for them, and re-layouts  5.51 us (3%)
    pallas_call x7, Pallas kernels, launch(): pl.pallas_call(kernel, out_shape=[jax.ShapeDtypeStruct(shape, F32) for sh...  73.2 us
    ppermute x12, starting transfers between devices, shift_along(): lax.ppermute(x, axis, [(i, (i + step) % devices) for i in range(devices)])  42.2 us
    ppermute x12, waiting for transfers between devices, shift_along(): lax.ppermute(x, axis, [(i, (i + step) % devices) for i in range(devices)])  37.2 us
    all_to_all x1, blocking collectives, body(): lax.all_to_all(jnp.broadcast_to(chunk[None], (nx * ny, 24, BZ)), ('gx', '...  30.8 us
    all_to_all x1, blocking collectives, body(): lax.all_to_all(jnp.broadcast_to(sums[:1], (nx * ny, BZ)), ('gx', 'gy'), 0...  15.6 us
    all_to_all x1, blocking collectives, body(): lax.all_to_all(jnp.broadcast_to(total, (nz, BZ)), 'gz', 0, 0, tiled=True)  12.5 us
  transfers between devices with their start and end apart: 12, of which 10 were waited for; matrix products, arithmetic and copies ran while one was open for 0% of the time, Pallas kernels for 0%

profile of v1, /device:TPU:1, one launch (start us, length us, event | category | flops | bytes accessed | tf_op | source)
XLA Modules:
  0.0 219.4 jit_solution(5952994906065823050)
XLA Ops:
  0.6 0.6 pad_add_fusion.pos
  1.2 2.8 %shard_map.94 = (f32[8,8,16,128]{3,2,1,0:T(8,128)}, f32[8,16,128]{2,1,0:T(8,128)}, f32[8,16,128]{2,1,0:T(8,128)}) custom-call(s32[6]{0:T(128)} %pad_add_fusion.pos, f32[3,8,16,128]{3,2,1,0:T(8,128)} %right.1, f32[3,8,16,128]{3,2,1,0:T(8,128)} %iterate.1, f32[3,8,16,128]{3,2,1,0:T(8,128)} %state.5, s32[8,16,128]{2,1,0:T(8,128)} %classes.1, ...), custom_call_target="tpu_custom_call" | custom-call | tf_op jit(solution)/shard_map/pallas_call | solution.py:69
  4.1 4.0 %collective-permute-start = (f32[8,16,128]{2,1,0:T(8,128)}, f32[8,16,128]{2,1,0:T(8,128)S(1)}, u32[]{:S(2)}, u32[]{:S(2)}) collective-permute-start(f32[8,16,128]{2,1,0:T(8,128)} %get-tuple-element.37), channel_id=1, source_target_pairs={{0,1},{1,2},{2,3},{3,4},{4,5},{5,6},{6,7},{7,0},{8,9},{9,10},{10,1... | collective-permute-start | bytes 196616 | tf_op jit(solution)/shard_map/ppermute | solution.py:81
  8.1 3.8 %collective-permute-start.1 = (f32[8,16,128]{2,1,0:T(8,128)}, f32[8,16,128]{2,1,0:T(8,128)S(1)}, u32[]{:S(2)}, u32[]{:S(2)}) collective-permute-start(f32[8,16,128]{2,1,0:T(8,128)} %get-tuple-element.38), channel_id=1, source_target_pairs={{0,7},{1,0},{2,1},{3,2},{4,3},{5,4},{6,5},{7,6},{8,15},{9,8},{10,9... | collective-permute-start | bytes 196616 | tf_op jit(solution)/shard_map/ppermute | solution.py:81
  11.9 0.0 collective-permute-done.from_lower
  11.9 0.0 copy-start.7
  12.0 1.6 collective-permute-done.1.from_upper
  13.6 0.0 copy-start.8
  13.6 0.0 copy-done.7
  13.6 0.6 copy-done.8
  14.2 2.2 shard_map.95
  16.4 4.0 %collective-permute-start.2 = (f32[12,8,8,128]{3,2,1,0:T(8,128)}, f32[12,8,8,128]{3,2,1,0:T(8,128)S(1)}, u32[]{:S(2)}, u32[]{:S(2)}) collective-permute-start(f32[12,8,8,128]{3,2,1,0:T(8,128)} %get-tuple-element.40), channel_id=1, source_target_pairs={{0,8},{8,16},{16,24},{24,32},{32,40},{40,48},{48,56},{56,0},{1,9},... | collective-permute-start | bytes 1179656 | tf_op jit(solution)/shard_map/ppermute | solution.py:81
  20.4 8.6 %collective-permute-start.3 = (f32[12,8,8,128]{3,2,1,0:T(8,128)}, f32[12,8,8,128]{3,2,1,0:T(8,128)S(1)}, u32[]{:S(2)}, u32[]{:S(2)}) collective-permute-start(f32[12,8,8,128]{3,2,1,0:T(8,128)} %get-tuple-element.41), channel_id=1, source_target_pairs={{0,56},{8,0},{16,8},{24,16},{32,24},{40,32},{48,40},{56,48},{1,57}... | collective-permute-start | bytes 1179656 | tf_op jit(solution)/shard_map/ppermute | solution.py:81
  29.0 5.8 %collective-permute-done.2.from_lower = f32[12,8,8,128]{3,2,1,0:T(8,128)S(1)} collective-permute-done((f32[12,8,8,128]{3,2,1,0:T(8,128)}, f32[12,8,8,128]{3,2,1,0:T(8,128)S(1)}, u32[]{:S(2)}, u32[]{:S(2)}) %collective-permute-start.2) | collective-permute-done | bytes 393248 | tf_op jit(solution)/shard_map/ppermute | solution.py:81
  34.8 0.0 copy-start.5
  34.8 1.0 collective-permute-done.3.from_upper
  35.8 0.0 copy-start.6
  35.8 0.0 copy-done.5
  35.8 0.7 copy-done.6
  36.5 3.5 %shard_map.96 = (f32[12,8,32,128]{3,2,1,0:T(8,128)}, f32[72,32,128]{2,1,0:T(8,128)}, f32[72,32,128]{2,1,0:T(8,128)}) custom-call(s32[6]{0:T(128)} %pad_add_fusion.pos, f32[8,8,16,128]{3,2,1,0:T(8,128)} %get-tuple-element.36.main, f32[8,16,128]{2,1,0:T(8,128)} %get-tuple-element.39.packed, f32[3,8,16,128]{3,2,1,0:T(8,128)} %state.5, ...), custom_call_target="tpu_custom_call" | custom-call | tf_op jit(solution)/shard_map/pallas_call | solution.py:69
  40.0 3.9 %collective-permute-start.4 = (f32[72,32,128]{2,1,0:T(8,128)}, f32[72,32,128]{2,1,0:T(8,128)S(1)}, u32[]{:S(2)}, u32[]{:S(2)}) collective-permute-start(f32[72,32,128]{2,1,0:T(8,128)} %get-tuple-element.43), channel_id=1, source_target_pairs={{0,64},{64,128},{128,192},{192,256},{256,320},{320,384},{384,448},... | collective-permute-start | bytes 3538952 | tf_op jit(solution)/shard_map/ppermute | solution.py:81
  43.9 0.0 collective-permute-start.5
  43.9 13.5 %collective-permute-done.4.lower = f32[72,32,128]{2,1,0:T(8,128)S(1)} collective-permute-done((f32[72,32,128]{2,1,0:T(8,128)}, f32[72,32,128]{2,1,0:T(8,128)S(1)}, u32[]{:S(2)}, u32[]{:S(2)}) %collective-permute-start.4) | collective-permute-done | bytes 1179680 | tf_op jit(solution)/shard_map/ppermute | solution.py:81
  57.4 0.0 copy-start.1
  57.4 2.4 %collective-permute-done.5.upper = f32[72,32,128]{2,1,0:T(8,128)S(1)} collective-permute-done((f32[72,32,128]{2,1,0:T(8,128)}, f32[72,32,128]{2,1,0:T(8,128)S(1)}, u32[]{:S(2)}, u32[]{:S(2)}) %collective-permute-start.5) | collective-permute-done | bytes 1179680 | tf_op jit(solution)/shard_map/ppermute | solution.py:81
  59.8 0.0 copy-start.2
  59.8 0.0 copy-done.1
  59.8 1.1 copy-done.2
  60.9 22.0 %shard_map.97 = (f32[44,8,128]{2,1,0:T(8,128)}, f32[3,22,32,256]{3,2,1,0:T(8,128)}, f32[3,22,32,256]{3,2,1,0:T(8,128)}, f32[22,32,256]{2,1,0:T(8,128)}, f32[22,3...) custom-call(s32[6]{0:T(128)} %pad_add_fusion.pos, ...), custom_call_target="tpu_custom_call" | custom-call | tf_op jit(solution)/shard_map/pallas_call | solution.py:69
  82.8 3.0 %collective-permute-start.7 = (f32[44,8,128]{2,1,0:T(8,128)}, f32[44,8,128]{2,1,0:T(8,128)S(1)}, u32[]{:S(2)}, u32[]{:S(2)}) collective-permute-start(f32[44,8,128]{2,1,0:T(8,128)} %get-tuple-element.45), channel_id=1, source_target_pairs={{0,1},{1,2},{2,3},{3,4},{4,5},{5,6},{6,7},{7,0},{8,9},{9,10},{10,1... | collective-permute-start | bytes 540680 | tf_op jit(solution)/shard_map/ppermute | solution.py:81
  85.8 3.7 %collective-permute-start.6 = (f32[44,8,128]{2,1,0:T(8,128)}, f32[44,8,128]{2,1,0:T(8,128)S(1)}, u32[]{:S(2)}, u32[]{:S(2)}) collective-permute-start(f32[44,8,128]{2,1,0:T(8,128)} %get-tuple-element.45), channel_id=1, source_target_pairs={{0,7},{1,0},{2,1},{3,2},{4,3},{5,4},{6,5},{7,6},{8,15},{9,8},{10,9... | collective-permute-start | bytes 540680 | tf_op jit(solution)/shard_map/ppermute | solution.py:81
  89.6 2.6 %collective-permute-done.7 = f32[44,8,128]{2,1,0:T(8,128)S(1)} collective-permute-done((f32[44,8,128]{2,1,0:T(8,128)}, f32[44,8,128]{2,1,0:T(8,128)S(1)}, u32[]{:S(2)}, u32[]{:S(2)}) %collective-permute-start.7) | collective-permute-done | bytes 180256 | tf_op jit(solution)/shard_map/ppermute | solution.py:81
  92.2 2.2 collective-permute-done.6
  94.4 0.9 select_select_fusion
  95.3 1.9 collective-permute-start.9
  97.3 5.2 %collective-permute-start.8 = (f32[44,8,128]{2,1,0:T(8,128)S(1)}, f32[44,8,128]{2,1,0:T(8,128)S(1)}, u32[]{:S(2)}, u32[]{:S(2)}) collective-permute-start(f32[44,8,128]{2,1,0:T(8,128)S(1)} %select_select_fusion), channel_id=1, source_target_pairs={{0,56},{8,0},{16,8},{24,16},{32,24},{40,32},{48,40},{56,48},{1,57}... | collective-permute-start | bytes 540680 | tf_op jit(solution)/shard_map/ppermute | solution.py:81
  102.5 1.5 collective-permute-done.9
  104.1 0.9 collective-permute-done.8
  104.9 0.1 pad_maximum_fusion.own
  105.0 0.0 copy-start
  105.1 2.3 %collective-permute-start.11 = (f32[32,24,128]{2,1,0:T(8,128)S(1)}, f32[32,24,128]{2,1,0:T(8,128)S(1)}, u32[]{:S(2)}, u32[]{:S(2)}) collective-permute-start(f32[32,24,128]{2,1,0:T(8,128)S(1)} %get-tuple-element.69), channel_id=1, source_target_pairs={{0,448},{64,0},{128,64},{192,128},{256,192},{320,256},{384,320},{4... | collective-permute-start | bytes 1179656 | tf_op jit(solution)/shard_map/ppermute | solution.py:81
  107.5 1.7 collective-permute-start.10
  109.1 5.7 %collective-permute-done.11.upper = f32[32,24,128]{2,1,0:T(8,128)S(1)} collective-permute-done((f32[32,24,128]{2,1,0:T(8,128)S(1)}, f32[32,24,128]{2,1,0:T(8,128)S(1)}, u32[]{:S(2)}, u32[]{:S(2)}) %collective-permute-start.11) | collective-permute-done | bytes 393248 | tf_op jit(solution)/shard_map/ppermute | solution.py:81
  114.8 0.0 copy-start.3
  114.8 0.0 collective-permute-done.10.lower
  114.9 0.0 copy-done
  114.9 0.7 copy-done.3
  115.6 0.0 copy-start.4
  115.6 0.8 copy-done.4
  116.3 7.1 %shard_map.98 = (f32[24,128]{1,0:T(8,128)}, f32[3,18,24,128]{3,2,1,0:T(8,128)}, f32[3,18,24,128]{3,2,1,0:T(8,128)}, f32[18,24,128]{2,1,0:T(8,128)}, f32[18,24,12...) custom-call(s32[6]{0:T(128)} %pad_add_fusion.pos, ...), custom_call_target="tpu_custom_call" | custom-call | tf_op jit(solution)/shard_map/pallas_call | solution.py:69
  123.4 0.8 broadcast_in_dim.25
  124.2 30.8 %all_to_all.19.gathered = f32[64,24,128]{2,1,0:T(8,128)} all-to-all(f32[64,24,128]{2,1,0:T(8,128)S(1)} %broadcast_in_dim.25), channel_id=1, replica_groups=mesh['gx'=8,'gy'=8,'gz'=8] {'gx','gy'}, dimensions={0} | all-to-all | bytes 1572864 | tf_op jit(solution)/shard_map/all_to_all | solution.py:688
  155.0 27.9 %shard_map.99 = (f32[3,14,32,256]{3,2,1,0:T(8,128)}, f32[3,8,16,128]{3,2,1,0:T(8,128)}, f32[8,128]{1,0:T(8,128)}) custom-call(s32[6]{0:T(128)} %pad_add_fusion.pos, f32[64,24,128]{2,1,0:T(8,128)} %all_to_all.19.gathered, f32[3,18,24,128]{3,2,1,0:T(8,128)} %get-tuple-element.47.v1, f32[3,18,24,128]{3,2,1,0:T(8,128)} %get-tuple-element.48.f1, ...), custom_call_target="tpu_custom_call" | custom-call | tf_op jit(solution)/shard_map/pallas_call | solution.py:69
  182.9 0.7 slice_bitcast_fusion
  183.6 15.6 %all_to_all.20 = f32[64,1,128]{2,1,0:T(1,128)S(1)} all-to-all(f32[64,1,128]{2,1,0:T(1,128)S(1)} %broadcast_in_dim.26), channel_id=1, replica_groups=mesh['gx'=8,'gy'=8,'gz'=8] {'gx','gy'}, dimensions={0} | all-to-all | bytes 65536 | tf_op jit(solution)/shard_map/all_to_all | solution.py:701
  199.2 12.5 %all_to_all.21 = f32[8,1,128]{2,1,0:T(1,128)} all-to-all(f32[8,1,128]{2,1,0:T(1,128)S(1)} %broadcast_in_dim.27), channel_id=1, replica_groups=mesh['gx'=8,'gy'=8,'gz'=8] {'gz'}, dimensions={0} | all-to-all | bytes 8192 | tf_op jit(solution)/shard_map/all_to_all | solution.py:703
  211.7 7.7 %shard_map.100 = (f32[3,8,16,128]{3,2,1,0:T(8,128)}, f32[3,8,16,128]{3,2,1,0:T(8,128)}, f32[8,16,128]{2,1,0:T(8,128)}) custom-call(s32[6]{0:T(128)} %pad_add_fusion.pos, f32[8,128]{1,0:T(8,128)} %bitcast.8, f32[3,14,32,256]{3,2,1,0:T(8,128)} %get-tuple-element.64.precond, f32[3,8,16,128]{3,2,1,0:T(8,128)} %get-tuple-element.65.image, ...), custom_call_target="tpu_custom_call" | custom-call | tf_op jit(solution)/shard_map/pallas_call | solution.py:69
  (12 shorter events, 0.2 us)
Async XLA Ops:
  4.1 7.9 %collective-permute-start = (f32[8,16,128]{2,1,0:T(8,128)}, f32[8,16,128]{2,1,0:T(8,128)S(1)}, u32[]{:S(2)}, u32[]{:S(2)}) collective-permute-start(f32[8,16,128]{2,1,0:T(8,128)} %get-tuple-element.37), channel_id=1, source_target_pairs={{0,1},{1,2},{2,3},{3,4},{4,5},{5,6},{6,7},{7,0},{8,9},{9,10},{10,1... | collective-permute-start | bytes 196616 | tf_op jit(solution)/shard_map/ppermute | solution.py:81
  8.1 5.4 %collective-permute-start.1 = (f32[8,16,128]{2,1,0:T(8,128)}, f32[8,16,128]{2,1,0:T(8,128)S(1)}, u32[]{:S(2)}, u32[]{:S(2)}) collective-permute-start(f32[8,16,128]{2,1,0:T(8,128)} %get-tuple-element.38), channel_id=1, source_target_pairs={{0,7},{1,0},{2,1},{3,2},{4,3},{5,4},{6,5},{7,6},{8,15},{9,8},{10,9... | collective-permute-start | bytes 196616 | tf_op jit(solution)/shard_map/ppermute | solution.py:81
  11.9 1.6 copy-start.7
  13.6 0.6 copy-start.8
  16.4 18.4 %collective-permute-start.2 = (f32[12,8,8,128]{3,2,1,0:T(8,128)}, f32[12,8,8,128]{3,2,1,0:T(8,128)S(1)}, u32[]{:S(2)}, u32[]{:S(2)}) collective-permute-start(f32[12,8,8,128]{3,2,1,0:T(8,128)} %get-tuple-element.40), channel_id=1, source_target_pairs={{0,8},{8,16},{16,24},{24,32},{32,40},{40,48},{48,56},{56,0},{1,9},... | collective-permute-start | bytes 1179656 | tf_op jit(solution)/shard_map/ppermute | solution.py:81
  20.4 15.4 %collective-permute-start.3 = (f32[12,8,8,128]{3,2,1,0:T(8,128)}, f32[12,8,8,128]{3,2,1,0:T(8,128)S(1)}, u32[]{:S(2)}, u32[]{:S(2)}) collective-permute-start(f32[12,8,8,128]{3,2,1,0:T(8,128)} %get-tuple-element.41), channel_id=1, source_target_pairs={{0,56},{8,0},{16,8},{24,16},{32,24},{40,32},{48,40},{56,48},{1,57}... | collective-permute-start | bytes 1179656 | tf_op jit(solution)/shard_map/ppermute | solution.py:81
  34.8 1.0 copy-start.5
  35.8 0.7 copy-start.6
  40.0 17.4 %collective-permute-start.4 = (f32[72,32,128]{2,1,0:T(8,128)}, f32[72,32,128]{2,1,0:T(8,128)S(1)}, u32[]{:S(2)}, u32[]{:S(2)}) collective-permute-start(f32[72,32,128]{2,1,0:T(8,128)} %get-tuple-element.43), channel_id=1, source_target_pairs={{0,64},{64,128},{128,192},{192,256},{256,320},{320,384},{384,448},... | collective-permute-start | bytes 3538952 | tf_op jit(solution)/shard_map/ppermute | solution.py:81
  43.9 15.8 %collective-permute-start.5 = (f32[72,32,128]{2,1,0:T(8,128)}, f32[72,32,128]{2,1,0:T(8,128)S(1)}, u32[]{:S(2)}, u32[]{:S(2)}) collective-permute-start(f32[72,32,128]{2,1,0:T(8,128)} %get-tuple-element.44), channel_id=1, source_target_pairs={{0,448},{64,0},{128,64},{192,128},{256,192},{320,256},{384,320},{4... | collective-permute-start | bytes 3538952 | tf_op jit(solution)/shard_map/ppermute | solution.py:81
  57.4 2.4 %copy-start.1 = (f32[72,32,128]{2,1,0:T(8,128)}, f32[72,32,128]{2,1,0:T(8,128)S(1)}, u32[]{:S(2)}) copy-start(f32[72,32,128]{2,1,0:T(8,128)S(1)} %collective-permute-done.4.lower) | copy-start | bytes 3538948
  59.8 1.1 copy-start.2
  82.8 9.4 %collective-permute-start.7 = (f32[44,8,128]{2,1,0:T(8,128)}, f32[44,8,128]{2,1,0:T(8,128)S(1)}, u32[]{:S(2)}, u32[]{:S(2)}) collective-permute-start(f32[44,8,128]{2,1,0:T(8,128)} %get-tuple-element.45), channel_id=1, source_target_pairs={{0,1},{1,2},{2,3},{3,4},{4,5},{5,6},{6,7},{7,0},{8,9},{9,10},{10,1... | collective-permute-start | bytes 540680 | tf_op jit(solution)/shard_map/ppermute | solution.py:81
  85.8 8.6 %collective-permute-start.6 = (f32[44,8,128]{2,1,0:T(8,128)}, f32[44,8,128]{2,1,0:T(8,128)S(1)}, u32[]{:S(2)}, u32[]{:S(2)}) collective-permute-start(f32[44,8,128]{2,1,0:T(8,128)} %get-tuple-element.45), channel_id=1, source_target_pairs={{0,7},{1,0},{2,1},{3,2},{4,3},{5,4},{6,5},{7,6},{8,15},{9,8},{10,9... | collective-permute-start | bytes 540680 | tf_op jit(solution)/shard_map/ppermute | solution.py:81
  95.3 8.7 %collective-permute-start.9 = (f32[44,8,128]{2,1,0:T(8,128)S(1)}, f32[44,8,128]{2,1,0:T(8,128)S(1)}, u32[]{:S(2)}, u32[]{:S(2)}) collective-permute-start(f32[44,8,128]{2,1,0:T(8,128)S(1)} %select_select_fusion), channel_id=1, source_target_pairs={{0,8},{8,16},{16,24},{24,32},{32,40},{40,48},{48,56},{56,0},{1,9},... | collective-permute-start | bytes 540680 | tf_op jit(solution)/shard_map/ppermute | solution.py:81
  97.3 7.6 %collective-permute-start.8 = (f32[44,8,128]{2,1,0:T(8,128)S(1)}, f32[44,8,128]{2,1,0:T(8,128)S(1)}, u32[]{:S(2)}, u32[]{:S(2)}) collective-permute-start(f32[44,8,128]{2,1,0:T(8,128)S(1)} %select_select_fusion), channel_id=1, source_target_pairs={{0,56},{8,0},{16,8},{24,16},{32,24},{40,32},{48,40},{56,48},{1,57}... | collective-permute-start | bytes 540680 | tf_op jit(solution)/shard_map/ppermute | solution.py:81
  105.0 9.9 %copy-start = (f32[44,24,128]{2,1,0:T(8,128)}, f32[44,24,128]{2,1,0:T(8,128)S(1)}, u32[]{:S(2)}) copy-start(f32[44,24,128]{2,1,0:T(8,128)S(1)} %pad_maximum_fusion.own) | copy-start | bytes 1622020
  105.1 9.7 %collective-permute-start.11 = (f32[32,24,128]{2,1,0:T(8,128)S(1)}, f32[32,24,128]{2,1,0:T(8,128)S(1)}, u32[]{:S(2)}, u32[]{:S(2)}) collective-permute-start(f32[32,24,128]{2,1,0:T(8,128)S(1)} %get-tuple-element.69), channel_id=1, source_target_pairs={{0,448},{64,0},{128,64},{192,128},{256,192},{320,256},{384,320},{4... | collective-permute-start | bytes 1179656 | tf_op jit(solution)/shard_map/ppermute | solution.py:81
  107.5 7.4 %collective-permute-start.10 = (f32[32,24,128]{2,1,0:T(8,128)S(1)}, f32[32,24,128]{2,1,0:T(8,128)S(1)}, u32[]{:S(2)}, u32[]{:S(2)}) collective-permute-start(f32[32,24,128]{2,1,0:T(8,128)S(1)} %get-tuple-element.70), channel_id=1, source_target_pairs={{0,64},{64,128},{128,192},{192,256},{256,320},{320,384},{384,448},... | collective-permute-start | bytes 1179656 | tf_op jit(solution)/shard_map/ppermute | solution.py:81
  114.8 0.7 copy-start.3
  115.6 0.8 copy-start.4

commit v2 on v1

--- a/solution.py
+++ b/solution.py
@@ -31,7 +31,7 @@
 STATE = ((9, 52, 3), (10, 55, 3), (11, 58, 3))
 HALF = BZ // 2
 
-VMEM_LIMIT = 56 * 1024 * 1024
+VMEM_LIMIT = 34 * 1024 * 1024
 
 
 def iota(shape, dim):
@@ -42,16 +42,19 @@
     return pltpu.roll(x, shift % x.shape[axis], axis)
 
 
-def loop(lower, upper, step):
+def loop(lower, upper, step, unroll=4):
     def run(i, carry):
         step(i)
         return carry
 
-    lax.fori_loop(lower, upper, run, 0)
+    lax.fori_loop(lower, upper, run, 0, unroll=unroll)
 
 
 def times(x, m):
-    return jnp.dot(x, m, precision=lax.Precision.HIGHEST, preferred_element_type=F32)
+    m = m.astype(jnp.bfloat16)
+    high = x.astype(jnp.bfloat16)
+    low = (x - high.astype(F32)).astype(jnp.bfloat16)
+    return jnp.dot(high, m, preferred_element_type=F32) + jnp.dot(low, m, preferred_element_type=F32)
 
 
 def matrix(shape, rule):

time: 220 us -> 201 us (0.914)
  Pallas kernels: 73.2 us -> 33.6 us
  local copies, waits for them, and re-layouts: 5.51 us -> 23.2 us
    pallas_call x7, Pallas kernels: 73.2 us -> 33.6 us  [launch(): pl.pallas_call(kernel, out_shape=[jax.ShapeDtypeStruct(shape, F32) for sh...]
    unnamed x22 -> x60, local copies, waits for them, and re-layouts: 4.02 us -> 23.1 us
where the time goes in v2:
time: 201 us; the launch traced here: 200 us
  blocking collectives  59.8 us (30%)
  starting transfers between devices  41.1 us (20%)
  waiting for transfers between devices  37.6 us (19%)
  Pallas kernels  33.6 us (17%)
  local copies, waits for them, and re-layouts  23.2 us (12%)
  other arithmetic  3.67 us (2%)
    ppermute x12, starting transfers between devices, shift_along(): lax.ppermute(x, axis, [(i, (i + step) % devices) for i in range(devices)])  41.1 us
    ppermute x12, waiting for transfers between devices, shift_along(): lax.ppermute(x, axis, [(i, (i + step) % devices) for i in range(devices)])  37.6 us
    pallas_call x7, Pallas kernels, launch(): pl.pallas_call(kernel, out_shape=[jax.ShapeDtypeStruct(shape, F32) for sh...  33.6 us
    all_to_all x1, blocking collectives, body(): lax.all_to_all(jnp.broadcast_to(chunk[None], (nx * ny, 24, BZ)), ('gx', '...  31.8 us
    unnamed x60, local copies, waits for them, and re-layouts  23.1 us
    all_to_all x1, blocking collectives, body(): lax.all_to_all(jnp.broadcast_to(sums[:1], (nx * ny, BZ)), ('gx', 'gy'), 0...  15.5 us
    all_to_all x1, blocking collectives, body(): lax.all_to_all(jnp.broadcast_to(total, (nz, BZ)), 'gz', 0, 0, tiled=True)  12.5 us
  transfers between devices with their start and end apart: 12, of which 10 were waited for; matrix products, arithmetic and copies ran while one was open for 0% of the time, Pallas kernels for 0%

profile of v2, /device:TPU:1, one launch (start us, length us, event | category | flops | bytes accessed | tf_op | source)
XLA Modules:
  0.0 199.8 jit_solution(16837719647738943276)
XLA Ops:
  0.6 0.1 pad_add_fusion.pos
  0.7 0.9 copy-done.4
  1.7 0.9 copy-done.23
  2.6 0.9 copy-done.24
  3.5 0.8 copy-done.25
  4.4 0.8 copy-done.26
  5.2 0.8 copy-done.27
  6.0 1.1 shard_map.94
  7.1 4.0 %collective-permute-start = (f32[8,16,128]{2,1,0:T(8,128)S(1)}, f32[8,16,128]{2,1,0:T(8,128)S(1)}, u32[]{:S(2)}, u32[]{:S(2)}) collective-permute-start(f32[8,16,128]{2,1,0:T(8,128)S(1)} %get-tuple-element.37), channel_id=1, source_target_pairs={{0,1},{1,2},{2,3},{3,4},{4,5},{5,6},{6,7},{7,0},{8,9},{9,10},{10,1... | collective-permute-start | bytes 196616 | tf_op jit(solution)/shard_map/ppermute | solution.py:84
  11.1 3.8 %collective-permute-start.1 = (f32[8,16,128]{2,1,0:T(8,128)S(1)}, f32[8,16,128]{2,1,0:T(8,128)S(1)}, u32[]{:S(2)}, u32[]{:S(2)}) collective-permute-start(f32[8,16,128]{2,1,0:T(8,128)S(1)} %get-tuple-element.38), channel_id=1, source_target_pairs={{0,7},{1,0},{2,1},{3,2},{4,3},{5,4},{6,5},{7,6},{8,15},{9,8},{10,9... | collective-permute-start | bytes 196616 | tf_op jit(solution)/shard_map/ppermute | solution.py:84
  15.0 0.0 collective-permute-done.from_lower
  15.0 1.3 collective-permute-done.1.from_upper
  16.3 0.6 shard_map.95
  16.9 4.0 %collective-permute-start.2 = (f32[12,8,8,128]{3,2,1,0:T(8,128)S(1)}, f32[12,8,8,128]{3,2,1,0:T(8,128)S(1)}, u32[]{:S(2)}, u32[]{:S(2)}) collective-permute-start(f32[12,8,8,128]{3,2,1,0:T(8,128)S(1)} %get-tuple-element.40), channel_id=1, source_target_pairs={{0,8},{8,16},{16,24},{24,32},{32,40},{40,48},{48,56},{56,0},{1,9},... | collective-permute-start | bytes 1179656 | tf_op jit(solution)/shard_map/ppermute | solution.py:84
  20.9 8.6 %collective-permute-start.3 = (f32[12,8,8,128]{3,2,1,0:T(8,128)S(1)}, f32[12,8,8,128]{3,2,1,0:T(8,128)S(1)}, u32[]{:S(2)}, u32[]{:S(2)}) collective-permute-start(f32[12,8,8,128]{3,2,1,0:T(8,128)S(1)} %get-tuple-element.41), channel_id=1, source_target_pairs={{0,56},{8,0},{16,8},{24,16},{32,24},{40,32},{48,40},{56,48},{1,57}... | collective-permute-start | bytes 1179656 | tf_op jit(solution)/shard_map/ppermute | solution.py:84
  29.5 5.5 %collective-permute-done.2.from_lower = f32[12,8,8,128]{3,2,1,0:T(8,128)S(1)} collective-permute-done((f32[12,8,8,128]{3,2,1,0:T(8,128)S(1)}, f32[12,8,8,128]{3,2,1,0:T(8,128)S(1)}, u32[]{:S(2)}, u32[]{:S(2)}) %collective-permute-start.2) | collective-permute-done | bytes 393248 | tf_op jit(solution)/shard_map/ppermute | solution.py:84
  35.0 0.9 collective-permute-done.3.from_upper
  35.9 0.8 shard_map.96
  36.7 4.0 %collective-permute-start.4 = (f32[72,32,128]{2,1,0:T(8,128)S(1)}, f32[72,32,128]{2,1,0:T(8,128)S(1)}, u32[]{:S(2)}, u32[]{:S(2)}) collective-permute-start(f32[72,32,128]{2,1,0:T(8,128)S(1)} %get-tuple-element.43), channel_id=1, source_target_pairs={{0,64},{64,128},{128,192},{192,256},{256,320},{320,384},{384,448},... | collective-permute-start | bytes 3538952 | tf_op jit(solution)/shard_map/ppermute | solution.py:84
  40.8 0.0 collective-permute-start.5
  40.8 13.1 %collective-permute-done.4.lower = f32[72,32,128]{2,1,0:T(8,128)S(1)} collective-permute-done((f32[72,32,128]{2,1,0:T(8,128)S(1)}, f32[72,32,128]{2,1,0:T(8,128)S(1)}, u32[]{:S(2)}, u32[]{:S(2)}) %collective-permute-start.4) | collective-permute-done | bytes 1179680 | tf_op jit(solution)/shard_map/ppermute | solution.py:84
  53.9 2.5 %collective-permute-done.5.upper = f32[72,32,128]{2,1,0:T(8,128)S(1)} collective-permute-done((f32[72,32,128]{2,1,0:T(8,128)S(1)}, f32[72,32,128]{2,1,0:T(8,128)S(1)}, u32[]{:S(2)}, u32[]{:S(2)}) %collective-permute-start.5) | collective-permute-done | bytes 1179680 | tf_op jit(solution)/shard_map/ppermute | solution.py:84
  56.4 11.3 %shard_map.97 = (f32[44,8,128]{2,1,0:T(8,128)}, f32[3,22,32,256]{3,2,1,0:T(8,128)S(1)}, f32[3,22,32,256]{3,2,1,0:T(8,128)S(1)}, f32[22,32,256]{2,1,0:T(8,128)S(1...) custom-call(s32[6]{0:T(128)S(1)} %pad_add_fusion.pos, ...), custom_call_target="tpu_custom_call" | custom-call | tf_op jit(solution)/shard_map/pallas_call | solution.py:72
  67.7 1.3 copy-done
  69.0 1.4 copy-done.2
  70.4 1.1 copy-done.5
  71.6 0.9 copy-done.9
  72.4 0.9 copy-done.11
  73.4 0.9 copy-done.13
  74.2 0.8 copy-done.15
  75.1 0.9 copy-done.17
  76.0 0.8 copy-done.19
  76.8 3.1 %collective-permute-start.7 = (f32[44,8,128]{2,1,0:T(8,128)}, f32[44,8,128]{2,1,0:T(8,128)}, u32[]{:S(2)}, u32[]{:S(2)}) collective-permute-start(f32[44,8,128]{2,1,0:T(8,128)} %get-tuple-element.45), channel_id=1, source_target_pairs={{0,1},{1,2},{2,3},{3,4},{4,5},{5,6},{6,7},{7,0},{8,9},{9,10},{10,1... | collective-permute-start | bytes 540680 | tf_op jit(solution)/shard_map/ppermute | solution.py:84
  79.8 3.7 %collective-permute-start.6 = (f32[44,8,128]{2,1,0:T(8,128)}, f32[44,8,128]{2,1,0:T(8,128)}, u32[]{:S(2)}, u32[]{:S(2)}) collective-permute-start(f32[44,8,128]{2,1,0:T(8,128)} %get-tuple-element.45), channel_id=1, source_target_pairs={{0,7},{1,0},{2,1},{3,2},{4,3},{5,4},{6,5},{7,6},{8,15},{9,8},{10,9... | collective-permute-start | bytes 540680 | tf_op jit(solution)/shard_map/ppermute | solution.py:84
  83.6 3.2 %collective-permute-done.7 = f32[44,8,128]{2,1,0:T(8,128)} collective-permute-done((f32[44,8,128]{2,1,0:T(8,128)}, f32[44,8,128]{2,1,0:T(8,128)}, u32[]{:S(2)}, u32[]{:S(2)}) %collective-permute-start.7) | collective-permute-done | bytes 180256 | tf_op jit(solution)/shard_map/ppermute | solution.py:84
  86.8 2.2 %collective-permute-done.6 = f32[44,8,128]{2,1,0:T(8,128)} collective-permute-done((f32[44,8,128]{2,1,0:T(8,128)}, f32[44,8,128]{2,1,0:T(8,128)}, u32[]{:S(2)}, u32[]{:S(2)}) %collective-permute-start.6) | collective-permute-done | bytes 180256 | tf_op jit(solution)/shard_map/ppermute | solution.py:84
  89.0 1.7 select_select_fusion
  90.7 1.9 collective-permute-start.9
  92.6 5.3 %collective-permute-start.8 = (f32[44,8,128]{2,1,0:T(8,128)}, f32[44,8,128]{2,1,0:T(8,128)S(1)}, u32[]{:S(2)}, u32[]{:S(2)}) collective-permute-start(f32[44,8,128]{2,1,0:T(8,128)} %select_select_fusion), channel_id=1, source_target_pairs={{0,56},{8,0},{16,8},{24,16},{32,24},{40,32},{48,40},{56,48},{1,57}... | collective-permute-start | bytes 540680 | tf_op jit(solution)/shard_map/ppermute | solution.py:84
  97.9 2.3 %collective-permute-done.9 = f32[44,8,128]{2,1,0:T(8,128)} collective-permute-done((f32[44,8,128]{2,1,0:T(8,128)}, f32[44,8,128]{2,1,0:T(8,128)}, u32[]{:S(2)}, u32[]{:S(2)}) %collective-permute-start.9) | collective-permute-done | bytes 180256 | tf_op jit(solution)/shard_map/ppermute | solution.py:84
  100.3 0.8 collective-permute-done.8
  101.2 0.0 copy-start.12
  101.2 1.1 pad_maximum_fusion.own
  102.3 0.0 copy-start.3
  102.4 1.9 collective-permute-start.11
  104.2 0.8 collective-permute-start.10
  105.0 5.7 %collective-permute-done.11.upper = f32[32,24,128]{2,1,0:T(8,128)S(1)} collective-permute-done((f32[32,24,128]{2,1,0:T(8,128)S(1)}, f32[32,24,128]{2,1,0:T(8,128)S(1)}, u32[]{:S(2)}, u32[]{:S(2)}) %collective-permute-start.11) | collective-permute-done | bytes 393248 | tf_op jit(solution)/shard_map/ppermute | solution.py:84
  110.7 0.0 collective-permute-done.10.lower
  110.7 2.4 %shard_map.98 = (f32[24,128]{1,0:T(8,128)S(1)}, f32[3,18,24,128]{3,2,1,0:T(8,128)S(1)}, f32[3,18,24,128]{3,2,1,0:T(8,128)S(1)}, f32[18,24,128]{2,1,0:T(8,128)S(1...) custom-call(s32[6]{0:T(128)S(1)} %pad_add_fusion.pos, ...), custom_call_target="tpu_custom_call" | custom-call | tf_op jit(solution)/shard_map/pallas_call | solution.py:72
  113.2 0.1 broadcast_in_dim.25
  113.3 31.8 %all_to_all.19.gathered = f32[64,24,128]{2,1,0:T(8,128)S(1)} all-to-all(f32[64,24,128]{2,1,0:T(8,128)S(1)} %broadcast_in_dim.25), channel_id=1, replica_groups=mesh['gx'=8,'gy'=8,'gz'=8] {'gx','gy'}, dimensions={0} | all-to-all | bytes 1572864 | tf_op jit(solution)/shard_map/all_to_all | solution.py:691
  145.1 1.1 copy-done.16
  146.2 1.1 copy-done.18
  147.3 13.0 %shard_map.99 = (f32[3,14,32,256]{3,2,1,0:T(8,128)S(1)}, f32[3,8,16,128]{3,2,1,0:T(8,128)S(1)}, f32[8,128]{1,0:T(8,128)S(1)}) custom-call(s32[6]{0:T(128)S(1)} %pad_add_fusion.pos, f32[64,24,128]{2,1,0:T(8,128)S(1)} %all_to_all.19.gathered, f32[3,18,24,128]{3,2,1,0:T(8,128)S(1)} %get-tuple-element.47.v1, f32[3,18,24,128]{3,2,1,0:T(8,128)S(1)} %get-tuple-element.48.f1, ...), custom_call_target="tpu_custom_call" | custom-call | tf_op jit(solution)/shard_map/pallas_call | solution.py:72
  160.3 1.1 copy-done.7
  161.4 0.7 copy-done.21
  162.1 15.5 %all_to_all.20 = f32[64,1,128]{2,1,0:T(1,128)} all-to-all(f32[64,1,128]{2,1,0:T(1,128)S(1)} %broadcast_in_dim.26), channel_id=1, replica_groups=mesh['gx'=8,'gy'=8,'gz'=8] {'gx','gy'}, dimensions={0} | all-to-all | bytes 65536 | tf_op jit(solution)/shard_map/all_to_all | solution.py:704
  177.7 0.8 reduce_sum.9
  178.5 12.5 %all_to_all.21 = f32[8,1,128]{2,1,0:T(1,128)S(1)} all-to-all(f32[8,1,128]{2,1,0:T(1,128)S(1)} %broadcast_in_dim.27), channel_id=1, replica_groups=mesh['gx'=8,'gy'=8,'gz'=8] {'gz'}, dimensions={0} | all-to-all | bytes 8192 | tf_op jit(solution)/shard_map/all_to_all | solution.py:706
  190.9 1.3 copy-done.6
  192.3 1.3 copy-done.8
  193.6 1.0 copy-done.20
  194.6 0.9 copy-done.22
  195.5 4.3 %shard_map.100 = (f32[3,8,16,128]{3,2,1,0:T(8,128)}, f32[3,8,16,128]{3,2,1,0:T(8,128)}, f32[8,16,128]{2,1,0:T(8,128)}) custom-call(s32[6]{0:T(128)S(1)} %pad_add_fusion.pos, f32[8,128]{1,0:T(8,128)S(1)} %bitcast.7, f32[3,14,32,256]{3,2,1,0:T(8,128)S(1)} %copy-done.8, f32[3,8,16,128]{3,2,1,0:T(8,128)S(1)} %copy-done.22, ...), custom_call_target="tpu_custom_call" | custom-call | tf_op jit(solution)/shard_map/pallas_call | solution.py:72
  (43 shorter events, 0.2 us)
Async XLA Ops:
  0.7 0.9 copy-start.4
  1.7 0.9 copy-start.23
  2.6 0.9 copy-start.24
  3.5 0.8 copy-start.25
  4.4 0.8 copy-start.26
  5.2 0.8 copy-start.27
  7.1 7.9 %collective-permute-start = (f32[8,16,128]{2,1,0:T(8,128)S(1)}, f32[8,16,128]{2,1,0:T(8,128)S(1)}, u32[]{:S(2)}, u32[]{:S(2)}) collective-permute-start(f32[8,16,128]{2,1,0:T(8,128)S(1)} %get-tuple-element.37), channel_id=1, source_target_pairs={{0,1},{1,2},{2,3},{3,4},{4,5},{5,6},{6,7},{7,0},{8,9},{9,10},{10,1... | collective-permute-start | bytes 196616 | tf_op jit(solution)/shard_map/ppermute | solution.py:84
  11.1 5.1 %collective-permute-start.1 = (f32[8,16,128]{2,1,0:T(8,128)S(1)}, f32[8,16,128]{2,1,0:T(8,128)S(1)}, u32[]{:S(2)}, u32[]{:S(2)}) collective-permute-start(f32[8,16,128]{2,1,0:T(8,128)S(1)} %get-tuple-element.38), channel_id=1, source_target_pairs={{0,7},{1,0},{2,1},{3,2},{4,3},{5,4},{6,5},{7,6},{8,15},{9,8},{10,9... | collective-permute-start | bytes 196616 | tf_op jit(solution)/shard_map/ppermute | solution.py:84
  16.9 18.1 %collective-permute-start.2 = (f32[12,8,8,128]{3,2,1,0:T(8,128)S(1)}, f32[12,8,8,128]{3,2,1,0:T(8,128)S(1)}, u32[]{:S(2)}, u32[]{:S(2)}) collective-permute-start(f32[12,8,8,128]{3,2,1,0:T(8,128)S(1)} %get-tuple-element.40), channel_id=1, source_target_pairs={{0,8},{8,16},{16,24},{24,32},{32,40},{40,48},{48,56},{56,0},{1,9},... | collective-permute-start | bytes 1179656 | tf_op jit(solution)/shard_map/ppermute | solution.py:84
  20.9 15.0 %collective-permute-start.3 = (f32[12,8,8,128]{3,2,1,0:T(8,128)S(1)}, f32[12,8,8,128]{3,2,1,0:T(8,128)S(1)}, u32[]{:S(2)}, u32[]{:S(2)}) collective-permute-start(f32[12,8,8,128]{3,2,1,0:T(8,128)S(1)} %get-tuple-element.41), channel_id=1, source_target_pairs={{0,56},{8,0},{16,8},{24,16},{32,24},{40,32},{48,40},{56,48},{1,57}... | collective-permute-start | bytes 1179656 | tf_op jit(solution)/shard_map/ppermute | solution.py:84
  36.7 17.2 %collective-permute-start.4 = (f32[72,32,128]{2,1,0:T(8,128)S(1)}, f32[72,32,128]{2,1,0:T(8,128)S(1)}, u32[]{:S(2)}, u32[]{:S(2)}) collective-permute-start(f32[72,32,128]{2,1,0:T(8,128)S(1)} %get-tuple-element.43), channel_id=1, source_target_pairs={{0,64},{64,128},{128,192},{192,256},{256,320},{320,384},{384,448},... | collective-permute-start | bytes 3538952 | tf_op jit(solution)/shard_map/ppermute | solution.py:84
  40.8 15.6 %collective-permute-start.5 = (f32[72,32,128]{2,1,0:T(8,128)S(1)}, f32[72,32,128]{2,1,0:T(8,128)S(1)}, u32[]{:S(2)}, u32[]{:S(2)}) collective-permute-start(f32[72,32,128]{2,1,0:T(8,128)S(1)} %get-tuple-element.44), channel_id=1, source_target_pairs={{0,448},{64,0},{128,64},{192,128},{256,192},{320,256},{384,320},{4... | collective-permute-start | bytes 3538952 | tf_op jit(solution)/shard_map/ppermute | solution.py:84
  67.7 1.4 copy-start
  69.0 1.4 copy-start.2
  70.4 1.1 copy-start.5
  71.5 0.9 copy-start.9
  72.4 0.9 copy-start.11
  73.4 0.9 copy-start.13
  74.2 0.8 copy-start.15
  75.1 0.9 copy-start.17
  76.0 0.8 copy-start.19
  76.8 10.0 %collective-permute-start.7 = (f32[44,8,128]{2,1,0:T(8,128)}, f32[44,8,128]{2,1,0:T(8,128)}, u32[]{:S(2)}, u32[]{:S(2)}) collective-permute-start(f32[44,8,128]{2,1,0:T(8,128)} %get-tuple-element.45), channel_id=1, source_target_pairs={{0,1},{1,2},{2,3},{3,4},{4,5},{5,6},{6,7},{7,0},{8,9},{9,10},{10,1... | collective-permute-start | bytes 540680 | tf_op jit(solution)/shard_map/ppermute | solution.py:84
  79.8 9.1 %collective-permute-start.6 = (f32[44,8,128]{2,1,0:T(8,128)}, f32[44,8,128]{2,1,0:T(8,128)}, u32[]{:S(2)}, u32[]{:S(2)}) collective-permute-start(f32[44,8,128]{2,1,0:T(8,128)} %get-tuple-element.45), channel_id=1, source_target_pairs={{0,7},{1,0},{2,1},{3,2},{4,3},{5,4},{6,5},{7,6},{8,15},{9,8},{10,9... | collective-permute-start | bytes 540680 | tf_op jit(solution)/shard_map/ppermute | solution.py:84
  90.7 9.6 %collective-permute-start.9 = (f32[44,8,128]{2,1,0:T(8,128)}, f32[44,8,128]{2,1,0:T(8,128)}, u32[]{:S(2)}, u32[]{:S(2)}) collective-permute-start(f32[44,8,128]{2,1,0:T(8,128)} %select_select_fusion), channel_id=1, source_target_pairs={{0,8},{8,16},{16,24},{24,32},{32,40},{40,48},{48,56},{56,0},{1,9},... | collective-permute-start | bytes 540680 | tf_op jit(solution)/shard_map/ppermute | solution.py:84
  92.6 8.5 %collective-permute-start.8 = (f32[44,8,128]{2,1,0:T(8,128)}, f32[44,8,128]{2,1,0:T(8,128)S(1)}, u32[]{:S(2)}, u32[]{:S(2)}) collective-permute-start(f32[44,8,128]{2,1,0:T(8,128)} %select_select_fusion), channel_id=1, source_target_pairs={{0,56},{8,0},{16,8},{24,16},{32,24},{40,32},{48,40},{56,48},{1,57}... | collective-permute-start | bytes 540680 | tf_op jit(solution)/shard_map/ppermute | solution.py:84
  101.1 43.9 %copy-start.14 = (f32[22,32,256]{2,1,0:T(8,128)S(1)}, f32[22,32,256]{2,1,0:T(8,128)}, u32[]{:S(2)}) copy-start(f32[22,32,256]{2,1,0:T(8,128)} %copy-done.13) | copy-start | bytes 2162692
  101.2 43.9 %copy-start.12 = (f32[22,32,256]{2,1,0:T(8,128)S(1)}, f32[22,32,256]{2,1,0:T(8,128)}, u32[]{:S(2)}) copy-start(f32[22,32,256]{2,1,0:T(8,128)} %copy-done.11) | copy-start | bytes 2162692
  102.2 42.8 %copy-start.10 = (f32[22,32,256]{2,1,0:T(8,128)S(1)}, f32[22,32,256]{2,1,0:T(8,128)}, u32[]{:S(2)}) copy-start(f32[22,32,256]{2,1,0:T(8,128)} %copy-done.9) | copy-start | bytes 2162692
  102.3 42.8 %copy-start.3 = (f32[3,22,32,256]{3,2,1,0:T(8,128)S(1)}, f32[3,22,32,256]{3,2,1,0:T(8,128)}, u32[]{:S(2)}) copy-start(f32[3,22,32,256]{3,2,1,0:T(8,128)} %copy-done.2) | copy-start | bytes 6488068
  102.4 8.4 %collective-permute-start.11 = (f32[32,24,128]{2,1,0:T(8,128)S(1)}, f32[32,24,128]{2,1,0:T(8,128)S(1)}, u32[]{:S(2)}, u32[]{:S(2)}) collective-permute-start(f32[32,24,128]{2,1,0:T(8,128)S(1)} %get-tuple-element.69), channel_id=1, source_target_pairs={{0,448},{64,0},{128,64},{192,128},{256,192},{320,256},{384,320},{4... | collective-permute-start | bytes 1179656 | tf_op jit(solution)/shard_map/ppermute | solution.py:84
  104.2 6.5 %collective-permute-start.10 = (f32[32,24,128]{2,1,0:T(8,128)S(1)}, f32[32,24,128]{2,1,0:T(8,128)S(1)}, u32[]{:S(2)}, u32[]{:S(2)}) collective-permute-start(f32[32,24,128]{2,1,0:T(8,128)S(1)} %get-tuple-element.70), channel_id=1, source_target_pairs={{0,64},{64,128},{128,192},{192,256},{256,320},{320,384},{384,448},... | collective-permute-start | bytes 1179656 | tf_op jit(solution)/shard_map/ppermute | solution.py:84
  113.2 31.9 %copy-start.1 = (f32[3,22,32,256]{3,2,1,0:T(8,128)S(1)}, f32[3,22,32,256]{3,2,1,0:T(8,128)}, u32[]{:S(2)}) copy-start(f32[3,22,32,256]{3,2,1,0:T(8,128)} %copy-done) | copy-start | bytes 6488068
  145.1 1.1 copy-start.16
  146.2 1.1 copy-start.18
  160.3 1.1 copy-start.7
  161.4 0.7 copy-start.21
  190.9 1.3 copy-start.6
  192.3 1.3 copy-start.8
  193.6 1.0 copy-start.20
  194.6 0.9 copy-start.22

commit v3 on v2

v3 whole, which is shorter than its diff:
```python
import functools
import math

import jax
import jax.numpy as jnp
from jax import lax
from jax.experimental import pallas as pl
from jax.experimental.pallas import tpu as pltpu
from jax.sharding import PartitionSpec as P

F32 = jnp.float32
FLOOR = 0.25
CLASSES = 16
PENALTY = 4.0
FIRST = 0.55
SECOND = 1.05
COARSE = 0.6
RADIUS = 3

BX, BY, BZ = 8, 16, 128
HALO = 7
SLABS = BX + 2 * HALO
ROWS = 2 * BY
LANES = 2 * BZ

PACKED = 8
ITERATE = ((0, 0, 7), (1, 7, 7), (2, 14, 7))
RHO = (3, 21, 7)
LOAD = ((4, 28, 6), (5, 34, 6), (6, 40, 6))
PEN = (7, 46, 6)
STATE = ((9, 52, 3), (10, 55, 3), (11, 58, 3))
FIELDS = ITERATE + (RHO,) + LOAD + (PEN,) + STATE
HALF = BZ // 2

MIB = 1024 * 1024


def iota(shape, dim):
    return lax.broadcasted_iota(jnp.int32, shape, dim)


def roll(x, shift, axis):
    return pltpu.roll(x, shift % x.shape[axis], axis)


def loop(lower, upper, step, unroll=4):
    def run(i, carry):
        step(i)
        return carry

    lax.fori_loop(lower, upper, run, 0, unroll=unroll)


def times(x, m):
    m = m.astype(jnp.bfloat16)
    high = x.astype(jnp.bfloat16)
    low = (x - high.astype(F32)).astype(jnp.bfloat16)
    return jnp.dot(high, m, preferred_element_type=F32) + jnp.dot(low, m, preferred_element_type=F32)


def matrix(shape, rule):
    return jnp.where(rule(iota(shape, 0), iota(shape, 1)), 1.0, 0.0).astype(F32)


def face(a, b):
    total = a + b
    both = (a > 0.0) & (b > 0.0)
    return jnp.where(both, 2.0 * a * b / jnp.where(both, total, 1.0), total)


def launch(limit, kernel, outs, scratch, operands, far_outs=(), far=(), copies=0, cost=None):
    near_spec, far_spec = pl.BlockSpec(memory_space=pltpu.VMEM), pl.BlockSpec(memory_space=pltpu.HBM)
    specs = [pl.BlockSpec(memory_space=pltpu.SMEM)] + [near_spec] * (len(operands) - 1) + [far_spec] * len(far)
    return pl.pallas_call(
        kernel,
        out_shape=[jax.ShapeDtypeStruct(shape, F32) for shape in outs] + [pltpu.HBM(shape, F32) for shape in far_outs],
        in_specs=specs,
        out_specs=[near_spec] * len(outs) + [far_spec] * len(far_outs),
        scratch_shapes=[pltpu.VMEM(shape, F32) for shape in scratch] + ([pltpu.SemaphoreType.DMA((copies,))] if copies else []),
        compiler_params=pltpu.CompilerParams(vmem_limit_bytes=limit * MIB),
        cost_estimate=cost,
    )(*operands, *[pltpu.with_memory_space_constraint(x, pltpu.HBM) for x in far])


def shift_along(x, axis, step):
    devices = lax.axis_size(axis)
    return lax.ppermute(x, axis, [(i, (i + step) % devices) for i in range(devices)])


def prepare(pos, right_far, iterate_far, state_far, classes_far, load_far, fixed_far, main, to_upper, to_lower, right, copied):
    def rest(classes, load_mask, fixed_mask):
        moves = [
            pltpu.make_async_copy(source, target, copied.at[i])
            for i, (source, target) in enumerate((
                (classes_far, classes), (load_far, load_mask), (fixed_far, fixed_mask), (right_far, right),
                (iterate_far, main.at[0:3]), (state_far, main.at[8:11])))
        ]
        for move in moves:
            move.start()
        for move in moves:
            move.wait()
        lane = iota((BY, BZ), 1)

        def slab(x):
            mask = load_mask[x].astype(F32)
            main[3, x] = FLOOR + (1.0 - FLOOR) * classes[x].astype(F32) / (CLASSES - 1)
            main[7, x] = PENALTY * fixed_mask[x].astype(F32)
            for c in range(3):
                main[4 + c, x] = right[c, x] * mask
            last = jnp.zeros((BY, BZ), F32)
            first = jnp.zeros((BY, BZ), F32)
            for tile, offset, width in FIELDS:
                value = main[tile if tile < PACKED else tile - 1, x]
                last = jnp.where((lane >= offset) & (lane < offset + width), roll(value, offset + width, 1), last)
                low = HALF + offset
                first = jnp.where((lane >= low) & (lane < low + width), roll(value, low, 1), first)
            to_upper[x] = last
            to_lower[x] = first

        loop(0, BX, slab)

    cells = pltpu.VMEM((BX, BY, BZ), jnp.int32)
    pl.run_scoped(rest, cells, cells, cells)


def pack_rows(pos, main, from_lower, from_upper, packed, to_upper, to_lower):
    below = jnp.where(pos[2] > 0, 1.0, 0.0)
    above = jnp.where(pos[2] < pos[5] - 1, 1.0, 0.0)
    lane = iota((BY, BZ), 1)
    half = BY // 2

    def slab(x):
        joined = jnp.where(lane < HALF, from_lower[x] * below, from_upper[x] * above)
        packed[x] = joined
        for tile in range(12):
            value = joined if tile == PACKED else main[tile if tile < PACKED else tile - 1, x]
            to_upper[tile, x] = value[half:]
            to_lower[tile, x] = value[:half]

    loop(0, BX, slab)


def pack_slabs(pos, main, packed, from_lower, from_upper, own, to_upper, to_lower):
    below = jnp.where(pos[1] > 0, 1.0, 0.0)
    above = jnp.where(pos[1] < pos[4] - 1, 1.0, 0.0)

    def slab(x):
        for tile in range(12):
            value = packed[x] if tile == PACKED else main[tile if tile < PACKED else tile - 1, x]
            own[tile, x] = jnp.concatenate([value, from_upper[tile, x] * above, from_lower[tile, x] * below], 0)

    loop(0, BX, slab)
    for tile in range(9):
        for j in range(HALO):
            to_upper[tile * HALO + j] = own[tile, j + 1]
            to_lower[tile * HALO + j] = own[tile, j]
    for c in range(3):
        for j in range(3):
            to_upper[9 * HALO + 3 * c + j] = own[9 + c, BX - 3 + j]
            to_lower[9 * HALO + 3 * c + j] = own[9 + c, j]


def neighbours(field, c, s, kx, ky, kyp, kz, kzp, at=None):
    at = s if at is None else at
    v = field[c, s]
    x = kx[at] * field[c, s - 1] + kx[at + 1] * field[c, s + 1]
    y = ky[at] * roll(v, 1, 0) + kyp[at] * roll(v, -1, 0)
    z = kz[at] * roll(v, 1, 1) + kzp[at] * roll(v, -1, 1)
    return x + y + z + (x, y, z)[c]


def coefficients(stiff, pen, s, scale, kx, ky, kyp, kz, kzp, inverse, diagonal):
    e = stiff[s]
    upper = scale * face(e, stiff[s + 1])
    kx[s + 1] = upper
    y = scale * face(e, roll(e, 1, 0))
    ky[s] = y
    yp = roll(y, -1, 0)
    kyp[s] = yp
    z = scale * face(e, roll(e, 1, 1))
    kz[s] = z
    zp = roll(z, -1, 1)
    kzp[s] = zp
    pairs = (kx[s] + upper, y + yp, z + zp)
    total = pairs[0] + pairs[1] + pairs[2] + pen[s]
    for c in range(3):
        value = total + pairs[c]
        diagonal[c, s] = value
        inverse[c, s] = jnp.where(e > 0.0, 1.0 / jnp.where(e > 0.0, value, 1.0), 0.0)


def descend(pos, own, lower, upper, coarse, low_lanes, high_lanes, *rest):
    far, rest = rest[:11], rest[11:]
    (v1, start, kx, ky, kyp, kz, kzp, inverse, u, weights, forward, stiff, load, pen, diagonal, v0, half_rows, rows, copied) = rest
    moves = []

    def send(*pairs):
        for source, target in pairs:
            move = pltpu.make_async_copy(source, far[target], copied.at[target])
            move.start()
            moves.append(move)

    below = jnp.where(pos[0] > 0, 1.0, 0.0)
    above = jnp.where(pos[0] < pos[3] - 1, 1.0, 0.0)
    lane = iota((ROWS, BZ), 1)

    def spread(raw, packed, field, store):
        tile, offset, width = field
        store[0][store[1] + (slice(None), slice(0, BZ))] = raw(tile)
        tail = jnp.where(lane >= BZ - width, roll(packed, BZ - width - offset, 1), 0.0)
        tail = jnp.where(lane < width, roll(packed, -(HALF + offset), 1), tail)
        store[0][store[1] + (slice(None), slice(BZ, LANES))] = tail

    def expand(raw, s):
        packed = raw(PACKED)
        spread(raw, packed, RHO, (weights, (s,)))
        spread(raw, packed, PEN, (pen, (s,)))
        for c in range(3):
            spread(raw, packed, ITERATE[c], (u, (c, s)))
            spread(raw, packed, LOAD[c], (load, (c, s)))

    def expand_state(raw, packed, s):
        for c in range(3):
            spread(raw, packed, STATE[c], (forward, (c, s)))

    loop(0, HALO, lambda s: expand(lambda t: lower[t * HALO + s] * below, s))
    loop(0, BX, lambda s: expand(lambda t: own[t, s], s + HALO))
    loop(0, HALO, lambda s: expand(lambda t: upper[t * HALO + s] * above, s + HALO + BX))
    loop(0, 3, lambda s: expand_state(lambda t: lower[9 * HALO + 3 * (t - 9) + s] * below, lower[PACKED * HALO + s + HALO - 3] * below, s))
    loop(0, BX, lambda s: expand_state(lambda t: own[t, s], own[PACKED, s], s + 3))
    loop(0, 3, lambda s: expand_state(lambda t: upper[9 * HALO + 3 * (t - 9) + s] * above, upper[PACKED * HALO + s] * above, s + 3 + BX))

    send((u.at[:, 4:18], 8), (weights.at[4:18], 9), (forward, 10))

    def cube(s):
        rho = weights[s]
        stiff[s] = rho * rho * rho

    loop(0, SLABS, cube)
    kx[1] = face(stiff[0], stiff[1])
    loop(1, SLABS - 1, lambda s: coefficients(stiff, pen, s, 1.0, kx, ky, kyp, kz, kzp, inverse, diagonal))
    faces = (kx, ky, kyp, kz, kzp)
    send((kx.at[3:20], 2), (ky.at[3:19], 3), (kyp.at[3:19], 4), (kz.at[3:19], 5), (kzp.at[3:19], 6), (inverse.at[:, 3:19], 7))

    def begin(s):
        for c in range(3):
            f = load[c, s] - (diagonal[c, s] * u[c, s] - neighbours(u, c, s, *faces))
            start[c, s] = f
            v0[c, s] = FIRST * f * inverse[c, s]

    loop(1, SLABS - 1, begin)
    send((start.at[:, 3:19], 1))

    def sweep(s):
        for c in range(3):
            v1[c, s] = (1.0 - SECOND) * v0[c, s] + SECOND * inverse[c, s] * (start[c, s] + neighbours(v0, c, s, *faces))

    loop(2, SLABS - 2, sweep)
    send((v1.at[:, 2:20], 0))

    def remainder(c, s):
        r = start[c, s] - diagonal[c, s] * v1[c, s] + neighbours(v1, c, s, *faces)
        return r[:, :BZ]

    def gather_rows(at, value):
        half_rows[...] = value
        n = ROWS // 2
        rows[pl.ds(pl.multiple_of(at * n, n), n), :] = half_rows[pl.ds(0, n, stride=2), :] + half_rows[pl.ds(1, n, stride=2), :]

    def pair(i):
        for c in range(3):
            gather_rows(c * 8 + i, remainder(c, 3 + 2 * i) + remainder(c, 4 + 2 * i))

    loop(0, 8, pair)

    def pair_up(i):
        s = 1 + 2 * i
        gather_rows(24 + i, (stiff[s] + stiff[s + 1])[:, :BZ] * 0.125)
        gather_rows(34 + i, (pen[s] + pen[s + 1])[:, :BZ])

    loop(0, 10, pair_up)
    halve = matrix((BZ, BZ), lambda l, k: (l >> 1) == (k & (HALF - 1)))
    coarse[...] = times(rows[...], halve).reshape(44, 16, BZ)
    quarter = iota((8, BZ), 1) >> 5

    def pack(g):
        for h in range(2):
            low = jnp.zeros((8, BZ), F32)
            high = jnp.zeros((8, BZ), F32)
            for q in range(4):
                value = coarse[4 * g + q, 8 * h:8 * h + 8]
                turned = roll(value, 32, 1)
                one, two = (value, turned) if q % 2 == 0 else (turned, value)
                low = jnp.where(quarter == q, one, low)
                high = jnp.where(quarter == q, two, high)
            low_lanes[2 * g + h] = low
            high_lanes[2 * g + h] = high

    loop(0, 11, pack)
    for move in moves:
        move.wait()


def join_lanes(pos, coarse, from_lower, from_upper, out, center):
    below = jnp.where(pos[2] > 0, 1.0, 0.0)
    above = jnp.where(pos[2] < pos[5] - 1, 1.0, 0.0)
    lane = iota((8, BZ), 1)

    def unpack(g):
        for h in range(2):
            low, high = from_lower[2 * g + h] * below, from_upper[2 * g + h] * above
            for q in range(4):
                halo = jnp.where(lane < 96, roll(high, 64 - 32 * q, 1), roll(low, 96 - 32 * q, 1))
                value = jnp.where(lane < 64, coarse[4 * g + q, 8 * h:8 * h + 8], halo)
                out[4 * g + q, 8 * h:8 * h + 8] = value
                if h == 0:
                    center[4 * g + q] = value

    loop(0, 11, unpack)


def join_rows(pos, coarse, from_lower, from_upper, out, to_upper, to_lower):
    below = jnp.where(pos[1] > 0, 1.0, 0.0)
    above = jnp.where(pos[1] < pos[4] - 1, 1.0, 0.0)

    def join(i):
        out[i] = jnp.concatenate([coarse[i], from_upper[i] * above, from_lower[i] * below], 0)

    loop(0, 44, join)
    at = 0
    for base, count in ((0, 6), (8, 6), (16, 6), (24, 7), (34, 7)):
        shift = 2 if count == 6 else 3
        for j in range(count):
            to_upper[at] = out[base + j]
            to_lower[at] = out[base + shift + j]
            at += 1


def smooth_down(slabs, f, v0, v1, inverse, faces):
    def begin(s):
        for c in range(3):
            v0[c, s] = FIRST * f[c, s] * inverse[c, s]

    loop(1, slabs - 1, begin)

    def sweep(s):
        for c in range(3):
            v1[c, s] = (1.0 - SECOND) * v0[c, s] + SECOND * inverse[c, s] * (f[c, s] + neighbours(v0, c, s, *faces))

    loop(2, slabs - 2, sweep)


def level_one(pos, own, chunk, kx, ky, kyp, kz, kzp, inverse, diagonal, f, v0, v1, half_rows, rows, wide):
    stiff, pen = own.at[24:34], own.at[34:44]
    slabs = 10
    for c in range(3):
        for i in range(8):
            f[c, 1 + i] = own[8 * c + i]
    kx[1] = 2.0 * face(stiff[0], stiff[1])
    loop(1, slabs - 1, lambda s: coefficients(stiff, pen, s, 2.0, kx, ky, kyp, kz, kzp, inverse, diagonal))
    faces = (kx, ky, kyp, kz, kzp)
    smooth_down(slabs, f, v0, v1, inverse, faces)

    def gather_rows(at, value):
        half_rows[...] = value
        rows[pl.ds(at * 4, 4), :] = half_rows[pl.ds(0, 4, stride=2), :] + half_rows[pl.ds(1, 4, stride=2), :]

    for i in range(2):
        s = 3 + 2 * i
        for c in range(3):
            total = 0.0
            for at in (s, s + 1):
                total = total + (f[c, at] - diagonal[c, at] * v1[c, at] + neighbours(v1, c, at, *faces))[:8]
            gather_rows(2 * c + i, total)
        gather_rows(6 + i, (stiff[s] + stiff[s + 1])[:8] * 0.125)
        gather_rows(8 + i, (pen[s] + pen[s + 1])[:8])

    def rule(j, k):
        z = jnp.where(j < 96, j, j - BZ)
        return (z >> 1) == (k & 63) - 16

    wide[...] = times(rows[...], matrix((BZ, BZ), rule))
    lane = iota((4, BZ), 1)
    chunk[...] = jnp.zeros((24, BZ), F32)
    for field in range(5):
        chunk[4 * field:4 * field + 4] = jnp.where(lane < 64, wide[8 * field:8 * field + 4], wide[8 * field + 4:8 * field + 8])


def level_one_again(pos, own, lower, upper, v1, f, kx, ky, kyp, kz, kzp, inverse, stiff, pen, diagonal, v0):
    below = jnp.where(pos[0] > 0, 1.0, 0.0)
    above = jnp.where(pos[0] < pos[3] - 1, 1.0, 0.0)
    slabs = 18
    for field, at in ((stiff, 0), (pen, 1)):
        for j in range(7):
            field[j] = lower[18 + 7 * at + j] * below
            field[11 + j] = upper[18 + 7 * at + j] * above
        for j in range(4):
            field[7 + j] = own[24 + 10 * at + 3 + j]
    for c in range(3):
        for j in range(6):
            f[c, 1 + j] = lower[6 * c + j] * below
            f[c, 11 + j] = upper[6 * c + j] * above
        for j in range(4):
            f[c, 7 + j] = own[8 * c + 2 + j]
    kx[1] = 2.0 * face(stiff[0], stiff[1])
    loop(1, slabs - 1, lambda s: coefficients(stiff, pen, s, 2.0, kx, ky, kyp, kz, kzp, inverse, diagonal))
    smooth_down(slabs, f, v0, v1, inverse, (kx, ky, kyp, kz, kzp))


def coarse_levels(pos, gathered, out, nx, ny, work):
    (e2, p2, f2, kxm, kxp, kym, kyp, kzm, kzp, iv, dg, va, vb, tall, rows3, e3, p3, f3, jx, jym, jyp, jz, jzp, iv3, wa, wb, rows2) = work
    ys = 4 * ny
    pairs = nx
    lane = iota((ys, BZ), 1)
    row = iota((ys, BZ), 0)
    even = lane < 64
    zero = jnp.zeros((ys, BZ), F32)
    for field in (e2, p2):
        field[0] = zero
        field[pairs + 1] = zero
    for c in range(3):
        for field in (va, vb):
            field[c, 0] = zero
            field[c, pairs + 1] = zero

    def collect(g):
        for field in range(5):
            for yy in range(ny):
                value = gathered[g * ny + yy, pl.ds(4 * field, 4), :]
                if field < 3:
                    f2[field, g + 1, pl.ds(4 * yy, 4), :] = value
                else:
                    (e2, p2)[field - 3][g + 1, pl.ds(4 * yy, 4), :] = value

    loop(0, pairs, collect)

    def x_neighbours(below, mid, above):
        swapped = roll(mid, 64, 1)
        return jnp.where(even, roll(below, 64, 1), swapped), jnp.where(even, swapped, roll(above, 64, 1))

    def coefs(s):
        e = e2[s]
        xm, xp = x_neighbours(e2[s - 1], e, e2[s + 1])
        ym = jnp.where(row == 0, 0.0, roll(e, 1, 0))
        yp = jnp.where(row == ys - 1, 0.0, roll(e, -1, 0))
        a, b = 4.0 * face(e, xm), 4.0 * face(e, xp)
        c0, d = 4.0 * face(e, ym), 4.0 * face(e, yp)
        z = 4.0 * face(e, roll(e, 1, 1))
        zp = roll(z, -1, 1)
        kxm[s] = a
        kxp[s] = b
        kym[s] = jnp.where(row == 0, 0.0, c0)
        kyp[s] = jnp.where(row == ys - 1, 0.0, d)
        kzm[s] = z
        kzp[s] = zp
        sums = (a + b, c0 + d, z + zp)
        total = sums[0] + sums[1] + sums[2] + p2[s]
        for c in range(3):
            value = total + sums[c]
            dg[c, s] = value
            iv[c, s] = jnp.where(e > 0.0, 1.0 / jnp.where(e > 0.0, value, 1.0), 0.0)
            va[c, s] = FIRST * f2[c, s] * iv[c, s]

    loop(1, pairs + 1, coefs)

    def around(v, c, s):
        mid = v[c, s]
        below, above = x_neighbours(v[c, s - 1], mid, v[c, s + 1])
        x = kxm[s] * below + kxp[s] * above
        y = kym[s] * roll(mid, 1, 0) + kyp[s] * roll(mid, -1, 0)
        z = kzm[s] * roll(mid, 1, 1) + kzp[s] * roll(mid, -1, 1)
        return x + y + z + (x, y, z)[c]

    def sweep(source, target, weight):
        def step(s):
            for c in range(3):
                target[c, s] = (1.0 - weight) * source[c, s] + weight * iv[c, s] * (f2[c, s] + around(source, c, s))

        loop(1, pairs + 1, step)

    sweep(va, vb, SECOND)
    n3 = ys // 2

    def gather_rows(at, value):
        tall[...] = value
        rows3[pl.ds(pl.multiple_of(at * n3, 8), n3), :] = tall[pl.ds(0, n3, stride=2), :] + tall[pl.ds(1, n3, stride=2), :]

    def reduce(s):
        for c in range(3):
            gather_rows(c * pairs + s - 1, f2[c, s] - dg[c, s] * vb[c, s] + around(vb, c, s))
        gather_rows(3 * pairs + s - 1, e2[s] * 0.125)
        gather_rows(4 * pairs + s - 1, p2[s])

    loop(1, pairs + 1, reduce)
    down = matrix((BZ, BZ), lambda l, k: ((l & 63) >> 1) == (k & 31))
    rows3[...] = times(rows3[...], down)
    row3 = iota((n3, BZ), 0)
    zero3 = jnp.zeros((n3, BZ), F32)

    def third(at):
        return rows3[pl.ds(pl.multiple_of(at * n3, 8), n3), :]

    e3[0] = zero3
    e3[pairs + 1] = zero3
    for c in range(3):
        for field in (wa, wb):
            field[c, 0] = zero3
            field[c, pairs + 1] = zero3

    def place(s):
        e3[s] = third(3 * pairs + s - 1)

    loop(1, pairs + 1, place)

    def coefs3(s):
        e = e3[s]
        a, b = 8.0 * face(e, e3[s - 1]), 8.0 * face(e, e3[s + 1])
        c0 = 8.0 * face(e, jnp.where(row3 == 0, 0.0, roll(e, 1, 0)))
        d = 8.0 * face(e, jnp.where(row3 == n3 - 1, 0.0, roll(e, -1, 0)))
        z = 8.0 * face(e, roll(e, 1, 1))
        zp = roll(z, -1, 1)
        jx[s] = a
        jx[s + 1] = b
        jym[s] = jnp.where(row3 == 0, 0.0, c0)
        jyp[s] = jnp.where(row3 == n3 - 1, 0.0, d)
        jz[s] = z
        jzp[s] = zp
        sums = (a + b, c0 + d, z + zp)
        total = sums[0] + sums[1] + sums[2] + third(4 * pairs + s - 1)
        for c in range(3):
            value = total + sums[c]
            iv3[c, s] = jnp.where(e > 0.0, 1.0 / jnp.where(e > 0.0, value, 1.0), 0.0)
            wa[c, s] = COARSE * third(c * pairs + s - 1) * iv3[c, s]

    loop(1, pairs + 1, coefs3)
    source, target = wa, wb
    for sweep_at in range(3):
        def step(s, source=source, target=target):
            for c in range(3):
                near = neighbours(source, c, s, jx, jym, jyp, jz, jzp)
                target[c, s] = (1.0 - COARSE) * source[c, s] + COARSE * iv3[c, s] * (third(c * pairs + s - 1) + near)

        loop(1, pairs + 1, step)
        source, target = target, source
    up = matrix((BZ, BZ), lambda k, l: k == ((l & 63) >> 1))
    for c in range(3):
        rows2[...] = times(source[c, 1:pairs + 1].reshape(pairs * n3, BZ), up)

        def add(s, c=c):
            value = rows2[pl.ds(pl.multiple_of((s - 1) * n3, 8), n3), :]
            tall[pl.ds(0, n3, stride=2), :] = value
            tall[pl.ds(1, n3, stride=2), :] = value
            vb[c, s] = vb[c, s] + jnp.where(iv[c, s] > 0.0, tall[...], 0.0)

        loop(1, pairs + 1, add)
    sweep(vb, va, SECOND)

    for c in range(3):
        for at in (0, 1, pairs + 2, pairs + 3):
            out[c, at] = zero

    def last(s):
        for c in range(3):
            out[c, s + 1] = (1.0 - FIRST) * va[c, s] + FIRST * iv[c, s] * (f2[c, s] + around(va, c, s))

    loop(1, pairs + 1, last)


def ascend(pos, gathered, coarse, lower, upper, *rest, nx, ny):
    far, (sums, parts), rest = rest[:10], rest[10:12], rest[12:]
    near, rest = rest[:10], rest[10:]
    e2out, window, rows24, va1, vb1, rows32, spread, vb, precond, term, held = rest[:11]
    v1, f1, kx1, ky1, kyp1, kz1, kzp1, inverse1, stiff1, pen1, diagonal1, v01 = rest[11:23]
    work, copied = rest[23:-1], rest[-1]
    va, start, kx, ky, kyp, kz, kzp, inverse, forward, weights = near
    arrivals = [pltpu.make_async_copy(source, target, copied.at[i]) for i, (source, target) in enumerate(zip(far, near))]
    for move in arrivals:
        move.start()
    departures = []

    def send(lower, upper):
        move = pltpu.make_async_copy(held.at[lower:upper], parts.at[lower:upper], copied.at[10 + len(departures)])
        move.start()
        departures.append(move)

    level_one_again(
        pos, coarse, lower, upper, v1, f1, kx1, ky1, kyp1, kz1, kzp1, inverse1, stiff1, pen1, diagonal1, v01)
    coarse_levels(pos, gathered, e2out, nx, ny, work)
    gx, gy = pos[0], pos[1]
    ys = 4 * ny
    turn = lax.rem(ys - 4 * gy, ys)

    def rule(k, j):
        z = jnp.where((j & 127) < 96, j & 127, (j & 127) - BZ)
        return k == 64 * (j >> 7) + (z >> 1) + 16

    grow = matrix((BZ, LANES), rule)
    for c in range(3):
        for j in range(5):
            window[pl.ds((5 * c + j) * ys, ys), :] = times(pltpu.roll(e2out[c, gx + j], turn, 0), grow)
    for c in range(3):
        for s in range(2, 16):
            x2 = (s - 7) // 2
            j, part = (x2 + 4) // 2, (x2 + 4) % 2
            base = (5 * c + j) * ys
            cols = slice(128 * part, 128 * part + 128)
            if s % 2 == 1 or s == 2:
                low = window[base:base + 8, cols]
                high = window[base + ys - 4:base + ys, cols]
                for at in (0, 1):
                    rows24[pl.ds(at, 8, stride=2), :] = low
                    rows24[pl.ds(16 + at, 4, stride=2), :] = high
            va1[c, s] = v1[c, s] + jnp.where(inverse1[c, s] > 0.0, rows24[...], 0.0)
    faces1 = (kx1, ky1, kyp1, kz1, kzp1)

    def sweep1(source, target, weight, lower, upper):
        def step(s):
            for c in range(3):
                target[c, s] = (1.0 - weight) * source[c, s] + weight * inverse1[c, s] * (
                    f1[c, s] + neighbours(source, c, s, *faces1))

        loop(lower, upper, step)

    sweep1(va1, vb1, SECOND, 3, 15)
    sweep1(vb1, va1, FIRST, 4, 14)
    grow0 = matrix((BZ, LANES), lambda j, l: j == (l >> 1))
    for move in arrivals:
        move.wait()
    for c in range(3):
        spread[...] = times(va1[c, 4:14].reshape(240, BZ), grow0)
        for i in range(10):
            for half in (0, 1):
                cols = slice(BZ * half, BZ * half + BZ)
                value = spread[24 * i:24 * i + 24, cols]
                for at in (0, 1):
                    rows32[pl.ds(at, 12, stride=2), :] = value[:12]
                    rows32[pl.ds(24 + at, 4, stride=2), :] = value[20:]
                for s in (2 * i - 1, 2 * i):
                    if 0 <= s < 18:
                        va[c, s, :, cols] = va[c, s, :, cols] + rows32[...]
    faces = (kx, ky, kyp, kz, kzp)

    def sweep_one(t):
        for c in range(3):
            vb[c, t] = (1.0 - SECOND) * va[c, t + 1] + SECOND * inverse[c, t] * (
                start[c, t] + neighbours(va, c, t + 1, *faces, at=t))

    loop(0, 16, sweep_one)

    def sweep_two(t):
        for c in range(3):
            precond[c, t - 1] = (1.0 - FIRST) * vb[c, t] + FIRST * inverse[c, t] * (start[c, t] + neighbours(vb, c, t, *faces))

    loop(1, 15, sweep_two)

    def keep(x):
        for c in range(3):
            held[c, x] = precond[c, x + 3][:BY, :BZ]
            held[3 + c, x] = start[c, x + 4][:BY, :BZ]

    loop(0, BX, keep)
    send(0, 6)

    def inner(x, carry):
        one, two = carry
        for c in range(3):
            mid = held[c, x]
            value = mid / inverse[c, x + 4][:BY, :BZ] - neighbours(precond, c, x + 3, *faces, at=x + 4)[:BY, :BZ]
            held[6 + c, x] = value
            one = one + held[3 + c, x] * mid
            two = two + mid * value
        return one, two

    zero = jnp.zeros((BY, BZ), F32)
    one, two = lax.fori_loop(0, BX, inner, (zero, zero), unroll=4)
    send(6, 9)
    lane = iota((8, BZ), 1)
    sums[...] = jnp.where(lane == 0, jnp.sum(one), jnp.where(lane == 1, jnp.sum(two), 0.0))
    sensitivity(forward, precond, weights, term)

    def smooth(x):
        held[9, x] = weigh(term, x)

    loop(0, BX, smooth)
    send(9, 10)
    for move in departures:
        move.wait()


def distance_weight(square):
    return max(RADIUS - math.sqrt(square), 0.0)


def sensitivity(state, field, weights, term):
    def energy(i):
        s = i + 1
        total = jnp.zeros((ROWS, LANES), F32)
        for c in range(3):
            a, b = state[c, s], field[c, s]
            along = [(a - state[c, s - 1]) * (b - field[c, s - 1]) + (a - state[c, s + 1]) * (b - field[c, s + 1])]
            for axis in (0, 1):
                along.append(
                    (a - roll(a, 1, axis)) * (b - roll(b, 1, axis)) + (a - roll(a, -1, axis)) * (b - roll(b, -1, axis))
                )
            total = total + (along[0] + along[1] + along[2] + along[c])
        rho = weights[s]
        term[i] = rho * (-3.0 * rho * rho * (0.5 * total))

    loop(0, BX + 4, energy)


def weigh(field, x):
    classes = {}
    for a in range(-2, 3):
        t = field[x + 2 + a]
        for b, value in ((0, t), (1, roll(t, 1, 0) + roll(t, -1, 0)), (2, roll(t, 2, 0) + roll(t, -2, 0))):
            q = a * a + b * b
            classes[q] = value if q not in classes else classes[q] + value
    parts = []
    for z in (0, 1, 2):
        part = None
        for q, value in classes.items():
            w = distance_weight(q + z * z)
            if w > 0.0:
                part = w * value if part is None else part + w * value
        parts.append(part)
    result = parts[0] + roll(parts[1], 1, 1) + roll(parts[1], -1, 1) + roll(parts[2], 2, 1) + roll(parts[2], -2, 1)
    return result[:BY, :BZ]


def filter_iterate(pos, iterate, state, weights, out, term, inside):
    sensitivity(state, iterate, weights, term)

    def mark(i):
        inside[i] = jnp.where(weights[i + 1] > 0.0, 1.0, 0.0)

    loop(0, BX + 4, mark)

    def smooth(x):
        factor = 1.0 / (weights[x + 3][:BY, :BZ] * weigh(inside, x))
        out[0, x] = factor * weigh(term, x)
        out[1, x] = factor

    loop(0, BX, smooth)


def finish(pos, totals, *rest):
    far, (solution, residual, filtered), near, copied = rest[:3], rest[3:6], rest[6:9], rest[9]
    moves = [pltpu.make_async_copy(source, target, copied.at[i]) for i, (source, target) in enumerate(zip(far, near))]
    for move in moves:
        move.start()
    iterate, parts, smooth = near
    total = jnp.sum(totals[...], axis=0, keepdims=True)
    lane = iota((1, BZ), 1)
    one = jnp.sum(jnp.where(lane == 0, total, 0.0), axis=1, keepdims=True)
    two = jnp.sum(jnp.where(lane == 1, total, 0.0), axis=1, keepdims=True)
    alpha = one / two
    for move in moves:
        move.wait()

    def update(x):
        for c in range(3):
            solution[c, x] = iterate[c, x] + alpha * parts[c, x]
            residual[c, x] = parts[3 + c, x] - alpha * parts[6 + c, x]
        filtered[x] = smooth[0, x] + alpha * (parts[9, x] * smooth[1, x])

    loop(0, BX, update)


def body(right_side, iterate, state, classes, load_mask, fixed_mask):
    nx, ny, nz = (lax.axis_size(axis) for axis in ("gx", "gy", "gz"))
    pos = jnp.stack([lax.axis_index("gx"), lax.axis_index("gy"), lax.axis_index("gz")]).astype(jnp.int32)
    pos = jnp.concatenate([pos, jnp.array([nx, ny, nz], jnp.int32)])
    cells = (BX, BY, BZ)
    field = (3,) + cells
    main, last, first = launch(
        4, prepare, [(11,) + cells, cells, cells], [field], [pos],
        far=[right_side, iterate, state, classes, load_mask, fixed_mask], copies=6)
    from_lower, from_upper = shift_along(last, "gz", 1), shift_along(first, "gz", -1)
    edge = (12, BX, BY // 2, BZ)
    packed, to_upper, to_lower = launch(4, pack_rows, [cells, edge, edge], [], [pos, main, from_lower, from_upper])
    from_lower, from_upper = shift_along(to_upper, "gy", 1), shift_along(to_lower, "gy", -1)
    sides = (9 * HALO + 9, ROWS, BZ)
    own, to_upper, to_lower = launch(
        8, pack_slabs, [(12, BX, ROWS, BZ), sides, sides], [], [pos, main, packed, from_lower, from_upper])
    from_lower, from_upper = shift_along(to_upper, "gx", 1), shift_along(to_lower, "gx", -1)

    wide = (ROWS, LANES)

    def slabs(n):
        return (n,) + wide

    def fields(n):
        return (3, n) + wide

    one, three = slabs(SLABS), fields(SLABS)
    quarters = (22, 8, BZ)
    coarse, low, high, v1, start, kx, ky, kyp, kz, kzp, inverse, u, weights, forward = launch(
        24, descend, [(44, 16, BZ), quarters, quarters],
        [three, three, one, one, one, one, one, three, three, one, fields(14), one, three, one, three, three, (ROWS, BZ), (44 * 16, BZ)],
        [pos, own, from_lower, from_upper],
        far_outs=[fields(18), fields(16), slabs(17)] + [slabs(16)] * 4 + [fields(16), fields(14), slabs(14), fields(14)],
        copies=11)
    smooth = launch(
        8, filter_iterate, [(2,) + cells], [slabs(12), slabs(12)], [pos, u, forward, weights],
        cost=pl.CostEstimate(flops=12_000_000, bytes_accessed=4_000_000, transcendentals=0))[0]

    from_lower, from_upper = shift_along(high, "gz", 1), shift_along(low, "gz", -1)
    coarse, center = launch(4, join_lanes, [(44, 16, BZ), (44, 8, BZ)], [], [pos, coarse, from_lower, from_upper])
    from_lower, from_upper = shift_along(center, "gy", 1), shift_along(center, "gy", -1)
    wide1 = (16, BZ)
    one1, three1 = (10,) + wide1, (3, 10) + wide1
    chunk = launch(
        4, level_one, [(24, BZ)], [one1] * 5 + [three1] * 5 + [(8, BZ), (40, BZ), (40, BZ)], [pos, coarse])[0]
    column = lax.all_to_all(jnp.broadcast_to(chunk[None], (ny, 24, BZ)), "gy", 0, 0, tiled=True)
    side = (32, 24, BZ)
    center, to_upper, to_lower = launch(4, join_rows, [(44, 24, BZ), side, side], [], [pos, center, from_lower, from_upper])
    from_lower, from_upper = shift_along(to_upper, "gx", 1), shift_along(to_lower, "gx", -1)
    column = jnp.broadcast_to(column[None], (nx, ny, 24, BZ)).reshape(nx * ny, 24, BZ)
    gathered = lax.all_to_all(column, "gx", 0, 0, tiled=True)

    wide1 = (24, BZ)
    one1, three1 = (18,) + wide1, (3, 18) + wide1
    wide2, wide3 = (4 * ny, BZ), (2 * ny, BZ)
    one2, three2 = (nx + 2,) + wide2, (3, nx + 2) + wide2
    one3, three3 = (nx + 2,) + wide3, (3, nx + 2) + wide3
    work = [one2, one2, three2] + [one2] * 6 + [three2] * 4 + [wide2, (5 * nx * 2 * ny, BZ)]
    work += [one3, one3, three3] + [one3] * 5 + [three3] * 3 + [(nx * 2 * ny, BZ)]
    far = [v1, start, kx, ky, kyp, kz, kzp, inverse, forward, weights]
    parts = (10,) + cells
    scratch = [x.shape for x in far] + [
        (3, nx + 4) + wide2, (15 * 4 * ny, LANES), wide1, three1, three1, (ROWS, BZ), (240, LANES), fields(16), fields(14), slabs(12), parts
    ] + [three1] * 2 + [one1] * 5 + [three1, one1, one1, three1, three1] + work
    sums, parts = launch(
        28, functools.partial(ascend, nx=nx, ny=ny), [(8, BZ)], scratch, [pos, gathered, center, from_lower, from_upper],
        far_outs=[parts], far=far, copies=13)

    total = lax.all_to_all(jnp.broadcast_to(sums[:1], (nx * ny, BZ)), ("gx", "gy"), 0, 0, tiled=True)
    total = jnp.sum(total, axis=0, keepdims=True)
    total = lax.all_to_all(jnp.broadcast_to(total, (nz, BZ)), "gz", 0, 0, tiled=True)
    return tuple(launch(
        4, finish, [field, field, cells], [field, parts.shape, smooth.shape], [pos, total], far=[iterate, parts, smooth], copies=3))


def solution(mesh):
    field, cells = P(None, "gx", "gy", "gz"), P("gx", "gy", "gz")
    return jax.shard_map(
        body,
        mesh=mesh,
        in_specs=(field, field, field, cells, cells, cells),
        out_specs=(field, field, cells),
        check_vma=False,
    )
```

time: 201 us -> 167 us (0.83)
  blocking collectives: 59.8 us -> 28.4 us
  local copies, waits for them, and re-layouts: 23.2 us -> 6.68 us
  starting transfers between devices: 41.1 us -> 50.7 us
  Pallas kernels: 33.6 us -> 40.3 us
  other arithmetic: 3.67 us -> 0.1 us
  waiting for transfers between devices: 37.6 us -> 39.8 us
    all_to_all x2 -> x1, blocking collectives: 44.2 us -> 12.3 us  [body(): lax.all_to_all(jnp.broadcast_to(chunk[None], (ny, 24, BZ)), 'gy', 0, 0, t...]
    unnamed x60 -> x20, local copies, waits for them, and re-layouts: 23.1 us -> 5.04 us
    all_to_all x0 -> x2, starting transfers between devices: none -> 11.9 us  [the longest x1 6.05 us: body(): lax.all_to_all(jnp.broadcast_to(total, (nz, BZ)), 'gz', 0, 0, tiled=True)]
    pallas_call x7 -> x10, Pallas kernels: 33.6 us -> 40.3 us  [launch(): pl.pallas_call(kernel, out_shape=[jax.ShapeDtypeStruct(shape, F32) for sh...]
    ppermute x12, starting transfers between devices: 41.1 us -> 38.8 us  [shift_along(): lax.ppermute(x, axis, [(i, (i + step) % devices) for i in range(devices)])]
  transfers between devices with their start and end apart: 12 -> 14, of which waited for: 10 -> 12; matrix products, arithmetic and copies ran while one was open for 0% -> 0% of each run, Pallas kernels for 0% -> 2%
where the time goes in v3:
time: 167 us
  starting transfers between devices  50.7 us (30%)
  Pallas kernels  40.3 us (24%)
  waiting for transfers between devices  39.8 us (24%)
  blocking collectives  28.4 us (17%)
  local copies, waits for them, and re-layouts  6.68 us (4%)
    pallas_call x10, Pallas kernels, launch(): pl.pallas_call(kernel, out_shape=[jax.ShapeDtypeStruct(shape, F32) for sh...  40.3 us
    ppermute x12, waiting for transfers between devices, shift_along(): lax.ppermute(x, axis, [(i, (i + step) % devices) for i in range(devices)])  39.4 us
    ppermute x12, starting transfers between devices, shift_along(): lax.ppermute(x, axis, [(i, (i + step) % devices) for i in range(devices)])  38.8 us
    all_to_all x1, blocking collectives, body(): lax.all_to_all(jnp.broadcast_to(sums[:1], (nx * ny, BZ)), ('gx', 'gy'), 0...  16.1 us
    all_to_all x1, blocking collectives, body(): lax.all_to_all(jnp.broadcast_to(chunk[None], (ny, 24, BZ)), 'gy', 0, 0, t...  12.3 us
    all_to_all x1, starting transfers between devices, body(): lax.all_to_all(jnp.broadcast_to(total, (nz, BZ)), 'gz', 0, 0, tiled=True)  6.05 us
    all_to_all x1, starting transfers between devices, body(): gathered = lax.all_to_all(column, 'gx', 0, 0, tiled=True)  5.8 us
    unnamed x20, local copies, waits for them, and re-layouts  5.04 us
  transfers between devices with their start and end apart: 14, of which 12 were waited for; matrix products, arithmetic and copies ran while one was open for 0% of the time, Pallas kernels for 2%

profile of v3, /device:TPU:1, one launch (start us, length us, event | category | flops | bytes accessed | tf_op | source)
XLA Modules:
  0.0 166.8 jit_solution(698056113454148018)
XLA Ops:
  0.6 0.1 pad_add_fusion.pos
  0.7 0.0 copy-start.6
  0.7 2.3 %shard_map.94 = (f32[11,8,16,128]{3,2,1,0:T(8,128)S(1)}, f32[8,16,128]{2,1,0:T(8,128)S(1)}, f32[8,16,128]{2,1,0:T(8,128)S(1)}) custom-call(s32[6]{0:T(128)S(1)} %pad_add_fusion.pos, f32[3,8,16,128]{3,2,1,0:T(8,128)} %right_far.1, f32[3,8,16,128]{3,2,1,0:T(8,128)} %rest_0_.1, f32[3,8,16,128]{3,2,1,0:T(8,128)} %state_far.1, s32[8,16,128]{2,1,0:T(8,128)} %classes_far.1, ...), custom_call_target="tpu_custom_call" | custom-call | tf_op jit(solution)/shard_map/pallas_call | solution.py:74
  3.1 4.0 %collective-permute-start = (f32[8,16,128]{2,1,0:T(8,128)S(1)}, f32[8,16,128]{2,1,0:T(8,128)S(1)}, u32[]{:S(2)}, u32[]{:S(2)}) collective-permute-start(f32[8,16,128]{2,1,0:T(8,128)S(1)} %get-tuple-element.34), channel_id=1, source_target_pairs={{0,1},{1,2},{2,3},{3,4},{4,5},{5,6},{6,7},{7,0},{8,9},{9,10},{10,1... | collective-permute-start | bytes 196616 | tf_op jit(solution)/shard_map/ppermute | solution.py:87
  7.1 3.8 %collective-permute-start.1 = (f32[8,16,128]{2,1,0:T(8,128)S(1)}, f32[8,16,128]{2,1,0:T(8,128)S(1)}, u32[]{:S(2)}, u32[]{:S(2)}) collective-permute-start(f32[8,16,128]{2,1,0:T(8,128)S(1)} %get-tuple-element.35), channel_id=1, source_target_pairs={{0,7},{1,0},{2,1},{3,2},{4,3},{5,4},{6,5},{7,6},{8,15},{9,8},{10,9... | collective-permute-start | bytes 196616 | tf_op jit(solution)/shard_map/ppermute | solution.py:87
  10.9 0.0 collective-permute-done.from_lower
  10.9 1.3 collective-permute-done.1.from_upper
  12.2 0.6 shard_map.95
  12.9 4.0 %collective-permute-start.2 = (f32[12,8,8,128]{3,2,1,0:T(8,128)S(1)}, f32[12,8,8,128]{3,2,1,0:T(8,128)S(1)}, u32[]{:S(2)}, u32[]{:S(2)}) collective-permute-start(f32[12,8,8,128]{3,2,1,0:T(8,128)S(1)} %get-tuple-element.37), channel_id=1, source_target_pairs={{0,8},{8,16},{16,24},{24,32},{32,40},{40,48},{48,56},{56,0},{1,9},... | collective-permute-start | bytes 1179656 | tf_op jit(solution)/shard_map/ppermute | solution.py:87
  16.9 8.6 %collective-permute-start.3 = (f32[12,8,8,128]{3,2,1,0:T(8,128)S(1)}, f32[12,8,8,128]{3,2,1,0:T(8,128)S(1)}, u32[]{:S(2)}, u32[]{:S(2)}) collective-permute-start(f32[12,8,8,128]{3,2,1,0:T(8,128)S(1)} %get-tuple-element.38), channel_id=1, source_target_pairs={{0,56},{8,0},{16,8},{24,16},{32,24},{40,32},{48,40},{56,48},{1,57}... | collective-permute-start | bytes 1179656 | tf_op jit(solution)/shard_map/ppermute | solution.py:87
  25.5 5.5 %collective-permute-done.2.from_lower = f32[12,8,8,128]{3,2,1,0:T(8,128)S(1)} collective-permute-done((f32[12,8,8,128]{3,2,1,0:T(8,128)S(1)}, f32[12,8,8,128]{3,2,1,0:T(8,128)S(1)}, u32[]{:S(2)}, u32[]{:S(2)}) %collective-permute-start.2) | collective-permute-done | bytes 393248 | tf_op jit(solution)/shard_map/ppermute | solution.py:87
  31.0 0.9 collective-permute-done.3.from_upper
  31.9 0.8 shard_map.96
  32.7 4.0 %collective-permute-start.4 = (f32[72,32,128]{2,1,0:T(8,128)S(1)}, f32[72,32,128]{2,1,0:T(8,128)S(1)}, u32[]{:S(2)}, u32[]{:S(2)}) collective-permute-start(f32[72,32,128]{2,1,0:T(8,128)S(1)} %get-tuple-element.40), channel_id=1, source_target_pairs={{0,64},{64,128},{128,192},{192,256},{256,320},{320,384},{384,448},... | collective-permute-start | bytes 3538952 | tf_op jit(solution)/shard_map/ppermute | solution.py:87
  36.7 0.0 collective-permute-start.5
  36.7 13.1 %collective-permute-done.4.lower = f32[72,32,128]{2,1,0:T(8,128)S(1)} collective-permute-done((f32[72,32,128]{2,1,0:T(8,128)S(1)}, f32[72,32,128]{2,1,0:T(8,128)S(1)}, u32[]{:S(2)}, u32[]{:S(2)}) %collective-permute-start.4) | collective-permute-done | bytes 1179680 | tf_op jit(solution)/shard_map/ppermute | solution.py:87
  49.9 2.5 %collective-permute-done.5.upper = f32[72,32,128]{2,1,0:T(8,128)S(1)} collective-permute-done((f32[72,32,128]{2,1,0:T(8,128)S(1)}, f32[72,32,128]{2,1,0:T(8,128)S(1)}, u32[]{:S(2)}, u32[]{:S(2)}) %collective-permute-start.5) | collective-permute-done | bytes 1179680 | tf_op jit(solution)/shard_map/ppermute | solution.py:87
  52.4 11.0 %shard_map.97 = (f32[44,16,128]{2,1,0:T(8,128)S(1)}, f32[22,8,128]{2,1,0:T(8,128)S(1)}, f32[22,8,128]{2,1,0:T(8,128)S(1)}, f32[3,18,32,256]{3,2,1,0:T(8,128)}, f...) custom-call(s32[6]{0:T(128)S(1)} %pad_add_fusion.pos, ...), custom_call_target="tpu_custom_call" | custom-call | tf_op jit(solution)/shard_map/pallas_call | solution.py:74
  63.4 3.1 %collective-permute-start.6 = (f32[22,8,128]{2,1,0:T(8,128)S(1)}, f32[22,8,128]{2,1,0:T(8,128)S(1)}, u32[]{:S(2)}, u32[]{:S(2)}) collective-permute-start(f32[22,8,128]{2,1,0:T(8,128)S(1)} %get-tuple-element.43), channel_id=1, source_target_pairs={{0,1},{1,2},{2,3},{3,4},{4,5},{5,6},{6,7},{7,0},{8,9},{9,10},{10,1... | collective-permute-start | bytes 270344 | tf_op jit(solution)/shard_map/ppermute | solution.py:87
  66.5 3.7 %collective-permute-start.7 = (f32[22,8,128]{2,1,0:T(8,128)S(1)}, f32[22,8,128]{2,1,0:T(8,128)S(1)}, u32[]{:S(2)}, u32[]{:S(2)}) collective-permute-start(f32[22,8,128]{2,1,0:T(8,128)S(1)} %get-tuple-element.44), channel_id=1, source_target_pairs={{0,7},{1,0},{2,1},{3,2},{4,3},{5,4},{6,5},{7,6},{8,15},{9,8},{10,9... | collective-permute-start | bytes 270344 | tf_op jit(solution)/shard_map/ppermute | solution.py:87
  70.2 0.9 collective-permute-done.6.from_lower
  71.1 2.2 %collective-permute-done.7.from_upper = f32[22,8,128]{2,1,0:T(8,128)S(1)} collective-permute-done((f32[22,8,128]{2,1,0:T(8,128)S(1)}, f32[22,8,128]{2,1,0:T(8,128)S(1)}, u32[]{:S(2)}, u32[]{:S(2)}) %collective-permute-start.7) | collective-permute-done | bytes 90144 | tf_op jit(solution)/shard_map/ppermute | solution.py:87
  73.3 1.0 shard_map.98
  74.4 1.5 shard_map.99
  75.9 12.3 %all_to_all.24 = f32[8,24,128]{2,1,0:T(8,128)S(1)} all-to-all(f32[8,24,128]{2,1,0:T(8,128)S(1)} %broadcast_in_dim.8), channel_id=1, replica_groups=mesh['gx'=8,'gy'=8,'gz'=8] {'gy'}, dimensions={0} | all-to-all | bytes 196608 | tf_op jit(solution)/shard_map/all_to_all | solution.py:815
  88.2 1.0 broadcast_in_dim.9
  89.2 5.8 %all-to-all-start.1 = ((f32[64,24,128]{2,1,0:T(8,128)}), f32[64,24,128]{2,1,0:T(8,128)S(1)}, u32[]{:S(2)}, u32[]{:S(2)}) async-start(f32[64,24,128]{2,1,0:T(8,128)} %bitcast.3), calls=%async_computation.1 | async-start | bytes 1572864 | tf_op jit(solution)/shard_map/all_to_all | solution.py:820
  95.1 1.9 %collective-permute-start.9 = (f32[44,8,128]{2,1,0:T(8,128)S(1)}, f32[44,8,128]{2,1,0:T(8,128)S(1)}, u32[]{:S(2)}, u32[]{:S(2)}) collective-permute-start(f32[44,8,128]{2,1,0:T(8,128)S(1)} %get-tuple-element.46.coarse), channel_id=1, source_target_pairs={{0,56},{8,0},{16,8},{24,16},{32,24},{40,32},{48,40},{56,48},{1,57}... | collective-permute-start | bytes 540680 | tf_op jit(solution)/shard_map/ppermute | solution.py:87
  97.0 3.4 %collective-permute-start.8 = (f32[44,8,128]{2,1,0:T(8,128)S(1)}, f32[44,8,128]{2,1,0:T(8,128)S(1)}, u32[]{:S(2)}, u32[]{:S(2)}) collective-permute-start(f32[44,8,128]{2,1,0:T(8,128)S(1)} %get-tuple-element.46.coarse), channel_id=1, source_target_pairs={{0,8},{8,16},{16,24},{24,32},{32,40},{40,48},{48,56},{56,0},{1,9},... | collective-permute-start | bytes 540680 | tf_op jit(solution)/shard_map/ppermute | solution.py:87
  100.3 2.6 %collective-permute-done.9.from_upper = f32[44,8,128]{2,1,0:T(8,128)S(1)} collective-permute-done((f32[44,8,128]{2,1,0:T(8,128)S(1)}, f32[44,8,128]{2,1,0:T(8,128)S(1)}, u32[]{:S(2)}, u32[]{:S(2)}) %collective-permute-start.9) | collective-permute-done | bytes 180256 | tf_op jit(solution)/shard_map/ppermute | solution.py:87
  103.0 3.1 %collective-permute-done.8.from_lower = f32[44,8,128]{2,1,0:T(8,128)S(1)} collective-permute-done((f32[44,8,128]{2,1,0:T(8,128)S(1)}, f32[44,8,128]{2,1,0:T(8,128)S(1)}, u32[]{:S(2)}, u32[]{:S(2)}) %collective-permute-start.8) | collective-permute-done | bytes 180256 | tf_op jit(solution)/shard_map/ppermute | solution.py:87
  106.1 0.0 copy-done.6
  106.1 0.7 shard_map.100
  106.7 2.3 %collective-permute-start.10 = (f32[32,24,128]{2,1,0:T(8,128)S(1)}, f32[32,24,128]{2,1,0:T(8,128)S(1)}, u32[]{:S(2)}, u32[]{:S(2)}) collective-permute-start(f32[32,24,128]{2,1,0:T(8,128)S(1)} %get-tuple-element.48), channel_id=1, source_target_pairs={{0,64},{64,128},{128,192},{192,256},{256,320},{320,384},{384,448},... | collective-permute-start | bytes 1179656 | tf_op jit(solution)/shard_map/ppermute | solution.py:87
  109.0 0.0 collective-permute-start.11
  109.0 4.7 %collective-permute-done.10.lower = f32[32,24,128]{2,1,0:T(8,128)S(1)} collective-permute-done((f32[32,24,128]{2,1,0:T(8,128)S(1)}, f32[32,24,128]{2,1,0:T(8,128)S(1)}, u32[]{:S(2)}, u32[]{:S(2)}) %collective-permute-start.10) | collective-permute-done | bytes 393248 | tf_op jit(solution)/shard_map/ppermute | solution.py:87
  113.7 2.5 %collective-permute-done.11.upper = f32[32,24,128]{2,1,0:T(8,128)S(1)} collective-permute-done((f32[32,24,128]{2,1,0:T(8,128)S(1)}, f32[32,24,128]{2,1,0:T(8,128)S(1)}, u32[]{:S(2)}, u32[]{:S(2)}) %collective-permute-start.11) | collective-permute-done | bytes 393248 | tf_op jit(solution)/shard_map/ppermute | solution.py:87
  116.2 0.0 copy-start.4
  116.2 0.7 copy-done.4
  117.0 0.0 all-to-all-done.1.gathered
  117.0 0.0 copy-start.5
  117.0 1.0 copy-done.5
  118.0 0.0 copy-start.7
  118.0 0.7 copy-done.7
  118.6 0.0 copy-start
  118.6 0.0 copy-start.1
  118.6 16.4 %shard_map.101 = (f32[8,128]{1,0:T(8,128)S(1)}, f32[10,8,16,128]{3,2,1,0:T(8,128)}) custom-call(s32[6]{0:T(128)S(1)} %copy-done.7, f32[64,24,128]{2,1,0:T(8,128)S(1)} %all-to-all-done.1.gathered, f32[44,24,128]{2,1,0:T(8,128)S(1)} %get-tuple-element.47.coarse, f32[32,24,128]{2,1,0:T(8,128)S(1)} %collective-permute-done.10.lower, ...), custom_call_target="tpu_custom_call" | custom-call | tf_op jit(solution)/shard_map/pallas_call | solution.py:74
  135.0 16.1 %all_to_all.25 = f32[64,1,128]{2,1,0:T(1,128)S(1)} all-to-all(f32[64,1,128]{2,1,0:T(1,128)S(1)} %broadcast_in_dim.10), channel_id=1, replica_groups=mesh['gx'=8,'gy'=8,'gz'=8] {'gx','gy'}, dimensions={0} | all-to-all | bytes 65536 | tf_op jit(solution)/shard_map/all_to_all | solution.py:838
  151.1 0.6 broadcast_in_dim.11
  151.7 6.0 %all-to-all-start.3 = ((f32[8,1,128]{2,1,0:T(1,128)}), f32[8,1,128]{2,1,0:T(1,128)S(1)}, u32[]{:S(2)}, u32[]{:S(2)}) async-start(f32[8,1,128]{2,1,0:T(1,128)} %broadcast_in_dim.11), calls=%async_computation.3 | async-start | bytes 8192 | tf_op jit(solution)/shard_map/all_to_all | solution.py:840
  157.8 0.0 copy-done
  157.8 0.0 copy-done.1
  157.8 0.0 copy-start.2
  157.8 1.3 copy-done.2
  159.1 0.0 copy-start.8
  159.1 0.7 copy-done.8
  159.8 0.0 copy-start.9
  159.8 3.3 %shard_map.102.rest_2_ = f32[2,8,16,128]{3,2,1,0:T(8,128)S(1)} custom-call(s32[6]{0:T(128)S(1)} %copy-done.8, f32[3,14,32,256]{3,2,1,0:T(8,128)S(1)} %copy-done.2, f32[3,14,32,256]{3,2,1,0:T(8,128)S(1)} %copy-done, f32[14,32,256]{2,1,0:T(8,128)S(1)} %copy-done.1), custom_call_target="tpu_custom_call" | custom-call | flops 12000000 | bytes 4000000 | tf_op jit(solution)/shard_map/pallas_call | solution.py:74
  163.1 0.0 copy-start.3
  163.1 0.6 copy-done.3
  163.8 0.5 all-to-all-done.3
  164.2 0.0 copy-done.9
  164.2 2.6 %shard_map.103 = (f32[3,8,16,128]{3,2,1,0:T(8,128)}, f32[3,8,16,128]{3,2,1,0:T(8,128)}, f32[8,16,128]{2,1,0:T(8,128)}) custom-call(s32[6]{0:T(128)S(1)} %copy-done.9, f32[8,128]{1,0:T(8,128)S(1)} %bitcast.8, f32[3,8,16,128]{3,2,1,0:T(8,128)} %rest_0_.1, f32[10,8,16,128]{3,2,1,0:T(8,128)} %get-tuple-element.61.rest_1_, f32[2,8,16,128]{3,2,1,0:T(8,128)} %copy-done.3), custom_call_target="tpu_custom_call" | custom-call | tf_op jit(solution)/shard_map/pallas_call | solution.py:74
  (5 shorter events, 0.1 us)
Async XLA Ops:
  0.7 105.3 %copy-start.6 = (s32[6]{0:T(128)}, s32[6]{0:T(128)S(1)}, u32[]{:S(2)}) copy-start(s32[6]{0:T(128)S(1)} %pad_add_fusion.pos) | copy-start | bytes 76
  3.1 7.9 %collective-permute-start = (f32[8,16,128]{2,1,0:T(8,128)S(1)}, f32[8,16,128]{2,1,0:T(8,128)S(1)}, u32[]{:S(2)}, u32[]{:S(2)}) collective-permute-start(f32[8,16,128]{2,1,0:T(8,128)S(1)} %get-tuple-element.34), channel_id=1, source_target_pairs={{0,1},{1,2},{2,3},{3,4},{4,5},{5,6},{6,7},{7,0},{8,9},{9,10},{10,1... | collective-permute-start | bytes 196616 | tf_op jit(solution)/shard_map/ppermute | solution.py:87
  7.1 5.1 %collective-permute-start.1 = (f32[8,16,128]{2,1,0:T(8,128)S(1)}, f32[8,16,128]{2,1,0:T(8,128)S(1)}, u32[]{:S(2)}, u32[]{:S(2)}) collective-permute-start(f32[8,16,128]{2,1,0:T(8,128)S(1)} %get-tuple-element.35), channel_id=1, source_target_pairs={{0,7},{1,0},{2,1},{3,2},{4,3},{5,4},{6,5},{7,6},{8,15},{9,8},{10,9... | collective-permute-start | bytes 196616 | tf_op jit(solution)/shard_map/ppermute | solution.py:87
  12.9 18.1 %collective-permute-start.2 = (f32[12,8,8,128]{3,2,1,0:T(8,128)S(1)}, f32[12,8,8,128]{3,2,1,0:T(8,128)S(1)}, u32[]{:S(2)}, u32[]{:S(2)}) collective-permute-start(f32[12,8,8,128]{3,2,1,0:T(8,128)S(1)} %get-tuple-element.37), channel_id=1, source_target_pairs={{0,8},{8,16},{16,24},{24,32},{32,40},{40,48},{48,56},{56,0},{1,9},... | collective-permute-start | bytes 1179656 | tf_op jit(solution)/shard_map/ppermute | solution.py:87
  16.9 15.0 %collective-permute-start.3 = (f32[12,8,8,128]{3,2,1,0:T(8,128)S(1)}, f32[12,8,8,128]{3,2,1,0:T(8,128)S(1)}, u32[]{:S(2)}, u32[]{:S(2)}) collective-permute-start(f32[12,8,8,128]{3,2,1,0:T(8,128)S(1)} %get-tuple-element.38), channel_id=1, source_target_pairs={{0,56},{8,0},{16,8},{24,16},{32,24},{40,32},{48,40},{56,48},{1,57}... | collective-permute-start | bytes 1179656 | tf_op jit(solution)/shard_map/ppermute | solution.py:87
  32.7 17.2 %collective-permute-start.4 = (f32[72,32,128]{2,1,0:T(8,128)S(1)}, f32[72,32,128]{2,1,0:T(8,128)S(1)}, u32[]{:S(2)}, u32[]{:S(2)}) collective-permute-start(f32[72,32,128]{2,1,0:T(8,128)S(1)} %get-tuple-element.40), channel_id=1, source_target_pairs={{0,64},{64,128},{128,192},{192,256},{256,320},{320,384},{384,448},... | collective-permute-start | bytes 3538952 | tf_op jit(solution)/shard_map/ppermute | solution.py:87
  36.7 15.6 %collective-permute-start.5 = (f32[72,32,128]{2,1,0:T(8,128)S(1)}, f32[72,32,128]{2,1,0:T(8,128)S(1)}, u32[]{:S(2)}, u32[]{:S(2)}) collective-permute-start(f32[72,32,128]{2,1,0:T(8,128)S(1)} %get-tuple-element.41), channel_id=1, source_target_pairs={{0,448},{64,0},{128,64},{192,128},{256,192},{320,256},{384,320},{4... | collective-permute-start | bytes 3538952 | tf_op jit(solution)/shard_map/ppermute | solution.py:87
  63.4 7.8 %collective-permute-start.6 = (f32[22,8,128]{2,1,0:T(8,128)S(1)}, f32[22,8,128]{2,1,0:T(8,128)S(1)}, u32[]{:S(2)}, u32[]{:S(2)}) collective-permute-start(f32[22,8,128]{2,1,0:T(8,128)S(1)} %get-tuple-element.43), channel_id=1, source_target_pairs={{0,1},{1,2},{2,3},{3,4},{4,5},{5,6},{6,7},{7,0},{8,9},{9,10},{10,1... | collective-permute-start | bytes 270344 | tf_op jit(solution)/shard_map/ppermute | solution.py:87
  66.5 6.9 %collective-permute-start.7 = (f32[22,8,128]{2,1,0:T(8,128)S(1)}, f32[22,8,128]{2,1,0:T(8,128)S(1)}, u32[]{:S(2)}, u32[]{:S(2)}) collective-permute-start(f32[22,8,128]{2,1,0:T(8,128)S(1)} %get-tuple-element.44), channel_id=1, source_target_pairs={{0,7},{1,0},{2,1},{3,2},{4,3},{5,4},{6,5},{7,6},{8,15},{9,8},{10,9... | collective-permute-start | bytes 270344 | tf_op jit(solution)/shard_map/ppermute | solution.py:87
  89.2 27.7 %all-to-all-start.1 = ((f32[64,24,128]{2,1,0:T(8,128)}), f32[64,24,128]{2,1,0:T(8,128)S(1)}, u32[]{:S(2)}, u32[]{:S(2)}) async-start(f32[64,24,128]{2,1,0:T(8,128)} %bitcast.3), calls=%async_computation.1 | async-start | bytes 1572864 | tf_op jit(solution)/shard_map/all_to_all | solution.py:820
  95.1 7.9 %collective-permute-start.9 = (f32[44,8,128]{2,1,0:T(8,128)S(1)}, f32[44,8,128]{2,1,0:T(8,128)S(1)}, u32[]{:S(2)}, u32[]{:S(2)}) collective-permute-start(f32[44,8,128]{2,1,0:T(8,128)S(1)} %get-tuple-element.46.coarse), channel_id=1, source_target_pairs={{0,56},{8,0},{16,8},{24,16},{32,24},{40,32},{48,40},{56,48},{1,57}... | collective-permute-start | bytes 540680 | tf_op jit(solution)/shard_map/ppermute | solution.py:87
  97.0 9.1 %collective-permute-start.8 = (f32[44,8,128]{2,1,0:T(8,128)S(1)}, f32[44,8,128]{2,1,0:T(8,128)S(1)}, u32[]{:S(2)}, u32[]{:S(2)}) collective-permute-start(f32[44,8,128]{2,1,0:T(8,128)S(1)} %get-tuple-element.46.coarse), channel_id=1, source_target_pairs={{0,8},{8,16},{16,24},{24,32},{32,40},{40,48},{48,56},{56,0},{1,9},... | collective-permute-start | bytes 540680 | tf_op jit(solution)/shard_map/ppermute | solution.py:87
  106.7 7.0 %collective-permute-start.10 = (f32[32,24,128]{2,1,0:T(8,128)S(1)}, f32[32,24,128]{2,1,0:T(8,128)S(1)}, u32[]{:S(2)}, u32[]{:S(2)}) collective-permute-start(f32[32,24,128]{2,1,0:T(8,128)S(1)} %get-tuple-element.48), channel_id=1, source_target_pairs={{0,64},{64,128},{128,192},{192,256},{256,320},{320,384},{384,448},... | collective-permute-start | bytes 1179656 | tf_op jit(solution)/shard_map/ppermute | solution.py:87
  109.0 7.2 %collective-permute-start.11 = (f32[32,24,128]{2,1,0:T(8,128)S(1)}, f32[32,24,128]{2,1,0:T(8,128)S(1)}, u32[]{:S(2)}, u32[]{:S(2)}) collective-permute-start(f32[32,24,128]{2,1,0:T(8,128)S(1)} %get-tuple-element.49), channel_id=1, source_target_pairs={{0,448},{64,0},{128,64},{192,128},{256,192},{320,256},{384,320},{4... | collective-permute-start | bytes 1179656 | tf_op jit(solution)/shard_map/ppermute | solution.py:87
  116.2 0.7 copy-start.4
  117.0 1.0 copy-start.5
  118.0 0.7 copy-start.7
  118.6 39.2 %copy-start = (f32[3,14,32,256]{3,2,1,0:T(8,128)S(1)}, f32[3,14,32,256]{3,2,1,0:T(8,128)}, u32[]{:S(2)}) copy-start(f32[3,14,32,256]{3,2,1,0:T(8,128)} %get-tuple-element.58.rest_8_.state) | copy-start | bytes 4128772
  118.6 39.2 %copy-start.1 = (f32[14,32,256]{2,1,0:T(8,128)S(1)}, f32[14,32,256]{2,1,0:T(8,128)}, u32[]{:S(2)}) copy-start(f32[14,32,256]{2,1,0:T(8,128)} %get-tuple-element.59.rest_9_.weights) | copy-start | bytes 1376260
  151.7 12.5 %all-to-all-start.3 = ((f32[8,1,128]{2,1,0:T(1,128)}), f32[8,1,128]{2,1,0:T(1,128)S(1)}, u32[]{:S(2)}, u32[]{:S(2)}) async-start(f32[8,1,128]{2,1,0:T(1,128)} %broadcast_in_dim.11), calls=%async_computation.3 | async-start | bytes 8192 | tf_op jit(solution)/shard_map/all_to_all | solution.py:840
  157.8 1.3 copy-start.2
  159.1 0.7 copy-start.8
  159.8 4.4 %copy-start.9 = (s32[6]{0:T(128)S(1)}, s32[6]{0:T(128)}, u32[]{:S(2)}) copy-start(s32[6]{0:T(128)} %copy-done.6) | copy-start | bytes 76
  163.1 0.7 copy-start.3

commit v4 on v3

--- a/solution.py
+++ b/solution.py
@@ -68,18 +68,18 @@
     return jnp.where(both, 2.0 * a * b / jnp.where(both, total, 1.0), total)
 
 
-def launch(limit, kernel, outs, scratch, operands, far_outs=(), far=(), copies=0, cost=None):
+def launch(limit, kernel, outs, scratch, operands, far_outs=(), far=(), copies=0, cost=None, pin=False):
     near_spec, far_spec = pl.BlockSpec(memory_space=pltpu.VMEM), pl.BlockSpec(memory_space=pltpu.HBM)
     specs = [pl.BlockSpec(memory_space=pltpu.SMEM)] + [near_spec] * (len(operands) - 1) + [far_spec] * len(far)
     return pl.pallas_call(
         kernel,
-        out_shape=[jax.ShapeDtypeStruct(shape, F32) for shape in outs] + [pltpu.HBM(shape, F32) for shape in far_outs],
+        out_shape=[pltpu.VMEM(shape, F32) if pin else jax.ShapeDtypeStruct(shape, F32) for shape in outs] + [pltpu.HBM(shape, F32) for shape in far_outs],
         in_specs=specs,
         out_specs=[near_spec] * len(outs) + [far_spec] * len(far_outs),
         scratch_shapes=[pltpu.VMEM(shape, F32) for shape in scratch] + ([pltpu.SemaphoreType.DMA((copies,))] if copies else []),
         compiler_params=pltpu.CompilerParams(vmem_limit_bytes=limit * MIB),
         cost_estimate=cost,
-    )(*operands, *[pltpu.with_memory_space_constraint(x, pltpu.HBM) for x in far])
+    )(*(operands[:1] + [pltpu.with_memory_space_constraint(x, pltpu.VMEM) for x in operands[1:]] if pin else operands), *[pltpu.with_memory_space_constraint(x, pltpu.HBM) for x in far])
 
 
 def shift_along(x, axis, step):
@@ -319,7 +319,7 @@
     loop(0, 11, unpack)
 
 
-def join_rows(pos, coarse, from_lower, from_upper, out, to_upper, to_lower):
+def join_rows(pos, coarse, from_lower, from_upper, after, to_upper, to_lower, center, out, copied):
     below = jnp.where(pos[1] > 0, 1.0, 0.0)
     above = jnp.where(pos[1] < pos[4] - 1, 1.0, 0.0)
 
@@ -327,6 +327,8 @@
         out[i] = jnp.concatenate([coarse[i], from_upper[i] * above, from_lower[i] * below], 0)
 
     loop(0, 44, join)
+    move = pltpu.make_async_copy(out, center, copied.at[0])
+    move.start()
     at = 0
     for base, count in ((0, 6), (8, 6), (16, 6), (24, 7), (34, 7)):
         shift = 2 if count == 6 else 3
@@ -334,6 +336,7 @@
             to_upper[at] = out[base + j]
             to_lower[at] = out[base + shift + j]
             at += 1
+    move.wait()
 
 
 def smooth_down(slabs, f, v0, v1, inverse, faces):
@@ -384,6 +387,12 @@
     chunk[...] = jnp.zeros((24, BZ), F32)
     for field in range(5):
         chunk[4 * field:4 * field + 4] = jnp.where(lane < 64, wide[8 * field:8 * field + 4], wide[8 * field + 4:8 * field + 8])
+
+
+def pack_column(pos, column, out):
+    for i in range(out.shape[0]):
+        for j in range(column.shape[0]):
+            out[i, 20 * j:20 * j + 20] = column[j, 0:20]
 
 
 def level_one_again(pos, own, lower, upper, v1, f, kx, ky, kyp, kz, kzp, inverse, stiff, pen, diagonal, v0):
@@ -426,7 +435,7 @@
     def collect(g):
         for field in range(5):
             for yy in range(ny):
-                value = gathered[g * ny + yy, pl.ds(4 * field, 4), :]
+                value = gathered[g, 20 * yy + 4 * field:20 * yy + 4 * field + 4, :]
                 if field < 3:
                     f2[field, g + 1, pl.ds(4 * yy, 4), :] = value
                 else:
@@ -566,25 +575,29 @@
     loop(1, pairs + 1, last)
 
 
-def ascend(pos, gathered, coarse, lower, upper, *rest, nx, ny):
-    far, (sums, parts), rest = rest[:10], rest[10:12], rest[12:]
-    near, rest = rest[:10], rest[10:]
+def ascend(pos, *rest, nx, ny):
+    far, (sums, parts), rest = rest[:14], rest[14:16], rest[16:]
+    near, rest = rest[:14], rest[14:]
     e2out, window, rows24, va1, vb1, rows32, spread, vb, precond, term, held = rest[:11]
     v1, f1, kx1, ky1, kyp1, kz1, kzp1, inverse1, stiff1, pen1, diagonal1, v01 = rest[11:23]
     work, copied = rest[23:-1], rest[-1]
-    va, start, kx, ky, kyp, kz, kzp, inverse, forward, weights = near
+    gathered, center, lower, upper = near[:4]
+    va, start, kx, ky, kyp, kz, kzp, inverse, forward, weights = near[4:]
     arrivals = [pltpu.make_async_copy(source, target, copied.at[i]) for i, (source, target) in enumerate(zip(far, near))]
     for move in arrivals:
         move.start()
     departures = []
 
-    def send(lower, upper):
-        move = pltpu.make_async_copy(held.at[lower:upper], parts.at[lower:upper], copied.at[10 + len(departures)])
+    def send(source, target):
+        move = pltpu.make_async_copy(source, target, copied.at[14 + len(departures)])
         move.start()
         departures.append(move)
 
+    for move in arrivals[1:4]:
+        move.wait()
     level_one_again(
-        pos, coarse, lower, upper, v1, f1, kx1, ky1, kyp1, kz1, kzp1, inverse1, stiff1, pen1, diagonal1, v01)
+        pos, center, lower, upper, v1, f1, kx1, ky1, kyp1, kz1, kzp1, inverse1, stiff1, pen1, diagonal1, v01)
+    arrivals[0].wait()
     coarse_levels(pos, gathered, e2out, nx, ny, work)
     gx, gy = pos[0], pos[1]
     ys = 4 * ny
@@ -624,7 +637,7 @@
     sweep1(va1, vb1, SECOND, 3, 15)
     sweep1(vb1, va1, FIRST, 4, 14)
     grow0 = matrix((BZ, LANES), lambda j, l: j == (l >> 1))
-    for move in arrivals:
+    for move in arrivals[4:]:
         move.wait()
     for c in range(3):
         spread[...] = times(va1[c, 4:14].reshape(240, BZ), grow0)
@@ -659,7 +672,7 @@
             held[3 + c, x] = start[c, x + 4][:BY, :BZ]
 
     loop(0, BX, keep)
-    send(0, 6)
+    send(held.at[0:6], parts.at[0:6])
 
     def inner(x, carry):
         one, two = carry
@@ -673,7 +686,7 @@
 
     zero = jnp.zeros((BY, BZ), F32)
     one, two = lax.fori_loop(0, BX, inner, (zero, zero), unroll=4)
-    send(6, 9)
+    send(held.at[6:9], parts.at[6:9])
     lane = iota((8, BZ), 1)
     sums[...] = jnp.where(lane == 0, jnp.sum(one), jnp.where(lane == 1, jnp.sum(two), 0.0))
     sensitivity(forward, precond, weights, term)
@@ -682,7 +695,7 @@
         held[9, x] = weigh(term, x)
 
     loop(0, BX, smooth)
-    send(9, 10)
+    send(held.at[9:10], parts.at[9:10])
     for move in departures:
         move.wait()
 
@@ -728,7 +741,18 @@
     return result[:BY, :BZ]
 
 
-def filter_iterate(pos, iterate, state, weights, out, term, inside):
+def arrive(far, near, copied):
+    moves = [pltpu.make_async_copy(source, target, copied.at[i]) for i, (source, target) in enumerate(zip(far, near))]
+    for move in moves:
+        move.start()
+    for move in moves:
+        move.wait()
+
+
+def filter_iterate(pos, *rest):
+    far, out, near, (term, inside, copied) = rest[:3], rest[3], rest[4:7], rest[7:]
+    arrive(far, near, copied)
+    iterate, state, weights = near
     sensitivity(state, iterate, weights, term)
 
     def mark(i):
@@ -802,7 +826,8 @@
         far_outs=[fields(18), fields(16), slabs(17)] + [slabs(16)] * 4 + [fields(16), fields(14), slabs(14), fields(14)],
         copies=11)
     smooth = launch(
-        8, filter_iterate, [(2,) + cells], [slabs(12), slabs(12)], [pos, u, forward, weights],
+        10, filter_iterate, [(2,) + cells], [fields(14), fields(14), slabs(14), slabs(12), slabs(12)], [pos],
+        far=[u, forward, weights], copies=3,
         cost=pl.CostEstimate(flops=12_000_000, bytes_accessed=4_000_000, transcendentals=0))[0]
 
     from_lower, from_upper = shift_along(high, "gz", 1), shift_along(low, "gz", -1)
@@ -812,12 +837,14 @@
     one1, three1 = (10,) + wide1, (3, 10) + wide1
     chunk = launch(
         4, level_one, [(24, BZ)], [one1] * 5 + [three1] * 5 + [(8, BZ), (40, BZ), (40, BZ)], [pos, coarse])[0]
+    side = (32, 24, BZ)
     column = lax.all_to_all(jnp.broadcast_to(chunk[None], (ny, 24, BZ)), "gy", 0, 0, tiled=True)
-    side = (32, 24, BZ)
-    center, to_upper, to_lower = launch(4, join_rows, [(44, 24, BZ), side, side], [], [pos, center, from_lower, from_upper])
+    to_upper, to_lower, center = launch(
+        4, join_rows, [side, side], [(44, 24, BZ)], [pos, center, from_lower, from_upper], far=[smooth],
+        far_outs=[(44, 24, BZ)], copies=1)
+    column = launch(8, pack_column, [(nx, 20 * ny, BZ)], [], [pos, column])[0]
+    gathered = lax.all_to_all(column, "gx", 0, 0, tiled=True)
     from_lower, from_upper = shift_along(to_upper, "gx", 1), shift_along(to_lower, "gx", -1)
-    column = jnp.broadcast_to(column[None], (nx, ny, 24, BZ)).reshape(nx * ny, 24, BZ)
-    gathered = lax.all_to_all(column, "gx", 0, 0, tiled=True)
 
     wide1 = (24, BZ)
     one1, three1 = (18,) + wide1, (3, 18) + wide1
@@ -826,20 +853,20 @@
     one3, three3 = (nx + 2,) + wide3, (3, nx + 2) + wide3
     work = [one2, one2, three2] + [one2] * 6 + [three2] * 4 + [wide2, (5 * nx * 2 * ny, BZ)]
     work += [one3, one3, three3] + [one3] * 5 + [three3] * 3 + [(nx * 2 * ny, BZ)]
-    far = [v1, start, kx, ky, kyp, kz, kzp, inverse, forward, weights]
     parts = (10,) + cells
+    far = [gathered, center, from_lower, from_upper, v1, start, kx, ky, kyp, kz, kzp, inverse, forward, weights]
     scratch = [x.shape for x in far] + [
         (3, nx + 4) + wide2, (15 * 4 * ny, LANES), wide1, three1, three1, (ROWS, BZ), (240, LANES), fields(16), fields(14), slabs(12), parts
     ] + [three1] * 2 + [one1] * 5 + [three1, one1, one1, three1, three1] + work
     sums, parts = launch(
-        28, functools.partial(ascend, nx=nx, ny=ny), [(8, BZ)], scratch, [pos, gathered, center, from_lower, from_upper],
-        far_outs=[parts], far=far, copies=13)
+        30, functools.partial(ascend, nx=nx, ny=ny), [(8, BZ)], scratch, [pos], far_outs=[parts], far=far, copies=17)
 
     total = lax.all_to_all(jnp.broadcast_to(sums[:1], (nx * ny, BZ)), ("gx", "gy"), 0, 0, tiled=True)
     total = jnp.sum(total, axis=0, keepdims=True)
     total = lax.all_to_all(jnp.broadcast_to(total, (nz, BZ)), "gz", 0, 0, tiled=True)
     return tuple(launch(
-        4, finish, [field, field, cells], [field, parts.shape, smooth.shape], [pos, total], far=[iterate, parts, smooth], copies=3))
+        4, finish, [field, field, cells], [field, parts.shape, smooth.shape], [pos, total],
+        far=[iterate, parts, smooth], copies=3))
 
 
 def solution(mesh):

time: 167 us -> 163 us (0.976)
  Pallas kernels: 40.3 us -> 45.8 us
  waiting for transfers between devices: 39.8 us -> 34.8 us
  local copies, waits for them, and re-layouts: 6.68 us -> 2.28 us
    ppermute x12, waiting for transfers between devices: 39.4 us -> 33.7 us  [shift_along(): lax.ppermute(x, axis, [(i, (i + step) % devices) for i in range(devices)])]
    pallas_call x10 -> x11, Pallas kernels: 40.3 us -> 45.8 us  [launch(): pl.pallas_call(kernel, out_shape=[pltpu.VMEM(shape, F32) if pin else jax....]
    unnamed x20 -> x8, local copies, waits for them, and re-layouts: 5.04 us -> 1.6 us
  transfers between devices with their start and end apart: 14 -> 14, of which waited for: 12 -> 10; matrix products, arithmetic and copies ran while one was open for 0% -> 0% of each run, Pallas kernels for 2% -> 5%
where the time goes in v4:
time: 163 us
  starting transfers between devices  50.1 us (31%)
  Pallas kernels  45.8 us (28%)
  waiting for transfers between devices  34.8 us (21%)
  blocking collectives  28.5 us (17%)
  local copies, waits for them, and re-layouts  2.28 us (1%)
    pallas_call x11, Pallas kernels, launch(): pl.pallas_call(kernel, out_shape=[pltpu.VMEM(shape, F32) if pin else jax....  45.8 us
    ppermute x12, starting transfers between devices, shift_along(): lax.ppermute(x, axis, [(i, (i + step) % devices) for i in range(devices)])  39.4 us
    ppermute x12, waiting for transfers between devices, shift_along(): lax.ppermute(x, axis, [(i, (i + step) % devices) for i in range(devices)])  33.7 us
    all_to_all x1, blocking collectives, body(): lax.all_to_all(jnp.broadcast_to(sums[:1], (nx * ny, BZ)), ('gx', 'gy'), 0...  16.2 us
    all_to_all x1, blocking collectives, body(): lax.all_to_all(jnp.broadcast_to(total, (nz, BZ)), 'gz', 0, 0, tiled=True)  12.4 us
    all_to_all x1, starting transfers between devices, body(): gathered = lax.all_to_all(column, 'gx', 0, 0, tiled=True)  5.8 us
    all_to_all x1, starting transfers between devices, body(): lax.all_to_all(jnp.broadcast_to(chunk[None], (ny, 24, BZ)), 'gy', 0, 0, t...  4.93 us
  transfers between devices with their start and end apart: 14, of which 10 were waited for; matrix products, arithmetic and copies ran while one was open for 0% of the time, Pallas kernels for 5%

profile of v4, /device:TPU:1, one launch (start us, length us, event | category | flops | bytes accessed | tf_op | source)
XLA Modules:
  0.0 162.6 jit_solution(15657471390228114603)
XLA Ops:
  0.6 0.1 pad_add_fusion.pos
  0.7 2.3 %shard_map.94 = (f32[11,8,16,128]{3,2,1,0:T(8,128)S(1)}, f32[8,16,128]{2,1,0:T(8,128)S(1)}, f32[8,16,128]{2,1,0:T(8,128)S(1)}) custom-call(s32[6]{0:T(128)S(1)} %pad_add_fusion.pos, f32[3,8,16,128]{3,2,1,0:T(8,128)} %right_far.1, f32[3,8,16,128]{3,2,1,0:T(8,128)} %rest_0_.1, f32[3,8,16,128]{3,2,1,0:T(8,128)} %state_far.1, s32[8,16,128]{2,1,0:T(8,128)} %classes_far.1, ...), custom_call_target="tpu_custom_call" | custom-call | tf_op jit(solution)/shard_map/pallas_call | solution.py:74
  3.1 4.0 %collective-permute-start = (f32[8,16,128]{2,1,0:T(8,128)S(1)}, f32[8,16,128]{2,1,0:T(8,128)S(1)}, u32[]{:S(2)}, u32[]{:S(2)}) collective-permute-start(f32[8,16,128]{2,1,0:T(8,128)S(1)} %get-tuple-element.34), channel_id=1, source_target_pairs={{0,1},{1,2},{2,3},{3,4},{4,5},{5,6},{6,7},{7,0},{8,9},{9,10},{10,1... | collective-permute-start | bytes 196616 | tf_op jit(solution)/shard_map/ppermute | solution.py:87
  7.1 3.8 %collective-permute-start.1 = (f32[8,16,128]{2,1,0:T(8,128)S(1)}, f32[8,16,128]{2,1,0:T(8,128)S(1)}, u32[]{:S(2)}, u32[]{:S(2)}) collective-permute-start(f32[8,16,128]{2,1,0:T(8,128)S(1)} %get-tuple-element.35), channel_id=1, source_target_pairs={{0,7},{1,0},{2,1},{3,2},{4,3},{5,4},{6,5},{7,6},{8,15},{9,8},{10,9... | collective-permute-start | bytes 196616 | tf_op jit(solution)/shard_map/ppermute | solution.py:87
  10.9 0.0 collective-permute-done.from_lower
  10.9 1.3 collective-permute-done.1.from_upper
  12.2 0.6 shard_map.95
  12.9 4.0 %collective-permute-start.2 = (f32[12,8,8,128]{3,2,1,0:T(8,128)S(1)}, f32[12,8,8,128]{3,2,1,0:T(8,128)S(1)}, u32[]{:S(2)}, u32[]{:S(2)}) collective-permute-start(f32[12,8,8,128]{3,2,1,0:T(8,128)S(1)} %get-tuple-element.37), channel_id=1, source_target_pairs={{0,8},{8,16},{16,24},{24,32},{32,40},{40,48},{48,56},{56,0},{1,9},... | collective-permute-start | bytes 1179656 | tf_op jit(solution)/shard_map/ppermute | solution.py:87
  16.9 8.6 %collective-permute-start.3 = (f32[12,8,8,128]{3,2,1,0:T(8,128)S(1)}, f32[12,8,8,128]{3,2,1,0:T(8,128)S(1)}, u32[]{:S(2)}, u32[]{:S(2)}) collective-permute-start(f32[12,8,8,128]{3,2,1,0:T(8,128)S(1)} %get-tuple-element.38), channel_id=1, source_target_pairs={{0,56},{8,0},{16,8},{24,16},{32,24},{40,32},{48,40},{56,48},{1,57}... | collective-permute-start | bytes 1179656 | tf_op jit(solution)/shard_map/ppermute | solution.py:87
  25.5 5.5 %collective-permute-done.2.from_lower = f32[12,8,8,128]{3,2,1,0:T(8,128)S(1)} collective-permute-done((f32[12,8,8,128]{3,2,1,0:T(8,128)S(1)}, f32[12,8,8,128]{3,2,1,0:T(8,128)S(1)}, u32[]{:S(2)}, u32[]{:S(2)}) %collective-permute-start.2) | collective-permute-done | bytes 393248 | tf_op jit(solution)/shard_map/ppermute | solution.py:87
  31.0 0.9 collective-permute-done.3.from_upper
  31.9 0.8 shard_map.96
  32.7 4.0 %collective-permute-start.4 = (f32[72,32,128]{2,1,0:T(8,128)S(1)}, f32[72,32,128]{2,1,0:T(8,128)S(1)}, u32[]{:S(2)}, u32[]{:S(2)}) collective-permute-start(f32[72,32,128]{2,1,0:T(8,128)S(1)} %get-tuple-element.40), channel_id=1, source_target_pairs={{0,64},{64,128},{128,192},{192,256},{256,320},{320,384},{384,448},... | collective-permute-start | bytes 3538952 | tf_op jit(solution)/shard_map/ppermute | solution.py:87
  36.7 0.0 collective-permute-start.5
  36.7 13.1 %collective-permute-done.4.lower = f32[72,32,128]{2,1,0:T(8,128)S(1)} collective-permute-done((f32[72,32,128]{2,1,0:T(8,128)S(1)}, f32[72,32,128]{2,1,0:T(8,128)S(1)}, u32[]{:S(2)}, u32[]{:S(2)}) %collective-permute-start.4) | collective-permute-done | bytes 1179680 | tf_op jit(solution)/shard_map/ppermute | solution.py:87
  49.9 2.5 %collective-permute-done.5.upper = f32[72,32,128]{2,1,0:T(8,128)S(1)} collective-permute-done((f32[72,32,128]{2,1,0:T(8,128)S(1)}, f32[72,32,128]{2,1,0:T(8,128)S(1)}, u32[]{:S(2)}, u32[]{:S(2)}) %collective-permute-start.5) | collective-permute-done | bytes 1179680 | tf_op jit(solution)/shard_map/ppermute | solution.py:87
  52.4 11.0 %shard_map.97 = (f32[44,16,128]{2,1,0:T(8,128)S(1)}, f32[22,8,128]{2,1,0:T(8,128)S(1)}, f32[22,8,128]{2,1,0:T(8,128)S(1)}, f32[3,18,32,256]{3,2,1,0:T(8,128)}, f...) custom-call(s32[6]{0:T(128)S(1)} %pad_add_fusion.pos, ...), custom_call_target="tpu_custom_call" | custom-call | tf_op jit(solution)/shard_map/pallas_call | solution.py:74
  63.4 3.1 %collective-permute-start.6 = (f32[22,8,128]{2,1,0:T(8,128)S(1)}, f32[22,8,128]{2,1,0:T(8,128)S(1)}, u32[]{:S(2)}, u32[]{:S(2)}) collective-permute-start(f32[22,8,128]{2,1,0:T(8,128)S(1)} %get-tuple-element.43), channel_id=1, source_target_pairs={{0,1},{1,2},{2,3},{3,4},{4,5},{5,6},{6,7},{7,0},{8,9},{9,10},{10,1... | collective-permute-start | bytes 270344 | tf_op jit(solution)/shard_map/ppermute | solution.py:87
  66.5 3.7 %collective-permute-start.7 = (f32[22,8,128]{2,1,0:T(8,128)S(1)}, f32[22,8,128]{2,1,0:T(8,128)S(1)}, u32[]{:S(2)}, u32[]{:S(2)}) collective-permute-start(f32[22,8,128]{2,1,0:T(8,128)S(1)} %get-tuple-element.44), channel_id=1, source_target_pairs={{0,7},{1,0},{2,1},{3,2},{4,3},{5,4},{6,5},{7,6},{8,15},{9,8},{10,9... | collective-permute-start | bytes 270344 | tf_op jit(solution)/shard_map/ppermute | solution.py:87
  70.2 0.9 collective-permute-done.6.from_lower
  71.1 2.2 %collective-permute-done.7.from_upper = f32[22,8,128]{2,1,0:T(8,128)S(1)} collective-permute-done((f32[22,8,128]{2,1,0:T(8,128)S(1)}, f32[22,8,128]{2,1,0:T(8,128)S(1)}, u32[]{:S(2)}, u32[]{:S(2)}) %collective-permute-start.7) | collective-permute-done | bytes 90144 | tf_op jit(solution)/shard_map/ppermute | solution.py:87
  73.3 1.0 shard_map.98
  74.4 1.5 shard_map.99
  75.9 0.7 broadcast_in_dim.6
  76.5 4.9 %all-to-all-start = ((f32[8,24,128]{2,1,0:T(8,128)}), f32[8,24,128]{2,1,0:T(8,128)S(1)}, u32[]{:S(2)}, u32[]{:S(2)}) async-start(f32[8,24,128]{2,1,0:T(8,128)} %broadcast_in_dim.6), calls=%async_computation | async-start | bytes 196608 | tf_op jit(solution)/shard_map/all_to_all | solution.py:841
  81.5 4.6 %collective-permute-start.9 = (f32[44,8,128]{2,1,0:T(8,128)S(1)}, f32[44,8,128]{2,1,0:T(8,128)S(1)}, u32[]{:S(2)}, u32[]{:S(2)}) collective-permute-start(f32[44,8,128]{2,1,0:T(8,128)S(1)} %get-tuple-element.46.coarse), channel_id=1, source_target_pairs={{0,56},{8,0},{16,8},{24,16},{32,24},{40,32},{48,40},{56,48},{1,57}... | collective-permute-start | bytes 540680 | tf_op jit(solution)/shard_map/ppermute | solution.py:87
  86.1 1.9 %collective-permute-start.8 = (f32[44,8,128]{2,1,0:T(8,128)S(1)}, f32[44,8,128]{2,1,0:T(8,128)S(1)}, u32[]{:S(2)}, u32[]{:S(2)}) collective-permute-start(f32[44,8,128]{2,1,0:T(8,128)S(1)} %get-tuple-element.46.coarse), channel_id=1, source_target_pairs={{0,8},{8,16},{16,24},{24,32},{32,40},{40,48},{48,56},{56,0},{1,9},... | collective-permute-start | bytes 540680 | tf_op jit(solution)/shard_map/ppermute | solution.py:87
  88.0 1.1 all-to-all-done.column
  89.1 1.4 shard_map.100
  90.5 5.8 %all-to-all-start.1 = ((f32[8,160,128]{2,1,0:T(8,128)}), f32[8,160,128]{2,1,0:T(8,128)S(1)}, u32[]{:S(2)}, u32[]{:S(2)}) async-start(f32[8,160,128]{2,1,0:T(8,128)} %shard_map.100), calls=%async_computation.1 | async-start | bytes 1310720 | tf_op jit(solution)/shard_map/all_to_all | solution.py:846
  96.3 5.1 %shard_map.101.after.rest_2_ = f32[2,8,16,128]{3,2,1,0:T(8,128)S(1)} custom-call(s32[6]{0:T(128)S(1)} %pad_add_fusion.pos, f32[3,14,32,256]{3,2,1,0:T(8,128)} %get-tuple-element.47.rest_0_, f32[3,14,32,256]{3,2,1,0:T(8,128)} %get-tuple-element.48.rest_1_.rest_12_, f32[14,32,256]{2,1,0:T(8,128)} %get-tuple-element.49.rest_2_.rest_13_), custom_call_target="tpu_custom_call" | custom-call | flops 12000000 | bytes 4000000 | tf_op jit(solution)/shard_map/pallas_call | solution.py:74
  101.4 0.0 copy-start
  101.4 0.6 copy-done
  102.1 0.0 collective-permute-done.9.from_upper
  102.1 0.0 collective-permute-done.8.from_lower
  102.1 1.5 shard_map.102
  103.5 1.6 %collective-permute-start.10 = (f32[32,24,128]{2,1,0:T(8,128)S(1)}, f32[32,24,128]{2,1,0:T(8,128)S(1)}, u32[]{:S(2)}, u32[]{:S(2)}) collective-permute-start(f32[32,24,128]{2,1,0:T(8,128)S(1)} %get-tuple-element.51), channel_id=1, source_target_pairs={{0,64},{64,128},{128,192},{192,256},{256,320},{320,384},{384,448},... | collective-permute-start | bytes 1179656 | tf_op jit(solution)/shard_map/ppermute | solution.py:87
  105.2 0.0 collective-permute-start.11
  105.2 4.7 %collective-permute-done.10.rest_2_ = f32[32,24,128]{2,1,0:T(8,128)S(1)} collective-permute-done((f32[32,24,128]{2,1,0:T(8,128)S(1)}, f32[32,24,128]{2,1,0:T(8,128)S(1)}, u32[]{:S(2)}, u32[]{:S(2)}) %collective-permute-start.10) | collective-permute-done | bytes 393248 | tf_op jit(solution)/shard_map/ppermute | solution.py:87
  109.9 0.0 copy-start.2
  109.9 2.5 %collective-permute-done.11.rest_3_ = f32[32,24,128]{2,1,0:T(8,128)S(1)} collective-permute-done((f32[32,24,128]{2,1,0:T(8,128)S(1)}, f32[32,24,128]{2,1,0:T(8,128)S(1)}, u32[]{:S(2)}, u32[]{:S(2)}) %collective-permute-start.11) | collective-permute-done | bytes 393248 | tf_op jit(solution)/shard_map/ppermute | solution.py:87
  112.4 0.0 copy-start.3
  112.4 0.0 all-to-all-done.1.rest_0_
  112.4 0.0 copy-start.1
  112.4 0.0 copy-done.2
  112.4 0.7 copy-done.3
  113.1 0.2 copy-done.1
  113.4 17.9 %shard_map.103 = (f32[8,128]{1,0:T(8,128)S(1)}, f32[10,8,16,128]{3,2,1,0:T(8,128)}) custom-call(s32[6]{0:T(128)S(1)} %pad_add_fusion.pos, f32[8,160,128]{2,1,0:T(8,128)} %copy-done.1, f32[44,24,128]{2,1,0:T(8,128)} %get-tuple-element.50.rest_1_, f32[32,24,128]{2,1,0:T(8,128)} %copy-done.2, f32[32,24,128]{2,1,0:T(8,128)} %copy-done.3, ...), custom_call_target="tpu_custom_call" | custom-call | tf_op jit(solution)/shard_map/pallas_call | solution.py:74
  131.3 16.2 %all_to_all.24 = f32[64,1,128]{2,1,0:T(1,128)S(1)} all-to-all(f32[64,1,128]{2,1,0:T(1,128)S(1)} %broadcast_in_dim.7), channel_id=1, replica_groups=mesh['gx'=8,'gy'=8,'gz'=8] {'gx','gy'}, dimensions={0} | all-to-all | bytes 65536 | tf_op jit(solution)/shard_map/all_to_all | solution.py:864
  147.5 12.4 %all_to_all.25 = f32[8,1,128]{2,1,0:T(1,128)S(1)} all-to-all(f32[8,1,128]{2,1,0:T(1,128)S(1)} %broadcast_in_dim.8), channel_id=1, replica_groups=mesh['gx'=8,'gy'=8,'gz'=8] {'gz'}, dimensions={0} | all-to-all | bytes 8192 | tf_op jit(solution)/shard_map/all_to_all | solution.py:866
  159.8 2.6 %shard_map.104 = (f32[3,8,16,128]{3,2,1,0:T(8,128)}, f32[3,8,16,128]{3,2,1,0:T(8,128)}, f32[8,16,128]{2,1,0:T(8,128)}) custom-call(s32[6]{0:T(128)S(1)} %pad_add_fusion.pos, f32[8,128]{1,0:T(8,128)S(1)} %bitcast.7, f32[3,8,16,128]{3,2,1,0:T(8,128)} %rest_0_.1, f32[10,8,16,128]{3,2,1,0:T(8,128)} %get-tuple-element.62.rest_1_, f32[2,8,16,128]{3,2,1,0:T(8,128)} %copy-done), custom_call_target="tpu_custom_call" | custom-call | tf_op jit(solution)/shard_map/pallas_call | solution.py:74
  (5 shorter events, 0.1 us)
Async XLA Ops:
  3.1 7.9 %collective-permute-start = (f32[8,16,128]{2,1,0:T(8,128)S(1)}, f32[8,16,128]{2,1,0:T(8,128)S(1)}, u32[]{:S(2)}, u32[]{:S(2)}) collective-permute-start(f32[8,16,128]{2,1,0:T(8,128)S(1)} %get-tuple-element.34), channel_id=1, source_target_pairs={{0,1},{1,2},{2,3},{3,4},{4,5},{5,6},{6,7},{7,0},{8,9},{9,10},{10,1... | collective-permute-start | bytes 196616 | tf_op jit(solution)/shard_map/ppermute | solution.py:87
  7.1 5.1 %collective-permute-start.1 = (f32[8,16,128]{2,1,0:T(8,128)S(1)}, f32[8,16,128]{2,1,0:T(8,128)S(1)}, u32[]{:S(2)}, u32[]{:S(2)}) collective-permute-start(f32[8,16,128]{2,1,0:T(8,128)S(1)} %get-tuple-element.35), channel_id=1, source_target_pairs={{0,7},{1,0},{2,1},{3,2},{4,3},{5,4},{6,5},{7,6},{8,15},{9,8},{10,9... | collective-permute-start | bytes 196616 | tf_op jit(solution)/shard_map/ppermute | solution.py:87
  12.9 18.1 %collective-permute-start.2 = (f32[12,8,8,128]{3,2,1,0:T(8,128)S(1)}, f32[12,8,8,128]{3,2,1,0:T(8,128)S(1)}, u32[]{:S(2)}, u32[]{:S(2)}) collective-permute-start(f32[12,8,8,128]{3,2,1,0:T(8,128)S(1)} %get-tuple-element.37), channel_id=1, source_target_pairs={{0,8},{8,16},{16,24},{24,32},{32,40},{40,48},{48,56},{56,0},{1,9},... | collective-permute-start | bytes 1179656 | tf_op jit(solution)/shard_map/ppermute | solution.py:87
  16.9 15.0 %collective-permute-start.3 = (f32[12,8,8,128]{3,2,1,0:T(8,128)S(1)}, f32[12,8,8,128]{3,2,1,0:T(8,128)S(1)}, u32[]{:S(2)}, u32[]{:S(2)}) collective-permute-start(f32[12,8,8,128]{3,2,1,0:T(8,128)S(1)} %get-tuple-element.38), channel_id=1, source_target_pairs={{0,56},{8,0},{16,8},{24,16},{32,24},{40,32},{48,40},{56,48},{1,57}... | collective-permute-start | bytes 1179656 | tf_op jit(solution)/shard_map/ppermute | solution.py:87
  32.7 17.2 %collective-permute-start.4 = (f32[72,32,128]{2,1,0:T(8,128)S(1)}, f32[72,32,128]{2,1,0:T(8,128)S(1)}, u32[]{:S(2)}, u32[]{:S(2)}) collective-permute-start(f32[72,32,128]{2,1,0:T(8,128)S(1)} %get-tuple-element.40), channel_id=1, source_target_pairs={{0,64},{64,128},{128,192},{192,256},{256,320},{320,384},{384,448},... | collective-permute-start | bytes 3538952 | tf_op jit(solution)/shard_map/ppermute | solution.py:87
  36.7 15.6 %collective-permute-start.5 = (f32[72,32,128]{2,1,0:T(8,128)S(1)}, f32[72,32,128]{2,1,0:T(8,128)S(1)}, u32[]{:S(2)}, u32[]{:S(2)}) collective-permute-start(f32[72,32,128]{2,1,0:T(8,128)S(1)} %get-tuple-element.41), channel_id=1, source_target_pairs={{0,448},{64,0},{128,64},{192,128},{256,192},{320,256},{384,320},{4... | collective-permute-start | bytes 3538952 | tf_op jit(solution)/shard_map/ppermute | solution.py:87
  63.4 7.8 %collective-permute-start.6 = (f32[22,8,128]{2,1,0:T(8,128)S(1)}, f32[22,8,128]{2,1,0:T(8,128)S(1)}, u32[]{:S(2)}, u32[]{:S(2)}) collective-permute-start(f32[22,8,128]{2,1,0:T(8,128)S(1)} %get-tuple-element.43), channel_id=1, source_target_pairs={{0,1},{1,2},{2,3},{3,4},{4,5},{5,6},{6,7},{7,0},{8,9},{9,10},{10,1... | collective-permute-start | bytes 270344 | tf_op jit(solution)/shard_map/ppermute | solution.py:87
  66.5 6.9 %collective-permute-start.7 = (f32[22,8,128]{2,1,0:T(8,128)S(1)}, f32[22,8,128]{2,1,0:T(8,128)S(1)}, u32[]{:S(2)}, u32[]{:S(2)}) collective-permute-start(f32[22,8,128]{2,1,0:T(8,128)S(1)} %get-tuple-element.44), channel_id=1, source_target_pairs={{0,7},{1,0},{2,1},{3,2},{4,3},{5,4},{6,5},{7,6},{8,15},{9,8},{10,9... | collective-permute-start | bytes 270344 | tf_op jit(solution)/shard_map/ppermute | solution.py:87
  76.5 12.5 %all-to-all-start = ((f32[8,24,128]{2,1,0:T(8,128)}), f32[8,24,128]{2,1,0:T(8,128)S(1)}, u32[]{:S(2)}, u32[]{:S(2)}) async-start(f32[8,24,128]{2,1,0:T(8,128)} %broadcast_in_dim.6), calls=%async_computation | async-start | bytes 196608 | tf_op jit(solution)/shard_map/all_to_all | solution.py:841
  81.5 20.6 %collective-permute-start.9 = (f32[44,8,128]{2,1,0:T(8,128)S(1)}, f32[44,8,128]{2,1,0:T(8,128)S(1)}, u32[]{:S(2)}, u32[]{:S(2)}) collective-permute-start(f32[44,8,128]{2,1,0:T(8,128)S(1)} %get-tuple-element.46.coarse), channel_id=1, source_target_pairs={{0,56},{8,0},{16,8},{24,16},{32,24},{40,32},{48,40},{56,48},{1,57}... | collective-permute-start | bytes 540680 | tf_op jit(solution)/shard_map/ppermute | solution.py:87
  86.1 16.0 %collective-permute-start.8 = (f32[44,8,128]{2,1,0:T(8,128)S(1)}, f32[44,8,128]{2,1,0:T(8,128)S(1)}, u32[]{:S(2)}, u32[]{:S(2)}) collective-permute-start(f32[44,8,128]{2,1,0:T(8,128)S(1)} %get-tuple-element.46.coarse), channel_id=1, source_target_pairs={{0,8},{8,16},{16,24},{24,32},{32,40},{40,48},{48,56},{56,0},{1,9},... | collective-permute-start | bytes 540680 | tf_op jit(solution)/shard_map/ppermute | solution.py:87
  90.5 21.9 %all-to-all-start.1 = ((f32[8,160,128]{2,1,0:T(8,128)}), f32[8,160,128]{2,1,0:T(8,128)S(1)}, u32[]{:S(2)}, u32[]{:S(2)}) async-start(f32[8,160,128]{2,1,0:T(8,128)} %shard_map.100), calls=%async_computation.1 | async-start | bytes 1310720 | tf_op jit(solution)/shard_map/all_to_all | solution.py:846
  101.4 0.6 copy-start
  103.5 6.4 %collective-permute-start.10 = (f32[32,24,128]{2,1,0:T(8,128)S(1)}, f32[32,24,128]{2,1,0:T(8,128)S(1)}, u32[]{:S(2)}, u32[]{:S(2)}) collective-permute-start(f32[32,24,128]{2,1,0:T(8,128)S(1)} %get-tuple-element.51), channel_id=1, source_target_pairs={{0,64},{64,128},{128,192},{192,256},{256,320},{320,384},{384,448},... | collective-permute-start | bytes 1179656 | tf_op jit(solution)/shard_map/ppermute | solution.py:87
  105.2 7.2 %collective-permute-start.11 = (f32[32,24,128]{2,1,0:T(8,128)S(1)}, f32[32,24,128]{2,1,0:T(8,128)S(1)}, u32[]{:S(2)}, u32[]{:S(2)}) collective-permute-start(f32[32,24,128]{2,1,0:T(8,128)S(1)} %get-tuple-element.52), channel_id=1, source_target_pairs={{0,448},{64,0},{128,64},{192,128},{256,192},{320,256},{384,320},{4... | collective-permute-start | bytes 1179656 | tf_op jit(solution)/shard_map/ppermute | solution.py:87
  109.9 2.5 %copy-start.2 = (f32[32,24,128]{2,1,0:T(8,128)}, f32[32,24,128]{2,1,0:T(8,128)S(1)}, u32[]{:S(2)}) copy-start(f32[32,24,128]{2,1,0:T(8,128)S(1)} %collective-permute-done.10.rest_2_) | copy-start | bytes 1179652
  112.4 0.8 copy-start.3
  112.4 1.0 copy-start.1

commit v5 on v4

--- a/solution.py
+++ b/solution.py
@@ -138,26 +138,6 @@
             to_lower[tile, x] = value[:half]
 
     loop(0, BX, slab)
-
-
-def pack_slabs(pos, main, packed, from_lower, from_upper, own, to_upper, to_lower):
-    below = jnp.where(pos[1] > 0, 1.0, 0.0)
-    above = jnp.where(pos[1] < pos[4] - 1, 1.0, 0.0)
-
-    def slab(x):
-        for tile in range(12):
-            value = packed[x] if tile == PACKED else main[tile if tile < PACKED else tile - 1, x]
-            own[tile, x] = jnp.concatenate([value, from_upper[tile, x] * above, from_lower[tile, x] * below], 0)
-
-    loop(0, BX, slab)
-    for tile in range(9):
-        for j in range(HALO):
-            to_upper[tile * HALO + j] = own[tile, j + 1]
-            to_lower[tile * HALO + j] = own[tile, j]
-    for c in range(3):
-        for j in range(3):
-            to_upper[9 * HALO + 3 * c + j] = own[9 + c, BX - 3 + j]
-            to_lower[9 * HALO + 3 * c + j] = own[9 + c, j]
 
 
 def neighbours(field, c, s, kx, ky, kyp, kz, kzp, at=None):
@@ -186,12 +166,75 @@
     for c in range(3):
         value = total + pairs[c]
         diagonal[c, s] = value
-        inverse[c, s] = jnp.where(e > 0.0, 1.0 / jnp.where(e > 0.0, value, 1.0), 0.0)
+        if inverse is not None:
+            inverse[c, s] = jnp.where(e > 0.0, 1.0 / jnp.where(e > 0.0, value, 1.0), 0.0)
+
+
+def spread(value, packed, field, ref, at):
+    _, offset, width = field
+    lane = iota((ROWS, BZ), 1)
+    ref[at + (slice(None), slice(0, BZ))] = value
+    tail = jnp.where(lane >= BZ - width, roll(packed, BZ - width - offset, 1), 0.0)
+    tail = jnp.where(lane < width, roll(packed, -(HALF + offset), 1), tail)
+    ref[at + (slice(None), slice(BZ, LANES))] = tail
+
+
+LAYERS = ((RHO[0], 7), (PACKED, 7)) + tuple((f[0], 6) for f in LOAD + (PEN,)) + tuple((f[0], 3) for f in ITERATE + STATE)
+PLACE = {}
+SENT = 0
+for _tile, _count in LAYERS:
+    PLACE[_tile] = SENT
+    SENT += _count
+
+
+def pack_slabs(pos, main, packed, from_lower, from_upper, own, to_upper, to_lower,
+               rho, stiff, pen, u, load, kx, ky, kyp, kz, kzp, diagonal):
+    below = jnp.where(pos[1] > 0, 1.0, 0.0)
+    above = jnp.where(pos[1] < pos[4] - 1, 1.0, 0.0)
+
+    def slab(x):
+        for tile in range(12):
+            value = packed[x] if tile == PACKED else main[tile if tile < PACKED else tile - 1, x]
+            own[tile, x] = jnp.concatenate([value, from_upper[tile, x] * above, from_lower[tile, x] * below], 0)
+
+    loop(0, BX, slab)
+
+    def expand(x):
+        halo = own[PACKED, x]
+        spread(own[RHO[0], x], halo, RHO, rho, (x,))
+        spread(own[PEN[0], x], halo, PEN, pen, (x,))
+        for c in range(3):
+            spread(own[ITERATE[c][0], x], halo, ITERATE[c], u, (c, x))
+            spread(own[LOAD[c][0], x], halo, LOAD[c], load, (c, x))
+        stiff[x] = rho[x] * rho[x] * rho[x]
+
+    loop(0, BX, expand)
+    kx[1] = face(stiff[0], stiff[1])
+    loop(1, BX - 1, lambda x: coefficients(stiff, pen, x, 1.0, kx, ky, kyp, kz, kzp, None, diagonal))
+    lane = iota((ROWS, BZ), 1)
+
+    def begin(x):
+        halo = own[PACKED, x]
+        for c in range(3):
+            f = load[c, x] - (diagonal[c, x] * u[c, x] - neighbours(u, c, x, kx, ky, kyp, kz, kzp))
+            tile, offset, width = LOAD[c]
+            own[tile, x] = f[:, :BZ]
+            tail = f[:, BZ:]
+            halo = jnp.where((lane >= offset) & (lane < offset + width), roll(tail, offset + width, 1), halo)
+            low = HALF + offset
+            halo = jnp.where((lane >= low) & (lane < low + width), roll(tail, low, 1), halo)
+        own[PACKED, x] = halo
+
+    loop(1, BX - 1, begin)
+    for tile, count in LAYERS:
+        for j in range(count):
+            to_upper[PLACE[tile] + j] = own[tile, BX - count + j]
+            to_lower[PLACE[tile] + j] = own[tile, j]
 
 
 def descend(pos, own, lower, upper, coarse, low_lanes, high_lanes, *rest):
     far, rest = rest[:11], rest[11:]
-    (v1, start, kx, ky, kyp, kz, kzp, inverse, u, weights, forward, stiff, load, pen, diagonal, v0, half_rows, rows, copied) = rest
+    (v1, start, kx, ky, kyp, kz, kzp, inverse, u, weights, forward, stiff, pen, diagonal, v0, half_rows, rows, copied) = rest
     moves = []
 
     def send(*pairs):
@@ -202,34 +245,35 @@
 
     below = jnp.where(pos[0] > 0, 1.0, 0.0)
     above = jnp.where(pos[0] < pos[3] - 1, 1.0, 0.0)
-    lane = iota((ROWS, BZ), 1)
-
-    def spread(raw, packed, field, store):
-        tile, offset, width = field
-        store[0][store[1] + (slice(None), slice(0, BZ))] = raw(tile)
-        tail = jnp.where(lane >= BZ - width, roll(packed, BZ - width - offset, 1), 0.0)
-        tail = jnp.where(lane < width, roll(packed, -(HALF + offset), 1), tail)
-        store[0][store[1] + (slice(None), slice(BZ, LANES))] = tail
-
-    def expand(raw, s):
-        packed = raw(PACKED)
-        spread(raw, packed, RHO, (weights, (s,)))
-        spread(raw, packed, PEN, (pen, (s,)))
-        for c in range(3):
-            spread(raw, packed, ITERATE[c], (u, (c, s)))
-            spread(raw, packed, LOAD[c], (load, (c, s)))
-
-    def expand_state(raw, packed, s):
-        for c in range(3):
-            spread(raw, packed, STATE[c], (forward, (c, s)))
-
-    loop(0, HALO, lambda s: expand(lambda t: lower[t * HALO + s] * below, s))
-    loop(0, BX, lambda s: expand(lambda t: own[t, s], s + HALO))
-    loop(0, HALO, lambda s: expand(lambda t: upper[t * HALO + s] * above, s + HALO + BX))
-    loop(0, 3, lambda s: expand_state(lambda t: lower[9 * HALO + 3 * (t - 9) + s] * below, lower[PACKED * HALO + s + HALO - 3] * below, s))
-    loop(0, BX, lambda s: expand_state(lambda t: own[t, s], own[PACKED, s], s + 3))
-    loop(0, 3, lambda s: expand_state(lambda t: upper[9 * HALO + 3 * (t - 9) + s] * above, upper[PACKED * HALO + s] * above, s + 3 + BX))
-
+
+    def expand(raw, s, fields):
+        halo = raw(PACKED)
+        for field, ref, at in fields:
+            spread(raw(field[0]), halo, field, ref, at)
+
+    def densities(s):
+        return [(RHO, weights, (s,))]
+
+    def loads(s):
+        return [(PEN, pen, (s,))] + [(LOAD[c], start, (c, s)) for c in range(3)]
+
+    def motions(s):
+        return [(ITERATE[c], u, (c, s)) for c in range(3)] + [(STATE[c], forward, (c, s - 4)) for c in range(3)]
+
+    def lower_raw(s):
+        return lambda t: lower[PLACE[t] + s - (HALO - dict(LAYERS)[t])] * below
+
+    def upper_raw(s):
+        return lambda t: upper[PLACE[t] + s - (HALO + BX)] * above
+
+    after = HALO + BX
+    loop(0, HALO, lambda s: expand(lower_raw(s), s, densities(s)))
+    loop(1, HALO, lambda s: expand(lower_raw(s), s, loads(s)))
+    loop(4, HALO, lambda s: expand(lower_raw(s), s, motions(s)))
+    loop(HALO, after, lambda s: expand(lambda t: own[t, s - HALO], s, densities(s) + loads(s) + motions(s)))
+    loop(after, after + 7, lambda s: expand(upper_raw(s), s, densities(s)))
+    loop(after, after + 6, lambda s: expand(upper_raw(s), s, loads(s)))
+    loop(after, after + 3, lambda s: expand(upper_raw(s), s, motions(s)))
     send((u.at[:, 4:18], 8), (weights.at[4:18], 9), (forward, 10))
 
     def cube(s):
@@ -242,11 +286,13 @@
     faces = (kx, ky, kyp, kz, kzp)
     send((kx.at[3:20], 2), (ky.at[3:19], 3), (kyp.at[3:19], 4), (kz.at[3:19], 5), (kzp.at[3:19], 6), (inverse.at[:, 3:19], 7))
 
+    for s in (HALO - 1, HALO, HALO + BX - 1, HALO + BX):
+        for c in range(3):
+            start[c, s] = start[c, s] - (diagonal[c, s] * u[c, s] - neighbours(u, c, s, *faces))
+
     def begin(s):
         for c in range(3):
-            f = load[c, s] - (diagonal[c, s] * u[c, s] - neighbours(u, c, s, *faces))
-            start[c, s] = f
-            v0[c, s] = FIRST * f * inverse[c, s]
+            v0[c, s] = FIRST * start[c, s] * inverse[c, s]
 
     loop(1, SLABS - 1, begin)
     send((start.at[:, 3:19], 1))
@@ -319,7 +365,7 @@
     loop(0, 11, unpack)
 
 
-def join_rows(pos, coarse, from_lower, from_upper, after, to_upper, to_lower, center, out, copied):
+def join_rows(pos, coarse, from_lower, from_upper, to_upper, to_lower, center, out, copied):
     below = jnp.where(pos[1] > 0, 1.0, 0.0)
     above = jnp.where(pos[1] < pos[4] - 1, 1.0, 0.0)
 
@@ -384,9 +430,10 @@
 
     wide[...] = times(rows[...], matrix((BZ, BZ), rule))
     lane = iota((4, BZ), 1)
-    chunk[...] = jnp.zeros((24, BZ), F32)
-    for field in range(5):
-        chunk[4 * field:4 * field + 4] = jnp.where(lane < 64, wide[8 * field:8 * field + 4], wide[8 * field + 4:8 * field + 8])
+    parts = [jnp.where(lane < 64, wide[8 * field:8 * field + 4], wide[8 * field + 4:8 * field + 8]) for field in range(5)]
+    value = jnp.concatenate(parts + [jnp.zeros((4, BZ), F32)], 0)
+    for i in range(chunk.shape[0]):
+        chunk[i] = value
 
 
 def pack_column(pos, column, out):
@@ -576,7 +623,7 @@
 
 
 def ascend(pos, *rest, nx, ny):
-    far, (sums, parts), rest = rest[:14], rest[14:16], rest[16:]
+    far, (sums, parts), rest = rest[:14], rest[15:17], rest[17:]
     near, rest = rest[:14], rest[14:]
     e2out, window, rows24, va1, vb1, rows32, spread, vb, precond, term, held = rest[:11]
     v1, f1, kx1, ky1, kyp1, kz1, kzp1, inverse1, stiff1, pen1, diagonal1, v01 = rest[11:23]
@@ -797,6 +844,14 @@
     pos = jnp.concatenate([pos, jnp.array([nx, ny, nz], jnp.int32)])
     cells = (BX, BY, BZ)
     field = (3,) + cells
+    wide = (ROWS, LANES)
+
+    def slabs(n):
+        return (n,) + wide
+
+    def fields(n):
+        return (3, n) + wide
+
     main, last, first = launch(
         4, prepare, [(11,) + cells, cells, cells], [field], [pos],
         far=[right_side, iterate, state, classes, load_mask, fixed_mask], copies=6)
@@ -804,24 +859,17 @@
     edge = (12, BX, BY // 2, BZ)
     packed, to_upper, to_lower = launch(4, pack_rows, [cells, edge, edge], [], [pos, main, from_lower, from_upper])
     from_lower, from_upper = shift_along(to_upper, "gy", 1), shift_along(to_lower, "gy", -1)
-    sides = (9 * HALO + 9, ROWS, BZ)
+    sides = (SENT, ROWS, BZ)
     own, to_upper, to_lower = launch(
-        8, pack_slabs, [(12, BX, ROWS, BZ), sides, sides], [], [pos, main, packed, from_lower, from_upper])
+        14, pack_slabs, [(12, BX, ROWS, BZ), sides, sides],
+        [slabs(BX)] * 3 + [fields(BX)] * 2 + [slabs(BX)] * 5 + [fields(BX)], [pos, main, packed, from_lower, from_upper])
     from_lower, from_upper = shift_along(to_upper, "gx", 1), shift_along(to_lower, "gx", -1)
-
-    wide = (ROWS, LANES)
-
-    def slabs(n):
-        return (n,) + wide
-
-    def fields(n):
-        return (3, n) + wide
 
     one, three = slabs(SLABS), fields(SLABS)
     quarters = (22, 8, BZ)
     coarse, low, high, v1, start, kx, ky, kyp, kz, kzp, inverse, u, weights, forward = launch(
         24, descend, [(44, 16, BZ), quarters, quarters],
-        [three, three, one, one, one, one, one, three, three, one, fields(14), one, three, one, three, three, (ROWS, BZ), (44 * 16, BZ)],
+        [three, three, one, one, one, one, one, three, three, one, fields(14), one, one, three, three, (ROWS, BZ), (44 * 16, BZ)],
         [pos, own, from_lower, from_upper],
         far_outs=[fields(18), fields(16), slabs(17)] + [slabs(16)] * 4 + [fields(16), fields(14), slabs(14), fields(14)],
         copies=11)
@@ -836,11 +884,11 @@
     wide1 = (16, BZ)
     one1, three1 = (10,) + wide1, (3, 10) + wide1
     chunk = launch(
-        4, level_one, [(24, BZ)], [one1] * 5 + [three1] * 5 + [(8, BZ), (40, BZ), (40, BZ)], [pos, coarse])[0]
+        4, level_one, [(ny, 24, BZ)], [one1] * 5 + [three1] * 5 + [(8, BZ), (40, BZ), (40, BZ)], [pos, coarse])[0]
     side = (32, 24, BZ)
-    column = lax.all_to_all(jnp.broadcast_to(chunk[None], (ny, 24, BZ)), "gy", 0, 0, tiled=True)
+    column = lax.all_to_all(chunk, "gy", 0, 0, tiled=True)
     to_upper, to_lower, center = launch(
-        4, join_rows, [side, side], [(44, 24, BZ)], [pos, center, from_lower, from_upper], far=[smooth],
+        4, join_rows, [side, side], [(44, 24, BZ)], [pos, center, from_lower, from_upper],
         far_outs=[(44, 24, BZ)], copies=1)
     column = launch(8, pack_column, [(nx, 20 * ny, BZ)], [], [pos, column])[0]
     gathered = lax.all_to_all(column, "gx", 0, 0, tiled=True)
@@ -859,7 +907,7 @@
         (3, nx + 4) + wide2, (15 * 4 * ny, LANES), wide1, three1, three1, (ROWS, BZ), (240, LANES), fields(16), fields(14), slabs(12), parts
     ] + [three1] * 2 + [one1] * 5 + [three1, one1, one1, three1, three1] + work
     sums, parts = launch(
-        30, functools.partial(ascend, nx=nx, ny=ny), [(8, BZ)], scratch, [pos], far_outs=[parts], far=far, copies=17)
+        30, functools.partial(ascend, nx=nx, ny=ny), [(8, BZ)], scratch, [pos], far_outs=[parts], far=far + [smooth], copies=17)
 
     total = lax.all_to_all(jnp.broadcast_to(sums[:1], (nx * ny, BZ)), ("gx", "gy"), 0, 0, tiled=True)
     total = jnp.sum(total, axis=0, keepdims=True)

time: 163 us -> 159 us (0.975)
  waiting for transfers between devices: 34.8 us -> 30 us
  Pallas kernels: 45.8 us -> 47.5 us
    ppermute x12, waiting for transfers between devices: 33.7 us -> 28.9 us  [shift_along(): lax.ppermute(x, axis, [(i, (i + step) % devices) for i in range(devices)])]
    pallas_call x11, Pallas kernels: 45.8 us -> 47.5 us  [launch(): pl.pallas_call(kernel, out_shape=[pltpu.VMEM(shape, F32) if pin else jax....]
where the time goes in v5:
time: 159 us
  starting transfers between devices  50.1 us (32%)
  Pallas kernels  47.5 us (30%)
  waiting for transfers between devices  30 us (19%)
  blocking collectives  28.3 us (18%)
  local copies, waits for them, and re-layouts  1.63 us (1%)
    pallas_call x11, Pallas kernels, launch(): pl.pallas_call(kernel, out_shape=[pltpu.VMEM(shape, F32) if pin else jax....  47.5 us
    ppermute x12, starting transfers between devices, shift_along(): lax.ppermute(x, axis, [(i, (i + step) % devices) for i in range(devices)])  39.4 us
    ppermute x12, waiting for transfers between devices, shift_along(): lax.ppermute(x, axis, [(i, (i + step) % devices) for i in range(devices)])  28.9 us
    all_to_all x1, blocking collectives, body(): lax.all_to_all(jnp.broadcast_to(sums[:1], (nx * ny, BZ)), ('gx', 'gy'), 0...  15.9 us
    all_to_all x1, blocking collectives, body(): lax.all_to_all(jnp.broadcast_to(total, (nz, BZ)), 'gz', 0, 0, tiled=True)  12.4 us
    all_to_all x1, starting transfers between devices, body(): gathered = lax.all_to_all(column, 'gx', 0, 0, tiled=True)  5.8 us
    all_to_all x1, starting transfers between devices, body(): column = lax.all_to_all(chunk, 'gy', 0, 0, tiled=True)  4.93 us
  transfers between devices with their start and end apart: 14, of which 10 were waited for; matrix products, arithmetic and copies ran while one was open for 0% of the time, Pallas kernels for 5%

profile of v5, /device:TPU:1, one launch (start us, length us, event | category | flops | bytes accessed | tf_op | source)
XLA Modules:
  0.0 158.7 jit_solution(93584011809833139)
XLA Ops:
  0.6 0.1 pad_add_fusion.pos
  0.7 2.3 %shard_map.94 = (f32[11,8,16,128]{3,2,1,0:T(8,128)S(1)}, f32[8,16,128]{2,1,0:T(8,128)S(1)}, f32[8,16,128]{2,1,0:T(8,128)S(1)}) custom-call(s32[6]{0:T(128)S(1)} %pad_add_fusion.pos, f32[3,8,16,128]{3,2,1,0:T(8,128)} %right_far.1, f32[3,8,16,128]{3,2,1,0:T(8,128)} %rest_0_.1, f32[3,8,16,128]{3,2,1,0:T(8,128)} %state_far.1, s32[8,16,128]{2,1,0:T(8,128)} %classes_far.1, ...), custom_call_target="tpu_custom_call" | custom-call | tf_op jit(solution)/shard_map/pallas_call | solution.py:74
  3.1 4.0 %collective-permute-start = (f32[8,16,128]{2,1,0:T(8,128)S(1)}, f32[8,16,128]{2,1,0:T(8,128)S(1)}, u32[]{:S(2)}, u32[]{:S(2)}) collective-permute-start(f32[8,16,128]{2,1,0:T(8,128)S(1)} %get-tuple-element.34), channel_id=1, source_target_pairs={{0,1},{1,2},{2,3},{3,4},{4,5},{5,6},{6,7},{7,0},{8,9},{9,10},{10,1... | collective-permute-start | bytes 196616 | tf_op jit(solution)/shard_map/ppermute | solution.py:87
  7.1 3.8 %collective-permute-start.1 = (f32[8,16,128]{2,1,0:T(8,128)S(1)}, f32[8,16,128]{2,1,0:T(8,128)S(1)}, u32[]{:S(2)}, u32[]{:S(2)}) collective-permute-start(f32[8,16,128]{2,1,0:T(8,128)S(1)} %get-tuple-element.35), channel_id=1, source_target_pairs={{0,7},{1,0},{2,1},{3,2},{4,3},{5,4},{6,5},{7,6},{8,15},{9,8},{10,9... | collective-permute-start | bytes 196616 | tf_op jit(solution)/shard_map/ppermute | solution.py:87
  10.9 0.0 collective-permute-done.from_lower
  10.9 1.3 collective-permute-done.1.from_upper
  12.2 0.6 shard_map.95
  12.9 4.0 %collective-permute-start.2 = (f32[12,8,8,128]{3,2,1,0:T(8,128)S(1)}, f32[12,8,8,128]{3,2,1,0:T(8,128)S(1)}, u32[]{:S(2)}, u32[]{:S(2)}) collective-permute-start(f32[12,8,8,128]{3,2,1,0:T(8,128)S(1)} %get-tuple-element.37), channel_id=1, source_target_pairs={{0,8},{8,16},{16,24},{24,32},{32,40},{40,48},{48,56},{56,0},{1,9},... | collective-permute-start | bytes 1179656 | tf_op jit(solution)/shard_map/ppermute | solution.py:87
  16.9 8.6 %collective-permute-start.3 = (f32[12,8,8,128]{3,2,1,0:T(8,128)S(1)}, f32[12,8,8,128]{3,2,1,0:T(8,128)S(1)}, u32[]{:S(2)}, u32[]{:S(2)}) collective-permute-start(f32[12,8,8,128]{3,2,1,0:T(8,128)S(1)} %get-tuple-element.38), channel_id=1, source_target_pairs={{0,56},{8,0},{16,8},{24,16},{32,24},{40,32},{48,40},{56,48},{1,57}... | collective-permute-start | bytes 1179656 | tf_op jit(solution)/shard_map/ppermute | solution.py:87
  25.5 5.5 %collective-permute-done.2.from_lower = f32[12,8,8,128]{3,2,1,0:T(8,128)S(1)} collective-permute-done((f32[12,8,8,128]{3,2,1,0:T(8,128)S(1)}, f32[12,8,8,128]{3,2,1,0:T(8,128)S(1)}, u32[]{:S(2)}, u32[]{:S(2)}) %collective-permute-start.2) | collective-permute-done | bytes 393248 | tf_op jit(solution)/shard_map/ppermute | solution.py:87
  31.0 0.9 collective-permute-done.3.from_upper
  31.9 3.3 %shard_map.96 = (f32[12,8,32,128]{3,2,1,0:T(8,128)S(1)}, f32[56,32,128]{2,1,0:T(8,128)S(1)}, f32[56,32,128]{2,1,0:T(8,128)S(1)}) custom-call(s32[6]{0:T(128)S(1)} %pad_add_fusion.pos, f32[11,8,16,128]{3,2,1,0:T(8,128)S(1)} %get-tuple-element.33.main, f32[8,16,128]{2,1,0:T(8,128)S(1)} %get-tuple-element.36.packed, ...), custom_call_target="tpu_custom_call" | custom-call | tf_op jit(solution)/shard_map/pallas_call | solution.py:74
  35.2 4.0 %collective-permute-start.4 = (f32[56,32,128]{2,1,0:T(8,128)S(1)}, f32[56,32,128]{2,1,0:T(8,128)S(1)}, u32[]{:S(2)}, u32[]{:S(2)}) collective-permute-start(f32[56,32,128]{2,1,0:T(8,128)S(1)} %get-tuple-element.40), channel_id=1, source_target_pairs={{0,64},{64,128},{128,192},{192,256},{256,320},{320,384},{384,448},... | collective-permute-start | bytes 2752520 | tf_op jit(solution)/shard_map/ppermute | solution.py:87
  39.3 0.0 collective-permute-start.5
  39.3 10.3 %collective-permute-done.4.lower = f32[56,32,128]{2,1,0:T(8,128)S(1)} collective-permute-done((f32[56,32,128]{2,1,0:T(8,128)S(1)}, f32[56,32,128]{2,1,0:T(8,128)S(1)}, u32[]{:S(2)}, u32[]{:S(2)}) %collective-permute-start.4) | collective-permute-done | bytes 917536 | tf_op jit(solution)/shard_map/ppermute | solution.py:87
  49.6 2.5 %collective-permute-done.5.upper = f32[56,32,128]{2,1,0:T(8,128)S(1)} collective-permute-done((f32[56,32,128]{2,1,0:T(8,128)S(1)}, f32[56,32,128]{2,1,0:T(8,128)S(1)}, u32[]{:S(2)}, u32[]{:S(2)}) %collective-permute-start.5) | collective-permute-done | bytes 917536 | tf_op jit(solution)/shard_map/ppermute | solution.py:87
  52.1 9.5 %shard_map.97 = (f32[44,16,128]{2,1,0:T(8,128)S(1)}, f32[22,8,128]{2,1,0:T(8,128)S(1)}, f32[22,8,128]{2,1,0:T(8,128)S(1)}, f32[3,18,32,256]{3,2,1,0:T(8,128)}, f...) custom-call(s32[6]{0:T(128)S(1)} %pad_add_fusion.pos, ...), custom_call_target="tpu_custom_call" | custom-call | tf_op jit(solution)/shard_map/pallas_call | solution.py:74
  61.6 3.1 %collective-permute-start.6 = (f32[22,8,128]{2,1,0:T(8,128)S(1)}, f32[22,8,128]{2,1,0:T(8,128)S(1)}, u32[]{:S(2)}, u32[]{:S(2)}) collective-permute-start(f32[22,8,128]{2,1,0:T(8,128)S(1)} %get-tuple-element.43), channel_id=1, source_target_pairs={{0,1},{1,2},{2,3},{3,4},{4,5},{5,6},{6,7},{7,0},{8,9},{9,10},{10,1... | collective-permute-start | bytes 270344 | tf_op jit(solution)/shard_map/ppermute | solution.py:87
  64.7 3.7 %collective-permute-start.7 = (f32[22,8,128]{2,1,0:T(8,128)S(1)}, f32[22,8,128]{2,1,0:T(8,128)S(1)}, u32[]{:S(2)}, u32[]{:S(2)}) collective-permute-start(f32[22,8,128]{2,1,0:T(8,128)S(1)} %get-tuple-element.44), channel_id=1, source_target_pairs={{0,7},{1,0},{2,1},{3,2},{4,3},{5,4},{6,5},{7,6},{8,15},{9,8},{10,9... | collective-permute-start | bytes 270344 | tf_op jit(solution)/shard_map/ppermute | solution.py:87
  68.5 0.9 collective-permute-done.6.from_lower
  69.4 2.2 %collective-permute-done.7.from_upper = f32[22,8,128]{2,1,0:T(8,128)S(1)} collective-permute-done((f32[22,8,128]{2,1,0:T(8,128)S(1)}, f32[22,8,128]{2,1,0:T(8,128)S(1)}, u32[]{:S(2)}, u32[]{:S(2)}) %collective-permute-start.7) | collective-permute-done | bytes 90144 | tf_op jit(solution)/shard_map/ppermute | solution.py:87
  71.6 1.0 shard_map.98
  72.6 2.2 %shard_map.99 = f32[8,24,128]{2,1,0:T(8,128)} custom-call(s32[6]{0:T(128)S(1)} %pad_add_fusion.pos, f32[44,16,128]{2,1,0:T(8,128)S(1)} %get-tuple-element.45.own), custom_call_target="tpu_custom_call" | custom-call | tf_op jit(solution)/shard_map/pallas_call | solution.py:74
  74.8 4.9 %all-to-all-start = ((f32[8,24,128]{2,1,0:T(8,128)}), f32[8,24,128]{2,1,0:T(8,128)S(1)}, u32[]{:S(2)}, u32[]{:S(2)}) async-start(f32[8,24,128]{2,1,0:T(8,128)} %shard_map.99), calls=%async_computation | async-start | bytes 196608 | tf_op jit(solution)/shard_map/all_to_all | solution.py:889
  79.7 4.6 %collective-permute-start.9 = (f32[44,8,128]{2,1,0:T(8,128)S(1)}, f32[44,8,128]{2,1,0:T(8,128)S(1)}, u32[]{:S(2)}, u32[]{:S(2)}) collective-permute-start(f32[44,8,128]{2,1,0:T(8,128)S(1)} %get-tuple-element.46.coarse), channel_id=1, source_target_pairs={{0,56},{8,0},{16,8},{24,16},{32,24},{40,32},{48,40},{56,48},{1,57}... | collective-permute-start | bytes 540680 | tf_op jit(solution)/shard_map/ppermute | solution.py:87
  84.3 1.9 %collective-permute-start.8 = (f32[44,8,128]{2,1,0:T(8,128)S(1)}, f32[44,8,128]{2,1,0:T(8,128)S(1)}, u32[]{:S(2)}, u32[]{:S(2)}) collective-permute-start(f32[44,8,128]{2,1,0:T(8,128)S(1)} %get-tuple-element.46.coarse), channel_id=1, source_target_pairs={{0,8},{8,16},{16,24},{24,32},{32,40},{40,48},{48,56},{56,0},{1,9},... | collective-permute-start | bytes 540680 | tf_op jit(solution)/shard_map/ppermute | solution.py:87
  86.2 1.1 all-to-all-done.column
  87.3 1.4 shard_map.100
  88.8 5.8 %all-to-all-start.1 = ((f32[8,160,128]{2,1,0:T(8,128)}), f32[8,160,128]{2,1,0:T(8,128)S(1)}, u32[]{:S(2)}, u32[]{:S(2)}) async-start(f32[8,160,128]{2,1,0:T(8,128)} %shard_map.100), calls=%async_computation.1 | async-start | bytes 1310720 | tf_op jit(solution)/shard_map/all_to_all | solution.py:894
  94.6 0.0 collective-permute-done.9.from_upper
  94.6 0.0 collective-permute-done.8.from_lower
  94.6 1.4 shard_map.101
  96.0 1.6 %collective-permute-start.10 = (f32[32,24,128]{2,1,0:T(8,128)S(1)}, f32[32,24,128]{2,1,0:T(8,128)S(1)}, u32[]{:S(2)}, u32[]{:S(2)}) collective-permute-start(f32[32,24,128]{2,1,0:T(8,128)S(1)} %get-tuple-element.48), channel_id=1, source_target_pairs={{0,64},{64,128},{128,192},{192,256},{256,320},{320,384},{384,448},... | collective-permute-start | bytes 1179656 | tf_op jit(solution)/shard_map/ppermute | solution.py:87
  97.7 0.0 collective-permute-start.11
  97.7 5.1 %shard_map.102.rest_14_.rest_2_ = f32[2,8,16,128]{3,2,1,0:T(8,128)S(1)} custom-call(s32[6]{0:T(128)S(1)} %pad_add_fusion.pos, f32[3,14,32,256]{3,2,1,0:T(8,128)} %get-tuple-element.60.rest_0_, f32[3,14,32,256]{3,2,1,0:T(8,128)} %get-tuple-element.58.rest_1_.rest_12_, f32[14,32,256]{2,1,0:T(8,128)} %get-tuple-element.59.rest_2_.rest_13_), custom_call_target="tpu_custom_call" | custom-call | flops 12000000 | bytes 4000000 | tf_op jit(solution)/shard_map/pallas_call | solution.py:74
  102.8 0.0 copy-start
  102.8 0.6 copy-done
  103.4 3.1 %collective-permute-done.10.rest_2_ = f32[32,24,128]{2,1,0:T(8,128)S(1)} collective-permute-done((f32[32,24,128]{2,1,0:T(8,128)S(1)}, f32[32,24,128]{2,1,0:T(8,128)S(1)}, u32[]{:S(2)}, u32[]{:S(2)}) %collective-permute-start.10) | collective-permute-done | bytes 393248 | tf_op jit(solution)/shard_map/ppermute | solution.py:87
  106.6 0.0 copy-start.2
  106.6 2.1 %collective-permute-done.11.rest_3_ = f32[32,24,128]{2,1,0:T(8,128)S(1)} collective-permute-done((f32[32,24,128]{2,1,0:T(8,128)S(1)}, f32[32,24,128]{2,1,0:T(8,128)S(1)}, u32[]{:S(2)}, u32[]{:S(2)}) %collective-permute-start.11) | collective-permute-done | bytes 393248 | tf_op jit(solution)/shard_map/ppermute | solution.py:87
  108.7 0.0 copy-start.3
  108.7 0.0 all-to-all-done.1.rest_0_
  108.7 0.0 copy-start.1
  108.7 0.0 copy-done.2
  108.7 0.7 copy-done.3
  109.4 0.2 copy-done.1
  109.7 17.9 %shard_map.103 = (f32[8,128]{1,0:T(8,128)S(1)}, f32[10,8,16,128]{3,2,1,0:T(8,128)}) custom-call(s32[6]{0:T(128)S(1)} %pad_add_fusion.pos, f32[8,160,128]{2,1,0:T(8,128)} %copy-done.1, f32[44,24,128]{2,1,0:T(8,128)} %get-tuple-element.47.rest_1_, f32[32,24,128]{2,1,0:T(8,128)} %copy-done.2, f32[32,24,128]{2,1,0:T(8,128)} %copy-done.3, ...), custom_call_target="tpu_custom_call" | custom-call | tf_op jit(solution)/shard_map/pallas_call | solution.py:74
  127.6 15.9 %all_to_all.24 = f32[64,1,128]{2,1,0:T(1,128)S(1)} all-to-all(f32[64,1,128]{2,1,0:T(1,128)S(1)} %broadcast_in_dim.4), channel_id=1, replica_groups=mesh['gx'=8,'gy'=8,'gz'=8] {'gx','gy'}, dimensions={0} | all-to-all | bytes 65536 | tf_op jit(solution)/shard_map/all_to_all | solution.py:912
  143.5 12.4 %all_to_all.25 = f32[8,1,128]{2,1,0:T(1,128)S(1)} all-to-all(f32[8,1,128]{2,1,0:T(1,128)S(1)} %broadcast_in_dim.5), channel_id=1, replica_groups=mesh['gx'=8,'gy'=8,'gz'=8] {'gz'}, dimensions={0} | all-to-all | bytes 8192 | tf_op jit(solution)/shard_map/all_to_all | solution.py:914
  155.9 2.6 %shard_map.104 = (f32[3,8,16,128]{3,2,1,0:T(8,128)}, f32[3,8,16,128]{3,2,1,0:T(8,128)}, f32[8,16,128]{2,1,0:T(8,128)}) custom-call(s32[6]{0:T(128)S(1)} %pad_add_fusion.pos, f32[8,128]{1,0:T(8,128)S(1)} %bitcast.7, f32[3,8,16,128]{3,2,1,0:T(8,128)} %rest_0_.1, f32[10,8,16,128]{3,2,1,0:T(8,128)} %get-tuple-element.62.rest_1_, f32[2,8,16,128]{3,2,1,0:T(8,128)} %copy-done), custom_call_target="tpu_custom_call" | custom-call | tf_op jit(solution)/shard_map/pallas_call | solution.py:74
  (5 shorter events, 0.1 us)
Async XLA Ops:
  3.1 7.9 %collective-permute-start = (f32[8,16,128]{2,1,0:T(8,128)S(1)}, f32[8,16,128]{2,1,0:T(8,128)S(1)}, u32[]{:S(2)}, u32[]{:S(2)}) collective-permute-start(f32[8,16,128]{2,1,0:T(8,128)S(1)} %get-tuple-element.34), channel_id=1, source_target_pairs={{0,1},{1,2},{2,3},{3,4},{4,5},{5,6},{6,7},{7,0},{8,9},{9,10},{10,1... | collective-permute-start | bytes 196616 | tf_op jit(solution)/shard_map/ppermute | solution.py:87
  7.1 5.1 %collective-permute-start.1 = (f32[8,16,128]{2,1,0:T(8,128)S(1)}, f32[8,16,128]{2,1,0:T(8,128)S(1)}, u32[]{:S(2)}, u32[]{:S(2)}) collective-permute-start(f32[8,16,128]{2,1,0:T(8,128)S(1)} %get-tuple-element.35), channel_id=1, source_target_pairs={{0,7},{1,0},{2,1},{3,2},{4,3},{5,4},{6,5},{7,6},{8,15},{9,8},{10,9... | collective-permute-start | bytes 196616 | tf_op jit(solution)/shard_map/ppermute | solution.py:87
  12.9 18.1 %collective-permute-start.2 = (f32[12,8,8,128]{3,2,1,0:T(8,128)S(1)}, f32[12,8,8,128]{3,2,1,0:T(8,128)S(1)}, u32[]{:S(2)}, u32[]{:S(2)}) collective-permute-start(f32[12,8,8,128]{3,2,1,0:T(8,128)S(1)} %get-tuple-element.37), channel_id=1, source_target_pairs={{0,8},{8,16},{16,24},{24,32},{32,40},{40,48},{48,56},{56,0},{1,9},... | collective-permute-start | bytes 1179656 | tf_op jit(solution)/shard_map/ppermute | solution.py:87
  16.9 15.0 %collective-permute-start.3 = (f32[12,8,8,128]{3,2,1,0:T(8,128)S(1)}, f32[12,8,8,128]{3,2,1,0:T(8,128)S(1)}, u32[]{:S(2)}, u32[]{:S(2)}) collective-permute-start(f32[12,8,8,128]{3,2,1,0:T(8,128)S(1)} %get-tuple-element.38), channel_id=1, source_target_pairs={{0,56},{8,0},{16,8},{24,16},{32,24},{40,32},{48,40},{56,48},{1,57}... | collective-permute-start | bytes 1179656 | tf_op jit(solution)/shard_map/ppermute | solution.py:87
  35.2 14.4 %collective-permute-start.4 = (f32[56,32,128]{2,1,0:T(8,128)S(1)}, f32[56,32,128]{2,1,0:T(8,128)S(1)}, u32[]{:S(2)}, u32[]{:S(2)}) collective-permute-start(f32[56,32,128]{2,1,0:T(8,128)S(1)} %get-tuple-element.40), channel_id=1, source_target_pairs={{0,64},{64,128},{128,192},{192,256},{256,320},{320,384},{384,448},... | collective-permute-start | bytes 2752520 | tf_op jit(solution)/shard_map/ppermute | solution.py:87
  39.3 12.8 %collective-permute-start.5 = (f32[56,32,128]{2,1,0:T(8,128)S(1)}, f32[56,32,128]{2,1,0:T(8,128)S(1)}, u32[]{:S(2)}, u32[]{:S(2)}) collective-permute-start(f32[56,32,128]{2,1,0:T(8,128)S(1)} %get-tuple-element.41), channel_id=1, source_target_pairs={{0,448},{64,0},{128,64},{192,128},{256,192},{320,256},{384,320},{4... | collective-permute-start | bytes 2752520 | tf_op jit(solution)/shard_map/ppermute | solution.py:87
  61.6 7.8 %collective-permute-start.6 = (f32[22,8,128]{2,1,0:T(8,128)S(1)}, f32[22,8,128]{2,1,0:T(8,128)S(1)}, u32[]{:S(2)}, u32[]{:S(2)}) collective-permute-start(f32[22,8,128]{2,1,0:T(8,128)S(1)} %get-tuple-element.43), channel_id=1, source_target_pairs={{0,1},{1,2},{2,3},{3,4},{4,5},{5,6},{6,7},{7,0},{8,9},{9,10},{10,1... | collective-permute-start | bytes 270344 | tf_op jit(solution)/shard_map/ppermute | solution.py:87
  64.7 6.9 %collective-permute-start.7 = (f32[22,8,128]{2,1,0:T(8,128)S(1)}, f32[22,8,128]{2,1,0:T(8,128)S(1)}, u32[]{:S(2)}, u32[]{:S(2)}) collective-permute-start(f32[22,8,128]{2,1,0:T(8,128)S(1)} %get-tuple-element.44), channel_id=1, source_target_pairs={{0,7},{1,0},{2,1},{3,2},{4,3},{5,4},{6,5},{7,6},{8,15},{9,8},{10,9... | collective-permute-start | bytes 270344 | tf_op jit(solution)/shard_map/ppermute | solution.py:87
  74.8 12.5 %all-to-all-start = ((f32[8,24,128]{2,1,0:T(8,128)}), f32[8,24,128]{2,1,0:T(8,128)S(1)}, u32[]{:S(2)}, u32[]{:S(2)}) async-start(f32[8,24,128]{2,1,0:T(8,128)} %shard_map.99), calls=%async_computation | async-start | bytes 196608 | tf_op jit(solution)/shard_map/all_to_all | solution.py:889
  79.7 14.8 %collective-permute-start.9 = (f32[44,8,128]{2,1,0:T(8,128)S(1)}, f32[44,8,128]{2,1,0:T(8,128)S(1)}, u32[]{:S(2)}, u32[]{:S(2)}) collective-permute-start(f32[44,8,128]{2,1,0:T(8,128)S(1)} %get-tuple-element.46.coarse), channel_id=1, source_target_pairs={{0,56},{8,0},{16,8},{24,16},{32,24},{40,32},{48,40},{56,48},{1,57}... | collective-permute-start | bytes 540680 | tf_op jit(solution)/shard_map/ppermute | solution.py:87
  84.3 10.3 %collective-permute-start.8 = (f32[44,8,128]{2,1,0:T(8,128)S(1)}, f32[44,8,128]{2,1,0:T(8,128)S(1)}, u32[]{:S(2)}, u32[]{:S(2)}) collective-permute-start(f32[44,8,128]{2,1,0:T(8,128)S(1)} %get-tuple-element.46.coarse), channel_id=1, source_target_pairs={{0,8},{8,16},{16,24},{24,32},{32,40},{40,48},{48,56},{56,0},{1,9},... | collective-permute-start | bytes 540680 | tf_op jit(solution)/shard_map/ppermute | solution.py:87
  88.8 19.9 %all-to-all-start.1 = ((f32[8,160,128]{2,1,0:T(8,128)}), f32[8,160,128]{2,1,0:T(8,128)S(1)}, u32[]{:S(2)}, u32[]{:S(2)}) async-start(f32[8,160,128]{2,1,0:T(8,128)} %shard_map.100), calls=%async_computation.1 | async-start | bytes 1310720 | tf_op jit(solution)/shard_map/all_to_all | solution.py:894
  96.0 10.5 %collective-permute-start.10 = (f32[32,24,128]{2,1,0:T(8,128)S(1)}, f32[32,24,128]{2,1,0:T(8,128)S(1)}, u32[]{:S(2)}, u32[]{:S(2)}) collective-permute-start(f32[32,24,128]{2,1,0:T(8,128)S(1)} %get-tuple-element.48), channel_id=1, source_target_pairs={{0,64},{64,128},{128,192},{192,256},{256,320},{320,384},{384,448},... | collective-permute-start | bytes 1179656 | tf_op jit(solution)/shard_map/ppermute | solution.py:87
  97.7 11.0 %collective-permute-start.11 = (f32[32,24,128]{2,1,0:T(8,128)S(1)}, f32[32,24,128]{2,1,0:T(8,128)S(1)}, u32[]{:S(2)}, u32[]{:S(2)}) collective-permute-start(f32[32,24,128]{2,1,0:T(8,128)S(1)} %get-tuple-element.49), channel_id=1, source_target_pairs={{0,448},{64,0},{128,64},{192,128},{256,192},{320,256},{384,320},{4... | collective-permute-start | bytes 1179656 | tf_op jit(solution)/shard_map/ppermute | solution.py:87
  102.8 0.6 copy-start
  106.6 2.1 %copy-start.2 = (f32[32,24,128]{2,1,0:T(8,128)}, f32[32,24,128]{2,1,0:T(8,128)S(1)}, u32[]{:S(2)}) copy-start(f32[32,24,128]{2,1,0:T(8,128)S(1)} %collective-permute-done.10.rest_2_) | copy-start | bytes 1179652
  108.7 0.8 copy-start.3
  108.7 1.0 copy-start.1

commit v6 on v5

--- a/solution.py
+++ b/solution.py
@@ -140,27 +140,25 @@
     loop(0, BX, slab)
 
 
-def neighbours(field, c, s, kx, ky, kyp, kz, kzp, at=None):
+def neighbours(field, c, s, kx, ky, kz, at=None):
     at = s if at is None else at
     v = field[c, s]
     x = kx[at] * field[c, s - 1] + kx[at + 1] * field[c, s + 1]
-    y = ky[at] * roll(v, 1, 0) + kyp[at] * roll(v, -1, 0)
-    z = kz[at] * roll(v, 1, 1) + kzp[at] * roll(v, -1, 1)
+    y = ky[at] * roll(v, 1, 0) + roll(ky[at] * v, -1, 0)
+    z = kz[at] * roll(v, 1, 1) + roll(kz[at] * v, -1, 1)
     return x + y + z + (x, y, z)[c]
 
 
-def coefficients(stiff, pen, s, scale, kx, ky, kyp, kz, kzp, inverse, diagonal):
+def coefficients(stiff, pen, s, scale, kx, ky, kz, inverse, diagonal):
     e = stiff[s]
     upper = scale * face(e, stiff[s + 1])
     kx[s + 1] = upper
     y = scale * face(e, roll(e, 1, 0))
     ky[s] = y
     yp = roll(y, -1, 0)
-    kyp[s] = yp
     z = scale * face(e, roll(e, 1, 1))
     kz[s] = z
     zp = roll(z, -1, 1)
-    kzp[s] = zp
     pairs = (kx[s] + upper, y + yp, z + zp)
     total = pairs[0] + pairs[1] + pairs[2] + pen[s]
     for c in range(3):
@@ -188,7 +186,7 @@
 
 
 def pack_slabs(pos, main, packed, from_lower, from_upper, own, to_upper, to_lower,
-               rho, stiff, pen, u, load, kx, ky, kyp, kz, kzp, diagonal):
+               rho, stiff, pen, u, load, kx, ky, kz, diagonal):
     below = jnp.where(pos[1] > 0, 1.0, 0.0)
     above = jnp.where(pos[1] < pos[4] - 1, 1.0, 0.0)
 
@@ -210,13 +208,13 @@
 
     loop(0, BX, expand)
     kx[1] = face(stiff[0], stiff[1])
-    loop(1, BX - 1, lambda x: coefficients(stiff, pen, x, 1.0, kx, ky, kyp, kz, kzp, None, diagonal))
+    loop(1, BX - 1, lambda x: coefficients(stiff, pen, x, 1.0, kx, ky, kz, None, diagonal))
     lane = iota((ROWS, BZ), 1)
 
     def begin(x):
         halo = own[PACKED, x]
         for c in range(3):
-            f = load[c, x] - (diagonal[c, x] * u[c, x] - neighbours(u, c, x, kx, ky, kyp, kz, kzp))
+            f = load[c, x] - (diagonal[c, x] * u[c, x] - neighbours(u, c, x, kx, ky, kz))
             tile, offset, width = LOAD[c]
             own[tile, x] = f[:, :BZ]
             tail = f[:, BZ:]
@@ -233,8 +231,8 @@
 
 
 def descend(pos, own, lower, upper, coarse, low_lanes, high_lanes, *rest):
-    far, rest = rest[:11], rest[11:]
-    (v1, start, kx, ky, kyp, kz, kzp, inverse, u, weights, forward, stiff, pen, diagonal, v0, half_rows, rows, copied) = rest
+    far, rest = rest[:9], rest[9:]
+    (v1, start, kx, ky, kz, inverse, u, weights, forward, stiff, pen, diagonal, v0, half_rows, rows, copied) = rest
     moves = []
 
     def send(*pairs):
@@ -274,7 +272,7 @@
     loop(after, after + 7, lambda s: expand(upper_raw(s), s, densities(s)))
     loop(after, after + 6, lambda s: expand(upper_raw(s), s, loads(s)))
     loop(after, after + 3, lambda s: expand(upper_raw(s), s, motions(s)))
-    send((u.at[:, 4:18], 8), (weights.at[4:18], 9), (forward, 10))
+    send((u.at[:, 4:18], 6), (weights.at[4:18], 7), (forward, 8))
 
     def cube(s):
         rho = weights[s]
@@ -282,9 +280,9 @@
 
     loop(0, SLABS, cube)
     kx[1] = face(stiff[0], stiff[1])
-    loop(1, SLABS - 1, lambda s: coefficients(stiff, pen, s, 1.0, kx, ky, kyp, kz, kzp, inverse, diagonal))
-    faces = (kx, ky, kyp, kz, kzp)
-    send((kx.at[3:20], 2), (ky.at[3:19], 3), (kyp.at[3:19], 4), (kz.at[3:19], 5), (kzp.at[3:19], 6), (inverse.at[:, 3:19], 7))
+    loop(1, SLABS - 1, lambda s: coefficients(stiff, pen, s, 1.0, kx, ky, kz, inverse, diagonal))
+    faces = (kx, ky, kz)
+    send((kx.at[3:20], 2), (ky.at[3:19], 3), (kz.at[3:19], 4), (inverse.at[:, 3:19], 5))
 
     for s in (HALO - 1, HALO, HALO + BX - 1, HALO + BX):
         for c in range(3):
@@ -399,15 +397,15 @@
     loop(2, slabs - 2, sweep)
 
 
-def level_one(pos, own, chunk, kx, ky, kyp, kz, kzp, inverse, diagonal, f, v0, v1, half_rows, rows, wide):
+def level_one(pos, own, chunk, kx, ky, kz, inverse, diagonal, f, v0, v1, half_rows, rows, wide):
     stiff, pen = own.at[24:34], own.at[34:44]
     slabs = 10
     for c in range(3):
         for i in range(8):
             f[c, 1 + i] = own[8 * c + i]
     kx[1] = 2.0 * face(stiff[0], stiff[1])
-    loop(1, slabs - 1, lambda s: coefficients(stiff, pen, s, 2.0, kx, ky, kyp, kz, kzp, inverse, diagonal))
-    faces = (kx, ky, kyp, kz, kzp)
+    loop(1, slabs - 1, lambda s: coefficients(stiff, pen, s, 2.0, kx, ky, kz, inverse, diagonal))
+    faces = (kx, ky, kz)
     smooth_down(slabs, f, v0, v1, inverse, faces)
 
     def gather_rows(at, value):
@@ -442,7 +440,7 @@
             out[i, 20 * j:20 * j + 20] = column[j, 0:20]
 
 
-def level_one_again(pos, own, lower, upper, v1, f, kx, ky, kyp, kz, kzp, inverse, stiff, pen, diagonal, v0):
+def level_one_again(pos, own, lower, upper, v1, f, kx, ky, kz, inverse, stiff, pen, diagonal, v0):
     below = jnp.where(pos[0] > 0, 1.0, 0.0)
     above = jnp.where(pos[0] < pos[3] - 1, 1.0, 0.0)
     slabs = 18
@@ -459,12 +457,12 @@
         for j in range(4):
             f[c, 7 + j] = own[8 * c + 2 + j]
     kx[1] = 2.0 * face(stiff[0], stiff[1])
-    loop(1, slabs - 1, lambda s: coefficients(stiff, pen, s, 2.0, kx, ky, kyp, kz, kzp, inverse, diagonal))
-    smooth_down(slabs, f, v0, v1, inverse, (kx, ky, kyp, kz, kzp))
+    loop(1, slabs - 1, lambda s: coefficients(stiff, pen, s, 2.0, kx, ky, kz, inverse, diagonal))
+    smooth_down(slabs, f, v0, v1, inverse, (kx, ky, kz))
 
 
 def coarse_levels(pos, gathered, out, nx, ny, work):
-    (e2, p2, f2, kxm, kxp, kym, kyp, kzm, kzp, iv, dg, va, vb, tall, rows3, e3, p3, f3, jx, jym, jyp, jz, jzp, iv3, wa, wb, rows2) = work
+    (e2, p2, f2, kxm, kxp, kym, kzm, iv, dg, va, vb, tall, rows3, e3, p3, f3, jx, jym, jz, iv3, wa, wb, rows2) = work
     ys = 4 * ny
     pairs = nx
     lane = iota((ys, BZ), 1)
@@ -506,9 +504,7 @@
         kxm[s] = a
         kxp[s] = b
         kym[s] = jnp.where(row == 0, 0.0, c0)
-        kyp[s] = jnp.where(row == ys - 1, 0.0, d)
         kzm[s] = z
-        kzp[s] = zp
         sums = (a + b, c0 + d, z + zp)
         total = sums[0] + sums[1] + sums[2] + p2[s]
         for c in range(3):
@@ -523,8 +519,8 @@
         mid = v[c, s]
         below, above = x_neighbours(v[c, s - 1], mid, v[c, s + 1])
         x = kxm[s] * below + kxp[s] * above
-        y = kym[s] * roll(mid, 1, 0) + kyp[s] * roll(mid, -1, 0)
-        z = kzm[s] * roll(mid, 1, 1) + kzp[s] * roll(mid, -1, 1)
+        y = kym[s] * roll(mid, 1, 0) + roll(kym[s] * mid, -1, 0)
+        z = kzm[s] * roll(mid, 1, 1) + roll(kzm[s] * mid, -1, 1)
         return x + y + z + (x, y, z)[c]
 
     def sweep(source, target, weight):
@@ -578,9 +574,7 @@
         jx[s] = a
         jx[s + 1] = b
         jym[s] = jnp.where(row3 == 0, 0.0, c0)
-        jyp[s] = jnp.where(row3 == n3 - 1, 0.0, d)
         jz[s] = z
-        jzp[s] = zp
         sums = (a + b, c0 + d, z + zp)
         total = sums[0] + sums[1] + sums[2] + third(4 * pairs + s - 1)
         for c in range(3):
@@ -593,7 +587,7 @@
     for sweep_at in range(3):
         def step(s, source=source, target=target):
             for c in range(3):
-                near = neighbours(source, c, s, jx, jym, jyp, jz, jzp)
+                near = neighbours(source, c, s, jx, jym, jz)
                 target[c, s] = (1.0 - COARSE) * source[c, s] + COARSE * iv3[c, s] * (third(c * pairs + s - 1) + near)
 
         loop(1, pairs + 1, step)
@@ -622,28 +616,29 @@
     loop(1, pairs + 1, last)
 
 
-def ascend(pos, *rest, nx, ny):
-    far, (sums, parts), rest = rest[:14], rest[15:17], rest[17:]
-    near, rest = rest[:14], rest[14:]
-    e2out, window, rows24, va1, vb1, rows32, spread, vb, precond, term, held = rest[:11]
-    v1, f1, kx1, ky1, kyp1, kz1, kzp1, inverse1, stiff1, pen1, diagonal1, v01 = rest[11:23]
-    work, copied = rest[23:-1], rest[-1]
-    gathered, center, lower, upper = near[:4]
-    va, start, kx, ky, kyp, kz, kzp, inverse, forward, weights = near[4:]
+def ascend(pos, lower, upper, *rest, nx, ny):
+    far, (sums, parts, precond_far), rest = rest[:8], rest[9:12], rest[12:]
+    near, rest = rest[:8], rest[8:]
+    e2out, window, rows24, va1, vb1, rows32, spread, vb, precond, held = rest[:10]
+    v1, f1, kx1, ky1, kz1, inverse1, stiff1, pen1, diagonal1, v01 = rest[10:20]
+    work, copied = rest[20:-1], rest[-1]
+    gathered, center = near[:2]
+    va, start, kx, ky, kz, inverse = near[2:]
     arrivals = [pltpu.make_async_copy(source, target, copied.at[i]) for i, (source, target) in enumerate(zip(far, near))]
-    for move in arrivals:
-        move.start()
+    for i in (1, 0):
+        arrivals[i].start()
     departures = []
 
     def send(source, target):
-        move = pltpu.make_async_copy(source, target, copied.at[14 + len(departures)])
+        move = pltpu.make_async_copy(source, target, copied.at[8 + len(departures)])
         move.start()
         departures.append(move)
 
-    for move in arrivals[1:4]:
-        move.wait()
+    arrivals[1].wait()
+    for move in arrivals[2:]:
+        move.start()
     level_one_again(
-        pos, center, lower, upper, v1, f1, kx1, ky1, kyp1, kz1, kzp1, inverse1, stiff1, pen1, diagonal1, v01)
+        pos, center, lower, upper, v1, f1, kx1, ky1, kz1, inverse1, stiff1, pen1, diagonal1, v01)
     arrivals[0].wait()
     coarse_levels(pos, gathered, e2out, nx, ny, work)
     gx, gy = pos[0], pos[1]
@@ -671,7 +666,7 @@
                     rows24[pl.ds(at, 8, stride=2), :] = low
                     rows24[pl.ds(16 + at, 4, stride=2), :] = high
             va1[c, s] = v1[c, s] + jnp.where(inverse1[c, s] > 0.0, rows24[...], 0.0)
-    faces1 = (kx1, ky1, kyp1, kz1, kzp1)
+    faces1 = (kx1, ky1, kz1)
 
     def sweep1(source, target, weight, lower, upper):
         def step(s):
@@ -684,7 +679,7 @@
     sweep1(va1, vb1, SECOND, 3, 15)
     sweep1(vb1, va1, FIRST, 4, 14)
     grow0 = matrix((BZ, LANES), lambda j, l: j == (l >> 1))
-    for move in arrivals[4:]:
+    for move in arrivals[2:]:
         move.wait()
     for c in range(3):
         spread[...] = times(va1[c, 4:14].reshape(240, BZ), grow0)
@@ -698,7 +693,7 @@
                 for s in (2 * i - 1, 2 * i):
                     if 0 <= s < 18:
                         va[c, s, :, cols] = va[c, s, :, cols] + rows32[...]
-    faces = (kx, ky, kyp, kz, kzp)
+    faces = (kx, ky, kz)
 
     def sweep_one(t):
         for c in range(3):
@@ -720,6 +715,7 @@
 
     loop(0, BX, keep)
     send(held.at[0:6], parts.at[0:6])
+    send(precond, precond_far)
 
     def inner(x, carry):
         one, two = carry
@@ -736,13 +732,6 @@
     send(held.at[6:9], parts.at[6:9])
     lane = iota((8, BZ), 1)
     sums[...] = jnp.where(lane == 0, jnp.sum(one), jnp.where(lane == 1, jnp.sum(two), 0.0))
-    sensitivity(forward, precond, weights, term)
-
-    def smooth(x):
-        held[9, x] = weigh(term, x)
-
-    loop(0, BX, smooth)
-    send(held.at[9:10], parts.at[9:10])
     for move in departures:
         move.wait()
 
@@ -755,14 +744,16 @@
     def energy(i):
         s = i + 1
         total = jnp.zeros((ROWS, LANES), F32)
+        sums = [0.0, 0.0]
         for c in range(3):
             a, b = state[c, s], field[c, s]
-            along = [(a - state[c, s - 1]) * (b - field[c, s - 1]) + (a - state[c, s + 1]) * (b - field[c, s + 1])]
+            x = (a - state[c, s - 1]) * (b - field[c, s - 1]) + (a - state[c, s + 1]) * (b - field[c, s + 1])
+            total = total + (x + x if c == 0 else x)
             for axis in (0, 1):
-                along.append(
-                    (a - roll(a, 1, axis)) * (b - roll(b, 1, axis)) + (a - roll(a, -1, axis)) * (b - roll(b, -1, axis))
-                )
-            total = total + (along[0] + along[1] + along[2] + along[c])
+                part = (a - roll(a, 1, axis)) * (b - roll(b, 1, axis))
+                sums[axis] = sums[axis] + (part + part if c == axis + 1 else part)
+        for axis in (0, 1):
+            total = total + sums[axis] + roll(sums[axis], -1, axis)
         rho = weights[s]
         term[i] = rho * (-3.0 * rho * rho * (0.5 * total))
 
@@ -815,25 +806,31 @@
     loop(0, BX, smooth)
 
 
+def filter_precond(pos, *rest):
+    far, out, near, (term, copied) = rest[:6], rest[6], rest[7:13], rest[13:]
+    arrive(far, near, copied)
+    precond, state, weights = near[3:]
+    sensitivity(state, precond, weights, term)
+
+    def smooth(x):
+        out[x] = weigh(term, x)
+
+    loop(0, BX, smooth)
+
+
 def finish(pos, totals, *rest):
-    far, (solution, residual, filtered), near, copied = rest[:3], rest[3:6], rest[6:9], rest[9]
-    moves = [pltpu.make_async_copy(source, target, copied.at[i]) for i, (source, target) in enumerate(zip(far, near))]
-    for move in moves:
-        move.start()
-    iterate, parts, smooth = near
+    second, iterate, parts, smooth, solution, residual, filtered = rest
     total = jnp.sum(totals[...], axis=0, keepdims=True)
     lane = iota((1, BZ), 1)
     one = jnp.sum(jnp.where(lane == 0, total, 0.0), axis=1, keepdims=True)
     two = jnp.sum(jnp.where(lane == 1, total, 0.0), axis=1, keepdims=True)
     alpha = one / two
-    for move in moves:
-        move.wait()
 
     def update(x):
         for c in range(3):
             solution[c, x] = iterate[c, x] + alpha * parts[c, x]
             residual[c, x] = parts[3 + c, x] - alpha * parts[6 + c, x]
-        filtered[x] = smooth[0, x] + alpha * (parts[9, x] * smooth[1, x])
+        filtered[x] = smooth[0, x] + alpha * (second[x] * smooth[1, x])
 
     loop(0, BX, update)
 
@@ -862,17 +859,17 @@
     sides = (SENT, ROWS, BZ)
     own, to_upper, to_lower = launch(
         14, pack_slabs, [(12, BX, ROWS, BZ), sides, sides],
-        [slabs(BX)] * 3 + [fields(BX)] * 2 + [slabs(BX)] * 5 + [fields(BX)], [pos, main, packed, from_lower, from_upper])
+        [slabs(BX)] * 3 + [fields(BX)] * 2 + [slabs(BX)] * 3 + [fields(BX)], [pos, main, packed, from_lower, from_upper])
     from_lower, from_upper = shift_along(to_upper, "gx", 1), shift_along(to_lower, "gx", -1)
 
     one, three = slabs(SLABS), fields(SLABS)
     quarters = (22, 8, BZ)
-    coarse, low, high, v1, start, kx, ky, kyp, kz, kzp, inverse, u, weights, forward = launch(
+    coarse, low, high, v1, start, kx, ky, kz, inverse, u, weights, forward = launch(
         24, descend, [(44, 16, BZ), quarters, quarters],
-        [three, three, one, one, one, one, one, three, three, one, fields(14), one, one, three, three, (ROWS, BZ), (44 * 16, BZ)],
+        [three, three, one, one, one, three, three, one, fields(14), one, one, three, three, (ROWS, BZ), (44 * 16, BZ)],
         [pos, own, from_lower, from_upper],
-        far_outs=[fields(18), fields(16), slabs(17)] + [slabs(16)] * 4 + [fields(16), fields(14), slabs(14), fields(14)],
-        copies=11)
+        far_outs=[fields(18), fields(16), slabs(17)] + [slabs(16)] * 2 + [fields(16), fields(14), slabs(14), fields(14)],
+        copies=9)
     smooth = launch(
         10, filter_iterate, [(2,) + cells], [fields(14), fields(14), slabs(14), slabs(12), slabs(12)], [pos],
         far=[u, forward, weights], copies=3,
@@ -884,7 +881,7 @@
     wide1 = (16, BZ)
     one1, three1 = (10,) + wide1, (3, 10) + wide1
     chunk = launch(
-        4, level_one, [(ny, 24, BZ)], [one1] * 5 + [three1] * 5 + [(8, BZ), (40, BZ), (40, BZ)], [pos, coarse])[0]
+        4, level_one, [(ny, 24, BZ)], [one1] * 3 + [three1] * 5 + [(8, BZ), (40, BZ), (40, BZ)], [pos, coarse])[0]
     side = (32, 24, BZ)
     column = lax.all_to_all(chunk, "gy", 0, 0, tiled=True)
     to_upper, to_lower, center = launch(
@@ -899,22 +896,24 @@
     wide2, wide3 = (4 * ny, BZ), (2 * ny, BZ)
     one2, three2 = (nx + 2,) + wide2, (3, nx + 2) + wide2
     one3, three3 = (nx + 2,) + wide3, (3, nx + 2) + wide3
-    work = [one2, one2, three2] + [one2] * 6 + [three2] * 4 + [wide2, (5 * nx * 2 * ny, BZ)]
-    work += [one3, one3, three3] + [one3] * 5 + [three3] * 3 + [(nx * 2 * ny, BZ)]
-    parts = (10,) + cells
-    far = [gathered, center, from_lower, from_upper, v1, start, kx, ky, kyp, kz, kzp, inverse, forward, weights]
+    work = [one2, one2, three2] + [one2] * 4 + [three2] * 4 + [wide2, (5 * nx * 2 * ny, BZ)]
+    work += [one3, one3, three3] + [one3] * 3 + [three3] * 3 + [(nx * 2 * ny, BZ)]
+    parts = (9,) + cells
+    far = [gathered, center, v1, start, kx, ky, kz, inverse]
     scratch = [x.shape for x in far] + [
-        (3, nx + 4) + wide2, (15 * 4 * ny, LANES), wide1, three1, three1, (ROWS, BZ), (240, LANES), fields(16), fields(14), slabs(12), parts
-    ] + [three1] * 2 + [one1] * 5 + [three1, one1, one1, three1, three1] + work
-    sums, parts = launch(
-        30, functools.partial(ascend, nx=nx, ny=ny), [(8, BZ)], scratch, [pos], far_outs=[parts], far=far + [smooth], copies=17)
-
+        (3, nx + 4) + wide2, (15 * 4 * ny, LANES), wide1, three1, three1, (ROWS, BZ), (240, LANES), fields(16), fields(14), parts
+    ] + [three1] * 2 + [one1] * 3 + [three1, one1, one1, three1, three1] + work
+    sums, parts, precond = launch(
+        30, functools.partial(ascend, nx=nx, ny=ny), [(8, BZ)], scratch, [pos, from_lower, from_upper],
+        far_outs=[parts, fields(14)], far=far + [smooth], copies=11)
+    ready = launch(
+        12, filter_precond, [cells, field, parts.shape, smooth.shape], [fields(14), fields(14), slabs(14), slabs(12)], [pos],
+        far=[iterate, parts, smooth, precond, forward, weights], copies=6, pin=True,
+        cost=pl.CostEstimate(flops=8_000_000, bytes_accessed=4_000_000, transcendentals=0))
     total = lax.all_to_all(jnp.broadcast_to(sums[:1], (nx * ny, BZ)), ("gx", "gy"), 0, 0, tiled=True)
     total = jnp.sum(total, axis=0, keepdims=True)
     total = lax.all_to_all(jnp.broadcast_to(total, (nz, BZ)), "gz", 0, 0, tiled=True)
-    return tuple(launch(
-        4, finish, [field, field, cells], [field, parts.shape, smooth.shape], [pos, total],
-        far=[iterate, parts, smooth], copies=3))
+    return tuple(launch(4, finish, [field, field, cells], [], [pos, total, *ready]))
 
 
 def solution(mesh):

time: 159 us -> 156 us (0.981)
  blocking collectives: 28.3 us -> 15.9 us
  starting transfers between devices: 50.1 us -> 56.2 us
  waiting for transfers between devices: 30 us -> 31.8 us
    all_to_all x1 -> x0, blocking collectives: 12.4 us -> none  [body(): lax.all_to_all(jnp.broadcast_to(total, (nz, BZ)), 'gz', 0, 0, tiled=True)]
    all_to_all x0 -> x1, starting transfers between devices: none -> 6.05 us  [body(): lax.all_to_all(jnp.broadcast_to(total, (nz, BZ)), 'gz', 0, 0, tiled=True)]
    all_to_all x0 -> x1, waiting for transfers between devices: none -> 1.61 us  [body(): lax.all_to_all(jnp.broadcast_to(total, (nz, BZ)), 'gz', 0, 0, tiled=True)]
    pallas_call x11 -> x12, Pallas kernels: 47.5 us -> 48.3 us  [launch(): pl.pallas_call(kernel, out_shape=[pltpu.VMEM(shape, F32) if pin else jax....]
  transfers between devices with their start and end apart: 14 -> 15, of which waited for: 10 -> 11; matrix products, arithmetic and copies ran while one was open for 0% -> 0% of each run, Pallas kernels for 5% -> 8%
where the time goes in v6:
time: 156 us; the launch traced here: 155 us
  starting transfers between devices  56.2 us (36%)
  Pallas kernels  48.3 us (31%)
  waiting for transfers between devices  31.8 us (20%)
  blocking collectives  15.9 us (10%)
  local copies, waits for them, and re-layouts  2.18 us (1%)
    pallas_call x12, Pallas kernels, launch(): pl.pallas_call(kernel, out_shape=[pltpu.VMEM(shape, F32) if pin else jax....  48.3 us
    ppermute x12, starting transfers between devices, shift_along(): lax.ppermute(x, axis, [(i, (i + step) % devices) for i in range(devices)])  39.4 us
    ppermute x12, waiting for transfers between devices, shift_along(): lax.ppermute(x, axis, [(i, (i + step) % devices) for i in range(devices)])  29 us
    all_to_all x1, blocking collectives, body(): lax.all_to_all(jnp.broadcast_to(sums[:1], (nx * ny, BZ)), ('gx', 'gy'), 0...  15.9 us
    all_to_all x1, starting transfers between devices, body(): lax.all_to_all(jnp.broadcast_to(total, (nz, BZ)), 'gz', 0, 0, tiled=True)  6.05 us
    all_to_all x1, starting transfers between devices, body(): gathered = lax.all_to_all(column, 'gx', 0, 0, tiled=True)  5.8 us
    all_to_all x1, starting transfers between devices, body(): column = lax.all_to_all(chunk, 'gy', 0, 0, tiled=True)  4.93 us
  transfers between devices with their start and end apart: 15, of which 11 were waited for; matrix products, arithmetic and copies ran while one was open for 0% of the time, Pallas kernels for 8%

profile of v6, /device:TPU:1, one launch (start us, length us, event | category | flops | bytes accessed | tf_op | source)
XLA Modules:
  0.0 155.2 jit_solution(354983147424233838)
XLA Ops:
  0.6 0.1 pad_add_fusion.pos
  0.7 2.3 %shard_map.94 = (f32[11,8,16,128]{3,2,1,0:T(8,128)S(1)}, f32[8,16,128]{2,1,0:T(8,128)S(1)}, f32[8,16,128]{2,1,0:T(8,128)S(1)}) custom-call(s32[6]{0:T(128)S(1)} %pad_add_fusion.pos, f32[3,8,16,128]{3,2,1,0:T(8,128)} %right_far.1, f32[3,8,16,128]{3,2,1,0:T(8,128)} %rest_0_.1, f32[3,8,16,128]{3,2,1,0:T(8,128)} %state_far.1, s32[8,16,128]{2,1,0:T(8,128)} %classes_far.1, ...), custom_call_target="tpu_custom_call" | custom-call | tf_op jit(solution)/shard_map/pallas_call | solution.py:74
  3.1 4.0 %collective-permute-start = (f32[8,16,128]{2,1,0:T(8,128)S(1)}, f32[8,16,128]{2,1,0:T(8,128)S(1)}, u32[]{:S(2)}, u32[]{:S(2)}) collective-permute-start(f32[8,16,128]{2,1,0:T(8,128)S(1)} %get-tuple-element.37), channel_id=1, source_target_pairs={{0,1},{1,2},{2,3},{3,4},{4,5},{5,6},{6,7},{7,0},{8,9},{9,10},{10,1... | collective-permute-start | bytes 196616 | tf_op jit(solution)/shard_map/ppermute | solution.py:87
  7.1 3.8 %collective-permute-start.1 = (f32[8,16,128]{2,1,0:T(8,128)S(1)}, f32[8,16,128]{2,1,0:T(8,128)S(1)}, u32[]{:S(2)}, u32[]{:S(2)}) collective-permute-start(f32[8,16,128]{2,1,0:T(8,128)S(1)} %get-tuple-element.38), channel_id=1, source_target_pairs={{0,7},{1,0},{2,1},{3,2},{4,3},{5,4},{6,5},{7,6},{8,15},{9,8},{10,9... | collective-permute-start | bytes 196616 | tf_op jit(solution)/shard_map/ppermute | solution.py:87
  10.9 0.0 collective-permute-done.from_lower
  10.9 1.3 collective-permute-done.1.from_upper
  12.2 0.6 shard_map.95
  12.9 4.0 %collective-permute-start.2 = (f32[12,8,8,128]{3,2,1,0:T(8,128)S(1)}, f32[12,8,8,128]{3,2,1,0:T(8,128)S(1)}, u32[]{:S(2)}, u32[]{:S(2)}) collective-permute-start(f32[12,8,8,128]{3,2,1,0:T(8,128)S(1)} %get-tuple-element.40), channel_id=1, source_target_pairs={{0,8},{8,16},{16,24},{24,32},{32,40},{40,48},{48,56},{56,0},{1,9},... | collective-permute-start | bytes 1179656 | tf_op jit(solution)/shard_map/ppermute | solution.py:87
  16.9 8.6 %collective-permute-start.3 = (f32[12,8,8,128]{3,2,1,0:T(8,128)S(1)}, f32[12,8,8,128]{3,2,1,0:T(8,128)S(1)}, u32[]{:S(2)}, u32[]{:S(2)}) collective-permute-start(f32[12,8,8,128]{3,2,1,0:T(8,128)S(1)} %get-tuple-element.41), channel_id=1, source_target_pairs={{0,56},{8,0},{16,8},{24,16},{32,24},{40,32},{48,40},{56,48},{1,57}... | collective-permute-start | bytes 1179656 | tf_op jit(solution)/shard_map/ppermute | solution.py:87
  25.5 5.5 %collective-permute-done.2.from_lower = f32[12,8,8,128]{3,2,1,0:T(8,128)S(1)} collective-permute-done((f32[12,8,8,128]{3,2,1,0:T(8,128)S(1)}, f32[12,8,8,128]{3,2,1,0:T(8,128)S(1)}, u32[]{:S(2)}, u32[]{:S(2)}) %collective-permute-start.2) | collective-permute-done | bytes 393248 | tf_op jit(solution)/shard_map/ppermute | solution.py:87
  31.0 0.9 collective-permute-done.3.from_upper
  31.9 3.3 %shard_map.96 = (f32[12,8,32,128]{3,2,1,0:T(8,128)S(1)}, f32[56,32,128]{2,1,0:T(8,128)S(1)}, f32[56,32,128]{2,1,0:T(8,128)S(1)}) custom-call(s32[6]{0:T(128)S(1)} %pad_add_fusion.pos, f32[11,8,16,128]{3,2,1,0:T(8,128)S(1)} %get-tuple-element.36.main, f32[8,16,128]{2,1,0:T(8,128)S(1)} %get-tuple-element.39.packed, ...), custom_call_target="tpu_custom_call" | custom-call | tf_op jit(solution)/shard_map/pallas_call | solution.py:74
  35.2 4.0 %collective-permute-start.4 = (f32[56,32,128]{2,1,0:T(8,128)S(1)}, f32[56,32,128]{2,1,0:T(8,128)S(1)}, u32[]{:S(2)}, u32[]{:S(2)}) collective-permute-start(f32[56,32,128]{2,1,0:T(8,128)S(1)} %get-tuple-element.43), channel_id=1, source_target_pairs={{0,64},{64,128},{128,192},{192,256},{256,320},{320,384},{384,448},... | collective-permute-start | bytes 2752520 | tf_op jit(solution)/shard_map/ppermute | solution.py:87
  39.2 0.0 collective-permute-start.5
  39.2 10.3 %collective-permute-done.4.lower = f32[56,32,128]{2,1,0:T(8,128)S(1)} collective-permute-done((f32[56,32,128]{2,1,0:T(8,128)S(1)}, f32[56,32,128]{2,1,0:T(8,128)S(1)}, u32[]{:S(2)}, u32[]{:S(2)}) %collective-permute-start.4) | collective-permute-done | bytes 917536 | tf_op jit(solution)/shard_map/ppermute | solution.py:87
  49.6 2.5 %collective-permute-done.5.upper = f32[56,32,128]{2,1,0:T(8,128)S(1)} collective-permute-done((f32[56,32,128]{2,1,0:T(8,128)S(1)}, f32[56,32,128]{2,1,0:T(8,128)S(1)}, u32[]{:S(2)}, u32[]{:S(2)}) %collective-permute-start.5) | collective-permute-done | bytes 917536 | tf_op jit(solution)/shard_map/ppermute | solution.py:87
  52.1 9.5 %shard_map.97 = (f32[44,16,128]{2,1,0:T(8,128)S(1)}, f32[22,8,128]{2,1,0:T(8,128)S(1)}, f32[22,8,128]{2,1,0:T(8,128)S(1)}, f32[3,18,32,256]{3,2,1,0:T(8,128)}, f...) custom-call(s32[6]{0:T(128)S(1)} %pad_add_fusion.pos, ...), custom_call_target="tpu_custom_call" | custom-call | tf_op jit(solution)/shard_map/pallas_call | solution.py:74
  61.5 3.1 %collective-permute-start.6 = (f32[22,8,128]{2,1,0:T(8,128)S(1)}, f32[22,8,128]{2,1,0:T(8,128)S(1)}, u32[]{:S(2)}, u32[]{:S(2)}) collective-permute-start(f32[22,8,128]{2,1,0:T(8,128)S(1)} %get-tuple-element.46), channel_id=1, source_target_pairs={{0,1},{1,2},{2,3},{3,4},{4,5},{5,6},{6,7},{7,0},{8,9},{9,10},{10,1... | collective-permute-start | bytes 270344 | tf_op jit(solution)/shard_map/ppermute | solution.py:87
  64.6 3.7 %collective-permute-start.7 = (f32[22,8,128]{2,1,0:T(8,128)S(1)}, f32[22,8,128]{2,1,0:T(8,128)S(1)}, u32[]{:S(2)}, u32[]{:S(2)}) collective-permute-start(f32[22,8,128]{2,1,0:T(8,128)S(1)} %get-tuple-element.47), channel_id=1, source_target_pairs={{0,7},{1,0},{2,1},{3,2},{4,3},{5,4},{6,5},{7,6},{8,15},{9,8},{10,9... | collective-permute-start | bytes 270344 | tf_op jit(solution)/shard_map/ppermute | solution.py:87
  68.4 0.9 collective-permute-done.6.from_lower
  69.3 2.2 %collective-permute-done.7.from_upper = f32[22,8,128]{2,1,0:T(8,128)S(1)} collective-permute-done((f32[22,8,128]{2,1,0:T(8,128)S(1)}, f32[22,8,128]{2,1,0:T(8,128)S(1)}, u32[]{:S(2)}, u32[]{:S(2)}) %collective-permute-start.7) | collective-permute-done | bytes 90144 | tf_op jit(solution)/shard_map/ppermute | solution.py:87
  71.5 1.0 shard_map.98
  72.5 2.2 %shard_map.100 = f32[8,24,128]{2,1,0:T(8,128)} custom-call(s32[6]{0:T(128)S(1)} %pad_add_fusion.pos, f32[44,16,128]{2,1,0:T(8,128)S(1)} %get-tuple-element.51.own), custom_call_target="tpu_custom_call" | custom-call | tf_op jit(solution)/shard_map/pallas_call | solution.py:74
  74.7 4.9 %all-to-all-start = ((f32[8,24,128]{2,1,0:T(8,128)}), f32[8,24,128]{2,1,0:T(8,128)S(1)}, u32[]{:S(2)}, u32[]{:S(2)}) async-start(f32[8,24,128]{2,1,0:T(8,128)} %shard_map.100), calls=%async_computation | async-start | bytes 196608 | tf_op jit(solution)/shard_map/all_to_all | solution.py:886
  79.6 4.6 %collective-permute-start.9 = (f32[44,8,128]{2,1,0:T(8,128)S(1)}, f32[44,8,128]{2,1,0:T(8,128)S(1)}, u32[]{:S(2)}, u32[]{:S(2)}) collective-permute-start(f32[44,8,128]{2,1,0:T(8,128)S(1)} %get-tuple-element.48.coarse), channel_id=1, source_target_pairs={{0,56},{8,0},{16,8},{24,16},{32,24},{40,32},{48,40},{56,48},{1,57}... | collective-permute-start | bytes 540680 | tf_op jit(solution)/shard_map/ppermute | solution.py:87
  84.2 1.9 %collective-permute-start.8 = (f32[44,8,128]{2,1,0:T(8,128)S(1)}, f32[44,8,128]{2,1,0:T(8,128)S(1)}, u32[]{:S(2)}, u32[]{:S(2)}) collective-permute-start(f32[44,8,128]{2,1,0:T(8,128)S(1)} %get-tuple-element.48.coarse), channel_id=1, source_target_pairs={{0,8},{8,16},{16,24},{24,32},{32,40},{40,48},{48,56},{56,0},{1,9},... | collective-permute-start | bytes 540680 | tf_op jit(solution)/shard_map/ppermute | solution.py:87
  86.1 1.1 all-to-all-done.column
  87.2 1.5 shard_map.101
  88.7 5.8 %all-to-all-start.1 = ((f32[8,160,128]{2,1,0:T(8,128)}), f32[8,160,128]{2,1,0:T(8,128)S(1)}, u32[]{:S(2)}, u32[]{:S(2)}) async-start(f32[8,160,128]{2,1,0:T(8,128)} %shard_map.101), calls=%async_computation.1 | async-start | bytes 1310720 | tf_op jit(solution)/shard_map/all_to_all | solution.py:891
  94.5 0.0 collective-permute-done.9.from_upper
  94.5 0.0 collective-permute-done.8.from_lower
  94.5 1.4 shard_map.99
  96.0 1.6 %collective-permute-start.10 = (f32[32,24,128]{2,1,0:T(8,128)S(1)}, f32[32,24,128]{2,1,0:T(8,128)S(1)}, u32[]{:S(2)}, u32[]{:S(2)}) collective-permute-start(f32[32,24,128]{2,1,0:T(8,128)S(1)} %get-tuple-element.49), channel_id=1, source_target_pairs={{0,64},{64,128},{128,192},{192,256},{256,320},{320,384},{384,448},... | collective-permute-start | bytes 1179656 | tf_op jit(solution)/shard_map/ppermute | solution.py:87
  97.6 0.0 collective-permute-start.11
  97.6 5.0 %shard_map.102.rest_8_.rest_2_ = f32[2,8,16,128]{3,2,1,0:T(8,128)S(1)} custom-call(s32[6]{0:T(128)S(1)} %pad_add_fusion.pos, f32[3,14,32,256]{3,2,1,0:T(8,128)} %get-tuple-element.59.rest_0_, f32[3,14,32,256]{3,2,1,0:T(8,128)} %get-tuple-element.60.rest_1_.rest_4_, f32[14,32,256]{2,1,0:T(8,128)} %get-tuple-element.61.rest_2_.rest_5_), custom_call_target="tpu_custom_call" | custom-call | flops 12000000 | bytes 4000000 | tf_op jit(solution)/shard_map/pallas_call | solution.py:74
  102.6 0.0 copy-start
  102.6 0.6 copy-done
  103.2 3.3 %collective-permute-done.10.lower = f32[32,24,128]{2,1,0:T(8,128)S(1)} collective-permute-done((f32[32,24,128]{2,1,0:T(8,128)S(1)}, f32[32,24,128]{2,1,0:T(8,128)S(1)}, u32[]{:S(2)}, u32[]{:S(2)}) %collective-permute-start.10) | collective-permute-done | bytes 393248 | tf_op jit(solution)/shard_map/ppermute | solution.py:87
  106.5 2.1 %collective-permute-done.11.upper = f32[32,24,128]{2,1,0:T(8,128)S(1)} collective-permute-done((f32[32,24,128]{2,1,0:T(8,128)S(1)}, f32[32,24,128]{2,1,0:T(8,128)S(1)}, u32[]{:S(2)}, u32[]{:S(2)}) %collective-permute-start.11) | collective-permute-done | bytes 393248 | tf_op jit(solution)/shard_map/ppermute | solution.py:87
  108.6 0.0 all-to-all-done.1.rest_0_
  108.6 0.0 copy-start.1
  108.6 0.9 copy-done.1
  109.5 15.2 %shard_map.103 = (f32[8,128]{1,0:T(8,128)S(1)}, f32[9,8,16,128]{3,2,1,0:T(8,128)}, f32[3,14,32,256]{3,2,1,0:T(8,128)}) custom-call(s32[6]{0:T(128)S(1)} %pad_add_fusion.pos, f32[32,24,128]{2,1,0:T(8,128)S(1)} %collective-permute-done.10.lower, f32[32,24,128]{2,1,0:T(8,128)S(1)} %collective-permute-done.11.upper, f32[8,160,128]{2,1,0:T(8,128)} %copy-done.1, ...), custom_call_target="tpu_custom_call" | custom-call | tf_op jit(solution)/shard_map/pallas_call | solution.py:74
  124.8 15.9 %all_to_all.24 = f32[64,1,128]{2,1,0:T(1,128)S(1)} all-to-all(f32[64,1,128]{2,1,0:T(1,128)S(1)} %broadcast_in_dim.4), channel_id=1, replica_groups=mesh['gx'=8,'gy'=8,'gz'=8] {'gx','gy'}, dimensions={0} | all-to-all | bytes 65536 | tf_op jit(solution)/shard_map/all_to_all | solution.py:913
  140.6 0.6 broadcast_in_dim.5
  141.2 6.0 %all-to-all-start.3 = ((f32[8,1,128]{2,1,0:T(1,128)}), f32[8,1,128]{2,1,0:T(1,128)S(1)}, u32[]{:S(2)}, u32[]{:S(2)}) async-start(f32[8,1,128]{2,1,0:T(1,128)} %broadcast_in_dim.5), calls=%async_computation.3 | async-start | bytes 8192 | tf_op jit(solution)/shard_map/all_to_all | solution.py:915
  147.3 4.8 %shard_map.104 = (f32[8,16,128]{2,1,0:T(8,128)S(1)}, f32[3,8,16,128]{3,2,1,0:T(8,128)S(1)}, f32[9,8,16,128]{3,2,1,0:T(8,128)S(1)}, f32[2,8,16,128]{3,2,1,0:T(8,128)S(1)}) custom-call(s32[6]{0:T(128)S(1)} %pad_add_fusion.pos, f32[3,8,16,128]{3,2,1,0:T(8,128)} %rest_0_.1, f32[9,8,16,128]{3,2,1,0:T(8,128)} %get-tuple-element.63.rest_1_, ...), custom_call_target="tpu_custom_call" | custom-call | flops 8000000 | bytes 4000000 | tf_op jit(solution)/shard_map/pallas_call | solution.py:74
  152.1 1.6 %all-to-all-done.3 = f32[8,1,128]{2,1,0:T(1,128)S(1)} async-done(((f32[8,1,128]{2,1,0:T(1,128)}), f32[8,1,128]{2,1,0:T(1,128)S(1)}, u32[]{:S(2)}, u32[]{:S(2)}) %all-to-all-start.3) | async-done | bytes 4128 | tf_op jit(solution)/shard_map/all_to_all | solution.py:915
  153.7 1.4 shard_map.105
  (4 shorter events, 0.0 us)
Async XLA Ops:
  3.1 7.9 %collective-permute-start = (f32[8,16,128]{2,1,0:T(8,128)S(1)}, f32[8,16,128]{2,1,0:T(8,128)S(1)}, u32[]{:S(2)}, u32[]{:S(2)}) collective-permute-start(f32[8,16,128]{2,1,0:T(8,128)S(1)} %get-tuple-element.37), channel_id=1, source_target_pairs={{0,1},{1,2},{2,3},{3,4},{4,5},{5,6},{6,7},{7,0},{8,9},{9,10},{10,1... | collective-permute-start | bytes 196616 | tf_op jit(solution)/shard_map/ppermute | solution.py:87
  7.1 5.1 %collective-permute-start.1 = (f32[8,16,128]{2,1,0:T(8,128)S(1)}, f32[8,16,128]{2,1,0:T(8,128)S(1)}, u32[]{:S(2)}, u32[]{:S(2)}) collective-permute-start(f32[8,16,128]{2,1,0:T(8,128)S(1)} %get-tuple-element.38), channel_id=1, source_target_pairs={{0,7},{1,0},{2,1},{3,2},{4,3},{5,4},{6,5},{7,6},{8,15},{9,8},{10,9... | collective-permute-start | bytes 196616 | tf_op jit(solution)/shard_map/ppermute | solution.py:87
  12.9 18.1 %collective-permute-start.2 = (f32[12,8,8,128]{3,2,1,0:T(8,128)S(1)}, f32[12,8,8,128]{3,2,1,0:T(8,128)S(1)}, u32[]{:S(2)}, u32[]{:S(2)}) collective-permute-start(f32[12,8,8,128]{3,2,1,0:T(8,128)S(1)} %get-tuple-element.40), channel_id=1, source_target_pairs={{0,8},{8,16},{16,24},{24,32},{32,40},{40,48},{48,56},{56,0},{1,9},... | collective-permute-start | bytes 1179656 | tf_op jit(solution)/shard_map/ppermute | solution.py:87
  16.9 15.0 %collective-permute-start.3 = (f32[12,8,8,128]{3,2,1,0:T(8,128)S(1)}, f32[12,8,8,128]{3,2,1,0:T(8,128)S(1)}, u32[]{:S(2)}, u32[]{:S(2)}) collective-permute-start(f32[12,8,8,128]{3,2,1,0:T(8,128)S(1)} %get-tuple-element.41), channel_id=1, source_target_pairs={{0,56},{8,0},{16,8},{24,16},{32,24},{40,32},{48,40},{56,48},{1,57}... | collective-permute-start | bytes 1179656 | tf_op jit(solution)/shard_map/ppermute | solution.py:87
  35.2 14.4 %collective-permute-start.4 = (f32[56,32,128]{2,1,0:T(8,128)S(1)}, f32[56,32,128]{2,1,0:T(8,128)S(1)}, u32[]{:S(2)}, u32[]{:S(2)}) collective-permute-start(f32[56,32,128]{2,1,0:T(8,128)S(1)} %get-tuple-element.43), channel_id=1, source_target_pairs={{0,64},{64,128},{128,192},{192,256},{256,320},{320,384},{384,448},... | collective-permute-start | bytes 2752520 | tf_op jit(solution)/shard_map/ppermute | solution.py:87
  39.2 12.8 %collective-permute-start.5 = (f32[56,32,128]{2,1,0:T(8,128)S(1)}, f32[56,32,128]{2,1,0:T(8,128)S(1)}, u32[]{:S(2)}, u32[]{:S(2)}) collective-permute-start(f32[56,32,128]{2,1,0:T(8,128)S(1)} %get-tuple-element.44), channel_id=1, source_target_pairs={{0,448},{64,0},{128,64},{192,128},{256,192},{320,256},{384,320},{4... | collective-permute-start | bytes 2752520 | tf_op jit(solution)/shard_map/ppermute | solution.py:87
  61.5 7.8 %collective-permute-start.6 = (f32[22,8,128]{2,1,0:T(8,128)S(1)}, f32[22,8,128]{2,1,0:T(8,128)S(1)}, u32[]{:S(2)}, u32[]{:S(2)}) collective-permute-start(f32[22,8,128]{2,1,0:T(8,128)S(1)} %get-tuple-element.46), channel_id=1, source_target_pairs={{0,1},{1,2},{2,3},{3,4},{4,5},{5,6},{6,7},{7,0},{8,9},{9,10},{10,1... | collective-permute-start | bytes 270344 | tf_op jit(solution)/shard_map/ppermute | solution.py:87
  64.6 6.9 %collective-permute-start.7 = (f32[22,8,128]{2,1,0:T(8,128)S(1)}, f32[22,8,128]{2,1,0:T(8,128)S(1)}, u32[]{:S(2)}, u32[]{:S(2)}) collective-permute-start(f32[22,8,128]{2,1,0:T(8,128)S(1)} %get-tuple-element.47), channel_id=1, source_target_pairs={{0,7},{1,0},{2,1},{3,2},{4,3},{5,4},{6,5},{7,6},{8,15},{9,8},{10,9... | collective-permute-start | bytes 270344 | tf_op jit(solution)/shard_map/ppermute | solution.py:87
  74.7 12.5 %all-to-all-start = ((f32[8,24,128]{2,1,0:T(8,128)}), f32[8,24,128]{2,1,0:T(8,128)S(1)}, u32[]{:S(2)}, u32[]{:S(2)}) async-start(f32[8,24,128]{2,1,0:T(8,128)} %shard_map.100), calls=%async_computation | async-start | bytes 196608 | tf_op jit(solution)/shard_map/all_to_all | solution.py:886
  79.6 14.9 %collective-permute-start.9 = (f32[44,8,128]{2,1,0:T(8,128)S(1)}, f32[44,8,128]{2,1,0:T(8,128)S(1)}, u32[]{:S(2)}, u32[]{:S(2)}) collective-permute-start(f32[44,8,128]{2,1,0:T(8,128)S(1)} %get-tuple-element.48.coarse), channel_id=1, source_target_pairs={{0,56},{8,0},{16,8},{24,16},{32,24},{40,32},{48,40},{56,48},{1,57}... | collective-permute-start | bytes 540680 | tf_op jit(solution)/shard_map/ppermute | solution.py:87
  84.2 10.3 %collective-permute-start.8 = (f32[44,8,128]{2,1,0:T(8,128)S(1)}, f32[44,8,128]{2,1,0:T(8,128)S(1)}, u32[]{:S(2)}, u32[]{:S(2)}) collective-permute-start(f32[44,8,128]{2,1,0:T(8,128)S(1)} %get-tuple-element.48.coarse), channel_id=1, source_target_pairs={{0,8},{8,16},{16,24},{24,32},{32,40},{40,48},{48,56},{56,0},{1,9},... | collective-permute-start | bytes 540680 | tf_op jit(solution)/shard_map/ppermute | solution.py:87
  88.7 19.9 %all-to-all-start.1 = ((f32[8,160,128]{2,1,0:T(8,128)}), f32[8,160,128]{2,1,0:T(8,128)S(1)}, u32[]{:S(2)}, u32[]{:S(2)}) async-start(f32[8,160,128]{2,1,0:T(8,128)} %shard_map.101), calls=%async_computation.1 | async-start | bytes 1310720 | tf_op jit(solution)/shard_map/all_to_all | solution.py:891
  96.0 10.5 %collective-permute-start.10 = (f32[32,24,128]{2,1,0:T(8,128)S(1)}, f32[32,24,128]{2,1,0:T(8,128)S(1)}, u32[]{:S(2)}, u32[]{:S(2)}) collective-permute-start(f32[32,24,128]{2,1,0:T(8,128)S(1)} %get-tuple-element.49), channel_id=1, source_target_pairs={{0,64},{64,128},{128,192},{192,256},{256,320},{320,384},{384,448},... | collective-permute-start | bytes 1179656 | tf_op jit(solution)/shard_map/ppermute | solution.py:87
  97.6 11.0 %collective-permute-start.11 = (f32[32,24,128]{2,1,0:T(8,128)S(1)}, f32[32,24,128]{2,1,0:T(8,128)S(1)}, u32[]{:S(2)}, u32[]{:S(2)}) collective-permute-start(f32[32,24,128]{2,1,0:T(8,128)S(1)} %get-tuple-element.50), channel_id=1, source_target_pairs={{0,448},{64,0},{128,64},{192,128},{256,192},{320,256},{384,320},{4... | collective-permute-start | bytes 1179656 | tf_op jit(solution)/shard_map/ppermute | solution.py:87
  102.6 0.7 copy-start
  108.6 0.9 copy-start.1
  141.2 12.5 %all-to-all-start.3 = ((f32[8,1,128]{2,1,0:T(1,128)}), f32[8,1,128]{2,1,0:T(1,128)S(1)}, u32[]{:S(2)}, u32[]{:S(2)}) async-start(f32[8,1,128]{2,1,0:T(1,128)} %broadcast_in_dim.5), calls=%async_computation.3 | async-start | bytes 8192 | tf_op jit(solution)/shard_map/all_to_all | solution.py:915

commit v7 on v6

--- a/solution.py
+++ b/solution.py
@@ -127,15 +127,24 @@
     below = jnp.where(pos[2] > 0, 1.0, 0.0)
     above = jnp.where(pos[2] < pos[5] - 1, 1.0, 0.0)
     lane = iota((BY, BZ), 1)
+    row = iota((BY // 2, BZ), 0)
     half = BY // 2
 
     def slab(x):
         joined = jnp.where(lane < HALF, from_lower[x] * below, from_upper[x] * above)
         packed[x] = joined
-        for tile in range(12):
-            value = joined if tile == PACKED else main[tile if tile < PACKED else tile - 1, x]
-            to_upper[tile, x] = value[half:]
-            to_lower[tile, x] = value[:half]
+        values = [joined if tile == PACKED else main[tile if tile < PACKED else tile - 1, x] for tile in range(12)]
+        uppers = [value[half:] for value in values]
+        lowers = [value[:half] for value in values]
+        for c in range(3):
+            up, down = uppers[9 + c], lowers[9 + c]
+            uppers[LOAD[c][0]] = jnp.where(row < 2, roll(up, 3, 0), uppers[LOAD[c][0]])
+            uppers[ITERATE[c][0]] = jnp.where(row < 1, roll(up, 1, 0), uppers[ITERATE[c][0]])
+            lowers[LOAD[c][0]] = jnp.where(row >= 6, roll(down, 6, 0), lowers[LOAD[c][0]])
+            lowers[ITERATE[c][0]] = jnp.where(row >= 7, roll(down, 5, 0), lowers[ITERATE[c][0]])
+        for tile in range(9):
+            to_upper[tile, x] = uppers[tile]
+            to_lower[tile, x] = lowers[tile]
 
     loop(0, BX, slab)
 
@@ -189,11 +198,18 @@
                rho, stiff, pen, u, load, kx, ky, kz, diagonal):
     below = jnp.where(pos[1] > 0, 1.0, 0.0)
     above = jnp.where(pos[1] < pos[4] - 1, 1.0, 0.0)
+    row = iota((BY // 2, BZ), 0)
 
     def slab(x):
         for tile in range(12):
             value = packed[x] if tile == PACKED else main[tile if tile < PACKED else tile - 1, x]
-            own[tile, x] = jnp.concatenate([value, from_upper[tile, x] * above, from_lower[tile, x] * below], 0)
+            if tile <= PACKED:
+                high, low = from_upper[tile, x], from_lower[tile, x]
+            else:
+                load_at, iterate_at = LOAD[tile - 9][0], ITERATE[tile - 9][0]
+                high = jnp.where(row < 2, roll(from_upper[load_at, x], 2, 0), roll(from_upper[iterate_at, x], 3, 0))
+                low = jnp.where(row < 7, roll(from_lower[load_at, x], 5, 0), roll(from_lower[iterate_at, x], 7, 0))
+            own[tile, x] = jnp.concatenate([value, high * above, low * below], 0)
 
     loop(0, BX, slab)
 
@@ -616,31 +632,28 @@
     loop(1, pairs + 1, last)
 
 
-def ascend(pos, lower, upper, *rest, nx, ny):
-    far, (sums, parts, precond_far), rest = rest[:8], rest[9:12], rest[12:]
-    near, rest = rest[:8], rest[8:]
+def ascend(pos, lower, upper, gathered, *rest, nx, ny):
+    far, (sums, parts, precond_far), rest = rest[:7], rest[8:11], rest[11:]
+    near, rest = rest[:7], rest[7:]
     e2out, window, rows24, va1, vb1, rows32, spread, vb, precond, held = rest[:10]
     v1, f1, kx1, ky1, kz1, inverse1, stiff1, pen1, diagonal1, v01 = rest[10:20]
     work, copied = rest[20:-1], rest[-1]
-    gathered, center = near[:2]
-    va, start, kx, ky, kz, inverse = near[2:]
+    center = near[0]
+    va, start, kx, ky, kz, inverse = near[1:]
     arrivals = [pltpu.make_async_copy(source, target, copied.at[i]) for i, (source, target) in enumerate(zip(far, near))]
-    for i in (1, 0):
-        arrivals[i].start()
+    for move in arrivals:
+        move.start()
     departures = []
 
     def send(source, target):
-        move = pltpu.make_async_copy(source, target, copied.at[8 + len(departures)])
+        move = pltpu.make_async_copy(source, target, copied.at[7 + len(departures)])
         move.start()
         departures.append(move)
 
-    arrivals[1].wait()
-    for move in arrivals[2:]:
-        move.start()
+    coarse_levels(pos, gathered, e2out, nx, ny, work)
+    arrivals[0].wait()
     level_one_again(
         pos, center, lower, upper, v1, f1, kx1, ky1, kz1, inverse1, stiff1, pen1, diagonal1, v01)
-    arrivals[0].wait()
-    coarse_levels(pos, gathered, e2out, nx, ny, work)
     gx, gy = pos[0], pos[1]
     ys = 4 * ny
     turn = lax.rem(ys - 4 * gy, ys)
@@ -679,7 +692,7 @@
     sweep1(va1, vb1, SECOND, 3, 15)
     sweep1(vb1, va1, FIRST, 4, 14)
     grow0 = matrix((BZ, LANES), lambda j, l: j == (l >> 1))
-    for move in arrivals[2:]:
+    for move in arrivals[1:]:
         move.wait()
     for c in range(3):
         spread[...] = times(va1[c, 4:14].reshape(240, BZ), grow0)
@@ -808,7 +821,11 @@
 
 def filter_precond(pos, *rest):
     far, out, near, (term, copied) = rest[:6], rest[6], rest[7:13], rest[13:]
-    arrive(far, near, copied)
+    moves = [pltpu.make_async_copy(source, target, copied.at[i]) for i, (source, target) in enumerate(zip(far, near))]
+    for move in moves[3:] + moves[:3]:
+        move.start()
+    for move in moves[3:]:
+        move.wait()
     precond, state, weights = near[3:]
     sensitivity(state, precond, weights, term)
 
@@ -816,6 +833,8 @@
         out[x] = weigh(term, x)
 
     loop(0, BX, smooth)
+    for move in moves[:3]:
+        move.wait()
 
 
 def finish(pos, totals, *rest):
@@ -853,7 +872,7 @@
         4, prepare, [(11,) + cells, cells, cells], [field], [pos],
         far=[right_side, iterate, state, classes, load_mask, fixed_mask], copies=6)
     from_lower, from_upper = shift_along(last, "gz", 1), shift_along(first, "gz", -1)
-    edge = (12, BX, BY // 2, BZ)
+    edge = (9, BX, BY // 2, BZ)
     packed, to_upper, to_lower = launch(4, pack_rows, [cells, edge, edge], [], [pos, main, from_lower, from_upper])
     from_lower, from_upper = shift_along(to_upper, "gy", 1), shift_along(to_lower, "gy", -1)
     sides = (SENT, ROWS, BZ)
@@ -899,13 +918,13 @@
     work = [one2, one2, three2] + [one2] * 4 + [three2] * 4 + [wide2, (5 * nx * 2 * ny, BZ)]
     work += [one3, one3, three3] + [one3] * 3 + [three3] * 3 + [(nx * 2 * ny, BZ)]
     parts = (9,) + cells
-    far = [gathered, center, v1, start, kx, ky, kz, inverse]
+    far = [center, v1, start, kx, ky, kz, inverse]
     scratch = [x.shape for x in far] + [
         (3, nx + 4) + wide2, (15 * 4 * ny, LANES), wide1, three1, three1, (ROWS, BZ), (240, LANES), fields(16), fields(14), parts
     ] + [three1] * 2 + [one1] * 3 + [three1, one1, one1, three1, three1] + work
     sums, parts, precond = launch(
-        30, functools.partial(ascend, nx=nx, ny=ny), [(8, BZ)], scratch, [pos, from_lower, from_upper],
-        far_outs=[parts, fields(14)], far=far + [smooth], copies=11)
+        30, functools.partial(ascend, nx=nx, ny=ny), [(8, BZ)], scratch, [pos, from_lower, from_upper, gathered],
+        far_outs=[parts, fields(14)], far=far + [smooth], copies=10)
     ready = launch(
         12, filter_precond, [cells, field, parts.shape, smooth.shape], [fields(14), fields(14), slabs(14), slabs(12)], [pos],
         far=[iterate, parts, smooth, precond, forward, weights], copies=6, pin=True,

time: 156 us -> 152 us (0.974)
  waiting for transfers between devices: 31.8 us -> 29.9 us
    ppermute x12, waiting for transfers between devices: 29 us -> 26.9 us  [shift_along(): lax.ppermute(x, axis, [(i, (i + step) % devices) for i in range(devices)])]
where the time goes in v7:
time: 152 us; the launch traced here: 151 us
  starting transfers between devices  56.2 us (37%)
  Pallas kernels  46.9 us (31%)
  waiting for transfers between devices  29.9 us (20%)
  blocking collectives  15.9 us (10%)
    pallas_call x12, Pallas kernels, launch(): pl.pallas_call(kernel, out_shape=[pltpu.VMEM(shape, F32) if pin else jax....  46.9 us
    ppermute x12, starting transfers between devices, shift_along(): lax.ppermute(x, axis, [(i, (i + step) % devices) for i in range(devices)])  39.4 us
    ppermute x12, waiting for transfers between devices, shift_along(): lax.ppermute(x, axis, [(i, (i + step) % devices) for i in range(devices)])  26.9 us
    all_to_all x1, blocking collectives, body(): lax.all_to_all(jnp.broadcast_to(sums[:1], (nx * ny, BZ)), ('gx', 'gy'), 0...  15.9 us
    all_to_all x1, starting transfers between devices, body(): lax.all_to_all(jnp.broadcast_to(total, (nz, BZ)), 'gz', 0, 0, tiled=True)  6.05 us
    all_to_all x1, starting transfers between devices, body(): gathered = lax.all_to_all(column, 'gx', 0, 0, tiled=True)  5.8 us
    all_to_all x1, starting transfers between devices, body(): column = lax.all_to_all(chunk, 'gy', 0, 0, tiled=True)  4.93 us
  transfers between devices with their start and end apart: 15, of which 11 were waited for; matrix products, arithmetic and copies ran while one was open for 0% of the time, Pallas kernels for 8%

profile of v7, /device:TPU:1, one launch (start us, length us, event | category | flops | bytes accessed | tf_op | source)
XLA Modules:
  0.0 151.1 jit_solution(3426358690439261848)
XLA Ops:
  0.6 0.1 pad_add_fusion.pos
  0.7 2.3 %shard_map.94 = (f32[11,8,16,128]{3,2,1,0:T(8,128)S(1)}, f32[8,16,128]{2,1,0:T(8,128)S(1)}, f32[8,16,128]{2,1,0:T(8,128)S(1)}) custom-call(s32[6]{0:T(128)S(1)} %pad_add_fusion.pos, f32[3,8,16,128]{3,2,1,0:T(8,128)} %right_far.1, f32[3,8,16,128]{3,2,1,0:T(8,128)} %rest_0_.1, f32[3,8,16,128]{3,2,1,0:T(8,128)} %state_far.1, s32[8,16,128]{2,1,0:T(8,128)} %classes_far.1, ...), custom_call_target="tpu_custom_call" | custom-call | tf_op jit(solution)/shard_map/pallas_call | solution.py:74
  3.1 4.0 %collective-permute-start = (f32[8,16,128]{2,1,0:T(8,128)S(1)}, f32[8,16,128]{2,1,0:T(8,128)S(1)}, u32[]{:S(2)}, u32[]{:S(2)}) collective-permute-start(f32[8,16,128]{2,1,0:T(8,128)S(1)} %get-tuple-element.37), channel_id=1, source_target_pairs={{0,1},{1,2},{2,3},{3,4},{4,5},{5,6},{6,7},{7,0},{8,9},{9,10},{10,1... | collective-permute-start | bytes 196616 | tf_op jit(solution)/shard_map/ppermute | solution.py:87
  7.1 3.8 %collective-permute-start.1 = (f32[8,16,128]{2,1,0:T(8,128)S(1)}, f32[8,16,128]{2,1,0:T(8,128)S(1)}, u32[]{:S(2)}, u32[]{:S(2)}) collective-permute-start(f32[8,16,128]{2,1,0:T(8,128)S(1)} %get-tuple-element.38), channel_id=1, source_target_pairs={{0,7},{1,0},{2,1},{3,2},{4,3},{5,4},{6,5},{7,6},{8,15},{9,8},{10,9... | collective-permute-start | bytes 196616 | tf_op jit(solution)/shard_map/ppermute | solution.py:87
  10.9 0.0 collective-permute-done.from_lower
  10.9 1.3 collective-permute-done.1.from_upper
  12.2 0.6 shard_map.95
  12.9 4.0 %collective-permute-start.2 = (f32[9,8,8,128]{3,2,1,0:T(8,128)S(1)}, f32[9,8,8,128]{3,2,1,0:T(8,128)S(1)}, u32[]{:S(2)}, u32[]{:S(2)}) collective-permute-start(f32[9,8,8,128]{3,2,1,0:T(8,128)S(1)} %get-tuple-element.40), channel_id=1, source_target_pairs={{0,8},{8,16},{16,24},{24,32},{32,40},{40,48},{48,56},{56,0},{1,9},... | collective-permute-start | bytes 884744 | tf_op jit(solution)/shard_map/ppermute | solution.py:87
  16.9 8.6 %collective-permute-start.3 = (f32[9,8,8,128]{3,2,1,0:T(8,128)S(1)}, f32[9,8,8,128]{3,2,1,0:T(8,128)S(1)}, u32[]{:S(2)}, u32[]{:S(2)}) collective-permute-start(f32[9,8,8,128]{3,2,1,0:T(8,128)S(1)} %get-tuple-element.41), channel_id=1, source_target_pairs={{0,56},{8,0},{16,8},{24,16},{32,24},{40,32},{48,40},{56,48},{1,57}... | collective-permute-start | bytes 884744 | tf_op jit(solution)/shard_map/ppermute | solution.py:87
  25.5 3.4 %collective-permute-done.2.from_lower = f32[9,8,8,128]{3,2,1,0:T(8,128)S(1)} collective-permute-done((f32[9,8,8,128]{3,2,1,0:T(8,128)S(1)}, f32[9,8,8,128]{3,2,1,0:T(8,128)S(1)}, u32[]{:S(2)}, u32[]{:S(2)}) %collective-permute-start.2) | collective-permute-done | bytes 294944 | tf_op jit(solution)/shard_map/ppermute | solution.py:87
  28.9 0.9 collective-permute-done.3.from_upper
  29.8 3.3 %shard_map.96 = (f32[12,8,32,128]{3,2,1,0:T(8,128)S(1)}, f32[56,32,128]{2,1,0:T(8,128)S(1)}, f32[56,32,128]{2,1,0:T(8,128)S(1)}) custom-call(s32[6]{0:T(128)S(1)} %pad_add_fusion.pos, f32[11,8,16,128]{3,2,1,0:T(8,128)S(1)} %get-tuple-element.36.main, f32[8,16,128]{2,1,0:T(8,128)S(1)} %get-tuple-element.39.packed, ...), custom_call_target="tpu_custom_call" | custom-call | tf_op jit(solution)/shard_map/pallas_call | solution.py:74
  33.1 4.0 %collective-permute-start.4 = (f32[56,32,128]{2,1,0:T(8,128)S(1)}, f32[56,32,128]{2,1,0:T(8,128)S(1)}, u32[]{:S(2)}, u32[]{:S(2)}) collective-permute-start(f32[56,32,128]{2,1,0:T(8,128)S(1)} %get-tuple-element.43), channel_id=1, source_target_pairs={{0,64},{64,128},{128,192},{192,256},{256,320},{320,384},{384,448},... | collective-permute-start | bytes 2752520 | tf_op jit(solution)/shard_map/ppermute | solution.py:87
  37.1 0.0 collective-permute-start.5
  37.1 10.3 %collective-permute-done.4.lower = f32[56,32,128]{2,1,0:T(8,128)S(1)} collective-permute-done((f32[56,32,128]{2,1,0:T(8,128)S(1)}, f32[56,32,128]{2,1,0:T(8,128)S(1)}, u32[]{:S(2)}, u32[]{:S(2)}) %collective-permute-start.4) | collective-permute-done | bytes 917536 | tf_op jit(solution)/shard_map/ppermute | solution.py:87
  47.4 2.5 %collective-permute-done.5.upper = f32[56,32,128]{2,1,0:T(8,128)S(1)} collective-permute-done((f32[56,32,128]{2,1,0:T(8,128)S(1)}, f32[56,32,128]{2,1,0:T(8,128)S(1)}, u32[]{:S(2)}, u32[]{:S(2)}) %collective-permute-start.5) | collective-permute-done | bytes 917536 | tf_op jit(solution)/shard_map/ppermute | solution.py:87
  49.9 9.5 %shard_map.97 = (f32[44,16,128]{2,1,0:T(8,128)S(1)}, f32[22,8,128]{2,1,0:T(8,128)S(1)}, f32[22,8,128]{2,1,0:T(8,128)S(1)}, f32[3,18,32,256]{3,2,1,0:T(8,128)}, f...) custom-call(s32[6]{0:T(128)S(1)} %pad_add_fusion.pos, ...), custom_call_target="tpu_custom_call" | custom-call | tf_op jit(solution)/shard_map/pallas_call | solution.py:74
  59.4 3.1 %collective-permute-start.6 = (f32[22,8,128]{2,1,0:T(8,128)S(1)}, f32[22,8,128]{2,1,0:T(8,128)S(1)}, u32[]{:S(2)}, u32[]{:S(2)}) collective-permute-start(f32[22,8,128]{2,1,0:T(8,128)S(1)} %get-tuple-element.46), channel_id=1, source_target_pairs={{0,1},{1,2},{2,3},{3,4},{4,5},{5,6},{6,7},{7,0},{8,9},{9,10},{10,1... | collective-permute-start | bytes 270344 | tf_op jit(solution)/shard_map/ppermute | solution.py:87
  62.5 3.7 %collective-permute-start.7 = (f32[22,8,128]{2,1,0:T(8,128)S(1)}, f32[22,8,128]{2,1,0:T(8,128)S(1)}, u32[]{:S(2)}, u32[]{:S(2)}) collective-permute-start(f32[22,8,128]{2,1,0:T(8,128)S(1)} %get-tuple-element.47), channel_id=1, source_target_pairs={{0,7},{1,0},{2,1},{3,2},{4,3},{5,4},{6,5},{7,6},{8,15},{9,8},{10,9... | collective-permute-start | bytes 270344 | tf_op jit(solution)/shard_map/ppermute | solution.py:87
  66.2 0.9 collective-permute-done.6.from_lower
  67.1 2.2 %collective-permute-done.7.from_upper = f32[22,8,128]{2,1,0:T(8,128)S(1)} collective-permute-done((f32[22,8,128]{2,1,0:T(8,128)S(1)}, f32[22,8,128]{2,1,0:T(8,128)S(1)}, u32[]{:S(2)}, u32[]{:S(2)}) %collective-permute-start.7) | collective-permute-done | bytes 90144 | tf_op jit(solution)/shard_map/ppermute | solution.py:87
  69.3 1.0 shard_map.98
  70.4 2.2 %shard_map.100 = f32[8,24,128]{2,1,0:T(8,128)} custom-call(s32[6]{0:T(128)S(1)} %pad_add_fusion.pos, f32[44,16,128]{2,1,0:T(8,128)S(1)} %get-tuple-element.51.own), custom_call_target="tpu_custom_call" | custom-call | tf_op jit(solution)/shard_map/pallas_call | solution.py:74
  72.5 4.9 %all-to-all-start = ((f32[8,24,128]{2,1,0:T(8,128)}), f32[8,24,128]{2,1,0:T(8,128)S(1)}, u32[]{:S(2)}, u32[]{:S(2)}) async-start(f32[8,24,128]{2,1,0:T(8,128)} %shard_map.100), calls=%async_computation | async-start | bytes 196608 | tf_op jit(solution)/shard_map/all_to_all | solution.py:905
  77.5 4.6 %collective-permute-start.9 = (f32[44,8,128]{2,1,0:T(8,128)S(1)}, f32[44,8,128]{2,1,0:T(8,128)S(1)}, u32[]{:S(2)}, u32[]{:S(2)}) collective-permute-start(f32[44,8,128]{2,1,0:T(8,128)S(1)} %get-tuple-element.48.coarse), channel_id=1, source_target_pairs={{0,56},{8,0},{16,8},{24,16},{32,24},{40,32},{48,40},{56,48},{1,57}... | collective-permute-start | bytes 540680 | tf_op jit(solution)/shard_map/ppermute | solution.py:87
  82.0 1.9 %collective-permute-start.8 = (f32[44,8,128]{2,1,0:T(8,128)S(1)}, f32[44,8,128]{2,1,0:T(8,128)S(1)}, u32[]{:S(2)}, u32[]{:S(2)}) collective-permute-start(f32[44,8,128]{2,1,0:T(8,128)S(1)} %get-tuple-element.48.coarse), channel_id=1, source_target_pairs={{0,8},{8,16},{16,24},{24,32},{32,40},{40,48},{48,56},{56,0},{1,9},... | collective-permute-start | bytes 540680 | tf_op jit(solution)/shard_map/ppermute | solution.py:87
  84.0 1.1 all-to-all-done.column
  85.1 1.5 shard_map.101
  86.5 5.8 %all-to-all-start.1 = ((f32[8,160,128]{2,1,0:T(8,128)}), f32[8,160,128]{2,1,0:T(8,128)S(1)}, u32[]{:S(2)}, u32[]{:S(2)}) async-start(f32[8,160,128]{2,1,0:T(8,128)} %shard_map.101), calls=%async_computation.1 | async-start | bytes 1310720 | tf_op jit(solution)/shard_map/all_to_all | solution.py:910
  92.3 0.0 collective-permute-done.9.from_upper
  92.3 0.0 collective-permute-done.8.from_lower
  92.3 1.4 shard_map.99
  93.8 1.6 %collective-permute-start.10 = (f32[32,24,128]{2,1,0:T(8,128)S(1)}, f32[32,24,128]{2,1,0:T(8,128)S(1)}, u32[]{:S(2)}, u32[]{:S(2)}) collective-permute-start(f32[32,24,128]{2,1,0:T(8,128)S(1)} %get-tuple-element.49), channel_id=1, source_target_pairs={{0,64},{64,128},{128,192},{192,256},{256,320},{320,384},{384,448},... | collective-permute-start | bytes 1179656 | tf_op jit(solution)/shard_map/ppermute | solution.py:87
  95.4 0.0 collective-permute-start.11
  95.4 5.0 %shard_map.102.rest_7_.rest_2_ = f32[2,8,16,128]{3,2,1,0:T(8,128)S(1)} custom-call(s32[6]{0:T(128)S(1)} %pad_add_fusion.pos, f32[3,14,32,256]{3,2,1,0:T(8,128)} %get-tuple-element.59.rest_0_, f32[3,14,32,256]{3,2,1,0:T(8,128)} %get-tuple-element.60.rest_1_.rest_4_, f32[14,32,256]{2,1,0:T(8,128)} %get-tuple-element.61.rest_2_.rest_5_), custom_call_target="tpu_custom_call" | custom-call | flops 12000000 | bytes 4000000 | tf_op jit(solution)/shard_map/pallas_call | solution.py:74
  100.4 0.0 copy-start
  100.4 0.6 copy-done
  101.1 3.3 %collective-permute-done.10.lower = f32[32,24,128]{2,1,0:T(8,128)S(1)} collective-permute-done((f32[32,24,128]{2,1,0:T(8,128)S(1)}, f32[32,24,128]{2,1,0:T(8,128)S(1)}, u32[]{:S(2)}, u32[]{:S(2)}) %collective-permute-start.10) | collective-permute-done | bytes 393248 | tf_op jit(solution)/shard_map/ppermute | solution.py:87
  104.3 2.1 %collective-permute-done.11.upper = f32[32,24,128]{2,1,0:T(8,128)S(1)} collective-permute-done((f32[32,24,128]{2,1,0:T(8,128)S(1)}, f32[32,24,128]{2,1,0:T(8,128)S(1)}, u32[]{:S(2)}, u32[]{:S(2)}) %collective-permute-start.11) | collective-permute-done | bytes 393248 | tf_op jit(solution)/shard_map/ppermute | solution.py:87
  106.5 0.0 all-to-all-done.1.gathered
  106.5 14.1 %shard_map.103 = (f32[8,128]{1,0:T(8,128)S(1)}, f32[9,8,16,128]{3,2,1,0:T(8,128)}, f32[3,14,32,256]{3,2,1,0:T(8,128)}) custom-call(s32[6]{0:T(128)S(1)} %pad_add_fusion.pos, f32[32,24,128]{2,1,0:T(8,128)S(1)} %collective-permute-done.10.lower, f32[32,24,128]{2,1,0:T(8,128)S(1)} %collective-permute-done.11.upper, f32[8,160,128]{2,1,0:T(8,128)S(1)} %all-to-all-done.1.gathered, ...), custom_call_target="tpu_custom_call" | custom-call | tf_op jit(solution)/shard_map/pallas_call | solution.py:74
  120.6 15.9 %all_to_all.24 = f32[64,1,128]{2,1,0:T(1,128)S(1)} all-to-all(f32[64,1,128]{2,1,0:T(1,128)S(1)} %broadcast_in_dim.4), channel_id=1, replica_groups=mesh['gx'=8,'gy'=8,'gz'=8] {'gx','gy'}, dimensions={0} | all-to-all | bytes 65536 | tf_op jit(solution)/shard_map/all_to_all | solution.py:932
  136.5 0.6 broadcast_in_dim.5
  137.1 6.0 %all-to-all-start.3 = ((f32[8,1,128]{2,1,0:T(1,128)}), f32[8,1,128]{2,1,0:T(1,128)S(1)}, u32[]{:S(2)}, u32[]{:S(2)}) async-start(f32[8,1,128]{2,1,0:T(1,128)} %broadcast_in_dim.5), calls=%async_computation.3 | async-start | bytes 8192 | tf_op jit(solution)/shard_map/all_to_all | solution.py:934
  143.2 4.5 %shard_map.104 = (f32[8,16,128]{2,1,0:T(8,128)S(1)}, f32[3,8,16,128]{3,2,1,0:T(8,128)S(1)}, f32[9,8,16,128]{3,2,1,0:T(8,128)S(1)}, f32[2,8,16,128]{3,2,1,0:T(8,128)S(1)}) custom-call(s32[6]{0:T(128)S(1)} %pad_add_fusion.pos, f32[3,8,16,128]{3,2,1,0:T(8,128)} %rest_0_.1, f32[9,8,16,128]{3,2,1,0:T(8,128)} %get-tuple-element.63.rest_1_, ...), custom_call_target="tpu_custom_call" | custom-call | flops 8000000 | bytes 4000000 | tf_op jit(solution)/shard_map/pallas_call | solution.py:74
  147.7 1.9 %all-to-all-done.3 = f32[8,1,128]{2,1,0:T(1,128)S(1)} async-done(((f32[8,1,128]{2,1,0:T(1,128)}), f32[8,1,128]{2,1,0:T(1,128)S(1)}, u32[]{:S(2)}, u32[]{:S(2)}) %all-to-all-start.3) | async-done | bytes 4128 | tf_op jit(solution)/shard_map/all_to_all | solution.py:934
  149.6 1.4 shard_map.105
  (4 shorter events, 0.0 us)
Async XLA Ops:
  3.1 7.9 %collective-permute-start = (f32[8,16,128]{2,1,0:T(8,128)S(1)}, f32[8,16,128]{2,1,0:T(8,128)S(1)}, u32[]{:S(2)}, u32[]{:S(2)}) collective-permute-start(f32[8,16,128]{2,1,0:T(8,128)S(1)} %get-tuple-element.37), channel_id=1, source_target_pairs={{0,1},{1,2},{2,3},{3,4},{4,5},{5,6},{6,7},{7,0},{8,9},{9,10},{10,1... | collective-permute-start | bytes 196616 | tf_op jit(solution)/shard_map/ppermute | solution.py:87
  7.1 5.1 %collective-permute-start.1 = (f32[8,16,128]{2,1,0:T(8,128)S(1)}, f32[8,16,128]{2,1,0:T(8,128)S(1)}, u32[]{:S(2)}, u32[]{:S(2)}) collective-permute-start(f32[8,16,128]{2,1,0:T(8,128)S(1)} %get-tuple-element.38), channel_id=1, source_target_pairs={{0,7},{1,0},{2,1},{3,2},{4,3},{5,4},{6,5},{7,6},{8,15},{9,8},{10,9... | collective-permute-start | bytes 196616 | tf_op jit(solution)/shard_map/ppermute | solution.py:87
  12.9 16.0 %collective-permute-start.2 = (f32[9,8,8,128]{3,2,1,0:T(8,128)S(1)}, f32[9,8,8,128]{3,2,1,0:T(8,128)S(1)}, u32[]{:S(2)}, u32[]{:S(2)}) collective-permute-start(f32[9,8,8,128]{3,2,1,0:T(8,128)S(1)} %get-tuple-element.40), channel_id=1, source_target_pairs={{0,8},{8,16},{16,24},{24,32},{32,40},{40,48},{48,56},{56,0},{1,9},... | collective-permute-start | bytes 884744 | tf_op jit(solution)/shard_map/ppermute | solution.py:87
  16.9 12.9 %collective-permute-start.3 = (f32[9,8,8,128]{3,2,1,0:T(8,128)S(1)}, f32[9,8,8,128]{3,2,1,0:T(8,128)S(1)}, u32[]{:S(2)}, u32[]{:S(2)}) collective-permute-start(f32[9,8,8,128]{3,2,1,0:T(8,128)S(1)} %get-tuple-element.41), channel_id=1, source_target_pairs={{0,56},{8,0},{16,8},{24,16},{32,24},{40,32},{48,40},{56,48},{1,57}... | collective-permute-start | bytes 884744 | tf_op jit(solution)/shard_map/ppermute | solution.py:87
  33.1 14.4 %collective-permute-start.4 = (f32[56,32,128]{2,1,0:T(8,128)S(1)}, f32[56,32,128]{2,1,0:T(8,128)S(1)}, u32[]{:S(2)}, u32[]{:S(2)}) collective-permute-start(f32[56,32,128]{2,1,0:T(8,128)S(1)} %get-tuple-element.43), channel_id=1, source_target_pairs={{0,64},{64,128},{128,192},{192,256},{256,320},{320,384},{384,448},... | collective-permute-start | bytes 2752520 | tf_op jit(solution)/shard_map/ppermute | solution.py:87
  37.1 12.8 %collective-permute-start.5 = (f32[56,32,128]{2,1,0:T(8,128)S(1)}, f32[56,32,128]{2,1,0:T(8,128)S(1)}, u32[]{:S(2)}, u32[]{:S(2)}) collective-permute-start(f32[56,32,128]{2,1,0:T(8,128)S(1)} %get-tuple-element.44), channel_id=1, source_target_pairs={{0,448},{64,0},{128,64},{192,128},{256,192},{320,256},{384,320},{4... | collective-permute-start | bytes 2752520 | tf_op jit(solution)/shard_map/ppermute | solution.py:87
  59.4 7.8 %collective-permute-start.6 = (f32[22,8,128]{2,1,0:T(8,128)S(1)}, f32[22,8,128]{2,1,0:T(8,128)S(1)}, u32[]{:S(2)}, u32[]{:S(2)}) collective-permute-start(f32[22,8,128]{2,1,0:T(8,128)S(1)} %get-tuple-element.46), channel_id=1, source_target_pairs={{0,1},{1,2},{2,3},{3,4},{4,5},{5,6},{6,7},{7,0},{8,9},{9,10},{10,1... | collective-permute-start | bytes 270344 | tf_op jit(solution)/shard_map/ppermute | solution.py:87
  62.5 6.9 %collective-permute-start.7 = (f32[22,8,128]{2,1,0:T(8,128)S(1)}, f32[22,8,128]{2,1,0:T(8,128)S(1)}, u32[]{:S(2)}, u32[]{:S(2)}) collective-permute-start(f32[22,8,128]{2,1,0:T(8,128)S(1)} %get-tuple-element.47), channel_id=1, source_target_pairs={{0,7},{1,0},{2,1},{3,2},{4,3},{5,4},{6,5},{7,6},{8,15},{9,8},{10,9... | collective-permute-start | bytes 270344 | tf_op jit(solution)/shard_map/ppermute | solution.py:87
  72.5 12.5 %all-to-all-start = ((f32[8,24,128]{2,1,0:T(8,128)}), f32[8,24,128]{2,1,0:T(8,128)S(1)}, u32[]{:S(2)}, u32[]{:S(2)}) async-start(f32[8,24,128]{2,1,0:T(8,128)} %shard_map.100), calls=%async_computation | async-start | bytes 196608 | tf_op jit(solution)/shard_map/all_to_all | solution.py:905
  77.5 14.9 %collective-permute-start.9 = (f32[44,8,128]{2,1,0:T(8,128)S(1)}, f32[44,8,128]{2,1,0:T(8,128)S(1)}, u32[]{:S(2)}, u32[]{:S(2)}) collective-permute-start(f32[44,8,128]{2,1,0:T(8,128)S(1)} %get-tuple-element.48.coarse), channel_id=1, source_target_pairs={{0,56},{8,0},{16,8},{24,16},{32,24},{40,32},{48,40},{56,48},{1,57}... | collective-permute-start | bytes 540680 | tf_op jit(solution)/shard_map/ppermute | solution.py:87
  82.0 10.3 %collective-permute-start.8 = (f32[44,8,128]{2,1,0:T(8,128)S(1)}, f32[44,8,128]{2,1,0:T(8,128)S(1)}, u32[]{:S(2)}, u32[]{:S(2)}) collective-permute-start(f32[44,8,128]{2,1,0:T(8,128)S(1)} %get-tuple-element.48.coarse), channel_id=1, source_target_pairs={{0,8},{8,16},{16,24},{24,32},{32,40},{40,48},{48,56},{56,0},{1,9},... | collective-permute-start | bytes 540680 | tf_op jit(solution)/shard_map/ppermute | solution.py:87
  86.5 19.9 %all-to-all-start.1 = ((f32[8,160,128]{2,1,0:T(8,128)}), f32[8,160,128]{2,1,0:T(8,128)S(1)}, u32[]{:S(2)}, u32[]{:S(2)}) async-start(f32[8,160,128]{2,1,0:T(8,128)} %shard_map.101), calls=%async_computation.1 | async-start | bytes 1310720 | tf_op jit(solution)/shard_map/all_to_all | solution.py:910
  93.8 10.5 %collective-permute-start.10 = (f32[32,24,128]{2,1,0:T(8,128)S(1)}, f32[32,24,128]{2,1,0:T(8,128)S(1)}, u32[]{:S(2)}, u32[]{:S(2)}) collective-permute-start(f32[32,24,128]{2,1,0:T(8,128)S(1)} %get-tuple-element.49), channel_id=1, source_target_pairs={{0,64},{64,128},{128,192},{192,256},{256,320},{320,384},{384,448},... | collective-permute-start | bytes 1179656 | tf_op jit(solution)/shard_map/ppermute | solution.py:87
  95.4 11.0 %collective-permute-start.11 = (f32[32,24,128]{2,1,0:T(8,128)S(1)}, f32[32,24,128]{2,1,0:T(8,128)S(1)}, u32[]{:S(2)}, u32[]{:S(2)}) collective-permute-start(f32[32,24,128]{2,1,0:T(8,128)S(1)} %get-tuple-element.50), channel_id=1, source_target_pairs={{0,448},{64,0},{128,64},{192,128},{256,192},{320,256},{384,320},{4... | collective-permute-start | bytes 1179656 | tf_op jit(solution)/shard_map/ppermute | solution.py:87
  100.4 0.7 copy-start
  137.1 12.5 %all-to-all-start.3 = ((f32[8,1,128]{2,1,0:T(1,128)}), f32[8,1,128]{2,1,0:T(1,128)S(1)}, u32[]{:S(2)}, u32[]{:S(2)}) async-start(f32[8,1,128]{2,1,0:T(1,128)} %broadcast_in_dim.5), calls=%async_computation.3 | async-start | bytes 8192 | tf_op jit(solution)/shard_map/all_to_all | solution.py:934

commit v8 on v7

--- a/solution.py
+++ b/solution.py
@@ -49,6 +49,10 @@
         return carry
 
     lax.fori_loop(lower, upper, run, 0, unroll=unroll)
+
+
+def steps(lower, upper, step):
+    loop(lower, upper, step, unroll=8)
 
 
 def times(x, m):
@@ -296,19 +300,20 @@
 
     loop(0, SLABS, cube)
     kx[1] = face(stiff[0], stiff[1])
-    loop(1, SLABS - 1, lambda s: coefficients(stiff, pen, s, 1.0, kx, ky, kz, inverse, diagonal))
+
+    def prepare_slab(s):
+        coefficients(stiff, pen, s, 1.0, kx, ky, kz, inverse, diagonal)
+        for c in range(3):
+            v0[c, s] = FIRST * start[c, s] * inverse[c, s]
+
+    loop(1, SLABS - 1, prepare_slab)
     faces = (kx, ky, kz)
     send((kx.at[3:20], 2), (ky.at[3:19], 3), (kz.at[3:19], 4), (inverse.at[:, 3:19], 5))
 
     for s in (HALO - 1, HALO, HALO + BX - 1, HALO + BX):
         for c in range(3):
             start[c, s] = start[c, s] - (diagonal[c, s] * u[c, s] - neighbours(u, c, s, *faces))
-
-    def begin(s):
-        for c in range(3):
             v0[c, s] = FIRST * start[c, s] * inverse[c, s]
-
-    loop(1, SLABS - 1, begin)
     send((start.at[:, 3:19], 1))
 
     def sweep(s):
@@ -404,13 +409,13 @@
         for c in range(3):
             v0[c, s] = FIRST * f[c, s] * inverse[c, s]
 
-    loop(1, slabs - 1, begin)
+    steps(1, slabs - 1, begin)
 
     def sweep(s):
         for c in range(3):
             v1[c, s] = (1.0 - SECOND) * v0[c, s] + SECOND * inverse[c, s] * (f[c, s] + neighbours(v0, c, s, *faces))
 
-    loop(2, slabs - 2, sweep)
+    steps(2, slabs - 2, sweep)
 
 
 def level_one(pos, own, chunk, kx, ky, kz, inverse, diagonal, f, v0, v1, half_rows, rows, wide):
@@ -420,7 +425,7 @@
         for i in range(8):
             f[c, 1 + i] = own[8 * c + i]
     kx[1] = 2.0 * face(stiff[0], stiff[1])
-    loop(1, slabs - 1, lambda s: coefficients(stiff, pen, s, 2.0, kx, ky, kz, inverse, diagonal))
+    steps(1, slabs - 1, lambda s: coefficients(stiff, pen, s, 2.0, kx, ky, kz, inverse, diagonal))
     faces = (kx, ky, kz)
     smooth_down(slabs, f, v0, v1, inverse, faces)
 
@@ -473,7 +478,7 @@
         for j in range(4):
             f[c, 7 + j] = own[8 * c + 2 + j]
     kx[1] = 2.0 * face(stiff[0], stiff[1])
-    loop(1, slabs - 1, lambda s: coefficients(stiff, pen, s, 2.0, kx, ky, kz, inverse, diagonal))
+    steps(1, slabs - 1, lambda s: coefficients(stiff, pen, s, 2.0, kx, ky, kz, inverse, diagonal))
     smooth_down(slabs, f, v0, v1, inverse, (kx, ky, kz))
 
 
@@ -502,7 +507,7 @@
                 else:
                     (e2, p2)[field - 3][g + 1, pl.ds(4 * yy, 4), :] = value
 
-    loop(0, pairs, collect)
+    steps(0, pairs, collect)
 
     def x_neighbours(below, mid, above):
         swapped = roll(mid, 64, 1)
@@ -529,7 +534,7 @@
             iv[c, s] = jnp.where(e > 0.0, 1.0 / jnp.where(e > 0.0, value, 1.0), 0.0)
             va[c, s] = FIRST * f2[c, s] * iv[c, s]
 
-    loop(1, pairs + 1, coefs)
+    steps(1, pairs + 1, coefs)
 
     def around(v, c, s):
         mid = v[c, s]
@@ -544,7 +549,7 @@
             for c in range(3):
                 target[c, s] = (1.0 - weight) * source[c, s] + weight * iv[c, s] * (f2[c, s] + around(source, c, s))
 
-        loop(1, pairs + 1, step)
+        steps(1, pairs + 1, step)
 
     sweep(va, vb, SECOND)
     n3 = ys // 2
@@ -559,7 +564,7 @@
         gather_rows(3 * pairs + s - 1, e2[s] * 0.125)
         gather_rows(4 * pairs + s - 1, p2[s])
 
-    loop(1, pairs + 1, reduce)
+    steps(1, pairs + 1, reduce)
     down = matrix((BZ, BZ), lambda l, k: ((l & 63) >> 1) == (k & 31))
     rows3[...] = times(rows3[...], down)
     row3 = iota((n3, BZ), 0)
@@ -578,7 +583,7 @@
     def place(s):
         e3[s] = third(3 * pairs + s - 1)
 
-    loop(1, pairs + 1, place)
+    steps(1, pairs + 1, place)
 
     def coefs3(s):
         e = e3[s]
@@ -598,7 +603,7 @@
             iv3[c, s] = jnp.where(e > 0.0, 1.0 / jnp.where(e > 0.0, value, 1.0), 0.0)
             wa[c, s] = COARSE * third(c * pairs + s - 1) * iv3[c, s]
 
-    loop(1, pairs + 1, coefs3)
+    steps(1, pairs + 1, coefs3)
     source, target = wa, wb
     for sweep_at in range(3):
         def step(s, source=source, target=target):
@@ -606,7 +611,7 @@
                 near = neighbours(source, c, s, jx, jym, jz)
                 target[c, s] = (1.0 - COARSE) * source[c, s] + COARSE * iv3[c, s] * (third(c * pairs + s - 1) + near)
 
-        loop(1, pairs + 1, step)
+        steps(1, pairs + 1, step)
         source, target = target, source
     up = matrix((BZ, BZ), lambda k, l: k == ((l & 63) >> 1))
     for c in range(3):
@@ -618,7 +623,7 @@
             tall[pl.ds(1, n3, stride=2), :] = value
             vb[c, s] = vb[c, s] + jnp.where(iv[c, s] > 0.0, tall[...], 0.0)
 
-        loop(1, pairs + 1, add)
+        steps(1, pairs + 1, add)
     sweep(vb, va, SECOND)
 
     for c in range(3):
@@ -629,7 +634,7 @@
         for c in range(3):
             out[c, s + 1] = (1.0 - FIRST) * va[c, s] + FIRST * iv[c, s] * (f2[c, s] + around(va, c, s))
 
-    loop(1, pairs + 1, last)
+    steps(1, pairs + 1, last)
 
 
 def ascend(pos, lower, upper, gathered, *rest, nx, ny):
@@ -687,7 +692,7 @@
                 target[c, s] = (1.0 - weight) * source[c, s] + weight * inverse1[c, s] * (
                     f1[c, s] + neighbours(source, c, s, *faces1))
 
-        loop(lower, upper, step)
+        steps(lower, upper, step)
 
     sweep1(va1, vb1, SECOND, 3, 15)
     sweep1(vb1, va1, FIRST, 4, 14)

time: 152 us -> 151 us (level)
  no operation moved by 1% of the time
where the time goes in v8:
time: 151 us; the launch traced here: 150 us
  starting transfers between devices  56.2 us (37%)
  Pallas kernels  46.3 us (31%)
  waiting for transfers between devices  30 us (20%)
  blocking collectives  15.9 us (11%)
    pallas_call x12, Pallas kernels, launch(): pl.pallas_call(kernel, out_shape=[pltpu.VMEM(shape, F32) if pin else jax....  46.3 us
    ppermute x12, starting transfers between devices, shift_along(): lax.ppermute(x, axis, [(i, (i + step) % devices) for i in range(devices)])  39.4 us
    ppermute x12, waiting for transfers between devices, shift_along(): lax.ppermute(x, axis, [(i, (i + step) % devices) for i in range(devices)])  26.9 us
    all_to_all x1, blocking collectives, body(): lax.all_to_all(jnp.broadcast_to(sums[:1], (nx * ny, BZ)), ('gx', 'gy'), 0...  15.9 us
    all_to_all x1, starting transfers between devices, body(): lax.all_to_all(jnp.broadcast_to(total, (nz, BZ)), 'gz', 0, 0, tiled=True)  6.06 us
    all_to_all x1, starting transfers between devices, body(): gathered = lax.all_to_all(column, 'gx', 0, 0, tiled=True)  5.8 us
    all_to_all x1, starting transfers between devices, body(): column = lax.all_to_all(chunk, 'gy', 0, 0, tiled=True)  4.93 us
  transfers between devices with their start and end apart: 15, of which 11 were waited for; matrix products, arithmetic and copies ran while one was open for 0% of the time, Pallas kernels for 8%

profile of v8, /device:TPU:1, one launch (start us, length us, event | category | flops | bytes accessed | tf_op | source)
XLA Modules:
  0.0 150.5 jit_solution(10831453621756212926)
XLA Ops:
  0.6 0.1 pad_add_fusion.pos
  0.7 2.3 %shard_map.94 = (f32[11,8,16,128]{3,2,1,0:T(8,128)S(1)}, f32[8,16,128]{2,1,0:T(8,128)S(1)}, f32[8,16,128]{2,1,0:T(8,128)S(1)}) custom-call(s32[6]{0:T(128)S(1)} %pad_add_fusion.pos, f32[3,8,16,128]{3,2,1,0:T(8,128)} %right_far.1, f32[3,8,16,128]{3,2,1,0:T(8,128)} %rest_0_.1, f32[3,8,16,128]{3,2,1,0:T(8,128)} %state_far.1, s32[8,16,128]{2,1,0:T(8,128)} %classes_far.1, ...), custom_call_target="tpu_custom_call" | custom-call | tf_op jit(solution)/shard_map/pallas_call | solution.py:78
  3.1 4.0 %collective-permute-start = (f32[8,16,128]{2,1,0:T(8,128)S(1)}, f32[8,16,128]{2,1,0:T(8,128)S(1)}, u32[]{:S(2)}, u32[]{:S(2)}) collective-permute-start(f32[8,16,128]{2,1,0:T(8,128)S(1)} %get-tuple-element.37), channel_id=1, source_target_pairs={{0,1},{1,2},{2,3},{3,4},{4,5},{5,6},{6,7},{7,0},{8,9},{9,10},{10,1... | collective-permute-start | bytes 196616 | tf_op jit(solution)/shard_map/ppermute | solution.py:91
  7.1 3.8 %collective-permute-start.1 = (f32[8,16,128]{2,1,0:T(8,128)S(1)}, f32[8,16,128]{2,1,0:T(8,128)S(1)}, u32[]{:S(2)}, u32[]{:S(2)}) collective-permute-start(f32[8,16,128]{2,1,0:T(8,128)S(1)} %get-tuple-element.38), channel_id=1, source_target_pairs={{0,7},{1,0},{2,1},{3,2},{4,3},{5,4},{6,5},{7,6},{8,15},{9,8},{10,9... | collective-permute-start | bytes 196616 | tf_op jit(solution)/shard_map/ppermute | solution.py:91
  10.9 0.0 collective-permute-done.from_lower
  10.9 1.3 collective-permute-done.1.from_upper
  12.2 0.6 shard_map.95
  12.9 4.0 %collective-permute-start.2 = (f32[9,8,8,128]{3,2,1,0:T(8,128)S(1)}, f32[9,8,8,128]{3,2,1,0:T(8,128)S(1)}, u32[]{:S(2)}, u32[]{:S(2)}) collective-permute-start(f32[9,8,8,128]{3,2,1,0:T(8,128)S(1)} %get-tuple-element.40), channel_id=1, source_target_pairs={{0,8},{8,16},{16,24},{24,32},{32,40},{40,48},{48,56},{56,0},{1,9},... | collective-permute-start | bytes 884744 | tf_op jit(solution)/shard_map/ppermute | solution.py:91
  16.9 8.6 %collective-permute-start.3 = (f32[9,8,8,128]{3,2,1,0:T(8,128)S(1)}, f32[9,8,8,128]{3,2,1,0:T(8,128)S(1)}, u32[]{:S(2)}, u32[]{:S(2)}) collective-permute-start(f32[9,8,8,128]{3,2,1,0:T(8,128)S(1)} %get-tuple-element.41), channel_id=1, source_target_pairs={{0,56},{8,0},{16,8},{24,16},{32,24},{40,32},{48,40},{56,48},{1,57}... | collective-permute-start | bytes 884744 | tf_op jit(solution)/shard_map/ppermute | solution.py:91
  25.5 3.4 %collective-permute-done.2.from_lower = f32[9,8,8,128]{3,2,1,0:T(8,128)S(1)} collective-permute-done((f32[9,8,8,128]{3,2,1,0:T(8,128)S(1)}, f32[9,8,8,128]{3,2,1,0:T(8,128)S(1)}, u32[]{:S(2)}, u32[]{:S(2)}) %collective-permute-start.2) | collective-permute-done | bytes 294944 | tf_op jit(solution)/shard_map/ppermute | solution.py:91
  28.9 0.9 collective-permute-done.3.from_upper
  29.8 3.3 %shard_map.96 = (f32[12,8,32,128]{3,2,1,0:T(8,128)S(1)}, f32[56,32,128]{2,1,0:T(8,128)S(1)}, f32[56,32,128]{2,1,0:T(8,128)S(1)}) custom-call(s32[6]{0:T(128)S(1)} %pad_add_fusion.pos, f32[11,8,16,128]{3,2,1,0:T(8,128)S(1)} %get-tuple-element.36.main, f32[8,16,128]{2,1,0:T(8,128)S(1)} %get-tuple-element.39.packed, ...), custom_call_target="tpu_custom_call" | custom-call | tf_op jit(solution)/shard_map/pallas_call | solution.py:78
  33.1 4.0 %collective-permute-start.4 = (f32[56,32,128]{2,1,0:T(8,128)S(1)}, f32[56,32,128]{2,1,0:T(8,128)S(1)}, u32[]{:S(2)}, u32[]{:S(2)}) collective-permute-start(f32[56,32,128]{2,1,0:T(8,128)S(1)} %get-tuple-element.43), channel_id=1, source_target_pairs={{0,64},{64,128},{128,192},{192,256},{256,320},{320,384},{384,448},... | collective-permute-start | bytes 2752520 | tf_op jit(solution)/shard_map/ppermute | solution.py:91
  37.1 0.0 collective-permute-start.5
  37.1 10.3 %collective-permute-done.4.lower = f32[56,32,128]{2,1,0:T(8,128)S(1)} collective-permute-done((f32[56,32,128]{2,1,0:T(8,128)S(1)}, f32[56,32,128]{2,1,0:T(8,128)S(1)}, u32[]{:S(2)}, u32[]{:S(2)}) %collective-permute-start.4) | collective-permute-done | bytes 917536 | tf_op jit(solution)/shard_map/ppermute | solution.py:91
  47.4 2.5 %collective-permute-done.5.upper = f32[56,32,128]{2,1,0:T(8,128)S(1)} collective-permute-done((f32[56,32,128]{2,1,0:T(8,128)S(1)}, f32[56,32,128]{2,1,0:T(8,128)S(1)}, u32[]{:S(2)}, u32[]{:S(2)}) %collective-permute-start.5) | collective-permute-done | bytes 917536 | tf_op jit(solution)/shard_map/ppermute | solution.py:91
  49.9 9.3 %shard_map.97 = (f32[44,16,128]{2,1,0:T(8,128)S(1)}, f32[22,8,128]{2,1,0:T(8,128)S(1)}, f32[22,8,128]{2,1,0:T(8,128)S(1)}, f32[3,18,32,256]{3,2,1,0:T(8,128)}, f...) custom-call(s32[6]{0:T(128)S(1)} %pad_add_fusion.pos, ...), custom_call_target="tpu_custom_call" | custom-call | tf_op jit(solution)/shard_map/pallas_call | solution.py:78
  59.2 3.1 %collective-permute-start.6 = (f32[22,8,128]{2,1,0:T(8,128)S(1)}, f32[22,8,128]{2,1,0:T(8,128)S(1)}, u32[]{:S(2)}, u32[]{:S(2)}) collective-permute-start(f32[22,8,128]{2,1,0:T(8,128)S(1)} %get-tuple-element.46), channel_id=1, source_target_pairs={{0,1},{1,2},{2,3},{3,4},{4,5},{5,6},{6,7},{7,0},{8,9},{9,10},{10,1... | collective-permute-start | bytes 270344 | tf_op jit(solution)/shard_map/ppermute | solution.py:91
  62.3 3.7 %collective-permute-start.7 = (f32[22,8,128]{2,1,0:T(8,128)S(1)}, f32[22,8,128]{2,1,0:T(8,128)S(1)}, u32[]{:S(2)}, u32[]{:S(2)}) collective-permute-start(f32[22,8,128]{2,1,0:T(8,128)S(1)} %get-tuple-element.47), channel_id=1, source_target_pairs={{0,7},{1,0},{2,1},{3,2},{4,3},{5,4},{6,5},{7,6},{8,15},{9,8},{10,9... | collective-permute-start | bytes 270344 | tf_op jit(solution)/shard_map/ppermute | solution.py:91
  66.1 0.9 collective-permute-done.6.from_lower
  67.0 2.2 %collective-permute-done.7.from_upper = f32[22,8,128]{2,1,0:T(8,128)S(1)} collective-permute-done((f32[22,8,128]{2,1,0:T(8,128)S(1)}, f32[22,8,128]{2,1,0:T(8,128)S(1)}, u32[]{:S(2)}, u32[]{:S(2)}) %collective-permute-start.7) | collective-permute-done | bytes 90144 | tf_op jit(solution)/shard_map/ppermute | solution.py:91
  69.2 1.0 shard_map.98
  70.2 2.2 %shard_map.100 = f32[8,24,128]{2,1,0:T(8,128)} custom-call(s32[6]{0:T(128)S(1)} %pad_add_fusion.pos, f32[44,16,128]{2,1,0:T(8,128)S(1)} %get-tuple-element.51.own), custom_call_target="tpu_custom_call" | custom-call | tf_op jit(solution)/shard_map/pallas_call | solution.py:78
  72.4 4.9 %all-to-all-start = ((f32[8,24,128]{2,1,0:T(8,128)}), f32[8,24,128]{2,1,0:T(8,128)S(1)}, u32[]{:S(2)}, u32[]{:S(2)}) async-start(f32[8,24,128]{2,1,0:T(8,128)} %shard_map.100), calls=%async_computation | async-start | bytes 196608 | tf_op jit(solution)/shard_map/all_to_all | solution.py:910
  77.3 4.6 %collective-permute-start.9 = (f32[44,8,128]{2,1,0:T(8,128)S(1)}, f32[44,8,128]{2,1,0:T(8,128)S(1)}, u32[]{:S(2)}, u32[]{:S(2)}) collective-permute-start(f32[44,8,128]{2,1,0:T(8,128)S(1)} %get-tuple-element.48.coarse), channel_id=1, source_target_pairs={{0,56},{8,0},{16,8},{24,16},{32,24},{40,32},{48,40},{56,48},{1,57}... | collective-permute-start | bytes 540680 | tf_op jit(solution)/shard_map/ppermute | solution.py:91
  81.9 1.9 %collective-permute-start.8 = (f32[44,8,128]{2,1,0:T(8,128)S(1)}, f32[44,8,128]{2,1,0:T(8,128)S(1)}, u32[]{:S(2)}, u32[]{:S(2)}) collective-permute-start(f32[44,8,128]{2,1,0:T(8,128)S(1)} %get-tuple-element.48.coarse), channel_id=1, source_target_pairs={{0,8},{8,16},{16,24},{24,32},{32,40},{40,48},{48,56},{56,0},{1,9},... | collective-permute-start | bytes 540680 | tf_op jit(solution)/shard_map/ppermute | solution.py:91
  83.9 1.1 all-to-all-done.column
  84.9 1.5 shard_map.101
  86.4 5.8 %all-to-all-start.1 = ((f32[8,160,128]{2,1,0:T(8,128)}), f32[8,160,128]{2,1,0:T(8,128)S(1)}, u32[]{:S(2)}, u32[]{:S(2)}) async-start(f32[8,160,128]{2,1,0:T(8,128)} %shard_map.101), calls=%async_computation.1 | async-start | bytes 1310720 | tf_op jit(solution)/shard_map/all_to_all | solution.py:915
  92.2 0.0 collective-permute-done.9.from_upper
  92.2 0.0 collective-permute-done.8.from_lower
  92.2 1.4 shard_map.99
  93.7 1.6 %collective-permute-start.10 = (f32[32,24,128]{2,1,0:T(8,128)S(1)}, f32[32,24,128]{2,1,0:T(8,128)S(1)}, u32[]{:S(2)}, u32[]{:S(2)}) collective-permute-start(f32[32,24,128]{2,1,0:T(8,128)S(1)} %get-tuple-element.49), channel_id=1, source_target_pairs={{0,64},{64,128},{128,192},{192,256},{256,320},{320,384},{384,448},... | collective-permute-start | bytes 1179656 | tf_op jit(solution)/shard_map/ppermute | solution.py:91
  95.3 0.0 collective-permute-start.11
  95.3 5.0 %shard_map.102.rest_7_.rest_2_ = f32[2,8,16,128]{3,2,1,0:T(8,128)S(1)} custom-call(s32[6]{0:T(128)S(1)} %pad_add_fusion.pos, f32[3,14,32,256]{3,2,1,0:T(8,128)} %get-tuple-element.59.rest_0_, f32[3,14,32,256]{3,2,1,0:T(8,128)} %get-tuple-element.60.rest_1_.rest_4_, f32[14,32,256]{2,1,0:T(8,128)} %get-tuple-element.61.rest_2_.rest_5_), custom_call_target="tpu_custom_call" | custom-call | flops 12000000 | bytes 4000000 | tf_op jit(solution)/shard_map/pallas_call | solution.py:78
  100.3 0.0 copy-start
  100.3 0.6 copy-done
  101.0 3.3 %collective-permute-done.10.lower = f32[32,24,128]{2,1,0:T(8,128)S(1)} collective-permute-done((f32[32,24,128]{2,1,0:T(8,128)S(1)}, f32[32,24,128]{2,1,0:T(8,128)S(1)}, u32[]{:S(2)}, u32[]{:S(2)}) %collective-permute-start.10) | collective-permute-done | bytes 393248 | tf_op jit(solution)/shard_map/ppermute | solution.py:91
  104.2 2.1 %collective-permute-done.11.upper = f32[32,24,128]{2,1,0:T(8,128)S(1)} collective-permute-done((f32[32,24,128]{2,1,0:T(8,128)S(1)}, f32[32,24,128]{2,1,0:T(8,128)S(1)}, u32[]{:S(2)}, u32[]{:S(2)}) %collective-permute-start.11) | collective-permute-done | bytes 393248 | tf_op jit(solution)/shard_map/ppermute | solution.py:91
  106.3 0.0 all-to-all-done.1.gathered
  106.4 13.7 %shard_map.103 = (f32[8,128]{1,0:T(8,128)S(1)}, f32[9,8,16,128]{3,2,1,0:T(8,128)}, f32[3,14,32,256]{3,2,1,0:T(8,128)}) custom-call(s32[6]{0:T(128)S(1)} %pad_add_fusion.pos, f32[32,24,128]{2,1,0:T(8,128)S(1)} %collective-permute-done.10.lower, f32[32,24,128]{2,1,0:T(8,128)S(1)} %collective-permute-done.11.upper, f32[8,160,128]{2,1,0:T(8,128)S(1)} %all-to-all-done.1.gathered, ...), custom_call_target="tpu_custom_call" | custom-call | tf_op jit(solution)/shard_map/pallas_call | solution.py:78
  120.0 15.9 %all_to_all.24 = f32[64,1,128]{2,1,0:T(1,128)S(1)} all-to-all(f32[64,1,128]{2,1,0:T(1,128)S(1)} %broadcast_in_dim.4), channel_id=1, replica_groups=mesh['gx'=8,'gy'=8,'gz'=8] {'gx','gy'}, dimensions={0} | all-to-all | bytes 65536 | tf_op jit(solution)/shard_map/all_to_all | solution.py:937
  135.9 0.6 broadcast_in_dim.5
  136.5 6.1 %all-to-all-start.3 = ((f32[8,1,128]{2,1,0:T(1,128)}), f32[8,1,128]{2,1,0:T(1,128)S(1)}, u32[]{:S(2)}, u32[]{:S(2)}) async-start(f32[8,1,128]{2,1,0:T(1,128)} %broadcast_in_dim.5), calls=%async_computation.3 | async-start | bytes 8192 | tf_op jit(solution)/shard_map/all_to_all | solution.py:939
  142.6 4.5 %shard_map.104 = (f32[8,16,128]{2,1,0:T(8,128)S(1)}, f32[3,8,16,128]{3,2,1,0:T(8,128)S(1)}, f32[9,8,16,128]{3,2,1,0:T(8,128)S(1)}, f32[2,8,16,128]{3,2,1,0:T(8,128)S(1)}) custom-call(s32[6]{0:T(128)S(1)} %pad_add_fusion.pos, f32[3,8,16,128]{3,2,1,0:T(8,128)} %rest_0_.1, f32[9,8,16,128]{3,2,1,0:T(8,128)} %get-tuple-element.63.rest_1_, ...), custom_call_target="tpu_custom_call" | custom-call | flops 8000000 | bytes 4000000 | tf_op jit(solution)/shard_map/pallas_call | solution.py:78
  147.1 1.9 %all-to-all-done.3 = f32[8,1,128]{2,1,0:T(1,128)S(1)} async-done(((f32[8,1,128]{2,1,0:T(1,128)}), f32[8,1,128]{2,1,0:T(1,128)S(1)}, u32[]{:S(2)}, u32[]{:S(2)}) %all-to-all-start.3) | async-done | bytes 4128 | tf_op jit(solution)/shard_map/all_to_all | solution.py:939
  149.0 1.4 shard_map.105
  (4 shorter events, 0.0 us)
Async XLA Ops:
  3.1 7.9 %collective-permute-start = (f32[8,16,128]{2,1,0:T(8,128)S(1)}, f32[8,16,128]{2,1,0:T(8,128)S(1)}, u32[]{:S(2)}, u32[]{:S(2)}) collective-permute-start(f32[8,16,128]{2,1,0:T(8,128)S(1)} %get-tuple-element.37), channel_id=1, source_target_pairs={{0,1},{1,2},{2,3},{3,4},{4,5},{5,6},{6,7},{7,0},{8,9},{9,10},{10,1... | collective-permute-start | bytes 196616 | tf_op jit(solution)/shard_map/ppermute | solution.py:91
  7.1 5.1 %collective-permute-start.1 = (f32[8,16,128]{2,1,0:T(8,128)S(1)}, f32[8,16,128]{2,1,0:T(8,128)S(1)}, u32[]{:S(2)}, u32[]{:S(2)}) collective-permute-start(f32[8,16,128]{2,1,0:T(8,128)S(1)} %get-tuple-element.38), channel_id=1, source_target_pairs={{0,7},{1,0},{2,1},{3,2},{4,3},{5,4},{6,5},{7,6},{8,15},{9,8},{10,9... | collective-permute-start | bytes 196616 | tf_op jit(solution)/shard_map/ppermute | solution.py:91
  12.9 16.0 %collective-permute-start.2 = (f32[9,8,8,128]{3,2,1,0:T(8,128)S(1)}, f32[9,8,8,128]{3,2,1,0:T(8,128)S(1)}, u32[]{:S(2)}, u32[]{:S(2)}) collective-permute-start(f32[9,8,8,128]{3,2,1,0:T(8,128)S(1)} %get-tuple-element.40), channel_id=1, source_target_pairs={{0,8},{8,16},{16,24},{24,32},{32,40},{40,48},{48,56},{56,0},{1,9},... | collective-permute-start | bytes 884744 | tf_op jit(solution)/shard_map/ppermute | solution.py:91
  16.9 12.9 %collective-permute-start.3 = (f32[9,8,8,128]{3,2,1,0:T(8,128)S(1)}, f32[9,8,8,128]{3,2,1,0:T(8,128)S(1)}, u32[]{:S(2)}, u32[]{:S(2)}) collective-permute-start(f32[9,8,8,128]{3,2,1,0:T(8,128)S(1)} %get-tuple-element.41), channel_id=1, source_target_pairs={{0,56},{8,0},{16,8},{24,16},{32,24},{40,32},{48,40},{56,48},{1,57}... | collective-permute-start | bytes 884744 | tf_op jit(solution)/shard_map/ppermute | solution.py:91
  33.1 14.4 %collective-permute-start.4 = (f32[56,32,128]{2,1,0:T(8,128)S(1)}, f32[56,32,128]{2,1,0:T(8,128)S(1)}, u32[]{:S(2)}, u32[]{:S(2)}) collective-permute-start(f32[56,32,128]{2,1,0:T(8,128)S(1)} %get-tuple-element.43), channel_id=1, source_target_pairs={{0,64},{64,128},{128,192},{192,256},{256,320},{320,384},{384,448},... | collective-permute-start | bytes 2752520 | tf_op jit(solution)/shard_map/ppermute | solution.py:91
  37.1 12.8 %collective-permute-start.5 = (f32[56,32,128]{2,1,0:T(8,128)S(1)}, f32[56,32,128]{2,1,0:T(8,128)S(1)}, u32[]{:S(2)}, u32[]{:S(2)}) collective-permute-start(f32[56,32,128]{2,1,0:T(8,128)S(1)} %get-tuple-element.44), channel_id=1, source_target_pairs={{0,448},{64,0},{128,64},{192,128},{256,192},{320,256},{384,320},{4... | collective-permute-start | bytes 2752520 | tf_op jit(solution)/shard_map/ppermute | solution.py:91
  59.2 7.8 %collective-permute-start.6 = (f32[22,8,128]{2,1,0:T(8,128)S(1)}, f32[22,8,128]{2,1,0:T(8,128)S(1)}, u32[]{:S(2)}, u32[]{:S(2)}) collective-permute-start(f32[22,8,128]{2,1,0:T(8,128)S(1)} %get-tuple-element.46), channel_id=1, source_target_pairs={{0,1},{1,2},{2,3},{3,4},{4,5},{5,6},{6,7},{7,0},{8,9},{9,10},{10,1... | collective-permute-start | bytes 270344 | tf_op jit(solution)/shard_map/ppermute | solution.py:91
  62.3 6.9 %collective-permute-start.7 = (f32[22,8,128]{2,1,0:T(8,128)S(1)}, f32[22,8,128]{2,1,0:T(8,128)S(1)}, u32[]{:S(2)}, u32[]{:S(2)}) collective-permute-start(f32[22,8,128]{2,1,0:T(8,128)S(1)} %get-tuple-element.47), channel_id=1, source_target_pairs={{0,7},{1,0},{2,1},{3,2},{4,3},{5,4},{6,5},{7,6},{8,15},{9,8},{10,9... | collective-permute-start | bytes 270344 | tf_op jit(solution)/shard_map/ppermute | solution.py:91
  72.4 12.5 %all-to-all-start = ((f32[8,24,128]{2,1,0:T(8,128)}), f32[8,24,128]{2,1,0:T(8,128)S(1)}, u32[]{:S(2)}, u32[]{:S(2)}) async-start(f32[8,24,128]{2,1,0:T(8,128)} %shard_map.100), calls=%async_computation | async-start | bytes 196608 | tf_op jit(solution)/shard_map/all_to_all | solution.py:910
  77.3 14.9 %collective-permute-start.9 = (f32[44,8,128]{2,1,0:T(8,128)S(1)}, f32[44,8,128]{2,1,0:T(8,128)S(1)}, u32[]{:S(2)}, u32[]{:S(2)}) collective-permute-start(f32[44,8,128]{2,1,0:T(8,128)S(1)} %get-tuple-element.48.coarse), channel_id=1, source_target_pairs={{0,56},{8,0},{16,8},{24,16},{32,24},{40,32},{48,40},{56,48},{1,57}... | collective-permute-start | bytes 540680 | tf_op jit(solution)/shard_map/ppermute | solution.py:91
  81.9 10.3 %collective-permute-start.8 = (f32[44,8,128]{2,1,0:T(8,128)S(1)}, f32[44,8,128]{2,1,0:T(8,128)S(1)}, u32[]{:S(2)}, u32[]{:S(2)}) collective-permute-start(f32[44,8,128]{2,1,0:T(8,128)S(1)} %get-tuple-element.48.coarse), channel_id=1, source_target_pairs={{0,8},{8,16},{16,24},{24,32},{32,40},{40,48},{48,56},{56,0},{1,9},... | collective-permute-start | bytes 540680 | tf_op jit(solution)/shard_map/ppermute | solution.py:91
  86.4 19.9 %all-to-all-start.1 = ((f32[8,160,128]{2,1,0:T(8,128)}), f32[8,160,128]{2,1,0:T(8,128)S(1)}, u32[]{:S(2)}, u32[]{:S(2)}) async-start(f32[8,160,128]{2,1,0:T(8,128)} %shard_map.101), calls=%async_computation.1 | async-start | bytes 1310720 | tf_op jit(solution)/shard_map/all_to_all | solution.py:915
  93.7 10.5 %collective-permute-start.10 = (f32[32,24,128]{2,1,0:T(8,128)S(1)}, f32[32,24,128]{2,1,0:T(8,128)S(1)}, u32[]{:S(2)}, u32[]{:S(2)}) collective-permute-start(f32[32,24,128]{2,1,0:T(8,128)S(1)} %get-tuple-element.49), channel_id=1, source_target_pairs={{0,64},{64,128},{128,192},{192,256},{256,320},{320,384},{384,448},... | collective-permute-start | bytes 1179656 | tf_op jit(solution)/shard_map/ppermute | solution.py:91
  95.3 11.0 %collective-permute-start.11 = (f32[32,24,128]{2,1,0:T(8,128)S(1)}, f32[32,24,128]{2,1,0:T(8,128)S(1)}, u32[]{:S(2)}, u32[]{:S(2)}) collective-permute-start(f32[32,24,128]{2,1,0:T(8,128)S(1)} %get-tuple-element.50), channel_id=1, source_target_pairs={{0,448},{64,0},{128,64},{192,128},{256,192},{320,256},{384,320},{4... | collective-permute-start | bytes 1179656 | tf_op jit(solution)/shard_map/ppermute | solution.py:91
  100.3 0.7 copy-start
  136.5 12.5 %all-to-all-start.3 = ((f32[8,1,128]{2,1,0:T(1,128)}), f32[8,1,128]{2,1,0:T(1,128)S(1)}, u32[]{:S(2)}, u32[]{:S(2)}) async-start(f32[8,1,128]{2,1,0:T(1,128)} %broadcast_in_dim.5), calls=%async_computation.3 | async-start | bytes 8192 | tf_op jit(solution)/shard_map/all_to_all | solution.py:939

commit v9 on v8

--- a/solution.py
+++ b/solution.py
@@ -430,7 +430,7 @@
     smooth_down(slabs, f, v0, v1, inverse, faces)
 
     def gather_rows(at, value):
-        half_rows[...] = value
+        half_rows[0:8] = value
         rows[pl.ds(at * 4, 4), :] = half_rows[pl.ds(0, 4, stride=2), :] + half_rows[pl.ds(1, 4, stride=2), :]
 
     for i in range(2):
@@ -683,7 +683,7 @@
                 for at in (0, 1):
                     rows24[pl.ds(at, 8, stride=2), :] = low
                     rows24[pl.ds(16 + at, 4, stride=2), :] = high
-            va1[c, s] = v1[c, s] + jnp.where(inverse1[c, s] > 0.0, rows24[...], 0.0)
+            va1[c, s] = v1[c, s] + jnp.where(inverse1[c, s] > 0.0, rows24[0:24], 0.0)
     faces1 = (kx1, ky1, kz1)
 
     def sweep1(source, target, weight, lower, upper):
@@ -710,7 +710,7 @@
                     rows32[pl.ds(24 + at, 4, stride=2), :] = value[20:]
                 for s in (2 * i - 1, 2 * i):
                     if 0 <= s < 18:
-                        va[c, s, :, cols] = va[c, s, :, cols] + rows32[...]
+                        va[c, s, :, cols] = va[c, s, :, cols] + rows32[0:ROWS]
     faces = (kx, ky, kz)
 
     def sweep_one(t):
@@ -905,7 +905,7 @@
     wide1 = (16, BZ)
     one1, three1 = (10,) + wide1, (3, 10) + wide1
     chunk = launch(
-        4, level_one, [(ny, 24, BZ)], [one1] * 3 + [three1] * 5 + [(8, BZ), (40, BZ), (40, BZ)], [pos, coarse])[0]
+        4, level_one, [(ny, 24, BZ)], [one1] * 3 + [three1] * 5 + [(24, BZ), (40, BZ), (40, BZ)], [pos, coarse])[0]
     side = (32, 24, BZ)
     column = lax.all_to_all(chunk, "gy", 0, 0, tiled=True)
     to_upper, to_lower, center = launch(
@@ -925,7 +925,7 @@
     parts = (9,) + cells
     far = [center, v1, start, kx, ky, kz, inverse]
     scratch = [x.shape for x in far] + [
-        (3, nx + 4) + wide2, (15 * 4 * ny, LANES), wide1, three1, three1, (ROWS, BZ), (240, LANES), fields(16), fields(14), parts
+        (3, nx + 4) + wide2, (15 * 4 * ny, LANES), (40, BZ), three1, three1, (ROWS + 16, BZ), (240, LANES), fields(16), fields(14), parts
     ] + [three1] * 2 + [one1] * 3 + [three1, one1, one1, three1, three1] + work
     sums, parts, precond = launch(
         30, functools.partial(ascend, nx=nx, ny=ny), [(8, BZ)], scratch, [pos, from_lower, from_upper, gathered],

time: 151 us -> 151 us (level)
  no operation moved by 1% of the time
where the time goes in v9:
time: 151 us; the launch traced here: 150 us
  starting transfers between devices  56.2 us (37%)
  Pallas kernels  46.3 us (31%)
  waiting for transfers between devices  30 us (20%)
  blocking collectives  15.9 us (11%)
    pallas_call x12, Pallas kernels, launch(): pl.pallas_call(kernel, out_shape=[pltpu.VMEM(shape, F32) if pin else jax....  46.3 us
    ppermute x12, starting transfers between devices, shift_along(): lax.ppermute(x, axis, [(i, (i + step) % devices) for i in range(devices)])  39.4 us
    ppermute x12, waiting for transfers between devices, shift_along(): lax.ppermute(x, axis, [(i, (i + step) % devices) for i in range(devices)])  26.9 us
    all_to_all x1, blocking collectives, body(): lax.all_to_all(jnp.broadcast_to(sums[:1], (nx * ny, BZ)), ('gx', 'gy'), 0...  15.9 us
    all_to_all x1, starting transfers between devices, body(): lax.all_to_all(jnp.broadcast_to(total, (nz, BZ)), 'gz', 0, 0, tiled=True)  6.05 us
    all_to_all x1, starting transfers between devices, body(): gathered = lax.all_to_all(column, 'gx', 0, 0, tiled=True)  5.8 us
    all_to_all x1, starting transfers between devices, body(): column = lax.all_to_all(chunk, 'gy', 0, 0, tiled=True)  4.93 us
  transfers between devices with their start and end apart: 15, of which 11 were waited for; matrix products, arithmetic and copies ran while one was open for 0% of the time, Pallas kernels for 8%

profile of v9, /device:TPU:1, one launch (start us, length us, event | category | flops | bytes accessed | tf_op | source)
XLA Modules:
  0.0 150.5 jit_solution(2285530499384723959)
XLA Ops:
  0.6 0.1 pad_add_fusion.pos
  0.7 2.3 %shard_map.94 = (f32[11,8,16,128]{3,2,1,0:T(8,128)S(1)}, f32[8,16,128]{2,1,0:T(8,128)S(1)}, f32[8,16,128]{2,1,0:T(8,128)S(1)}) custom-call(s32[6]{0:T(128)S(1)} %pad_add_fusion.pos, f32[3,8,16,128]{3,2,1,0:T(8,128)} %right_far.1, f32[3,8,16,128]{3,2,1,0:T(8,128)} %rest_0_.1, f32[3,8,16,128]{3,2,1,0:T(8,128)} %state_far.1, s32[8,16,128]{2,1,0:T(8,128)} %classes_far.1, ...), custom_call_target="tpu_custom_call" | custom-call | tf_op jit(solution)/shard_map/pallas_call | solution.py:78
  3.1 4.0 %collective-permute-start = (f32[8,16,128]{2,1,0:T(8,128)S(1)}, f32[8,16,128]{2,1,0:T(8,128)S(1)}, u32[]{:S(2)}, u32[]{:S(2)}) collective-permute-start(f32[8,16,128]{2,1,0:T(8,128)S(1)} %get-tuple-element.37), channel_id=1, source_target_pairs={{0,1},{1,2},{2,3},{3,4},{4,5},{5,6},{6,7},{7,0},{8,9},{9,10},{10,1... | collective-permute-start | bytes 196616 | tf_op jit(solution)/shard_map/ppermute | solution.py:91
  7.1 3.8 %collective-permute-start.1 = (f32[8,16,128]{2,1,0:T(8,128)S(1)}, f32[8,16,128]{2,1,0:T(8,128)S(1)}, u32[]{:S(2)}, u32[]{:S(2)}) collective-permute-start(f32[8,16,128]{2,1,0:T(8,128)S(1)} %get-tuple-element.38), channel_id=1, source_target_pairs={{0,7},{1,0},{2,1},{3,2},{4,3},{5,4},{6,5},{7,6},{8,15},{9,8},{10,9... | collective-permute-start | bytes 196616 | tf_op jit(solution)/shard_map/ppermute | solution.py:91
  10.9 0.0 collective-permute-done.from_lower
  10.9 1.3 collective-permute-done.1.from_upper
  12.2 0.6 shard_map.95
  12.9 4.0 %collective-permute-start.2 = (f32[9,8,8,128]{3,2,1,0:T(8,128)S(1)}, f32[9,8,8,128]{3,2,1,0:T(8,128)S(1)}, u32[]{:S(2)}, u32[]{:S(2)}) collective-permute-start(f32[9,8,8,128]{3,2,1,0:T(8,128)S(1)} %get-tuple-element.40), channel_id=1, source_target_pairs={{0,8},{8,16},{16,24},{24,32},{32,40},{40,48},{48,56},{56,0},{1,9},... | collective-permute-start | bytes 884744 | tf_op jit(solution)/shard_map/ppermute | solution.py:91
  16.9 8.6 %collective-permute-start.3 = (f32[9,8,8,128]{3,2,1,0:T(8,128)S(1)}, f32[9,8,8,128]{3,2,1,0:T(8,128)S(1)}, u32[]{:S(2)}, u32[]{:S(2)}) collective-permute-start(f32[9,8,8,128]{3,2,1,0:T(8,128)S(1)} %get-tuple-element.41), channel_id=1, source_target_pairs={{0,56},{8,0},{16,8},{24,16},{32,24},{40,32},{48,40},{56,48},{1,57}... | collective-permute-start | bytes 884744 | tf_op jit(solution)/shard_map/ppermute | solution.py:91
  25.5 3.4 %collective-permute-done.2.from_lower = f32[9,8,8,128]{3,2,1,0:T(8,128)S(1)} collective-permute-done((f32[9,8,8,128]{3,2,1,0:T(8,128)S(1)}, f32[9,8,8,128]{3,2,1,0:T(8,128)S(1)}, u32[]{:S(2)}, u32[]{:S(2)}) %collective-permute-start.2) | collective-permute-done | bytes 294944 | tf_op jit(solution)/shard_map/ppermute | solution.py:91
  28.9 0.9 collective-permute-done.3.from_upper
  29.8 3.3 %shard_map.96 = (f32[12,8,32,128]{3,2,1,0:T(8,128)S(1)}, f32[56,32,128]{2,1,0:T(8,128)S(1)}, f32[56,32,128]{2,1,0:T(8,128)S(1)}) custom-call(s32[6]{0:T(128)S(1)} %pad_add_fusion.pos, f32[11,8,16,128]{3,2,1,0:T(8,128)S(1)} %get-tuple-element.36.main, f32[8,16,128]{2,1,0:T(8,128)S(1)} %get-tuple-element.39.packed, ...), custom_call_target="tpu_custom_call" | custom-call | tf_op jit(solution)/shard_map/pallas_call | solution.py:78
  33.1 4.0 %collective-permute-start.4 = (f32[56,32,128]{2,1,0:T(8,128)S(1)}, f32[56,32,128]{2,1,0:T(8,128)S(1)}, u32[]{:S(2)}, u32[]{:S(2)}) collective-permute-start(f32[56,32,128]{2,1,0:T(8,128)S(1)} %get-tuple-element.43), channel_id=1, source_target_pairs={{0,64},{64,128},{128,192},{192,256},{256,320},{320,384},{384,448},... | collective-permute-start | bytes 2752520 | tf_op jit(solution)/shard_map/ppermute | solution.py:91
  37.1 0.0 collective-permute-start.5
  37.1 10.3 %collective-permute-done.4.lower = f32[56,32,128]{2,1,0:T(8,128)S(1)} collective-permute-done((f32[56,32,128]{2,1,0:T(8,128)S(1)}, f32[56,32,128]{2,1,0:T(8,128)S(1)}, u32[]{:S(2)}, u32[]{:S(2)}) %collective-permute-start.4) | collective-permute-done | bytes 917536 | tf_op jit(solution)/shard_map/ppermute | solution.py:91
  47.4 2.5 %collective-permute-done.5.upper = f32[56,32,128]{2,1,0:T(8,128)S(1)} collective-permute-done((f32[56,32,128]{2,1,0:T(8,128)S(1)}, f32[56,32,128]{2,1,0:T(8,128)S(1)}, u32[]{:S(2)}, u32[]{:S(2)}) %collective-permute-start.5) | collective-permute-done | bytes 917536 | tf_op jit(solution)/shard_map/ppermute | solution.py:91
  49.9 9.3 %shard_map.97 = (f32[44,16,128]{2,1,0:T(8,128)S(1)}, f32[22,8,128]{2,1,0:T(8,128)S(1)}, f32[22,8,128]{2,1,0:T(8,128)S(1)}, f32[3,18,32,256]{3,2,1,0:T(8,128)}, f...) custom-call(s32[6]{0:T(128)S(1)} %pad_add_fusion.pos, ...), custom_call_target="tpu_custom_call" | custom-call | tf_op jit(solution)/shard_map/pallas_call | solution.py:78
  59.2 3.1 %collective-permute-start.6 = (f32[22,8,128]{2,1,0:T(8,128)S(1)}, f32[22,8,128]{2,1,0:T(8,128)S(1)}, u32[]{:S(2)}, u32[]{:S(2)}) collective-permute-start(f32[22,8,128]{2,1,0:T(8,128)S(1)} %get-tuple-element.46), channel_id=1, source_target_pairs={{0,1},{1,2},{2,3},{3,4},{4,5},{5,6},{6,7},{7,0},{8,9},{9,10},{10,1... | collective-permute-start | bytes 270344 | tf_op jit(solution)/shard_map/ppermute | solution.py:91
  62.3 3.7 %collective-permute-start.7 = (f32[22,8,128]{2,1,0:T(8,128)S(1)}, f32[22,8,128]{2,1,0:T(8,128)S(1)}, u32[]{:S(2)}, u32[]{:S(2)}) collective-permute-start(f32[22,8,128]{2,1,0:T(8,128)S(1)} %get-tuple-element.47), channel_id=1, source_target_pairs={{0,7},{1,0},{2,1},{3,2},{4,3},{5,4},{6,5},{7,6},{8,15},{9,8},{10,9... | collective-permute-start | bytes 270344 | tf_op jit(solution)/shard_map/ppermute | solution.py:91
  66.1 0.9 collective-permute-done.6.from_lower
  67.0 2.2 %collective-permute-done.7.from_upper = f32[22,8,128]{2,1,0:T(8,128)S(1)} collective-permute-done((f32[22,8,128]{2,1,0:T(8,128)S(1)}, f32[22,8,128]{2,1,0:T(8,128)S(1)}, u32[]{:S(2)}, u32[]{:S(2)}) %collective-permute-start.7) | collective-permute-done | bytes 90144 | tf_op jit(solution)/shard_map/ppermute | solution.py:91
  69.2 1.0 shard_map.98
  70.2 2.2 %shard_map.100 = f32[8,24,128]{2,1,0:T(8,128)} custom-call(s32[6]{0:T(128)S(1)} %pad_add_fusion.pos, f32[44,16,128]{2,1,0:T(8,128)S(1)} %get-tuple-element.51.own), custom_call_target="tpu_custom_call" | custom-call | tf_op jit(solution)/shard_map/pallas_call | solution.py:78
  72.4 4.9 %all-to-all-start = ((f32[8,24,128]{2,1,0:T(8,128)}), f32[8,24,128]{2,1,0:T(8,128)S(1)}, u32[]{:S(2)}, u32[]{:S(2)}) async-start(f32[8,24,128]{2,1,0:T(8,128)} %shard_map.100), calls=%async_computation | async-start | bytes 196608 | tf_op jit(solution)/shard_map/all_to_all | solution.py:910
  77.3 4.6 %collective-permute-start.9 = (f32[44,8,128]{2,1,0:T(8,128)S(1)}, f32[44,8,128]{2,1,0:T(8,128)S(1)}, u32[]{:S(2)}, u32[]{:S(2)}) collective-permute-start(f32[44,8,128]{2,1,0:T(8,128)S(1)} %get-tuple-element.48.coarse), channel_id=1, source_target_pairs={{0,56},{8,0},{16,8},{24,16},{32,24},{40,32},{48,40},{56,48},{1,57}... | collective-permute-start | bytes 540680 | tf_op jit(solution)/shard_map/ppermute | solution.py:91
  81.9 1.9 %collective-permute-start.8 = (f32[44,8,128]{2,1,0:T(8,128)S(1)}, f32[44,8,128]{2,1,0:T(8,128)S(1)}, u32[]{:S(2)}, u32[]{:S(2)}) collective-permute-start(f32[44,8,128]{2,1,0:T(8,128)S(1)} %get-tuple-element.48.coarse), channel_id=1, source_target_pairs={{0,8},{8,16},{16,24},{24,32},{32,40},{40,48},{48,56},{56,0},{1,9},... | collective-permute-start | bytes 540680 | tf_op jit(solution)/shard_map/ppermute | solution.py:91
  83.9 1.1 all-to-all-done.column
  84.9 1.5 shard_map.101
  86.4 5.8 %all-to-all-start.1 = ((f32[8,160,128]{2,1,0:T(8,128)}), f32[8,160,128]{2,1,0:T(8,128)S(1)}, u32[]{:S(2)}, u32[]{:S(2)}) async-start(f32[8,160,128]{2,1,0:T(8,128)} %shard_map.101), calls=%async_computation.1 | async-start | bytes 1310720 | tf_op jit(solution)/shard_map/all_to_all | solution.py:915
  92.2 0.0 collective-permute-done.9.from_upper
  92.2 0.0 collective-permute-done.8.from_lower
  92.2 1.4 shard_map.99
  93.7 1.6 %collective-permute-start.10 = (f32[32,24,128]{2,1,0:T(8,128)S(1)}, f32[32,24,128]{2,1,0:T(8,128)S(1)}, u32[]{:S(2)}, u32[]{:S(2)}) collective-permute-start(f32[32,24,128]{2,1,0:T(8,128)S(1)} %get-tuple-element.49), channel_id=1, source_target_pairs={{0,64},{64,128},{128,192},{192,256},{256,320},{320,384},{384,448},... | collective-permute-start | bytes 1179656 | tf_op jit(solution)/shard_map/ppermute | solution.py:91
  95.3 0.0 collective-permute-start.11
  95.3 5.0 %shard_map.102.rest_7_.rest_2_ = f32[2,8,16,128]{3,2,1,0:T(8,128)S(1)} custom-call(s32[6]{0:T(128)S(1)} %pad_add_fusion.pos, f32[3,14,32,256]{3,2,1,0:T(8,128)} %get-tuple-element.59.rest_0_, f32[3,14,32,256]{3,2,1,0:T(8,128)} %get-tuple-element.60.rest_1_.rest_4_, f32[14,32,256]{2,1,0:T(8,128)} %get-tuple-element.61.rest_2_.rest_5_), custom_call_target="tpu_custom_call" | custom-call | flops 12000000 | bytes 4000000 | tf_op jit(solution)/shard_map/pallas_call | solution.py:78
  100.3 0.0 copy-start
  100.3 0.6 copy-done
  101.0 3.3 %collective-permute-done.10.lower = f32[32,24,128]{2,1,0:T(8,128)S(1)} collective-permute-done((f32[32,24,128]{2,1,0:T(8,128)S(1)}, f32[32,24,128]{2,1,0:T(8,128)S(1)}, u32[]{:S(2)}, u32[]{:S(2)}) %collective-permute-start.10) | collective-permute-done | bytes 393248 | tf_op jit(solution)/shard_map/ppermute | solution.py:91
  104.2 2.1 %collective-permute-done.11.upper = f32[32,24,128]{2,1,0:T(8,128)S(1)} collective-permute-done((f32[32,24,128]{2,1,0:T(8,128)S(1)}, f32[32,24,128]{2,1,0:T(8,128)S(1)}, u32[]{:S(2)}, u32[]{:S(2)}) %collective-permute-start.11) | collective-permute-done | bytes 393248 | tf_op jit(solution)/shard_map/ppermute | solution.py:91
  106.3 0.0 all-to-all-done.1.gathered
  106.4 13.6 %shard_map.103 = (f32[8,128]{1,0:T(8,128)S(1)}, f32[9,8,16,128]{3,2,1,0:T(8,128)}, f32[3,14,32,256]{3,2,1,0:T(8,128)}) custom-call(s32[6]{0:T(128)S(1)} %pad_add_fusion.pos, f32[32,24,128]{2,1,0:T(8,128)S(1)} %collective-permute-done.10.lower, f32[32,24,128]{2,1,0:T(8,128)S(1)} %collective-permute-done.11.upper, f32[8,160,128]{2,1,0:T(8,128)S(1)} %all-to-all-done.1.gathered, ...), custom_call_target="tpu_custom_call" | custom-call | tf_op jit(solution)/shard_map/pallas_call | solution.py:78
  120.0 15.9 %all_to_all.24 = f32[64,1,128]{2,1,0:T(1,128)S(1)} all-to-all(f32[64,1,128]{2,1,0:T(1,128)S(1)} %broadcast_in_dim.4), channel_id=1, replica_groups=mesh['gx'=8,'gy'=8,'gz'=8] {'gx','gy'}, dimensions={0} | all-to-all | bytes 65536 | tf_op jit(solution)/shard_map/all_to_all | solution.py:937
  135.9 0.6 broadcast_in_dim.5
  136.5 6.0 %all-to-all-start.3 = ((f32[8,1,128]{2,1,0:T(1,128)}), f32[8,1,128]{2,1,0:T(1,128)S(1)}, u32[]{:S(2)}, u32[]{:S(2)}) async-start(f32[8,1,128]{2,1,0:T(1,128)} %broadcast_in_dim.5), calls=%async_computation.3 | async-start | bytes 8192 | tf_op jit(solution)/shard_map/all_to_all | solution.py:939
  142.6 4.5 %shard_map.104 = (f32[8,16,128]{2,1,0:T(8,128)S(1)}, f32[3,8,16,128]{3,2,1,0:T(8,128)S(1)}, f32[9,8,16,128]{3,2,1,0:T(8,128)S(1)}, f32[2,8,16,128]{3,2,1,0:T(8,128)S(1)}) custom-call(s32[6]{0:T(128)S(1)} %pad_add_fusion.pos, f32[3,8,16,128]{3,2,1,0:T(8,128)} %rest_0_.1, f32[9,8,16,128]{3,2,1,0:T(8,128)} %get-tuple-element.63.rest_1_, ...), custom_call_target="tpu_custom_call" | custom-call | flops 8000000 | bytes 4000000 | tf_op jit(solution)/shard_map/pallas_call | solution.py:78
  147.1 1.9 %all-to-all-done.3 = f32[8,1,128]{2,1,0:T(1,128)S(1)} async-done(((f32[8,1,128]{2,1,0:T(1,128)}), f32[8,1,128]{2,1,0:T(1,128)S(1)}, u32[]{:S(2)}, u32[]{:S(2)}) %all-to-all-start.3) | async-done | bytes 4128 | tf_op jit(solution)/shard_map/all_to_all | solution.py:939
  149.0 1.4 shard_map.105
  (4 shorter events, 0.0 us)
Async XLA Ops:
  3.1 7.9 %collective-permute-start = (f32[8,16,128]{2,1,0:T(8,128)S(1)}, f32[8,16,128]{2,1,0:T(8,128)S(1)}, u32[]{:S(2)}, u32[]{:S(2)}) collective-permute-start(f32[8,16,128]{2,1,0:T(8,128)S(1)} %get-tuple-element.37), channel_id=1, source_target_pairs={{0,1},{1,2},{2,3},{3,4},{4,5},{5,6},{6,7},{7,0},{8,9},{9,10},{10,1... | collective-permute-start | bytes 196616 | tf_op jit(solution)/shard_map/ppermute | solution.py:91
  7.1 5.1 %collective-permute-start.1 = (f32[8,16,128]{2,1,0:T(8,128)S(1)}, f32[8,16,128]{2,1,0:T(8,128)S(1)}, u32[]{:S(2)}, u32[]{:S(2)}) collective-permute-start(f32[8,16,128]{2,1,0:T(8,128)S(1)} %get-tuple-element.38), channel_id=1, source_target_pairs={{0,7},{1,0},{2,1},{3,2},{4,3},{5,4},{6,5},{7,6},{8,15},{9,8},{10,9... | collective-permute-start | bytes 196616 | tf_op jit(solution)/shard_map/ppermute | solution.py:91
  12.9 16.0 %collective-permute-start.2 = (f32[9,8,8,128]{3,2,1,0:T(8,128)S(1)}, f32[9,8,8,128]{3,2,1,0:T(8,128)S(1)}, u32[]{:S(2)}, u32[]{:S(2)}) collective-permute-start(f32[9,8,8,128]{3,2,1,0:T(8,128)S(1)} %get-tuple-element.40), channel_id=1, source_target_pairs={{0,8},{8,16},{16,24},{24,32},{32,40},{40,48},{48,56},{56,0},{1,9},... | collective-permute-start | bytes 884744 | tf_op jit(solution)/shard_map/ppermute | solution.py:91
  16.9 12.9 %collective-permute-start.3 = (f32[9,8,8,128]{3,2,1,0:T(8,128)S(1)}, f32[9,8,8,128]{3,2,1,0:T(8,128)S(1)}, u32[]{:S(2)}, u32[]{:S(2)}) collective-permute-start(f32[9,8,8,128]{3,2,1,0:T(8,128)S(1)} %get-tuple-element.41), channel_id=1, source_target_pairs={{0,56},{8,0},{16,8},{24,16},{32,24},{40,32},{48,40},{56,48},{1,57}... | collective-permute-start | bytes 884744 | tf_op jit(solution)/shard_map/ppermute | solution.py:91
  33.1 14.4 %collective-permute-start.4 = (f32[56,32,128]{2,1,0:T(8,128)S(1)}, f32[56,32,128]{2,1,0:T(8,128)S(1)}, u32[]{:S(2)}, u32[]{:S(2)}) collective-permute-start(f32[56,32,128]{2,1,0:T(8,128)S(1)} %get-tuple-element.43), channel_id=1, source_target_pairs={{0,64},{64,128},{128,192},{192,256},{256,320},{320,384},{384,448},... | collective-permute-start | bytes 2752520 | tf_op jit(solution)/shard_map/ppermute | solution.py:91
  37.1 12.8 %collective-permute-start.5 = (f32[56,32,128]{2,1,0:T(8,128)S(1)}, f32[56,32,128]{2,1,0:T(8,128)S(1)}, u32[]{:S(2)}, u32[]{:S(2)}) collective-permute-start(f32[56,32,128]{2,1,0:T(8,128)S(1)} %get-tuple-element.44), channel_id=1, source_target_pairs={{0,448},{64,0},{128,64},{192,128},{256,192},{320,256},{384,320},{4... | collective-permute-start | bytes 2752520 | tf_op jit(solution)/shard_map/ppermute | solution.py:91
  59.2 7.8 %collective-permute-start.6 = (f32[22,8,128]{2,1,0:T(8,128)S(1)}, f32[22,8,128]{2,1,0:T(8,128)S(1)}, u32[]{:S(2)}, u32[]{:S(2)}) collective-permute-start(f32[22,8,128]{2,1,0:T(8,128)S(1)} %get-tuple-element.46), channel_id=1, source_target_pairs={{0,1},{1,2},{2,3},{3,4},{4,5},{5,6},{6,7},{7,0},{8,9},{9,10},{10,1... | collective-permute-start | bytes 270344 | tf_op jit(solution)/shard_map/ppermute | solution.py:91
  62.3 6.9 %collective-permute-start.7 = (f32[22,8,128]{2,1,0:T(8,128)S(1)}, f32[22,8,128]{2,1,0:T(8,128)S(1)}, u32[]{:S(2)}, u32[]{:S(2)}) collective-permute-start(f32[22,8,128]{2,1,0:T(8,128)S(1)} %get-tuple-element.47), channel_id=1, source_target_pairs={{0,7},{1,0},{2,1},{3,2},{4,3},{5,4},{6,5},{7,6},{8,15},{9,8},{10,9... | collective-permute-start | bytes 270344 | tf_op jit(solution)/shard_map/ppermute | solution.py:91
  72.4 12.5 %all-to-all-start = ((f32[8,24,128]{2,1,0:T(8,128)}), f32[8,24,128]{2,1,0:T(8,128)S(1)}, u32[]{:S(2)}, u32[]{:S(2)}) async-start(f32[8,24,128]{2,1,0:T(8,128)} %shard_map.100), calls=%async_computation | async-start | bytes 196608 | tf_op jit(solution)/shard_map/all_to_all | solution.py:910
  77.3 14.9 %collective-permute-start.9 = (f32[44,8,128]{2,1,0:T(8,128)S(1)}, f32[44,8,128]{2,1,0:T(8,128)S(1)}, u32[]{:S(2)}, u32[]{:S(2)}) collective-permute-start(f32[44,8,128]{2,1,0:T(8,128)S(1)} %get-tuple-element.48.coarse), channel_id=1, source_target_pairs={{0,56},{8,0},{16,8},{24,16},{32,24},{40,32},{48,40},{56,48},{1,57}... | collective-permute-start | bytes 540680 | tf_op jit(solution)/shard_map/ppermute | solution.py:91
  81.9 10.3 %collective-permute-start.8 = (f32[44,8,128]{2,1,0:T(8,128)S(1)}, f32[44,8,128]{2,1,0:T(8,128)S(1)}, u32[]{:S(2)}, u32[]{:S(2)}) collective-permute-start(f32[44,8,128]{2,1,0:T(8,128)S(1)} %get-tuple-element.48.coarse), channel_id=1, source_target_pairs={{0,8},{8,16},{16,24},{24,32},{32,40},{40,48},{48,56},{56,0},{1,9},... | collective-permute-start | bytes 540680 | tf_op jit(solution)/shard_map/ppermute | solution.py:91
  86.4 19.9 %all-to-all-start.1 = ((f32[8,160,128]{2,1,0:T(8,128)}), f32[8,160,128]{2,1,0:T(8,128)S(1)}, u32[]{:S(2)}, u32[]{:S(2)}) async-start(f32[8,160,128]{2,1,0:T(8,128)} %shard_map.101), calls=%async_computation.1 | async-start | bytes 1310720 | tf_op jit(solution)/shard_map/all_to_all | solution.py:915
  93.7 10.5 %collective-permute-start.10 = (f32[32,24,128]{2,1,0:T(8,128)S(1)}, f32[32,24,128]{2,1,0:T(8,128)S(1)}, u32[]{:S(2)}, u32[]{:S(2)}) collective-permute-start(f32[32,24,128]{2,1,0:T(8,128)S(1)} %get-tuple-element.49), channel_id=1, source_target_pairs={{0,64},{64,128},{128,192},{192,256},{256,320},{320,384},{384,448},... | collective-permute-start | bytes 1179656 | tf_op jit(solution)/shard_map/ppermute | solution.py:91
  95.3 11.0 %collective-permute-start.11 = (f32[32,24,128]{2,1,0:T(8,128)S(1)}, f32[32,24,128]{2,1,0:T(8,128)S(1)}, u32[]{:S(2)}, u32[]{:S(2)}) collective-permute-start(f32[32,24,128]{2,1,0:T(8,128)S(1)} %get-tuple-element.50), channel_id=1, source_target_pairs={{0,448},{64,0},{128,64},{192,128},{256,192},{320,256},{384,320},{4... | collective-permute-start | bytes 1179656 | tf_op jit(solution)/shard_map/ppermute | solution.py:91
  100.3 0.7 copy-start
  136.5 12.5 %all-to-all-start.3 = ((f32[8,1,128]{2,1,0:T(1,128)}), f32[8,1,128]{2,1,0:T(1,128)S(1)}, u32[]{:S(2)}, u32[]{:S(2)}) async-start(f32[8,1,128]{2,1,0:T(1,128)} %broadcast_in_dim.5), calls=%async_computation.3 | async-start | bytes 8192 | tf_op jit(solution)/shard_map/all_to_all | solution.py:939
